TPU v7x, 32 devices: a whole 2x2x4 slice. The times are simulated.
32 devices in a mesh: grid: 8 (over z, y), lev: 4 (over x, core).
Axes of the slice: x: 2, y: 2, z: 4, core: 2. Of those that a mesh axis runs over, the one named last changes fastest.
Arguments:
- prior_fields: float32 [128, 8, 4096], P('grid', 'lev'), may hold values from -6 to 6
- channel_weights: float32 [8, 4], P('lev'), may hold values from 0.1 to 1
- obs_owner: int32 [4], replicated, may hold values from 0 to 7
- obs_offset: int32 [4, 4, 64], replicated, may hold values from 0 to 511
- obs_value: float32 [4, 4, 64], P(None, 'lev'), may hold values from -30 to 30
- obs_error: float32 [4, 4, 64], P(None, 'lev'), may hold values from 0.5 to 2
- ancestors: int32 [4, 4, 8, 128], P(None, 'lev', 'grid'), may hold values from 0 to 127
Outputs:
- posterior_fields: float32 [128, 8, 4096], P('grid', 'lev')
All inputs are finite; a program needn't handle non-finite values.
Results may differ from a plain program's by a relative error of at most 0.0003.
Values sent between devices are 32-bit elements; how exact they have to be, the bound alone decides.
No kernel may reach another device: no remote copies, remote signals or barrier semaphores. Data moves between devices by JAX's collectives and lax.ppermute only.
A program may use at most 128 MiB of HBM per device.

v0:
```python
import functools

import jax
import jax.numpy as jnp
from jax import lax
from jax.experimental import pallas as pl
from jax.experimental.pallas import tpu as pltpu
from jax.sharding import PartitionSpec as P

NB = 4
HIGH = lax.Precision.HIGHEST
LANES = 128
SPARE = 16
F32 = jnp.float32
VMEM = pl.BlockSpec(memory_space=pltpu.VMEM)
SMEM = pl.BlockSpec(memory_space=pltpu.SMEM)
LIMIT = 48 * 1024 * 1024


def call(kernel, out_shapes, in_specs, scratch=(), flops=0, moved=0):
    many = isinstance(out_shapes, (list, tuple))
    return pl.pallas_call(
        kernel,
        out_shape=out_shapes,
        in_specs=in_specs,
        out_specs=[VMEM] * len(out_shapes) if many else VMEM,
        scratch_shapes=list(scratch),
        compiler_params=pltpu.CompilerParams(vmem_limit_bytes=LIMIT),
        cost_estimate=pl.CostEstimate(flops=flops, bytes_accessed=moved, transcendentals=0),
    )


def high_dot(a, b, dims=((1,), (0,))):
    return lax.dot_general(a, b, (dims, ((), ())), precision=HIGH, preferred_element_type=F32)


def pick_kernel(shape, owner, weights, offsets, extras, prior, out):
    n, slab, depth, block_cells, groups, count = shape
    width = groups * count
    group_of = lax.broadcasted_iota(jnp.int32, (1, width), 1) // count
    cell = lax.broadcasted_iota(jnp.int32, (block_cells, width), 0)
    for b in range(NB):
        start = pl.multiple_of(owner[b] * block_cells, LANES)
        pieces = []
        for level in range(depth):
            value = prior[:, level, pl.ds(start, block_cells)]
            first = value.astype(jnp.bfloat16)
            rest = value - first.astype(F32)
            second = rest.astype(jnp.bfloat16)
            third = (rest - second.astype(F32)).astype(jnp.bfloat16)
            pieces += [first.astype(F32), second.astype(F32), third.astype(F32)]
        onehot = (cell == offsets[b : b + 1, :]).astype(jnp.bfloat16)
        stacked = jnp.concatenate(pieces, axis=0).astype(jnp.bfloat16)
        found = jnp.dot(stacked, onehot, preferred_element_type=F32)
        total = jnp.zeros((slab, width), F32)
        for level in range(depth):
            base = 3 * level * slab
            exact = found[base : base + slab] + (
                found[base + slab : base + 2 * slab] + found[base + 2 * slab : base + 3 * slab]
            )
            row = jnp.zeros((1, width), F32)
            for g in range(groups):
                row = jnp.where(group_of == g, weights[level, g], row)
            total = total + exact * row
        for d in range(n):
            out[d, :, b * width : (b + 1) * width] = total
    for d in range(n):
        out[d, :, NB * width :] = extras[...]


def retile_kernel(shape, prior, out):
    n, slab, depth, block_cells = shape
    for r in range(n):
        for level in range(depth):
            out[r, level] = prior[:, level, r * block_cells : (r + 1) * block_cells]


PAIRS = [(e, b) for b in range(1, NB) for e in range(b)]


def turn_kernel(shape, owner, gathered, out):
    n, slab, width = shape
    members = n * slab
    for i in range(width // LANES):
        block = gathered[:, :, i * LANES : (i + 1) * LANES].reshape(members, LANES)
        out[i * LANES : (i + 1) * LANES, :] = block.T

    def slot(region, s):
        lane = width + (s // slab) * LANES
        row = s % slab
        return gathered[region, row : row + 1, lane : lane + LANES]

    for i, (e, b) in enumerate(PAIRS):
        out[width + i : width + i + 1, :] = slot(owner[b], e)
    for i in range(4):
        out[width + 8 + i : width + 9 + i, :] = slot(0, NB + i)
    out[width + 6 : width + 8, :] = jnp.zeros((2, LANES), F32)
    out[width + 12 : width + 16, :] = jnp.zeros((4, LANES), F32)


def region_column(owner, block):
    row = lax.broadcasted_iota(jnp.int32, (8, 1), 0)
    value = jnp.full((8, 1), block, jnp.int32)
    for b in range(1, NB):
        value = jnp.where(row == b - 1, owner[b], value)
    return value.astype(F32)


def tapers(owner, offs, region, b, block_cells, scale):
    cells = owner[b] * block_cells + offs
    position = cells.astype(F32) / block_cells
    distance = (region + 0.5 - position) / scale
    return jnp.exp(-0.5 * distance * distance)


def alpha_of(taper, count):
    return 0.8 * (1.0 - jnp.exp(-jnp.sum(taper, axis=1, keepdims=True) / count))


def onehot_rows(parents, members):
    member = lax.broadcasted_iota(jnp.int32, (members, members), 0)
    return (member == parents).astype(F32)


def mix_kernel(shape, owner, offsets, ancestors, fields, out):
    n, slab, depth, block_cells, count, scale = shape
    members = n * slab
    block, group = lax.axis_index("grid"), lax.axis_index("lev")
    region = jnp.full((8, 1), block, jnp.int32).astype(F32)
    row = lax.broadcasted_iota(jnp.int32, (members, members), 0)
    column = lax.broadcasted_iota(jnp.int32, (members, members), 1)
    eye = (row == column).astype(F32)
    total = None
    for b in range(NB):
        taper = tapers(owner, offsets[b, pl.ds(group, 1), :], region, b, block_cells, scale)
        alpha = alpha_of(taper, count)[0:1, 0:1]
        step = alpha * onehot_rows(ancestors[b : b + 1, :], members) + (1.0 - alpha) * eye
        total = step if total is None else high_dot(total, step)
    back = total.T
    for level in range(depth):
        value = fields[:, level].reshape(members, block_cells)
        out[:, level] = high_dot(back, value).reshape(n, slab, block_cells)


def chain_kernel(
    shape, owner, offsets, ancestors, own, near, far, cross, fields, out, taper_at, alpha_at, weight_at, column_at
):
    n, slab, depth, block_cells, groups, count, scale = shape
    members = n * slab
    width = groups * count
    base = NB * width
    block, group = lax.axis_index("grid"), lax.axis_index("lev")
    sources = [own, near, far, cross]
    index = [lax.bitwise_xor(group, p) for p in range(4)]
    region = region_column(owner, block)
    for b in range(NB):
        for g in range(groups):
            taper = tapers(owner, offsets[b, g : g + 1, :], region, b, block_cells, scale)
            taper_at[b, g] = taper
            alpha_at[b, g] = jnp.broadcast_to(alpha_of(taper, count), (8, LANES))
    parents = []
    for p, source in enumerate(sources):
        column_at[index[p]] = source[base + 8 : base + 16, :].T
        parents.append(source[base : base + 8, :].astype(jnp.int32))
    for b in range(NB):
        for c in range(groups):
            total = jnp.zeros((count, members), F32)
            tilted = jnp.zeros((count, members), F32)
            for p, source in enumerate(sources):
                start = b * width + c * count
                value = source[start : start + count, :]
                for e in range(b):
                    tilted = tilted + value * weight_at[e, index[p]][b - 1 : b, :]
                    alpha = alpha_at[e, index[p]][b - 1 : b, :]
                    line = PAIRS.index((e, b))
                    where = jnp.broadcast_to(parents[p][line : line + 1, :], (count, members))
                    moved = jnp.take_along_axis(value, where, axis=1, mode="promise_in_bounds")
                    value = alpha * moved + (1.0 - alpha) * value
                total = total + value
            if b > 0:
                total = total + jnp.sum(tilted, axis=1, keepdims=True)
            low = (b % 2) * count
            observed = column_at[c, low : low + count, b // 2 : b // 2 + 1]
            error = column_at[c, low : low + count, 2 + b // 2 : 3 + b // 2]
            scaled = (observed - total) / error
            log_weight = (-0.5 / count) * high_dot(taper_at[b, c], scaled * scaled)
            expo = jnp.exp(log_weight - jnp.max(log_weight, axis=1, keepdims=True))
            weight_at[b, c] = expo / jnp.sum(expo, axis=1, keepdims=True) - 1.0 / members
    pulled = weight_at[NB - 1, group]
    for b in reversed(range(NB - 1)):
        alpha = alpha_at[b, group]
        spread = high_dot(pulled, onehot_rows(ancestors[b : b + 1, :], members), ((1,), (1,)))
        pulled = weight_at[b, group] + alpha * spread + (1.0 - alpha) * pulled
    for level in range(depth):
        value = fields[:, level].reshape(members, block_cells)
        shift = high_dot(pulled, value)[3:4]
        for d in range(n):
            out[d, level : level + 1, :] = shift


def final_kernel(shape, moved, shift, out):
    n, slab, depth, block_cells = shape
    for r in range(n):
        for level in range(depth):
            value = moved[r, level] + shift[r, level : level + 1, :]
            out[:, level, r * block_cells : (r + 1) * block_cells] = value


def body(prior, channel_weights, obs_owner, obs_offset, obs_value, obs_error, ancestors):
    n, lev = lax.axis_size("grid"), lax.axis_size("lev")
    slab, depth, cells = prior.shape
    members = slab * n
    block_cells = cells // n
    groups = channel_weights.shape[1]
    count = obs_offset.shape[2]
    width = NB * groups * count
    scale = n / 2.0
    shape = jax.ShapeDtypeStruct
    parents = ancestors[:, 0, 0]

    slots = jnp.concatenate(
        [parents.astype(F32), obs_value.reshape(-1, LANES), obs_error.reshape(-1, LANES)], axis=0
    )
    blocks = -(-slots.shape[0] // slab)
    slots = jnp.pad(slots, ((0, blocks * slab - slots.shape[0]), (0, 0)))
    slots = slots.reshape(blocks, slab, LANES).transpose(1, 0, 2).reshape(slab, blocks * LANES)

    send = call(
        functools.partial(pick_kernel, (n, slab, depth, block_cells, groups, count)),
        shape((n, slab, width + blocks * LANES), F32),
        [SMEM, SMEM, VMEM, VMEM, VMEM],
        flops=10**8,
        moved=10**6,
    )(obs_owner, channel_weights, obs_offset.reshape(NB, -1), slots, prior)
    gathered = lax.all_to_all(send, "grid", 0, 0, tiled=True)

    send = call(
        functools.partial(retile_kernel, (n, slab, depth, block_cells)),
        shape((n, depth, slab, block_cells), F32),
        [VMEM],
        moved=10**6,
    )(prior)
    fields = lax.all_to_all(send, "grid", 0, 0, tiled=True)

    own = call(
        functools.partial(turn_kernel, (n, slab, width)),
        shape((width + SPARE, members), F32),
        [SMEM, VMEM],
        moved=10**6,
    )(obs_owner, gathered)
    far = lax.ppermute(own, "lev", [(j, j ^ 2) for j in range(lev)])
    near = lax.ppermute(own, "lev", [(j, j ^ 1) for j in range(lev)])
    cross = lax.ppermute(far, "lev", [(j, j ^ 1) for j in range(lev)])

    send = call(
        functools.partial(mix_kernel, (n, slab, depth, block_cells, count, scale)),
        shape((n, depth, slab, block_cells), F32),
        [SMEM, VMEM, VMEM, VMEM],
        flops=10**8,
        moved=10**6,
    )(obs_owner, obs_offset, parents, fields)
    moved = lax.all_to_all(send, "grid", 0, 0, tiled=True)

    send = call(
        functools.partial(chain_kernel, (n, slab, depth, block_cells, groups, count, scale)),
        shape((n, depth, block_cells), F32),
        [SMEM] + [VMEM] * 7,
        scratch=[
            pltpu.VMEM((NB, groups, 8, count), F32),
            pltpu.VMEM((NB, groups, 8, LANES), F32),
            pltpu.VMEM((NB, groups, 8, LANES), F32),
            pltpu.VMEM((groups, LANES, 8), F32),
        ],
        flops=10**9,
        moved=10**7,
    )(obs_owner, obs_offset, parents, own, near, far, cross, fields)
    shift = lax.all_to_all(send, "grid", 0, 0, tiled=True)

    return call(
        functools.partial(final_kernel, (n, slab, depth, block_cells)),
        shape((slab, depth, cells), F32),
        [VMEM, VMEM],
        moved=10**6,
    )(moved, shift)


def solution(mesh):
    in_specs = (
        P("grid", "lev", None),
        P("lev", None),
        P(),
        P(),
        P(None, "lev", None),
        P(None, "lev", None),
        P(None, "lev", "grid", None),
    )
    out_specs = P("grid", "lev", None)
    return jax.shard_map(body, mesh=mesh, in_specs=in_specs, out_specs=out_specs, check_vma=False)
```

profile of v0, /device:TPU:0, one launch (start us, length us, event | category | flops | bytes accessed | tf_op | source)
XLA Modules:
  0.0 81.1 jit_solution(12794904705275036333)
XLA Ops:
  0.0 0.0 copy-start.6
  0.0 0.0 copy-start.7
  0.0 0.7 convert_element_type.5
  0.7 0.0 copy-start.2
  0.7 0.5 broadcast.16
  1.2 0.0 copy-done.6
  1.2 0.7 reduce.7
  1.9 0.1 reshape.10
  2.0 0.0 copy-done.7
  2.0 0.7 reduce.6
  2.6 0.1 reshape.11
  2.7 0.0 copy-done.2
  2.7 0.1 reshape.9.offsets
  2.8 0.0 copy-start.4
  2.8 0.0 copy-start.5
  2.8 0.6 copy-done.4
  3.5 0.0 copy-done.5
  3.5 0.0 copy-start
  3.5 1.0 %copy-done = f32[16,2,4096]{2,1,0:T(2,128)S(1)} copy-done((f32[16,2,4096]{2,1,0:T(2,128)S(1)}, f32[16,2,4096]{2,1,0:T(2,128)}, u32[]{:S(2)}) %copy-start) | copy-done | bytes 524312
  4.6 2.9 %shard_map.75 = f32[8,16,1152]{2,1,0:T(8,128)} custom-call(s32[4]{0:T(128)S(1)} %copy-done.4, f32[2,4]{1,0:T(2,128)S(1)} %copy-done.5, s32[4,256]{1,0:T(4,128)S(1)} %reshape.9.offsets, f32[16,128]{1,0:T(8,128)S(1)} %select_maximum_fusion.extras, f32[16,2,4096]{2,1,0:T(2,128)S(1)} %copy-done), custom_call_target="tpu_custom_call" | custom-call | flops 100000000 | bytes 1000000 | tf_op jit(solution)/shard_map/pallas_call | solution.py:228
  7.5 0.0 copy-start.1
  7.5 7.4 %all-to-all-start.2 = ((f32[8,16,1152]{2,1,0:T(8,128)}), f32[8,16,1152]{2,1,0:T(8,128)S(1)}, u32[]{:S(2)}, u32[]{:S(2)}) async-start(f32[8,16,1152]{2,1,0:T(8,128)} %shard_map.75), calls=%async_computation.2 | async-start | bytes 1179648 | tf_op jit(solution)/shard_map/all_to_all | solution.py:235
  14.9 0.0 copy-done.1
  14.9 0.9 %shard_map.73 = f32[8,2,16,512]{3,2,1,0:T(8,128)} custom-call(f32[16,2,4096]{2,1,0:T(2,128)S(1)} %copy-done.1), custom_call_target="tpu_custom_call" | custom-call | bytes 1000000 | tf_op jit(solution)/shard_map/pallas_call | solution.py:237
  15.8 15.0 %all-to-all-done.2.gathered = f32[8,16,1152]{2,1,0:T(8,128)S(1)} async-done(((f32[8,16,1152]{2,1,0:T(8,128)}), f32[8,16,1152]{2,1,0:T(8,128)S(1)}, u32[]{:S(2)}, u32[]{:S(2)}) %all-to-all-start.2) | async-done | bytes 589856 | tf_op jit(solution)/shard_map/all_to_all | solution.py:235
  30.8 3.6 %all-to-all-start = ((f32[8,2,16,512]{3,2,1,0:T(8,128)}), f32[8,2,16,512]{3,2,1,0:T(8,128)S(1)}, u32[]{:S(2)}, u32[]{:S(2)}) async-start(f32[8,2,16,512]{3,2,1,0:T(8,128)} %shard_map.73), calls=%async_computation | async-start | bytes 1048576 | tf_op jit(solution)/shard_map/all_to_all | solution.py:243
  34.4 0.0 copy-start.3
  34.4 0.7 shard_map.76.own
  35.1 1.6 %collective-permute-start.1 = (f32[1040,128]{1,0:T(8,128)S(1)}, f32[1040,128]{1,0:T(8,128)S(1)}, u32[]{:S(2)}, u32[]{:S(2)}) collective-permute-start(f32[1040,128]{1,0:T(8,128)S(1)} %shard_map.76.own), channel_id=1, source_target_pairs={{0,2},{1,3},{2,0},{3,1},{4,6},{5,7},{6,4},{7,5},{8,10},{9,11},{10,... | collective-permute-start | bytes 1597448 | tf_op jit(solution)/shard_map/ppermute | solution.py:251
  36.7 12.4 %all-to-all-done.fields = f32[8,2,16,512]{3,2,1,0:T(8,128)S(1)} async-done(((f32[8,2,16,512]{3,2,1,0:T(8,128)}), f32[8,2,16,512]{3,2,1,0:T(8,128)S(1)}, u32[]{:S(2)}, u32[]{:S(2)}) %all-to-all-start) | async-done | bytes 524320 | tf_op jit(solution)/shard_map/all_to_all | solution.py:243
  49.1 0.0 copy-done.3
  49.1 2.7 %shard_map.74 = f32[8,2,16,512]{3,2,1,0:T(8,128)} custom-call(s32[4]{0:T(128)S(1)} %copy-done.4, s32[4,4,64]{2,1,0:T(4,128)S(1)} %copy-done.2, s32[4,128]{1,0:T(4,128)S(1)} %bitcast.2, f32[8,2,16,512]{3,2,1,0:T(8,128)S(1)} %all-to-all-done.fields), custom_call_target="tpu_custom_call" | custom-call | flops 100000000 | bytes 1000000 | tf_op jit(solution)/shard_map/pallas_call | solution.py:255
  51.8 3.6 %all-to-all-start.1 = ((f32[8,2,16,512]{3,2,1,0:T(8,128)}), f32[8,2,16,512]{3,2,1,0:T(8,128)S(1)}, u32[]{:S(2)}, u32[]{:S(2)}) async-start(f32[8,2,16,512]{3,2,1,0:T(8,128)} %shard_map.74), calls=%async_computation.1 | async-start | bytes 1048576 | tf_op jit(solution)/shard_map/all_to_all | solution.py:262
  55.4 0.0 collective-permute-start
  55.4 0.0 collective-permute-done.1.far
  55.4 0.5 collective-permute-start.2
  55.9 1.4 %collective-permute-done.near = f32[1040,128]{1,0:T(8,128)S(1)} collective-permute-done((f32[1040,128]{1,0:T(8,128)S(1)}, f32[1040,128]{1,0:T(8,128)S(1)}, u32[]{:S(2)}, u32[]{:S(2)}) %collective-permute-start) | collective-permute-done | bytes 532512 | tf_op jit(solution)/shard_map/ppermute | solution.py:252
  57.4 0.8 collective-permute-done.2.cross
  58.1 7.7 %shard_map.77 = f32[8,2,512]{2,1,0:T(2,128)S(1)} custom-call(s32[4]{0:T(128)S(1)} %copy-done.4, s32[4,4,64]{2,1,0:T(4,128)S(1)} %copy-done.2, s32[4,128]{1,0:T(4,128)S(1)} %bitcast.3, f32[1040,128]{1,0:T(8,128)S(1)} %shard_map.76.own, f32[1040,128]{1,0:T(8,128)S(1)} %collective-permute-done.near, f32[1040,128]{1,0:T(8,128)S(1)} %collective-permute-done.1.far, ...), custom_call_target="tpu_custom_call" | custom-call | flops 1000000000 | bytes 10000000 | tf_op jit(solution)/shard_map/pallas_call | solution.py:264
  65.8 4.3 %all-to-all-done.1.moved = f32[8,2,16,512]{3,2,1,0:T(8,128)S(1)} async-done(((f32[8,2,16,512]{3,2,1,0:T(8,128)}), f32[8,2,16,512]{3,2,1,0:T(8,128)S(1)}, u32[]{:S(2)}, u32[]{:S(2)}) %all-to-all-start.1) | async-done | bytes 524320 | tf_op jit(solution)/shard_map/all_to_all | solution.py:262
  70.1 10.1 %all_to_all.20.shift = f32[8,2,512]{2,1,0:T(2,128)S(1)} all-to-all(f32[8,2,512]{2,1,0:T(2,128)S(1)} %shard_map.77), channel_id=1, replica_groups=mesh['grid'=8,'lev'=4] {'grid'}, dimensions={0} | all-to-all | bytes 65536 | tf_op jit(solution)/shard_map/all_to_all | solution.py:277
  80.2 0.9 %shard_map.78 = f32[16,2,4096]{2,1,0:T(2,128)} custom-call(f32[8,2,16,512]{3,2,1,0:T(8,128)S(1)} %all-to-all-done.1.moved, f32[8,2,512]{2,1,0:T(2,128)S(1)} %all_to_all.20.shift), custom_call_target="tpu_custom_call" | custom-call | bytes 1000000 | tf_op jit(solution)/shard_map/pallas_call | solution.py:279
  (1 shorter events, 0.0 us)
Async XLA Ops:
  0.0 1.2 %copy-start.6 = (f32[4,1,64]{2,1,0:T(1,128)S(1)}, f32[4,1,64]{2,1,0:T(1,128)}, u32[]{:S(2)}) copy-start(f32[4,1,64]{2,1,0:T(1,128)} %param.11) | copy-start | bytes 3076
  0.0 2.0 %copy-start.7 = (f32[4,1,64]{2,1,0:T(1,128)S(1)}, f32[4,1,64]{2,1,0:T(1,128)}, u32[]{:S(2)}) copy-start(f32[4,1,64]{2,1,0:T(1,128)} %param.12) | copy-start | bytes 3076
  0.7 2.0 %copy-start.2 = (s32[4,4,64]{2,1,0:T(4,128)S(1)}, s32[4,4,64]{2,1,0:T(4,128)}, u32[]{:S(2)}) copy-start(s32[4,4,64]{2,1,0:T(4,128)} %offsets.3) | copy-start | bytes 12292
  2.8 0.7 copy-start.4
  2.8 0.7 copy-start.5
  3.5 1.0 %copy-start = (f32[16,2,4096]{2,1,0:T(2,128)S(1)}, f32[16,2,4096]{2,1,0:T(2,128)}, u32[]{:S(2)}) copy-start(f32[16,2,4096]{2,1,0:T(2,128)} %prior.3) | copy-start | bytes 1572868
  7.5 7.4 %copy-start.1 = (f32[16,2,4096]{2,1,0:T(2,128)S(1)}, f32[16,2,4096]{2,1,0:T(2,128)}, u32[]{:S(2)}) copy-start(f32[16,2,4096]{2,1,0:T(2,128)} %prior.3) | copy-start | bytes 1572868
  7.5 23.3 %all-to-all-start.2 = ((f32[8,16,1152]{2,1,0:T(8,128)}), f32[8,16,1152]{2,1,0:T(8,128)S(1)}, u32[]{:S(2)}, u32[]{:S(2)}) async-start(f32[8,16,1152]{2,1,0:T(8,128)} %shard_map.75), calls=%async_computation.2 | async-start | bytes 1179648 | tf_op jit(solution)/shard_map/all_to_all | solution.py:235
  30.8 18.3 %all-to-all-start = ((f32[8,2,16,512]{3,2,1,0:T(8,128)}), f32[8,2,16,512]{3,2,1,0:T(8,128)S(1)}, u32[]{:S(2)}, u32[]{:S(2)}) async-start(f32[8,2,16,512]{3,2,1,0:T(8,128)} %shard_map.73), calls=%async_computation | async-start | bytes 1048576 | tf_op jit(solution)/shard_map/all_to_all | solution.py:243
  34.4 14.7 %copy-start.3 = (s32[4,1,1,128]{3,2,1,0:T(1,128)S(1)}, s32[4,1,1,128]{3,2,1,0:T(1,128)}, u32[]{:S(2)}) copy-start(s32[4,1,1,128]{3,2,1,0:T(1,128)} %param.13) | copy-start | bytes 6148
  35.1 20.3 %collective-permute-start.1 = (f32[1040,128]{1,0:T(8,128)S(1)}, f32[1040,128]{1,0:T(8,128)S(1)}, u32[]{:S(2)}, u32[]{:S(2)}) collective-permute-start(f32[1040,128]{1,0:T(8,128)S(1)} %shard_map.76.own), channel_id=1, source_target_pairs={{0,2},{1,3},{2,0},{3,1},{4,6},{5,7},{6,4},{7,5},{8,10},{9,11},{10,... | collective-permute-start | bytes 1597448 | tf_op jit(solution)/shard_map/ppermute | solution.py:251
  51.8 18.3 %all-to-all-start.1 = ((f32[8,2,16,512]{3,2,1,0:T(8,128)}), f32[8,2,16,512]{3,2,1,0:T(8,128)S(1)}, u32[]{:S(2)}, u32[]{:S(2)}) async-start(f32[8,2,16,512]{3,2,1,0:T(8,128)} %shard_map.74), calls=%async_computation.1 | async-start | bytes 1048576 | tf_op jit(solution)/shard_map/all_to_all | solution.py:262
  55.4 1.9 %collective-permute-start = (f32[1040,128]{1,0:T(8,128)S(1)}, f32[1040,128]{1,0:T(8,128)S(1)}, u32[]{:S(2)}, u32[]{:S(2)}) collective-permute-start(f32[1040,128]{1,0:T(8,128)S(1)} %shard_map.76.own), channel_id=1, source_target_pairs={{0,1},{1,0},{2,3},{3,2},{4,5},{5,4},{6,7},{7,6},{8,9},{9,8},{10,11... | collective-permute-start | bytes 1597448 | tf_op jit(solution)/shard_map/ppermute | solution.py:252
  55.4 2.7 %collective-permute-start.2 = (f32[1040,128]{1,0:T(8,128)S(1)}, f32[1040,128]{1,0:T(8,128)S(1)}, u32[]{:S(2)}, u32[]{:S(2)}) collective-permute-start(f32[1040,128]{1,0:T(8,128)S(1)} %collective-permute-done.1.far), channel_id=1, source_target_pairs={{0,1},{1,0},{2,3},{3,2},{4,5},{5,4},{6,7},{7,6},{8,9},{9,8},{10,11... | collective-permute-start | bytes 1597448 | tf_op jit(solution)/shard_map/ppermute | solution.py:253
where the time goes:
time: 81.7 us; the launch traced here: 81.1 us
  waiting for transfers between devices  33.9 us (41%)
  starting transfers between devices  16.7 us (20%)
  Pallas kernels  15.8 us (19%)
  blocking collectives  10.1 us (12%)
  local copies, waits for them, and re-layouts  2.5 us (3%)
  other arithmetic  2.05 us (3%)
    all_to_all x1, waiting for transfers between devices, body(): gathered = lax.all_to_all(send, 'grid', 0, 0, tiled=True)  15 us
    all_to_all x1, waiting for transfers between devices, body(): fields = lax.all_to_all(send, 'grid', 0, 0, tiled=True)  12.4 us
    all_to_all x1, blocking collectives, body(): shift = lax.all_to_all(send, 'grid', 0, 0, tiled=True)  10.1 us
    pallas_call x1, Pallas kernels, body(): call(functools.partial(chain_kernel, (n, slab, depth, block_cells, groups...  7.66 us
    all_to_all x1, starting transfers between devices, body(): gathered = lax.all_to_all(send, 'grid', 0, 0, tiled=True)  7.41 us
    all_to_all x1, waiting for transfers between devices, body(): moved = lax.all_to_all(send, 'grid', 0, 0, tiled=True)  4.32 us
    all_to_all x1, starting transfers between devices, body(): moved = lax.all_to_all(send, 'grid', 0, 0, tiled=True)  3.64 us
    all_to_all x1, starting transfers between devices, body(): fields = lax.all_to_all(send, 'grid', 0, 0, tiled=True)  3.64 us
  transfers between devices with their start and end apart: 6, of which 5 were waited for; matrix products, arithmetic and copies ran while one was open for 0% of the time, Pallas kernels for 15%

commit v1 on v0

v1 whole, which is shorter than its diff:
```python
import functools

import jax
import jax.numpy as jnp
from jax import lax
from jax.experimental import pallas as pl
from jax.experimental.pallas import tpu as pltpu
from jax.sharding import PartitionSpec as P

NB = 4
HIGH = lax.Precision.HIGHEST
LANES = 128
F32 = jnp.float32
VMEM = pl.BlockSpec(memory_space=pltpu.VMEM)
SMEM = pl.BlockSpec(memory_space=pltpu.SMEM)
LIMIT = 48 * 1024 * 1024

PAIRS = [(e, b) for b in range(1, NB) for e in range(b)]
PARENT, ALPHA, LATER, VALUE, OWN, SPARE = 0, 6, 12, 18, 22, 32


def call(kernel, out_shapes, in_specs, scratch=(), flops=0, moved=0):
    many = isinstance(out_shapes, (list, tuple))
    return pl.pallas_call(
        kernel,
        out_shape=out_shapes,
        in_specs=in_specs,
        out_specs=[VMEM] * len(out_shapes) if many else VMEM,
        scratch_shapes=list(scratch),
        compiler_params=pltpu.CompilerParams(vmem_limit_bytes=LIMIT),
        cost_estimate=pl.CostEstimate(flops=flops, bytes_accessed=moved, transcendentals=0),
    )


def high_dot(a, b):
    return lax.dot_general(a, b, (((1,), (0,)), ((), ())), precision=HIGH, preferred_element_type=F32)


def lane_take(value, row):
    where = jnp.broadcast_to(row, value.shape)
    return jnp.take_along_axis(value, where, axis=1, mode="promise_in_bounds")


def pick_kernel(shape, owner, weights, offsets, ancestors, prior, out):
    slab, depth, block_cells, groups, count = shape
    width = groups * count
    per = LANES // count
    for b in range(NB):
        start = pl.multiple_of(owner[b] * block_cells, LANES)
        levels = [prior[:, level, pl.ds(start, block_cells)] for level in range(depth)]
        for c in range(width // LANES):
            cell = jnp.concatenate([offsets[b, g : g + 1, :] for g in range(c * per, (c + 1) * per)], axis=1)
            low, high = lax.rem(cell, LANES), lax.div(cell, LANES)
            total = jnp.zeros((slab, LANES), F32)
            for level in range(depth):
                found = jnp.zeros((slab, LANES), F32)
                for h in range(block_cells // LANES):
                    part = lane_take(levels[level][:, h * LANES : (h + 1) * LANES], low)
                    found = jnp.where(high == h, part, found)
                row = jnp.concatenate(
                    [
                        jnp.broadcast_to(weights[level : level + 1, g : g + 1], (1, count))
                        for g in range(c * per, (c + 1) * per)
                    ],
                    axis=1,
                )
                total = total + found * row
            lane = b * width + c * LANES
            out[:, lane : lane + LANES] = total
    lane = NB * width
    out[:, lane:] = jnp.zeros((slab, out.shape[1] - lane), F32)
    for b in range(NB):
        row, block = b % slab, lane + (b // slab) * LANES
        out[row : row + 1, block : block + LANES] = ancestors[b].astype(F32)


def retile_kernel(shape, prior, out):
    n, slab, depth, block_cells = shape
    for r in range(n):
        for level in range(depth):
            out[r, level] = prior[:, level, r * block_cells : (r + 1) * block_cells]


def prep_kernel(shape, owner, offsets, values, errors, ancestors, rows, steps):
    block_cells, count, scale, members = shape
    block, group = lax.axis_index("grid"), lax.axis_index("lev")
    index = lax.broadcasted_iota(jnp.int32, (8, 1), 0)
    region = jnp.full((8, 1), block, jnp.int32)
    for b in range(1, NB):
        region = jnp.where(index == b - 1, owner[b], region)
    centre = region.astype(F32) + 0.5
    rows[...] = jnp.zeros((SPARE, LANES), F32)
    row = lax.broadcasted_iota(jnp.int32, (members, members), 0)
    column = lax.broadcasted_iota(jnp.int32, (members, members), 1)
    turned = (row == column).astype(F32)
    for b in range(NB):
        cells = owner[b] * block_cells + offsets[b, pl.ds(group, 1), :]
        distance = (centre - cells.astype(F32) / block_cells) / scale
        taper = jnp.exp(-0.5 * distance * distance)
        alpha = 0.8 * (1.0 - jnp.exp(-jnp.sum(taper, axis=1, keepdims=True) / count))
        error = errors[b]
        part = (-0.5 / count) * (taper / (error * error))
        for later in range(b + 1, NB):
            i = PAIRS.index((b, later))
            rows[ALPHA + i : ALPHA + i + 1, :] = jnp.broadcast_to(alpha[later - 1 : later], (1, LANES))
            rows[LATER + i : LATER + i + 1, :count] = part[later - 1 : later]
        rows[VALUE + b : VALUE + b + 1, :count] = values[b]
        rows[OWN + b : OWN + b + 1, :count] = part[NB - 1 : NB]
        steps[b] = turned.T
        own = alpha[NB - 1 : NB]
        turned = own * lane_take(turned, ancestors[b]) + (1.0 - own) * turned
    steps[NB] = turned.T


def turn_kernel(shape, owner, rows, *refs):
    n, slab, width = shape
    pieces, out, held = refs[:-2], refs[-2], refs[-1]
    members = n * slab
    if len(pieces) == 1:
        held[...] = pieces[0][...]
    else:
        block = lax.axis_index("grid")
        for i, piece in enumerate(pieces):
            held[lax.bitwise_xor(block, i)] = piece[...]
    for i in range(width // LANES):
        lanes = slice(i * LANES, (i + 1) * LANES)
        out[lanes, :] = held[:, :, lanes].reshape(members, LANES).T
    out[width:, :] = rows[...]
    for i, (e, b) in enumerate(PAIRS):
        lane = width + (e // slab) * LANES
        line = e % slab
        out[width + PARENT + i : width + PARENT + i + 1, :] = held[owner[b], line : line + 1, lane : lane + LANES]


def mix_kernel(shape, steps, fields, out):
    n, slab, depth, block_cells = shape
    for level in range(depth):
        value = fields[:, level].reshape(n * slab, block_cells)
        out[:, level] = high_dot(steps[NB], value).reshape(n, slab, block_cells)


def chain_kernel(shape, own, near, far, cross, steps, fields, out):
    n, slab, depth, block_cells, groups, count = shape
    members = n * slab
    width = groups * count
    base = NB * width
    group = lax.axis_index("lev")
    sources = [own, near, far, cross]
    columns = [source[base : base + SPARE, :].T for source in sources]
    parents, alphas = [], []
    for source in sources:
        parents.append(source[base + PARENT : base + PARENT + 8, :].astype(jnp.int32))
        alphas.append(source[base + ALPHA : base + ALPHA + 6, :])
    tilts = {}
    pulled = []
    for b in range(NB):
        kinds = [(q, later) for q in range(groups) for later in range(b + 1, NB)] + [(0, None)]
        height = -(-len(kinds) // 8) * 8
        index = lax.broadcasted_iota(jnp.int32, (height, members), 0)
        logs = jnp.zeros((height, members), F32)
        for q in range(groups if b < NB - 1 else 1):
            start = pl.multiple_of(b * width + lax.bitwise_xor(group, q) * count, count)
            total = jnp.zeros((count, members), F32)
            tilted = jnp.zeros((count, members), F32)
            for p, source in enumerate(sources):
                value = source[pl.ds(start, count), :]
                for e in range(b):
                    i = PAIRS.index((e, b))
                    tilted = tilted + value * tilts[e, p, b]
                    alpha = alphas[p][i : i + 1]
                    moved = lane_take(value, parents[p][i : i + 1])
                    value = alpha * moved + (1.0 - alpha) * value
                total = total + value
            if b > 0:
                total = total + jnp.sum(tilted, axis=1, keepdims=True)
            miss = columns[q][:count, VALUE + b : VALUE + b + 1] - total
            square = miss * miss
            for row, (owner_group, later) in enumerate(kinds):
                if owner_group != q:
                    continue
                at = OWN + b if later is None else LATER + PAIRS.index((b, later))
                log = jnp.sum(columns[q][:count, at : at + 1] * square, axis=0, keepdims=True)
                logs = jnp.where(index == row, log, logs)
        expo = jnp.exp(logs - jnp.max(logs, axis=1, keepdims=True))
        tilt = expo / jnp.sum(expo, axis=1, keepdims=True) - 1.0 / members
        for row, (q, later) in enumerate(kinds):
            if later is None:
                pulled.append(tilt[row : row + 1])
            else:
                tilts[b, q, later] = tilt[row : row + 1]
    pull = jnp.zeros((8, members), F32)
    for b in range(NB):
        pull = pull + high_dot(jnp.broadcast_to(pulled[b], (8, members)), steps[b])
    for level in range(depth):
        value = fields[:, level].reshape(members, block_cells)
        shift = high_dot(pull, value)[0:1]
        for d in range(n):
            out[d, level : level + 1, :] = shift


def final_kernel(shape, moved, shift, out):
    n, slab, depth, block_cells = shape
    for r in range(n):
        for level in range(depth):
            value = moved[r, level] + shift[r, level : level + 1, :]
            out[:, level, r * block_cells : (r + 1) * block_cells] = value


def gather_pieces(piece, n):
    if n != 8:
        return [lax.all_to_all(jnp.broadcast_to(piece[None], (n,) + piece.shape), "grid", 0, 0, tiled=True)]
    pieces = [piece]
    for far in (2, 4, 6):
        pieces.append(lax.ppermute(piece, "grid", [(j, j ^ far) for j in range(n)]))
    result = []
    for part in pieces:
        result += [part, lax.ppermute(part, "grid", [(j, j ^ 1) for j in range(n)])]
    return result


def body(prior, channel_weights, obs_owner, obs_offset, obs_value, obs_error, ancestors):
    n, lev = lax.axis_size("grid"), lax.axis_size("lev")
    slab, depth, cells = prior.shape
    members = slab * n
    block_cells = cells // n
    groups = channel_weights.shape[1]
    count = obs_offset.shape[2]
    width = NB * groups * count
    scale = n / 2.0
    shape = jax.ShapeDtypeStruct
    parents = ancestors[:, 0]
    wide = width + -(-NB // slab) * LANES

    piece = call(
        functools.partial(pick_kernel, (slab, depth, block_cells, groups, count)),
        shape((slab, wide), F32),
        [SMEM, VMEM, VMEM, VMEM, VMEM],
        moved=10**6,
    )(obs_owner, channel_weights, obs_offset, parents, prior)
    pieces = gather_pieces(piece, n)

    send = call(
        functools.partial(retile_kernel, (n, slab, depth, block_cells)),
        shape((n, depth, slab, block_cells), F32),
        [VMEM],
        moved=10**6,
    )(prior)
    fields = lax.all_to_all(send, "grid", 0, 0, tiled=True)

    rows, steps = call(
        functools.partial(prep_kernel, (block_cells, count, scale, members)),
        [shape((SPARE, LANES), F32), shape((NB + 1, members, members), F32)],
        [SMEM, VMEM, VMEM, VMEM, VMEM],
        moved=10**6,
    )(obs_owner, obs_offset, obs_value, obs_error, parents)

    own = call(
        functools.partial(turn_kernel, (n, slab, width)),
        shape((width + SPARE, members), F32),
        [SMEM] + [VMEM] * (1 + len(pieces)),
        scratch=[pltpu.VMEM((n, slab, wide), F32)],
        moved=10**6,
    )(obs_owner, rows, *pieces)
    far = lax.ppermute(own, "lev", [(j, j ^ 2) for j in range(lev)])
    near = lax.ppermute(own, "lev", [(j, j ^ 1) for j in range(lev)])
    cross = lax.ppermute(far, "lev", [(j, j ^ 1) for j in range(lev)])

    send = call(
        functools.partial(mix_kernel, (n, slab, depth, block_cells)),
        shape((n, depth, slab, block_cells), F32),
        [VMEM, VMEM],
        flops=10**8,
        moved=10**6,
    )(steps, fields)
    moved = lax.all_to_all(send, "grid", 0, 0, tiled=True)

    send = call(
        functools.partial(chain_kernel, (n, slab, depth, block_cells, groups, count)),
        shape((n, depth, block_cells), F32),
        [VMEM] * 6,
        flops=10**9,
        moved=10**7,
    )(own, near, far, cross, steps, fields)
    shift = lax.all_to_all(send, "grid", 0, 0, tiled=True)

    return call(
        functools.partial(final_kernel, (n, slab, depth, block_cells)),
        shape((slab, depth, cells), F32),
        [VMEM, VMEM],
        moved=10**6,
    )(moved, shift)


def solution(mesh):
    in_specs = (
        P("grid", "lev", None),
        P("lev", None),
        P(),
        P(),
        P(None, "lev", None),
        P(None, "lev", None),
        P(None, "lev", "grid", None),
    )
    out_specs = P("grid", "lev", None)
    return jax.shard_map(body, mesh=mesh, in_specs=in_specs, out_specs=out_specs, check_vma=False)
```

time: 81.7 us -> 69.6 us (0.85)
  waiting for transfers between devices: 33.9 us -> 22.8 us
  Pallas kernels: 15.8 us -> 9.05 us
  blocking collectives: 10.1 us -> 13.9 us
  starting transfers between devices: 16.7 us -> 20.3 us
  other arithmetic: 2.05 us -> 0 us
    all_to_all x2 -> x1, waiting for transfers between devices: 19.3 us -> 6.11 us  [body(): shift = lax.all_to_all(send, 'grid', 0, 0, tiled=True)]
    ppermute x0 -> x7, starting transfers between devices: none -> 10.3 us  [the longest x3 5.68 us: gather_pieces(): pieces.append(lax.ppermute(piece, 'grid', [(j, j ^ far) for j in range(n)]))]
    all_to_all x2 -> x1, starting transfers between devices: 11.1 us -> 3.68 us  [body(): shift = lax.all_to_all(send, 'grid', 0, 0, tiled=True)]
    ppermute x0 -> x7, waiting for transfers between devices: none -> 5.44 us  [the longest x3 3.17 us: gather_pieces(): pieces.append(lax.ppermute(piece, 'grid', [(j, j ^ far) for j in range(n)]))]
    all_to_all x1, waiting for transfers between devices: 12.4 us -> 7.83 us  [body(): fields = lax.all_to_all(send, 'grid', 0, 0, tiled=True)]
    pallas_call x1, Pallas kernels: 7.66 us -> 3.7 us  [body(): call(functools.partial(chain_kernel, (n, slab, depth, block_cells, groups...]
    all_to_all x1, blocking collectives: 10.1 us -> 13.9 us  [body(): moved = lax.all_to_all(send, 'grid', 0, 0, tiled=True)]
    ppermute x1, waiting for transfers between devices: 0.01 us -> 3.42 us  [body(): far = lax.ppermute(own, 'lev', [(j, j ^ 2) for j in range(lev)])]
  transfers between devices with their start and end apart: 6 -> 12, of which waited for: 5 -> 6; matrix products, arithmetic and copies ran while one was open for 0% -> 0% of each run, Pallas kernels for 15% -> 4%
where the time goes in v1:
time: 69.6 us; the launch traced here: 69.2 us
  waiting for transfers between devices  22.8 us (33%)
  starting transfers between devices  20.3 us (29%)
  blocking collectives  13.9 us (20%)
  Pallas kernels  9.05 us (13%)
  local copies, waits for them, and re-layouts  3.11 us (4%)
    all_to_all x1, blocking collectives, body(): moved = lax.all_to_all(send, 'grid', 0, 0, tiled=True)  13.9 us
    all_to_all x1, waiting for transfers between devices, body(): fields = lax.all_to_all(send, 'grid', 0, 0, tiled=True)  7.83 us
    all_to_all x1, waiting for transfers between devices, body(): shift = lax.all_to_all(send, 'grid', 0, 0, tiled=True)  6.11 us
    ppermute x3, starting transfers between devices, gather_pieces(): pieces.append(lax.ppermute(piece, 'grid', [(j, j ^ far) for j in range(n)]))  5.68 us
    all_to_all x1, starting transfers between devices, body(): fields = lax.all_to_all(send, 'grid', 0, 0, tiled=True)  4.77 us
    ppermute x4, starting transfers between devices, gather_pieces(): result += [part, lax.ppermute(part, 'grid', [(j, j ^ 1) for j in range(n)])]  4.6 us
    pallas_call x1, Pallas kernels, body(): call(functools.partial(chain_kernel, (n, slab, depth, block_cells, groups...  3.7 us
    all_to_all x1, starting transfers between devices, body(): shift = lax.all_to_all(send, 'grid', 0, 0, tiled=True)  3.68 us
  transfers between devices with their start and end apart: 12, of which 6 were waited for; matrix products, arithmetic and copies ran while one was open for 0% of the time, Pallas kernels for 4%

profile of v1, /device:TPU:0, one launch (start us, length us, event | category | flops | bytes accessed | tf_op | source)
XLA Modules:
  0.0 69.2 jit_solution(16191075862570274156)
XLA Ops:
  0.0 0.0 copy-start.8
  0.0 0.0 copy-start.5
  0.0 0.7 copy-done.8
  0.7 0.0 copy-done.5
  0.7 0.0 copy-start
  0.7 1.0 %copy-done = f32[16,2,4096]{2,1,0:T(2,128)S(1)} copy-done((f32[16,2,4096]{2,1,0:T(2,128)S(1)}, f32[16,2,4096]{2,1,0:T(2,128)}, u32[]{:S(2)}) %copy-start) | copy-done | bytes 524312
  1.7 0.0 copy-start.2
  1.7 0.7 %copy-done.2 = s32[4,4,64]{2,1,0:T(4,128)S(1)} copy-done((s32[4,4,64]{2,1,0:T(4,128)S(1)}, s32[4,4,64]{2,1,0:T(4,128)}, u32[]{:S(2)}) %copy-start.2) | copy-done | bytes 4120
  2.4 0.0 copy-start.3
  2.4 0.7 copy-done.3
  3.1 0.0 copy-start.4
  3.1 0.0 copy-start.6
  3.1 1.2 %shard_map.76.refs_0_ = f32[16,1152]{1,0:T(8,128)S(1)} custom-call(s32[4]{0:T(128)S(1)} %copy-done.5, f32[2,4]{1,0:T(2,128)S(1)} %copy-done.8, s32[4,4,64]{2,1,0:T(4,128)S(1)} %copy-done.2, s32[4,1,128]{2,1,0:T(1,128)S(1)} %bitcast.1, f32[16,2,4096]{2,1,0:T(2,128)S(1)} %copy-done), custom_call_target="tpu_custom_call" | custom-call | bytes 1000000 | tf_op jit(solution)/shard_map/pallas_call | solution.py:234
  4.3 3.1 %collective-permute-start.1 = (f32[16,1152]{1,0:T(8,128)S(1)}, f32[16,1152]{1,0:T(8,128)S(1)}, u32[]{:S(2)}, u32[]{:S(2)}) collective-permute-start(f32[16,1152]{1,0:T(8,128)S(1)} %shard_map.76.refs_0_), channel_id=1, source_target_pairs={{0,8},{4,12},{8,0},{12,4},{16,24},{20,28},{24,16},{28,20},{1,9},{5... | collective-permute-start | bytes 221192 | tf_op jit(solution)/shard_map/ppermute | solution.py:214
  7.4 2.6 %collective-permute-start.3 = (f32[16,1152]{1,0:T(8,128)S(1)}, f32[16,1152]{1,0:T(8,128)S(1)}, u32[]{:S(2)}, u32[]{:S(2)}) collective-permute-start(f32[16,1152]{1,0:T(8,128)S(1)} %shard_map.76.refs_0_), channel_id=1, source_target_pairs={{0,16},{4,20},{8,24},{12,28},{16,0},{20,4},{24,8},{28,12},{1,17},{... | collective-permute-start | bytes 221192 | tf_op jit(solution)/shard_map/ppermute | solution.py:214
  10.0 0.0 collective-permute-start.5
  10.0 1.7 %collective-permute-start = (f32[16,1152]{1,0:T(8,128)S(1)}, f32[16,1152]{1,0:T(8,128)S(1)}, u32[]{:S(2)}, u32[]{:S(2)}) collective-permute-start(f32[16,1152]{1,0:T(8,128)S(1)} %shard_map.76.refs_0_), channel_id=1, source_target_pairs={{0,4},{4,0},{8,12},{12,8},{16,20},{20,16},{24,28},{28,24},{1,5},{5... | collective-permute-start | bytes 221192 | tf_op jit(solution)/shard_map/ppermute | solution.py:217
  11.7 0.0 collective-permute-done.1.refs_2_
  11.7 0.3 collective-permute-start.2
  12.0 3.2 %collective-permute-done.3.refs_4_ = f32[16,1152]{1,0:T(8,128)S(1)} collective-permute-done((f32[16,1152]{1,0:T(8,128)S(1)}, f32[16,1152]{1,0:T(8,128)S(1)}, u32[]{:S(2)}, u32[]{:S(2)}) %collective-permute-start.3) | collective-permute-done | bytes 73760 | tf_op jit(solution)/shard_map/ppermute | solution.py:214
  15.2 1.5 %collective-permute-start.4 = (f32[16,1152]{1,0:T(8,128)S(1)}, f32[16,1152]{1,0:T(8,128)S(1)}, u32[]{:S(2)}, u32[]{:S(2)}) collective-permute-start(f32[16,1152]{1,0:T(8,128)S(1)} %collective-permute-done.3.refs_4_), channel_id=1, source_target_pairs={{0,4},{4,0},{8,12},{12,8},{16,20},{20,16},{24,28},{28,24},{1,5},{5... | collective-permute-start | bytes 221192 | tf_op jit(solution)/shard_map/ppermute | solution.py:217
  16.7 0.0 collective-permute-done.5.refs_6_
  16.7 1.1 %collective-permute-start.6 = (f32[16,1152]{1,0:T(8,128)S(1)}, f32[16,1152]{1,0:T(8,128)S(1)}, u32[]{:S(2)}, u32[]{:S(2)}) collective-permute-start(f32[16,1152]{1,0:T(8,128)S(1)} %collective-permute-done.5.refs_6_), channel_id=1, source_target_pairs={{0,4},{4,0},{8,12},{12,8},{16,20},{20,16},{24,28},{28,24},{1,5},{5... | collective-permute-start | bytes 221192 | tf_op jit(solution)/shard_map/ppermute | solution.py:217
  17.8 0.0 copy-done.4
  17.8 0.0 copy-done.6
  17.8 0.0 copy-done.7
  17.8 1.0 %shard_map.73 = (f32[32,128]{1,0:T(8,128)S(1)}, f32[5,128,128]{2,1,0:T(8,128)S(1)}) custom-call(s32[4]{0:T(128)S(1)} %copy-done.5, s32[4,4,64]{2,1,0:T(4,128)S(1)} %copy-done.2, f32[4,1,64]{2,1,0:T(1,128)S(1)} %copy-done.6, f32[4,1,64]{2,1,0:T(1,128)S(1)} %copy-done.7, s32[4,1,128]{2,1,0:T(1,128)S(1)} %bitcast.2), custom_call_target="tpu_custom_call" | custom-call | bytes 1000000 | tf_op jit(solution)/shard_map/pallas_call | solution.py:250
  18.8 0.0 collective-permute-done.refs_1_
  18.8 0.0 collective-permute-done.2.refs_3_
  18.8 0.7 %collective-permute-done.4.refs_5_ = f32[16,1152]{1,0:T(8,128)S(1)} collective-permute-done((f32[16,1152]{1,0:T(8,128)S(1)}, f32[16,1152]{1,0:T(8,128)S(1)}, u32[]{:S(2)}, u32[]{:S(2)}) %collective-permute-start.4) | collective-permute-done | bytes 73760 | tf_op jit(solution)/shard_map/ppermute | solution.py:217
  19.5 1.5 %collective-permute-done.6.refs_7_ = f32[16,1152]{1,0:T(8,128)S(1)} collective-permute-done((f32[16,1152]{1,0:T(8,128)S(1)}, f32[16,1152]{1,0:T(8,128)S(1)}, u32[]{:S(2)}, u32[]{:S(2)}) %collective-permute-start.6) | collective-permute-done | bytes 73760 | tf_op jit(solution)/shard_map/ppermute | solution.py:217
  21.1 0.8 %shard_map.77.own = f32[1056,128]{1,0:T(8,128)S(1)} custom-call(s32[4]{0:T(128)S(1)} %copy-done.5, f32[32,128]{1,0:T(8,128)S(1)} %get-tuple-element.8.rows, f32[16,1152]{1,0:T(8,128)S(1)} %shard_map.76.refs_0_, f32[16,1152]{1,0:T(8,128)S(1)} %collective-permute-done.refs_1_, f32[16,1152]{1,0:T(8,128)S(1)} %collective-permute-done.1.refs_2_, ...), custom_call_target="tpu_custom_call" | custom-call | bytes 1000000 | tf_op jit(solution)/shard_map/pallas_call | solution.py:257
  21.8 1.6 %collective-permute-start.8 = (f32[1056,128]{1,0:T(8,128)S(1)}, f32[1056,128]{1,0:T(8,128)S(1)}, u32[]{:S(2)}, u32[]{:S(2)}) collective-permute-start(f32[1056,128]{1,0:T(8,128)S(1)} %shard_map.77.own), channel_id=1, source_target_pairs={{0,2},{1,3},{2,0},{3,1},{4,6},{5,7},{6,4},{7,5},{8,10},{9,11},{10,... | collective-permute-start | bytes 1622024 | tf_op jit(solution)/shard_map/ppermute | solution.py:264
  23.4 0.0 copy-done.1
  23.4 0.9 %shard_map.74 = f32[8,2,16,512]{3,2,1,0:T(8,128)} custom-call(f32[16,2,4096]{2,1,0:T(2,128)S(1)} %copy-done.1), custom_call_target="tpu_custom_call" | custom-call | bytes 1000000 | tf_op jit(solution)/shard_map/pallas_call | solution.py:242
  24.3 4.8 %all-to-all-start = ((f32[8,2,16,512]{3,2,1,0:T(8,128)}), f32[8,2,16,512]{3,2,1,0:T(8,128)S(1)}, u32[]{:S(2)}, u32[]{:S(2)}) async-start(f32[8,2,16,512]{3,2,1,0:T(8,128)} %shard_map.74), calls=%async_computation | async-start | bytes 1048576 | tf_op jit(solution)/shard_map/all_to_all | solution.py:248
  29.1 0.0 collective-permute-start.7
  29.1 3.4 %collective-permute-done.8.far = f32[1056,128]{1,0:T(8,128)S(1)} collective-permute-done((f32[1056,128]{1,0:T(8,128)S(1)}, f32[1056,128]{1,0:T(8,128)S(1)}, u32[]{:S(2)}, u32[]{:S(2)}) %collective-permute-start.8) | collective-permute-done | bytes 540704 | tf_op jit(solution)/shard_map/ppermute | solution.py:264
  32.5 0.0 collective-permute-start.9
  32.5 0.0 collective-permute-done.7.near
  32.5 7.8 %all-to-all-done.fields = f32[8,2,16,512]{3,2,1,0:T(8,128)S(1)} async-done(((f32[8,2,16,512]{3,2,1,0:T(8,128)}), f32[8,2,16,512]{3,2,1,0:T(8,128)S(1)}, u32[]{:S(2)}, u32[]{:S(2)}) %all-to-all-start) | async-done | bytes 524320 | tf_op jit(solution)/shard_map/all_to_all | solution.py:248
  40.3 0.0 collective-permute-done.9.cross
  40.3 3.7 %shard_map.78 = f32[8,2,512]{2,1,0:T(2,128)} custom-call(f32[1056,128]{1,0:T(8,128)S(1)} %shard_map.77.own, f32[1056,128]{1,0:T(8,128)S(1)} %collective-permute-done.7.near, f32[1056,128]{1,0:T(8,128)S(1)} %collective-permute-done.8.far, f32[1056,128]{1,0:T(8,128)S(1)} %collective-permute-done.9.cross, f32[5,128,128]{2,1,0:T(8,128)S(1)} %get-tuple-element.7.steps, ...), custom_call_target="tpu_custom_call" | custom-call | flops 1000000000 | bytes 10000000 | tf_op jit(solution)/shard_map/pallas_call | solution.py:277
  44.0 3.7 %all-to-all-start.2 = ((f32[8,2,512]{2,1,0:T(2,128)}), f32[8,2,512]{2,1,0:T(2,128)S(1)}, u32[]{:S(2)}, u32[]{:S(2)}) async-start(f32[8,2,512]{2,1,0:T(2,128)} %shard_map.78), calls=%async_computation.2 | async-start | bytes 65536 | tf_op jit(solution)/shard_map/all_to_all | solution.py:284
  47.7 0.6 shard_map.75
  48.3 6.1 %all-to-all-done.2.shift = f32[8,2,512]{2,1,0:T(2,128)S(1)} async-done(((f32[8,2,512]{2,1,0:T(2,128)}), f32[8,2,512]{2,1,0:T(2,128)S(1)}, u32[]{:S(2)}, u32[]{:S(2)}) %all-to-all-start.2) | async-done | bytes 32800 | tf_op jit(solution)/shard_map/all_to_all | solution.py:284
  54.4 13.9 %all_to_all.15.moved = f32[8,2,16,512]{3,2,1,0:T(8,128)S(1)} all-to-all(f32[8,2,16,512]{3,2,1,0:T(8,128)S(1)} %shard_map.75), channel_id=1, replica_groups=mesh['grid'=8,'lev'=4] {'grid'}, dimensions={0} | all-to-all | bytes 1048576 | tf_op jit(solution)/shard_map/all_to_all | solution.py:275
  68.3 0.9 %shard_map.79 = f32[16,2,4096]{2,1,0:T(2,128)} custom-call(f32[8,2,16,512]{3,2,1,0:T(8,128)S(1)} %all_to_all.15.moved, f32[8,2,512]{2,1,0:T(2,128)S(1)} %all-to-all-done.2.shift), custom_call_target="tpu_custom_call" | custom-call | bytes 1000000 | tf_op jit(solution)/shard_map/pallas_call | solution.py:286
  (2 shorter events, 0.0 us)
Async XLA Ops:
  0.0 0.7 copy-start.8
  0.0 0.7 copy-start.5
  0.7 1.0 %copy-start = (f32[16,2,4096]{2,1,0:T(2,128)S(1)}, f32[16,2,4096]{2,1,0:T(2,128)}, u32[]{:S(2)}) copy-start(f32[16,2,4096]{2,1,0:T(2,128)} %prior.3) | copy-start | bytes 1572868
  1.7 0.7 %copy-start.2 = (s32[4,4,64]{2,1,0:T(4,128)S(1)}, s32[4,4,64]{2,1,0:T(4,128)}, u32[]{:S(2)}) copy-start(s32[4,4,64]{2,1,0:T(4,128)} %offsets.3) | copy-start | bytes 12292
  2.4 0.7 copy-start.3
  3.1 14.6 %copy-start.4 = (s32[4,1,1,128]{3,2,1,0:T(1,128)S(1)}, s32[4,1,1,128]{3,2,1,0:T(1,128)}, u32[]{:S(2)}) copy-start(s32[4,1,1,128]{3,2,1,0:T(1,128)} %param.13) | copy-start | bytes 6148
  3.1 14.6 %copy-start.6 = (f32[4,1,64]{2,1,0:T(1,128)S(1)}, f32[4,1,64]{2,1,0:T(1,128)}, u32[]{:S(2)}) copy-start(f32[4,1,64]{2,1,0:T(1,128)} %values.1) | copy-start | bytes 3076
  3.1 14.6 %copy-start.7 = (f32[4,1,64]{2,1,0:T(1,128)S(1)}, f32[4,1,64]{2,1,0:T(1,128)}, u32[]{:S(2)}) copy-start(f32[4,1,64]{2,1,0:T(1,128)} %errors.1) | copy-start | bytes 3076
  4.3 7.4 %collective-permute-start.1 = (f32[16,1152]{1,0:T(8,128)S(1)}, f32[16,1152]{1,0:T(8,128)S(1)}, u32[]{:S(2)}, u32[]{:S(2)}) collective-permute-start(f32[16,1152]{1,0:T(8,128)S(1)} %shard_map.76.refs_0_), channel_id=1, source_target_pairs={{0,8},{4,12},{8,0},{12,4},{16,24},{20,28},{24,16},{28,20},{1,9},{5... | collective-permute-start | bytes 221192 | tf_op jit(solution)/shard_map/ppermute | solution.py:214
  7.4 7.8 %collective-permute-start.3 = (f32[16,1152]{1,0:T(8,128)S(1)}, f32[16,1152]{1,0:T(8,128)S(1)}, u32[]{:S(2)}, u32[]{:S(2)}) collective-permute-start(f32[16,1152]{1,0:T(8,128)S(1)} %shard_map.76.refs_0_), channel_id=1, source_target_pairs={{0,16},{4,20},{8,24},{12,28},{16,0},{20,4},{24,8},{28,12},{1,17},{... | collective-permute-start | bytes 221192 | tf_op jit(solution)/shard_map/ppermute | solution.py:214
  10.0 6.7 %collective-permute-start.5 = (f32[16,1152]{1,0:T(8,128)S(1)}, f32[16,1152]{1,0:T(8,128)S(1)}, u32[]{:S(2)}, u32[]{:S(2)}) collective-permute-start(f32[16,1152]{1,0:T(8,128)S(1)} %shard_map.76.refs_0_), channel_id=1, source_target_pairs={{0,24},{4,28},{8,16},{12,20},{16,8},{20,12},{24,0},{28,4},{1,25},{... | collective-permute-start | bytes 221192 | tf_op jit(solution)/shard_map/ppermute | solution.py:214
  10.0 8.8 %collective-permute-start = (f32[16,1152]{1,0:T(8,128)S(1)}, f32[16,1152]{1,0:T(8,128)S(1)}, u32[]{:S(2)}, u32[]{:S(2)}) collective-permute-start(f32[16,1152]{1,0:T(8,128)S(1)} %shard_map.76.refs_0_), channel_id=1, source_target_pairs={{0,4},{4,0},{8,12},{12,8},{16,20},{20,16},{24,28},{28,24},{1,5},{5... | collective-permute-start | bytes 221192 | tf_op jit(solution)/shard_map/ppermute | solution.py:217
  11.7 7.1 %collective-permute-start.2 = (f32[16,1152]{1,0:T(8,128)S(1)}, f32[16,1152]{1,0:T(8,128)S(1)}, u32[]{:S(2)}, u32[]{:S(2)}) collective-permute-start(f32[16,1152]{1,0:T(8,128)S(1)} %collective-permute-done.1.refs_2_), channel_id=1, source_target_pairs={{0,4},{4,0},{8,12},{12,8},{16,20},{20,16},{24,28},{28,24},{1,5},{5... | collective-permute-start | bytes 221192 | tf_op jit(solution)/shard_map/ppermute | solution.py:217
  15.2 4.4 %collective-permute-start.4 = (f32[16,1152]{1,0:T(8,128)S(1)}, f32[16,1152]{1,0:T(8,128)S(1)}, u32[]{:S(2)}, u32[]{:S(2)}) collective-permute-start(f32[16,1152]{1,0:T(8,128)S(1)} %collective-permute-done.3.refs_4_), channel_id=1, source_target_pairs={{0,4},{4,0},{8,12},{12,8},{16,20},{20,16},{24,28},{28,24},{1,5},{5... | collective-permute-start | bytes 221192 | tf_op jit(solution)/shard_map/ppermute | solution.py:217
  16.7 4.4 %collective-permute-start.6 = (f32[16,1152]{1,0:T(8,128)S(1)}, f32[16,1152]{1,0:T(8,128)S(1)}, u32[]{:S(2)}, u32[]{:S(2)}) collective-permute-start(f32[16,1152]{1,0:T(8,128)S(1)} %collective-permute-done.5.refs_6_), channel_id=1, source_target_pairs={{0,4},{4,0},{8,12},{12,8},{16,20},{20,16},{24,28},{28,24},{1,5},{5... | collective-permute-start | bytes 221192 | tf_op jit(solution)/shard_map/ppermute | solution.py:217
  21.0 2.3 %copy-start.1 = (f32[16,2,4096]{2,1,0:T(2,128)S(1)}, f32[16,2,4096]{2,1,0:T(2,128)}, u32[]{:S(2)}) copy-start(f32[16,2,4096]{2,1,0:T(2,128)} %prior.3) | copy-start | bytes 1572868
  21.8 10.7 %collective-permute-start.8 = (f32[1056,128]{1,0:T(8,128)S(1)}, f32[1056,128]{1,0:T(8,128)S(1)}, u32[]{:S(2)}, u32[]{:S(2)}) collective-permute-start(f32[1056,128]{1,0:T(8,128)S(1)} %shard_map.77.own), channel_id=1, source_target_pairs={{0,2},{1,3},{2,0},{3,1},{4,6},{5,7},{6,4},{7,5},{8,10},{9,11},{10,... | collective-permute-start | bytes 1622024 | tf_op jit(solution)/shard_map/ppermute | solution.py:264
  24.3 16.0 %all-to-all-start = ((f32[8,2,16,512]{3,2,1,0:T(8,128)}), f32[8,2,16,512]{3,2,1,0:T(8,128)S(1)}, u32[]{:S(2)}, u32[]{:S(2)}) async-start(f32[8,2,16,512]{3,2,1,0:T(8,128)} %shard_map.74), calls=%async_computation | async-start | bytes 1048576 | tf_op jit(solution)/shard_map/all_to_all | solution.py:248
  29.1 3.4 %collective-permute-start.7 = (f32[1056,128]{1,0:T(8,128)S(1)}, f32[1056,128]{1,0:T(8,128)S(1)}, u32[]{:S(2)}, u32[]{:S(2)}) collective-permute-start(f32[1056,128]{1,0:T(8,128)S(1)} %shard_map.77.own), channel_id=1, source_target_pairs={{0,1},{1,0},{2,3},{3,2},{4,5},{5,4},{6,7},{7,6},{8,9},{9,8},{10,11... | collective-permute-start | bytes 1622024 | tf_op jit(solution)/shard_map/ppermute | solution.py:265
  32.5 7.8 %collective-permute-start.9 = (f32[1056,128]{1,0:T(8,128)S(1)}, f32[1056,128]{1,0:T(8,128)S(1)}, u32[]{:S(2)}, u32[]{:S(2)}) collective-permute-start(f32[1056,128]{1,0:T(8,128)S(1)} %collective-permute-done.8.far), channel_id=1, source_target_pairs={{0,1},{1,0},{2,3},{3,2},{4,5},{5,4},{6,7},{7,6},{8,9},{9,8},{10,11... | collective-permute-start | bytes 1622024 | tf_op jit(solution)/shard_map/ppermute | solution.py:266
  44.0 10.4 %all-to-all-start.2 = ((f32[8,2,512]{2,1,0:T(2,128)}), f32[8,2,512]{2,1,0:T(2,128)S(1)}, u32[]{:S(2)}, u32[]{:S(2)}) async-start(f32[8,2,512]{2,1,0:T(2,128)} %shard_map.78), calls=%async_computation.2 | async-start | bytes 65536 | tf_op jit(solution)/shard_map/all_to_all | solution.py:284

commit v2 on v1

--- a/solution.py
+++ b/solution.py
@@ -13,13 +13,14 @@
 F32 = jnp.float32
 VMEM = pl.BlockSpec(memory_space=pltpu.VMEM)
 SMEM = pl.BlockSpec(memory_space=pltpu.SMEM)
+PLACE = pl.BlockSpec(memory_space=pl.ANY)
 LIMIT = 48 * 1024 * 1024
 
 PAIRS = [(e, b) for b in range(1, NB) for e in range(b)]
 PARENT, ALPHA, LATER, VALUE, OWN, SPARE = 0, 6, 12, 18, 22, 32
 
 
-def call(kernel, out_shapes, in_specs, scratch=(), flops=0, moved=0):
+def call(kernel, out_shapes, in_specs, scratch=(), flops=0, moved=0, limit=LIMIT):
     many = isinstance(out_shapes, (list, tuple))
     return pl.pallas_call(
         kernel,
@@ -27,7 +28,7 @@
         in_specs=in_specs,
         out_specs=[VMEM] * len(out_shapes) if many else VMEM,
         scratch_shapes=list(scratch),
-        compiler_params=pltpu.CompilerParams(vmem_limit_bytes=LIMIT),
+        compiler_params=pltpu.CompilerParams(vmem_limit_bytes=limit),
         cost_estimate=pl.CostEstimate(flops=flops, bytes_accessed=moved, transcendentals=0),
     )
 
@@ -41,8 +42,15 @@
     return jnp.take_along_axis(value, where, axis=1, mode="promise_in_bounds")
 
 
-def pick_kernel(shape, owner, weights, offsets, ancestors, prior, out):
+def pick_kernel(shape, owner, *refs):
     slab, depth, block_cells, groups, count = shape
+    out, arrivals = refs[4], refs[9]
+    copies = [pltpu.make_async_copy(refs[i], refs[5 + i], arrivals.at[i]) for i in range(4)]
+    for copy in copies:
+        copy.start()
+    for copy in copies:
+        copy.wait()
+    weights, offsets, ancestors, prior = refs[5:9]
     width = groups * count
     per = LANES // count
     for b in range(NB):
@@ -234,8 +242,16 @@
     piece = call(
         functools.partial(pick_kernel, (slab, depth, block_cells, groups, count)),
         shape((slab, wide), F32),
-        [SMEM, VMEM, VMEM, VMEM, VMEM],
-        moved=10**6,
+        [SMEM] + [PLACE] * 4,
+        scratch=[
+            pltpu.VMEM(channel_weights.shape, F32),
+            pltpu.VMEM(obs_offset.shape, jnp.int32),
+            pltpu.VMEM(parents.shape, jnp.int32),
+            pltpu.VMEM(prior.shape, F32),
+            pltpu.SemaphoreType.DMA((4,)),
+        ],
+        moved=10**6,
+        limit=None,
     )(obs_owner, channel_weights, obs_offset, parents, prior)
     pieces = gather_pieces(piece, n)
 
@@ -261,7 +277,8 @@
         scratch=[pltpu.VMEM((n, slab, wide), F32)],
         moved=10**6,
     )(obs_owner, rows, *pieces)
-    far = lax.ppermute(own, "lev", [(j, j ^ 2) for j in range(lev)])
+    ready, fields = lax.optimization_barrier((own, fields))
+    far = lax.ppermute(ready, "lev", [(j, j ^ 2) for j in range(lev)])
     near = lax.ppermute(own, "lev", [(j, j ^ 1) for j in range(lev)])
     cross = lax.ppermute(far, "lev", [(j, j ^ 1) for j in range(lev)])
 
@@ -281,6 +298,7 @@
         flops=10**9,
         moved=10**7,
     )(own, near, far, cross, steps, fields)
+    send, moved = lax.optimization_barrier((send, moved))
     shift = lax.all_to_all(send, "grid", 0, 0, tiled=True)
 
     return call(

time: 69.6 us -> 67.4 us (0.968)
  blocking collectives: 13.9 us -> 10.1 us
  starting transfers between devices: 20.3 us -> 23 us
  waiting for transfers between devices: 22.8 us -> 20.5 us
  Pallas kernels: 9.05 us -> 11.2 us
  local copies, waits for them, and re-layouts: 3.11 us -> 1.95 us
    all_to_all x1, waiting for transfers between devices: 7.83 us -> 0.01 us  [body(): fields = lax.all_to_all(send, 'grid', 0, 0, tiled=True)]
    ppermute x3, waiting for transfers between devices: 3.17 us -> 8.15 us  [gather_pieces(): pieces.append(lax.ppermute(piece, 'grid', [(j, j ^ far) for j in range(n)]))]
    all_to_all x1, blocking collectives: 13.9 us -> 10.1 us  [body(): shift = lax.all_to_all(send, 'grid', 0, 0, tiled=True)]
    all_to_all x1, waiting for transfers between devices: 6.11 us -> 3.12 us  [body(): moved = lax.all_to_all(send, 'grid', 0, 0, tiled=True)]
    all_to_all x1, starting transfers between devices: 4.77 us -> 7.28 us  [body(): fields = lax.all_to_all(send, 'grid', 0, 0, tiled=True)]
    pallas_call x1, Pallas kernels: 1.18 us -> 3.2 us  [body(): call(functools.partial(pick_kernel, (slab, depth, block_cells, groups, co...]
    ppermute x1, waiting for transfers between devices: 0.01 us -> 1.93 us  [body(): cross = lax.ppermute(far, 'lev', [(j, j ^ 1) for j in range(lev)])]
    ppermute x4, starting transfers between devices: 4.6 us -> 6.12 us  [gather_pieces(): result += [part, lax.ppermute(part, 'grid', [(j, j ^ 1) for j in range(n)])]]
  transfers between devices with their start and end apart: 12 -> 12, of which waited for: 6 -> 7; matrix products, arithmetic and copies ran while one was open for 0% -> 0% of each run, Pallas kernels for 4% -> 14%
where the time goes in v2:
time: 67.4 us; the launch traced here: 67 us
  starting transfers between devices  23 us (34%)
  waiting for transfers between devices  20.5 us (30%)
  Pallas kernels  11.2 us (17%)
  blocking collectives  10.1 us (15%)
  local copies, waits for them, and re-layouts  1.95 us (3%)
    all_to_all x1, blocking collectives, body(): shift = lax.all_to_all(send, 'grid', 0, 0, tiled=True)  10.1 us
    ppermute x3, waiting for transfers between devices, gather_pieces(): pieces.append(lax.ppermute(piece, 'grid', [(j, j ^ far) for j in range(n)]))  8.15 us
    all_to_all x1, starting transfers between devices, body(): fields = lax.all_to_all(send, 'grid', 0, 0, tiled=True)  7.28 us
    ppermute x4, starting transfers between devices, gather_pieces(): result += [part, lax.ppermute(part, 'grid', [(j, j ^ 1) for j in range(n)])]  6.12 us
    ppermute x1, waiting for transfers between devices, body(): far = lax.ppermute(ready, 'lev', [(j, j ^ 2) for j in range(lev)])  4.58 us
    ppermute x3, starting transfers between devices, gather_pieces(): pieces.append(lax.ppermute(piece, 'grid', [(j, j ^ far) for j in range(n)]))  4.51 us
    all_to_all x1, starting transfers between devices, body(): moved = lax.all_to_all(send, 'grid', 0, 0, tiled=True)  3.49 us
    pallas_call x1, Pallas kernels, body(): call(functools.partial(pick_kernel, (slab, depth, block_cells, groups, co...  3.2 us
  transfers between devices with their start and end apart: 12, of which 7 were waited for; matrix products, arithmetic and copies ran while one was open for 0% of the time, Pallas kernels for 14%

profile of v2, /device:TPU:0, one launch (start us, length us, event | category | flops | bytes accessed | tf_op | source)
XLA Modules:
  0.0 67.0 jit_solution(8729449197806436777)
XLA Ops:
  0.0 0.0 copy-start
  0.0 1.0 %copy-done = f32[16,2,4096]{2,1,0:T(2,128)S(1)} copy-done((f32[16,2,4096]{2,1,0:T(2,128)S(1)}, f32[16,2,4096]{2,1,0:T(2,128)}, u32[]{:S(2)}) %copy-start) | copy-done | bytes 524312
  1.0 0.9 %shard_map.76 = f32[8,2,16,512]{3,2,1,0:T(8,128)} custom-call(f32[16,2,4096]{2,1,0:T(2,128)S(1)} %copy-done), custom_call_target="tpu_custom_call" | custom-call | bytes 1000000 | tf_op jit(solution)/shard_map/pallas_call | solution.py:258
  1.9 7.3 %all-to-all-start = ((f32[8,2,16,512]{3,2,1,0:T(8,128)}), f32[8,2,16,512]{3,2,1,0:T(8,128)S(1)}, u32[]{:S(2)}, u32[]{:S(2)}) async-start(f32[8,2,16,512]{3,2,1,0:T(8,128)} %shard_map.76), calls=%async_computation | async-start | bytes 1048576 | tf_op jit(solution)/shard_map/all_to_all | solution.py:264
  9.2 0.0 copy-start.2
  9.2 0.0 copy-start.3
  9.2 0.0 copy-start.4
  9.2 0.0 copy-start.5
  9.3 0.0 copy-start.6
  9.3 3.2 %shard_map.74.refs_0_ = f32[16,1152]{1,0:T(8,128)} custom-call(s32[4]{0:T(128)} %owner.5, f32[2,4]{1,0:T(2,128)} %refs_0_.1, s32[4,4,64]{2,1,0:T(4,128)} %refs_1_.1, s32[4,1,128]{2,1,0:T(1,128)} %bitcast.1, f32[16,2,4096]{2,1,0:T(2,128)} %prior.1), custom_call_target="tpu_custom_call" | custom-call | bytes 1000000 | tf_op jit(solution)/shard_map/pallas_call | solution.py:242
  12.5 2.1 %collective-permute-start.1 = (f32[16,1152]{1,0:T(8,128)}, f32[16,1152]{1,0:T(8,128)S(1)}, u32[]{:S(2)}, u32[]{:S(2)}) collective-permute-start(f32[16,1152]{1,0:T(8,128)} %shard_map.74.refs_0_), channel_id=1, source_target_pairs={{0,8},{4,12},{8,0},{12,4},{16,24},{20,28},{24,16},{28,20},{1,9},{5... | collective-permute-start | bytes 221192 | tf_op jit(solution)/shard_map/ppermute | solution.py:222
  14.5 2.4 %collective-permute-start.3 = (f32[16,1152]{1,0:T(8,128)}, f32[16,1152]{1,0:T(8,128)S(1)}, u32[]{:S(2)}, u32[]{:S(2)}) collective-permute-start(f32[16,1152]{1,0:T(8,128)} %shard_map.74.refs_0_), channel_id=1, source_target_pairs={{0,16},{4,20},{8,24},{12,28},{16,0},{20,4},{24,8},{28,12},{1,17},{... | collective-permute-start | bytes 221192 | tf_op jit(solution)/shard_map/ppermute | solution.py:222
  16.9 0.1 collective-permute-start.5
  17.0 1.9 %collective-permute-start = (f32[16,1152]{1,0:T(8,128)}, f32[16,1152]{1,0:T(8,128)S(1)}, u32[]{:S(2)}, u32[]{:S(2)}) collective-permute-start(f32[16,1152]{1,0:T(8,128)} %shard_map.74.refs_0_), channel_id=1, source_target_pairs={{0,4},{4,0},{8,12},{12,8},{16,20},{20,16},{24,28},{28,24},{1,5},{5... | collective-permute-start | bytes 221192 | tf_op jit(solution)/shard_map/ppermute | solution.py:225
  18.9 1.7 %collective-permute-done.1.refs_2_ = f32[16,1152]{1,0:T(8,128)S(1)} collective-permute-done((f32[16,1152]{1,0:T(8,128)}, f32[16,1152]{1,0:T(8,128)S(1)}, u32[]{:S(2)}, u32[]{:S(2)}) %collective-permute-start.1) | collective-permute-done | bytes 73760 | tf_op jit(solution)/shard_map/ppermute | solution.py:222
  20.6 2.1 %collective-permute-start.2 = (f32[16,1152]{1,0:T(8,128)S(1)}, f32[16,1152]{1,0:T(8,128)S(1)}, u32[]{:S(2)}, u32[]{:S(2)}) collective-permute-start(f32[16,1152]{1,0:T(8,128)S(1)} %collective-permute-done.1.refs_2_), channel_id=1, source_target_pairs={{0,4},{4,0},{8,12},{12,8},{16,20},{20,16},{24,28},{28,24},{1,5},{5... | collective-permute-start | bytes 221192 | tf_op jit(solution)/shard_map/ppermute | solution.py:225
  22.8 6.5 %collective-permute-done.3.refs_4_ = f32[16,1152]{1,0:T(8,128)S(1)} collective-permute-done((f32[16,1152]{1,0:T(8,128)}, f32[16,1152]{1,0:T(8,128)S(1)}, u32[]{:S(2)}, u32[]{:S(2)}) %collective-permute-start.3) | collective-permute-done | bytes 73760 | tf_op jit(solution)/shard_map/ppermute | solution.py:222
  29.2 1.5 %collective-permute-start.4 = (f32[16,1152]{1,0:T(8,128)S(1)}, f32[16,1152]{1,0:T(8,128)S(1)}, u32[]{:S(2)}, u32[]{:S(2)}) collective-permute-start(f32[16,1152]{1,0:T(8,128)S(1)} %collective-permute-done.3.refs_4_), channel_id=1, source_target_pairs={{0,4},{4,0},{8,12},{12,8},{16,20},{20,16},{24,28},{28,24},{1,5},{5... | collective-permute-start | bytes 221192 | tf_op jit(solution)/shard_map/ppermute | solution.py:225
  30.7 0.0 collective-permute-done.5.refs_6_
  30.7 0.6 collective-permute-start.6
  31.3 0.0 copy-done.2
  31.3 0.0 copy-done.3
  31.3 0.0 copy-done.4
  31.3 0.0 copy-done.5
  31.3 0.0 copy-done.6
  31.3 1.0 %shard_map.73 = (f32[32,128]{1,0:T(8,128)S(1)}, f32[5,128,128]{2,1,0:T(8,128)S(1)}) custom-call(s32[4]{0:T(128)S(1)} %copy-done.4, s32[4,4,64]{2,1,0:T(4,128)S(1)} %copy-done.2, f32[4,1,64]{2,1,0:T(1,128)S(1)} %copy-done.5, f32[4,1,64]{2,1,0:T(1,128)S(1)} %copy-done.6, s32[4,1,128]{2,1,0:T(1,128)S(1)} %bitcast.2), custom_call_target="tpu_custom_call" | custom-call | bytes 1000000 | tf_op jit(solution)/shard_map/pallas_call | solution.py:266
  32.3 0.0 collective-permute-done.refs_1_
  32.3 0.0 collective-permute-done.2.refs_3_
  32.3 1.3 %collective-permute-done.4.refs_5_ = f32[16,1152]{1,0:T(8,128)S(1)} collective-permute-done((f32[16,1152]{1,0:T(8,128)S(1)}, f32[16,1152]{1,0:T(8,128)S(1)}, u32[]{:S(2)}, u32[]{:S(2)}) %collective-permute-start.4) | collective-permute-done | bytes 73760 | tf_op jit(solution)/shard_map/ppermute | solution.py:225
  33.6 1.5 %collective-permute-done.6.refs_7_ = f32[16,1152]{1,0:T(8,128)S(1)} collective-permute-done((f32[16,1152]{1,0:T(8,128)S(1)}, f32[16,1152]{1,0:T(8,128)S(1)}, u32[]{:S(2)}, u32[]{:S(2)}) %collective-permute-start.6) | collective-permute-done | bytes 73760 | tf_op jit(solution)/shard_map/ppermute | solution.py:225
  35.1 0.0 copy-start.1
  35.1 0.9 %copy-done.1 = f32[16,1152]{1,0:T(8,128)S(1)} copy-done((f32[16,1152]{1,0:T(8,128)S(1)}, f32[16,1152]{1,0:T(8,128)}, u32[]{:S(2)}) %copy-start.1) | copy-done | bytes 73752
  35.9 0.8 %shard_map.75.own = f32[1056,128]{1,0:T(8,128)S(1)} custom-call(s32[4]{0:T(128)S(1)} %copy-done.4, f32[32,128]{1,0:T(8,128)S(1)} %get-tuple-element.11.rows, f32[16,1152]{1,0:T(8,128)S(1)} %copy-done.1, f32[16,1152]{1,0:T(8,128)S(1)} %collective-permute-done.refs_1_, f32[16,1152]{1,0:T(8,128)S(1)} %collective-permute-done.1.refs_2_, ...), custom_call_target="tpu_custom_call" | custom-call | bytes 1000000 | tf_op jit(solution)/shard_map/pallas_call | solution.py:273
  36.7 0.0 all-to-all-done.fields
  36.7 1.6 %collective-permute-start.8 = (f32[1056,128]{1,0:T(8,128)S(1)}, f32[1056,128]{1,0:T(8,128)S(1)}, u32[]{:S(2)}, u32[]{:S(2)}) collective-permute-start(f32[1056,128]{1,0:T(8,128)S(1)} %shard_map.75.own), channel_id=1, source_target_pairs={{0,2},{1,3},{2,0},{3,1},{4,6},{5,7},{6,4},{7,5},{8,10},{9,11},{10,... | collective-permute-start | bytes 1622024 | tf_op jit(solution)/shard_map/ppermute | solution.py:281
  38.3 1.4 %shard_map.78 = f32[8,2,16,512]{3,2,1,0:T(8,128)} custom-call(f32[5,128,128]{2,1,0:T(8,128)S(1)} %get-tuple-element.13.steps, f32[8,2,16,512]{3,2,1,0:T(8,128)S(1)} %all-to-all-done.fields), custom_call_target="tpu_custom_call" | custom-call | flops 100000000 | bytes 1000000 | tf_op jit(solution)/shard_map/pallas_call | solution.py:285
  39.7 3.5 %all-to-all-start.1 = ((f32[8,2,16,512]{3,2,1,0:T(8,128)}), f32[8,2,16,512]{3,2,1,0:T(8,128)S(1)}, u32[]{:S(2)}, u32[]{:S(2)}) async-start(f32[8,2,16,512]{3,2,1,0:T(8,128)} %shard_map.78), calls=%async_computation.1 | async-start | bytes 1048576 | tf_op jit(solution)/shard_map/all_to_all | solution.py:292
  43.2 0.1 collective-permute-start.7
  43.2 4.6 %collective-permute-done.8.far = f32[1056,128]{1,0:T(8,128)S(1)} collective-permute-done((f32[1056,128]{1,0:T(8,128)S(1)}, f32[1056,128]{1,0:T(8,128)S(1)}, u32[]{:S(2)}, u32[]{:S(2)}) %collective-permute-start.8) | collective-permute-done | bytes 540704 | tf_op jit(solution)/shard_map/ppermute | solution.py:281
  47.8 0.0 collective-permute-start.9
  47.8 0.0 collective-permute-done.7.near
  47.8 1.9 %collective-permute-done.9.cross = f32[1056,128]{1,0:T(8,128)S(1)} collective-permute-done((f32[1056,128]{1,0:T(8,128)S(1)}, f32[1056,128]{1,0:T(8,128)S(1)}, u32[]{:S(2)}, u32[]{:S(2)}) %collective-permute-start.9) | collective-permute-done | bytes 540704 | tf_op jit(solution)/shard_map/ppermute | solution.py:283
  49.8 3.1 %shard_map.77 = f32[8,2,512]{2,1,0:T(2,128)S(1)} custom-call(f32[1056,128]{1,0:T(8,128)S(1)} %shard_map.75.own, f32[1056,128]{1,0:T(8,128)S(1)} %collective-permute-done.7.near, f32[1056,128]{1,0:T(8,128)S(1)} %collective-permute-done.8.far, f32[1056,128]{1,0:T(8,128)S(1)} %collective-permute-done.9.cross, f32[5,128,128]{2,1,0:T(8,128)S(1)} %get-tuple-element.13.steps, ...), custom_call_target="tpu_custom_call" | custom-call | flops 1000000000 | bytes 10000000 | tf_op jit(solution)/shard_map/pallas_call | solution.py:294
  52.8 3.1 %all-to-all-done.1.moved = f32[8,2,16,512]{3,2,1,0:T(8,128)S(1)} async-done(((f32[8,2,16,512]{3,2,1,0:T(8,128)}), f32[8,2,16,512]{3,2,1,0:T(8,128)S(1)}, u32[]{:S(2)}, u32[]{:S(2)}) %all-to-all-start.1) | async-done | bytes 524320 | tf_op jit(solution)/shard_map/all_to_all | solution.py:292
  55.9 10.1 %all_to_all.15.shift = f32[8,2,512]{2,1,0:T(2,128)S(1)} all-to-all(f32[8,2,512]{2,1,0:T(2,128)S(1)} %shard_map.77), channel_id=1, replica_groups=mesh['grid'=8,'lev'=4] {'grid'}, dimensions={0} | all-to-all | bytes 65536 | tf_op jit(solution)/shard_map/all_to_all | solution.py:302
  66.0 0.9 %shard_map.79 = f32[16,2,4096]{2,1,0:T(2,128)} custom-call(f32[8,2,16,512]{3,2,1,0:T(8,128)S(1)} %all-to-all-done.1.moved, f32[8,2,512]{2,1,0:T(2,128)S(1)} %all_to_all.15.shift), custom_call_target="tpu_custom_call" | custom-call | bytes 1000000 | tf_op jit(solution)/shard_map/pallas_call | solution.py:304
Async XLA Ops:
  0.0 1.0 %copy-start = (f32[16,2,4096]{2,1,0:T(2,128)S(1)}, f32[16,2,4096]{2,1,0:T(2,128)}, u32[]{:S(2)}) copy-start(f32[16,2,4096]{2,1,0:T(2,128)} %prior.1) | copy-start | bytes 1572868
  1.9 34.8 %all-to-all-start = ((f32[8,2,16,512]{3,2,1,0:T(8,128)}), f32[8,2,16,512]{3,2,1,0:T(8,128)S(1)}, u32[]{:S(2)}, u32[]{:S(2)}) async-start(f32[8,2,16,512]{3,2,1,0:T(8,128)} %shard_map.76), calls=%async_computation | async-start | bytes 1048576 | tf_op jit(solution)/shard_map/all_to_all | solution.py:264
  9.2 22.0 %copy-start.2 = (s32[4,4,64]{2,1,0:T(4,128)S(1)}, s32[4,4,64]{2,1,0:T(4,128)}, u32[]{:S(2)}) copy-start(s32[4,4,64]{2,1,0:T(4,128)} %refs_1_.1) | copy-start | bytes 12292
  9.2 22.0 %copy-start.3 = (s32[4,1,1,128]{3,2,1,0:T(1,128)S(1)}, s32[4,1,1,128]{3,2,1,0:T(1,128)}, u32[]{:S(2)}) copy-start(s32[4,1,1,128]{3,2,1,0:T(1,128)} %param.13) | copy-start | bytes 6148
  9.2 22.0 %copy-start.4 = (s32[4]{0:T(128)S(1)}, s32[4]{0:T(128)}, u32[]{:S(2)}) copy-start(s32[4]{0:T(128)} %owner.5) | copy-start | bytes 52
  9.2 22.0 %copy-start.5 = (f32[4,1,64]{2,1,0:T(1,128)S(1)}, f32[4,1,64]{2,1,0:T(1,128)}, u32[]{:S(2)}) copy-start(f32[4,1,64]{2,1,0:T(1,128)} %values.1) | copy-start | bytes 3076
  9.3 22.0 %copy-start.6 = (f32[4,1,64]{2,1,0:T(1,128)S(1)}, f32[4,1,64]{2,1,0:T(1,128)}, u32[]{:S(2)}) copy-start(f32[4,1,64]{2,1,0:T(1,128)} %errors.1) | copy-start | bytes 3076
  12.5 8.1 %collective-permute-start.1 = (f32[16,1152]{1,0:T(8,128)}, f32[16,1152]{1,0:T(8,128)S(1)}, u32[]{:S(2)}, u32[]{:S(2)}) collective-permute-start(f32[16,1152]{1,0:T(8,128)} %shard_map.74.refs_0_), channel_id=1, source_target_pairs={{0,8},{4,12},{8,0},{12,4},{16,24},{20,28},{24,16},{28,20},{1,9},{5... | collective-permute-start | bytes 221192 | tf_op jit(solution)/shard_map/ppermute | solution.py:222
  14.5 14.7 %collective-permute-start.3 = (f32[16,1152]{1,0:T(8,128)}, f32[16,1152]{1,0:T(8,128)S(1)}, u32[]{:S(2)}, u32[]{:S(2)}) collective-permute-start(f32[16,1152]{1,0:T(8,128)} %shard_map.74.refs_0_), channel_id=1, source_target_pairs={{0,16},{4,20},{8,24},{12,28},{16,0},{20,4},{24,8},{28,12},{1,17},{... | collective-permute-start | bytes 221192 | tf_op jit(solution)/shard_map/ppermute | solution.py:222
  16.9 13.8 %collective-permute-start.5 = (f32[16,1152]{1,0:T(8,128)}, f32[16,1152]{1,0:T(8,128)S(1)}, u32[]{:S(2)}, u32[]{:S(2)}) collective-permute-start(f32[16,1152]{1,0:T(8,128)} %shard_map.74.refs_0_), channel_id=1, source_target_pairs={{0,24},{4,28},{8,16},{12,20},{16,8},{20,12},{24,0},{28,4},{1,25},{... | collective-permute-start | bytes 221192 | tf_op jit(solution)/shard_map/ppermute | solution.py:222
  17.0 15.3 %collective-permute-start = (f32[16,1152]{1,0:T(8,128)}, f32[16,1152]{1,0:T(8,128)S(1)}, u32[]{:S(2)}, u32[]{:S(2)}) collective-permute-start(f32[16,1152]{1,0:T(8,128)} %shard_map.74.refs_0_), channel_id=1, source_target_pairs={{0,4},{4,0},{8,12},{12,8},{16,20},{20,16},{24,28},{28,24},{1,5},{5... | collective-permute-start | bytes 221192 | tf_op jit(solution)/shard_map/ppermute | solution.py:225
  20.6 11.7 %collective-permute-start.2 = (f32[16,1152]{1,0:T(8,128)S(1)}, f32[16,1152]{1,0:T(8,128)S(1)}, u32[]{:S(2)}, u32[]{:S(2)}) collective-permute-start(f32[16,1152]{1,0:T(8,128)S(1)} %collective-permute-done.1.refs_2_), channel_id=1, source_target_pairs={{0,4},{4,0},{8,12},{12,8},{16,20},{20,16},{24,28},{28,24},{1,5},{5... | collective-permute-start | bytes 221192 | tf_op jit(solution)/shard_map/ppermute | solution.py:225
  29.2 4.4 %collective-permute-start.4 = (f32[16,1152]{1,0:T(8,128)S(1)}, f32[16,1152]{1,0:T(8,128)S(1)}, u32[]{:S(2)}, u32[]{:S(2)}) collective-permute-start(f32[16,1152]{1,0:T(8,128)S(1)} %collective-permute-done.3.refs_4_), channel_id=1, source_target_pairs={{0,4},{4,0},{8,12},{12,8},{16,20},{20,16},{24,28},{28,24},{1,5},{5... | collective-permute-start | bytes 221192 | tf_op jit(solution)/shard_map/ppermute | solution.py:225
  30.7 4.4 %collective-permute-start.6 = (f32[16,1152]{1,0:T(8,128)S(1)}, f32[16,1152]{1,0:T(8,128)S(1)}, u32[]{:S(2)}, u32[]{:S(2)}) collective-permute-start(f32[16,1152]{1,0:T(8,128)S(1)} %collective-permute-done.5.refs_6_), channel_id=1, source_target_pairs={{0,4},{4,0},{8,12},{12,8},{16,20},{20,16},{24,28},{28,24},{1,5},{5... | collective-permute-start | bytes 221192 | tf_op jit(solution)/shard_map/ppermute | solution.py:225
  35.1 0.9 %copy-start.1 = (f32[16,1152]{1,0:T(8,128)S(1)}, f32[16,1152]{1,0:T(8,128)}, u32[]{:S(2)}) copy-start(f32[16,1152]{1,0:T(8,128)} %shard_map.74.refs_0_) | copy-start | bytes 221188
  36.7 11.1 %collective-permute-start.8 = (f32[1056,128]{1,0:T(8,128)S(1)}, f32[1056,128]{1,0:T(8,128)S(1)}, u32[]{:S(2)}, u32[]{:S(2)}) collective-permute-start(f32[1056,128]{1,0:T(8,128)S(1)} %shard_map.75.own), channel_id=1, source_target_pairs={{0,2},{1,3},{2,0},{3,1},{4,6},{5,7},{6,4},{7,5},{8,10},{9,11},{10,... | collective-permute-start | bytes 1622024 | tf_op jit(solution)/shard_map/ppermute | solution.py:281
  39.7 16.3 %all-to-all-start.1 = ((f32[8,2,16,512]{3,2,1,0:T(8,128)}), f32[8,2,16,512]{3,2,1,0:T(8,128)S(1)}, u32[]{:S(2)}, u32[]{:S(2)}) async-start(f32[8,2,16,512]{3,2,1,0:T(8,128)} %shard_map.78), calls=%async_computation.1 | async-start | bytes 1048576 | tf_op jit(solution)/shard_map/all_to_all | solution.py:292
  43.2 4.7 %collective-permute-start.7 = (f32[1056,128]{1,0:T(8,128)S(1)}, f32[1056,128]{1,0:T(8,128)S(1)}, u32[]{:S(2)}, u32[]{:S(2)}) collective-permute-start(f32[1056,128]{1,0:T(8,128)S(1)} %shard_map.75.own), channel_id=1, source_target_pairs={{0,1},{1,0},{2,3},{3,2},{4,5},{5,4},{6,7},{7,6},{8,9},{9,8},{10,11... | collective-permute-start | bytes 1622024 | tf_op jit(solution)/shard_map/ppermute | solution.py:282
  47.8 1.9 %collective-permute-start.9 = (f32[1056,128]{1,0:T(8,128)S(1)}, f32[1056,128]{1,0:T(8,128)S(1)}, u32[]{:S(2)}, u32[]{:S(2)}) collective-permute-start(f32[1056,128]{1,0:T(8,128)S(1)} %collective-permute-done.8.far), channel_id=1, source_target_pairs={{0,1},{1,0},{2,3},{3,2},{4,5},{5,4},{6,7},{7,6},{8,9},{9,8},{10,11... | collective-permute-start | bytes 1622024 | tf_op jit(solution)/shard_map/ppermute | solution.py:283

commit v3 on v2

--- a/solution.py
+++ b/solution.py
@@ -42,15 +42,15 @@
     return jnp.take_along_axis(value, where, axis=1, mode="promise_in_bounds")
 
 
-def pick_kernel(shape, owner, *refs):
+def pick_kernel(shape, *refs):
     slab, depth, block_cells, groups, count = shape
-    out, arrivals = refs[4], refs[9]
-    copies = [pltpu.make_async_copy(refs[i], refs[5 + i], arrivals.at[i]) for i in range(4)]
+    out, arrivals = refs[5], refs[11]
+    copies = [pltpu.make_async_copy(refs[i], refs[6 + i], arrivals.at[i]) for i in range(5)]
     for copy in copies:
         copy.start()
     for copy in copies:
         copy.wait()
-    weights, offsets, ancestors, prior = refs[5:9]
+    owner, weights, offsets, ancestors, prior = refs[6:11]
     width = groups * count
     per = LANES // count
     for b in range(NB):
@@ -82,7 +82,7 @@
         out[row : row + 1, block : block + LANES] = ancestors[b].astype(F32)
 
 
-def retile_kernel(shape, prior, out):
+def retile_kernel(shape, prior, after, out):
     n, slab, depth, block_cells = shape
     for r in range(n):
         for level in range(depth):
@@ -242,13 +242,14 @@
     piece = call(
         functools.partial(pick_kernel, (slab, depth, block_cells, groups, count)),
         shape((slab, wide), F32),
-        [SMEM] + [PLACE] * 4,
+        [PLACE] * 5,
         scratch=[
+            pltpu.SMEM(obs_owner.shape, jnp.int32),
             pltpu.VMEM(channel_weights.shape, F32),
             pltpu.VMEM(obs_offset.shape, jnp.int32),
             pltpu.VMEM(parents.shape, jnp.int32),
             pltpu.VMEM(prior.shape, F32),
-            pltpu.SemaphoreType.DMA((4,)),
+            pltpu.SemaphoreType.DMA((5,)),
         ],
         moved=10**6,
         limit=None,
@@ -258,9 +259,9 @@
     send = call(
         functools.partial(retile_kernel, (n, slab, depth, block_cells)),
         shape((n, depth, slab, block_cells), F32),
-        [VMEM],
-        moved=10**6,
-    )(prior)
+        [VMEM, PLACE],
+        moved=10**6,
+    )(prior, pieces[min(2, len(pieces) - 1)])
     fields = lax.all_to_all(send, "grid", 0, 0, tiled=True)
 
     rows, steps = call(
@@ -277,8 +278,7 @@
         scratch=[pltpu.VMEM((n, slab, wide), F32)],
         moved=10**6,
     )(obs_owner, rows, *pieces)
-    ready, fields = lax.optimization_barrier((own, fields))
-    far = lax.ppermute(ready, "lev", [(j, j ^ 2) for j in range(lev)])
+    far = lax.ppermute(own, "lev", [(j, j ^ 2) for j in range(lev)])
     near = lax.ppermute(own, "lev", [(j, j ^ 1) for j in range(lev)])
     cross = lax.ppermute(far, "lev", [(j, j ^ 1) for j in range(lev)])
 

time: 67.4 us -> 70.6 us (1.047)
  waiting for transfers between devices: 20.5 us -> 26.3 us
  local copies, waits for them, and re-layouts: 1.95 us -> 0.03 us
    ppermute x3, waiting for transfers between devices: 8.15 us -> 15 us  [gather_pieces(): pieces.append(lax.ppermute(piece, 'grid', [(j, j ^ far) for j in range(n)]))]
    ppermute x3, starting transfers between devices: 4.51 us -> 7.47 us  [gather_pieces(): pieces.append(lax.ppermute(piece, 'grid', [(j, j ^ far) for j in range(n)]))]
    ppermute x4, starting transfers between devices: 6.12 us -> 4.05 us  [gather_pieces(): result += [part, lax.ppermute(part, 'grid', [(j, j ^ 1) for j in range(n)])]]
    unnamed x14, local copies, waits for them, and re-layouts: 1.95 us -> 0.03 us
    all_to_all x1, starting transfers between devices: 7.28 us -> 6.42 us  [body(): fields = lax.all_to_all(send, 'grid', 0, 0, tiled=True)]
    pallas_call x1, Pallas kernels: 3.2 us -> 2.47 us  [body(): call(functools.partial(pick_kernel, (slab, depth, block_cells, groups, co...]
    ppermute x1, waiting for transfers between devices: 4.58 us -> 3.86 us  [body(): far = lax.ppermute(own, 'lev', [(j, j ^ 2) for j in range(lev)])]
  transfers between devices with their start and end apart: 12 -> 12, of which waited for: 7 -> 7; matrix products, arithmetic and copies ran while one was open for 0% -> 0% of each run, Pallas kernels for 14% -> 9%
where the time goes in v3:
time: 70.6 us; the launch traced here: 70.3 us
  waiting for transfers between devices  26.3 us (37%)
  starting transfers between devices  23.1 us (33%)
  Pallas kernels  10.6 us (15%)
  blocking collectives  10.2 us (14%)
    ppermute x3, waiting for transfers between devices, gather_pieces(): pieces.append(lax.ppermute(piece, 'grid', [(j, j ^ far) for j in range(n)]))  15 us
    all_to_all x1, blocking collectives, body(): shift = lax.all_to_all(send, 'grid', 0, 0, tiled=True)  10.2 us
    ppermute x3, starting transfers between devices, gather_pieces(): pieces.append(lax.ppermute(piece, 'grid', [(j, j ^ far) for j in range(n)]))  7.47 us
    all_to_all x1, starting transfers between devices, body(): fields = lax.all_to_all(send, 'grid', 0, 0, tiled=True)  6.42 us
    ppermute x4, starting transfers between devices, gather_pieces(): result += [part, lax.ppermute(part, 'grid', [(j, j ^ 1) for j in range(n)])]  4.05 us
    ppermute x1, waiting for transfers between devices, body(): far = lax.ppermute(own, 'lev', [(j, j ^ 2) for j in range(lev)])  3.86 us
    all_to_all x1, starting transfers between devices, body(): moved = lax.all_to_all(send, 'grid', 0, 0, tiled=True)  3.49 us
    pallas_call x1, Pallas kernels, body(): call(functools.partial(chain_kernel, (n, slab, depth, block_cells, groups...  3.11 us
  transfers between devices with their start and end apart: 12, of which 7 were waited for; matrix products, arithmetic and copies ran while one was open for 0% of the time, Pallas kernels for 9%

profile of v3, /device:TPU:0, one launch (start us, length us, event | category | flops | bytes accessed | tf_op | source)
XLA Modules:
  0.0 70.3 jit_solution(13830225080305217876)
XLA Ops:
  0.0 0.0 copy-start
  0.0 2.5 %shard_map.74.refs_0_ = f32[16,1152]{1,0:T(8,128)} custom-call(s32[4]{0:T(128)} %owner.3, f32[2,4]{1,0:T(2,128)} %refs_1_.1, s32[4,4,64]{2,1,0:T(4,128)} %refs_2_.1, s32[4,1,128]{2,1,0:T(1,128)} %bitcast.1, f32[16,2,4096]{2,1,0:T(2,128)} %prior.1), custom_call_target="tpu_custom_call" | custom-call | bytes 1000000 | tf_op jit(solution)/shard_map/pallas_call | solution.py:242
  2.5 3.1 %collective-permute-start.1 = (f32[16,1152]{1,0:T(8,128)}, f32[16,1152]{1,0:T(8,128)S(1)}, u32[]{:S(2)}, u32[]{:S(2)}) collective-permute-start(f32[16,1152]{1,0:T(8,128)} %shard_map.74.refs_0_), channel_id=1, source_target_pairs={{0,8},{4,12},{8,0},{12,4},{16,24},{20,28},{24,16},{28,20},{1,9},{5... | collective-permute-start | bytes 221192 | tf_op jit(solution)/shard_map/ppermute | solution.py:222
  5.6 2.5 %collective-permute-done.1.refs_2_.after = f32[16,1152]{1,0:T(8,128)S(1)} collective-permute-done((f32[16,1152]{1,0:T(8,128)}, f32[16,1152]{1,0:T(8,128)S(1)}, u32[]{:S(2)}, u32[]{:S(2)}) %collective-permute-start.1) | collective-permute-done | bytes 73760 | tf_op jit(solution)/shard_map/ppermute | solution.py:222
  8.1 0.0 copy-done
  8.1 0.9 %shard_map.76 = f32[8,2,16,512]{3,2,1,0:T(8,128)} custom-call(f32[16,2,4096]{2,1,0:T(2,128)S(1)} %copy-done, f32[16,1152]{1,0:T(8,128)S(1)} %collective-permute-done.1.refs_2_.after), custom_call_target="tpu_custom_call" | custom-call | bytes 1000000 | tf_op jit(solution)/shard_map/pallas_call | solution.py:259
  9.0 0.0 copy-start.1
  9.0 0.0 copy-start.2
  9.0 0.0 copy-start.3
  9.0 0.0 copy-start.4
  9.0 0.0 copy-start.5
  9.0 0.0 copy-start.6
  9.0 6.4 %all-to-all-start = ((f32[8,2,16,512]{3,2,1,0:T(8,128)}), f32[8,2,16,512]{3,2,1,0:T(8,128)S(1)}, u32[]{:S(2)}, u32[]{:S(2)}) async-start(f32[8,2,16,512]{3,2,1,0:T(8,128)} %shard_map.76), calls=%async_computation | async-start | bytes 1048576 | tf_op jit(solution)/shard_map/all_to_all | solution.py:265
  15.5 0.0 copy-done.1
  15.5 2.9 %collective-permute-start.3 = (f32[16,1152]{1,0:T(8,128)S(1)}, f32[16,1152]{1,0:T(8,128)S(1)}, u32[]{:S(2)}, u32[]{:S(2)}) collective-permute-start(f32[16,1152]{1,0:T(8,128)S(1)} %copy-done.1), channel_id=1, source_target_pairs={{0,16},{4,20},{8,24},{12,28},{16,0},{20,4},{24,8},{28,12},{1,17},{... | collective-permute-start | bytes 221192 | tf_op jit(solution)/shard_map/ppermute | solution.py:222
  18.4 1.5 %collective-permute-start.5 = (f32[16,1152]{1,0:T(8,128)S(1)}, f32[16,1152]{1,0:T(8,128)S(1)}, u32[]{:S(2)}, u32[]{:S(2)}) collective-permute-start(f32[16,1152]{1,0:T(8,128)S(1)} %copy-done.1), channel_id=1, source_target_pairs={{0,24},{4,28},{8,16},{12,20},{16,8},{20,12},{24,0},{28,4},{1,25},{... | collective-permute-start | bytes 221192 | tf_op jit(solution)/shard_map/ppermute | solution.py:222
  19.9 1.5 %collective-permute-start = (f32[16,1152]{1,0:T(8,128)S(1)}, f32[16,1152]{1,0:T(8,128)S(1)}, u32[]{:S(2)}, u32[]{:S(2)}) collective-permute-start(f32[16,1152]{1,0:T(8,128)S(1)} %copy-done.1), channel_id=1, source_target_pairs={{0,4},{4,0},{8,12},{12,8},{16,20},{20,16},{24,28},{28,24},{1,5},{5... | collective-permute-start | bytes 221192 | tf_op jit(solution)/shard_map/ppermute | solution.py:225
  21.3 0.6 collective-permute-start.2
  21.9 12.5 %collective-permute-done.3.refs_4_ = f32[16,1152]{1,0:T(8,128)S(1)} collective-permute-done((f32[16,1152]{1,0:T(8,128)S(1)}, f32[16,1152]{1,0:T(8,128)S(1)}, u32[]{:S(2)}, u32[]{:S(2)}) %collective-permute-start.3) | collective-permute-done | bytes 73760 | tf_op jit(solution)/shard_map/ppermute | solution.py:222
  34.3 1.5 %collective-permute-start.4 = (f32[16,1152]{1,0:T(8,128)S(1)}, f32[16,1152]{1,0:T(8,128)S(1)}, u32[]{:S(2)}, u32[]{:S(2)}) collective-permute-start(f32[16,1152]{1,0:T(8,128)S(1)} %collective-permute-done.3.refs_4_), channel_id=1, source_target_pairs={{0,4},{4,0},{8,12},{12,8},{16,20},{20,16},{24,28},{28,24},{1,5},{5... | collective-permute-start | bytes 221192 | tf_op jit(solution)/shard_map/ppermute | solution.py:225
  35.8 0.0 collective-permute-done.5.refs_6_
  35.8 0.6 collective-permute-start.6
  36.4 0.0 copy-done.2
  36.4 0.0 copy-done.3
  36.4 0.0 copy-done.4
  36.4 0.0 copy-done.5
  36.4 0.0 copy-done.6
  36.4 1.0 %shard_map.73 = (f32[32,128]{1,0:T(8,128)S(1)}, f32[5,128,128]{2,1,0:T(8,128)S(1)}) custom-call(s32[4]{0:T(128)S(1)} %copy-done.4, s32[4,4,64]{2,1,0:T(4,128)S(1)} %copy-done.2, f32[4,1,64]{2,1,0:T(1,128)S(1)} %copy-done.5, f32[4,1,64]{2,1,0:T(1,128)S(1)} %copy-done.6, s32[4,1,128]{2,1,0:T(1,128)S(1)} %bitcast.2), custom_call_target="tpu_custom_call" | custom-call | bytes 1000000 | tf_op jit(solution)/shard_map/pallas_call | solution.py:267
  37.4 0.0 collective-permute-done.refs_1_
  37.4 0.0 collective-permute-done.2.refs_3_
  37.4 1.3 %collective-permute-done.4.refs_5_ = f32[16,1152]{1,0:T(8,128)S(1)} collective-permute-done((f32[16,1152]{1,0:T(8,128)S(1)}, f32[16,1152]{1,0:T(8,128)S(1)}, u32[]{:S(2)}, u32[]{:S(2)}) %collective-permute-start.4) | collective-permute-done | bytes 73760 | tf_op jit(solution)/shard_map/ppermute | solution.py:225
  38.7 1.5 %collective-permute-done.6.refs_7_ = f32[16,1152]{1,0:T(8,128)S(1)} collective-permute-done((f32[16,1152]{1,0:T(8,128)S(1)}, f32[16,1152]{1,0:T(8,128)S(1)}, u32[]{:S(2)}, u32[]{:S(2)}) %collective-permute-start.6) | collective-permute-done | bytes 73760 | tf_op jit(solution)/shard_map/ppermute | solution.py:225
  40.2 0.8 %shard_map.75.own = f32[1056,128]{1,0:T(8,128)S(1)} custom-call(s32[4]{0:T(128)S(1)} %copy-done.4, f32[32,128]{1,0:T(8,128)S(1)} %get-tuple-element.9.rows, f32[16,1152]{1,0:T(8,128)S(1)} %copy-done.1, f32[16,1152]{1,0:T(8,128)S(1)} %collective-permute-done.refs_1_, f32[16,1152]{1,0:T(8,128)S(1)} %collective-permute-done.1.refs_2_.after, ...), custom_call_target="tpu_custom_call" | custom-call | bytes 1000000 | tf_op jit(solution)/shard_map/pallas_call | solution.py:274
  40.9 1.6 %collective-permute-start.8 = (f32[1056,128]{1,0:T(8,128)S(1)}, f32[1056,128]{1,0:T(8,128)S(1)}, u32[]{:S(2)}, u32[]{:S(2)}) collective-permute-start(f32[1056,128]{1,0:T(8,128)S(1)} %shard_map.75.own), channel_id=1, source_target_pairs={{0,2},{1,3},{2,0},{3,1},{4,6},{5,7},{6,4},{7,5},{8,10},{9,11},{10,... | collective-permute-start | bytes 1622024 | tf_op jit(solution)/shard_map/ppermute | solution.py:281
  42.5 0.0 all-to-all-done.fields
  42.5 1.4 %shard_map.78 = f32[8,2,16,512]{3,2,1,0:T(8,128)} custom-call(f32[5,128,128]{2,1,0:T(8,128)S(1)} %get-tuple-element.10.steps, f32[8,2,16,512]{3,2,1,0:T(8,128)S(1)} %all-to-all-done.fields), custom_call_target="tpu_custom_call" | custom-call | flops 100000000 | bytes 1000000 | tf_op jit(solution)/shard_map/pallas_call | solution.py:285
  43.9 3.5 %all-to-all-start.1 = ((f32[8,2,16,512]{3,2,1,0:T(8,128)}), f32[8,2,16,512]{3,2,1,0:T(8,128)S(1)}, u32[]{:S(2)}, u32[]{:S(2)}) async-start(f32[8,2,16,512]{3,2,1,0:T(8,128)} %shard_map.78), calls=%async_computation.1 | async-start | bytes 1048576 | tf_op jit(solution)/shard_map/all_to_all | solution.py:292
  47.4 0.1 collective-permute-start.7
  47.5 3.9 %collective-permute-done.8.far = f32[1056,128]{1,0:T(8,128)S(1)} collective-permute-done((f32[1056,128]{1,0:T(8,128)S(1)}, f32[1056,128]{1,0:T(8,128)S(1)}, u32[]{:S(2)}, u32[]{:S(2)}) %collective-permute-start.8) | collective-permute-done | bytes 540704 | tf_op jit(solution)/shard_map/ppermute | solution.py:281
  51.3 0.0 collective-permute-start.9
  51.3 0.0 collective-permute-done.7.near
  51.3 1.9 %collective-permute-done.9.cross = f32[1056,128]{1,0:T(8,128)S(1)} collective-permute-done((f32[1056,128]{1,0:T(8,128)S(1)}, f32[1056,128]{1,0:T(8,128)S(1)}, u32[]{:S(2)}, u32[]{:S(2)}) %collective-permute-start.9) | collective-permute-done | bytes 540704 | tf_op jit(solution)/shard_map/ppermute | solution.py:283
  53.3 3.1 %shard_map.77 = f32[8,2,512]{2,1,0:T(2,128)S(1)} custom-call(f32[1056,128]{1,0:T(8,128)S(1)} %shard_map.75.own, f32[1056,128]{1,0:T(8,128)S(1)} %collective-permute-done.7.near, f32[1056,128]{1,0:T(8,128)S(1)} %collective-permute-done.8.far, f32[1056,128]{1,0:T(8,128)S(1)} %collective-permute-done.9.cross, f32[5,128,128]{2,1,0:T(8,128)S(1)} %get-tuple-element.10.steps, ...), custom_call_target="tpu_custom_call" | custom-call | flops 1000000000 | bytes 10000000 | tf_op jit(solution)/shard_map/pallas_call | solution.py:294
  56.4 2.8 %all-to-all-done.1.moved = f32[8,2,16,512]{3,2,1,0:T(8,128)S(1)} async-done(((f32[8,2,16,512]{3,2,1,0:T(8,128)}), f32[8,2,16,512]{3,2,1,0:T(8,128)S(1)}, u32[]{:S(2)}, u32[]{:S(2)}) %all-to-all-start.1) | async-done | bytes 524320 | tf_op jit(solution)/shard_map/all_to_all | solution.py:292
  59.2 10.2 %all_to_all.15.shift = f32[8,2,512]{2,1,0:T(2,128)S(1)} all-to-all(f32[8,2,512]{2,1,0:T(2,128)S(1)} %shard_map.77), channel_id=1, replica_groups=mesh['grid'=8,'lev'=4] {'grid'}, dimensions={0} | all-to-all | bytes 65536 | tf_op jit(solution)/shard_map/all_to_all | solution.py:302
  69.3 0.9 %shard_map.79 = f32[16,2,4096]{2,1,0:T(2,128)} custom-call(f32[8,2,16,512]{3,2,1,0:T(8,128)S(1)} %all-to-all-done.1.moved, f32[8,2,512]{2,1,0:T(2,128)S(1)} %all_to_all.15.shift), custom_call_target="tpu_custom_call" | custom-call | bytes 1000000 | tf_op jit(solution)/shard_map/pallas_call | solution.py:304
Async XLA Ops:
  0.0 8.1 %copy-start = (f32[16,2,4096]{2,1,0:T(2,128)S(1)}, f32[16,2,4096]{2,1,0:T(2,128)}, u32[]{:S(2)}) copy-start(f32[16,2,4096]{2,1,0:T(2,128)} %prior.1) | copy-start | bytes 1572868
  2.5 5.6 %collective-permute-start.1 = (f32[16,1152]{1,0:T(8,128)}, f32[16,1152]{1,0:T(8,128)S(1)}, u32[]{:S(2)}, u32[]{:S(2)}) collective-permute-start(f32[16,1152]{1,0:T(8,128)} %shard_map.74.refs_0_), channel_id=1, source_target_pairs={{0,8},{4,12},{8,0},{12,4},{16,24},{20,28},{24,16},{28,20},{1,9},{5... | collective-permute-start | bytes 221192 | tf_op jit(solution)/shard_map/ppermute | solution.py:222
  9.0 6.5 %copy-start.1 = (f32[16,1152]{1,0:T(8,128)S(1)}, f32[16,1152]{1,0:T(8,128)}, u32[]{:S(2)}) copy-start(f32[16,1152]{1,0:T(8,128)} %shard_map.74.refs_0_) | copy-start | bytes 221188
  9.0 27.4 %copy-start.2 = (s32[4,4,64]{2,1,0:T(4,128)S(1)}, s32[4,4,64]{2,1,0:T(4,128)}, u32[]{:S(2)}) copy-start(s32[4,4,64]{2,1,0:T(4,128)} %refs_2_.1) | copy-start | bytes 12292
  9.0 27.4 %copy-start.3 = (s32[4,1,1,128]{3,2,1,0:T(1,128)S(1)}, s32[4,1,1,128]{3,2,1,0:T(1,128)}, u32[]{:S(2)}) copy-start(s32[4,1,1,128]{3,2,1,0:T(1,128)} %param.13) | copy-start | bytes 6148
  9.0 27.4 %copy-start.4 = (s32[4]{0:T(128)S(1)}, s32[4]{0:T(128)}, u32[]{:S(2)}) copy-start(s32[4]{0:T(128)} %owner.3) | copy-start | bytes 52
  9.0 27.4 %copy-start.5 = (f32[4,1,64]{2,1,0:T(1,128)S(1)}, f32[4,1,64]{2,1,0:T(1,128)}, u32[]{:S(2)}) copy-start(f32[4,1,64]{2,1,0:T(1,128)} %values.1) | copy-start | bytes 3076
  9.0 27.3 %copy-start.6 = (f32[4,1,64]{2,1,0:T(1,128)S(1)}, f32[4,1,64]{2,1,0:T(1,128)}, u32[]{:S(2)}) copy-start(f32[4,1,64]{2,1,0:T(1,128)} %errors.1) | copy-start | bytes 3076
  9.0 33.5 %all-to-all-start = ((f32[8,2,16,512]{3,2,1,0:T(8,128)}), f32[8,2,16,512]{3,2,1,0:T(8,128)S(1)}, u32[]{:S(2)}, u32[]{:S(2)}) async-start(f32[8,2,16,512]{3,2,1,0:T(8,128)} %shard_map.76), calls=%async_computation | async-start | bytes 1048576 | tf_op jit(solution)/shard_map/all_to_all | solution.py:265
  15.5 18.9 %collective-permute-start.3 = (f32[16,1152]{1,0:T(8,128)S(1)}, f32[16,1152]{1,0:T(8,128)S(1)}, u32[]{:S(2)}, u32[]{:S(2)}) collective-permute-start(f32[16,1152]{1,0:T(8,128)S(1)} %copy-done.1), channel_id=1, source_target_pairs={{0,16},{4,20},{8,24},{12,28},{16,0},{20,4},{24,8},{28,12},{1,17},{... | collective-permute-start | bytes 221192 | tf_op jit(solution)/shard_map/ppermute | solution.py:222
  18.4 17.4 %collective-permute-start.5 = (f32[16,1152]{1,0:T(8,128)S(1)}, f32[16,1152]{1,0:T(8,128)S(1)}, u32[]{:S(2)}, u32[]{:S(2)}) collective-permute-start(f32[16,1152]{1,0:T(8,128)S(1)} %copy-done.1), channel_id=1, source_target_pairs={{0,24},{4,28},{8,16},{12,20},{16,8},{20,12},{24,0},{28,4},{1,25},{... | collective-permute-start | bytes 221192 | tf_op jit(solution)/shard_map/ppermute | solution.py:222
  19.9 17.5 %collective-permute-start = (f32[16,1152]{1,0:T(8,128)S(1)}, f32[16,1152]{1,0:T(8,128)S(1)}, u32[]{:S(2)}, u32[]{:S(2)}) collective-permute-start(f32[16,1152]{1,0:T(8,128)S(1)} %copy-done.1), channel_id=1, source_target_pairs={{0,4},{4,0},{8,12},{12,8},{16,20},{20,16},{24,28},{28,24},{1,5},{5... | collective-permute-start | bytes 221192 | tf_op jit(solution)/shard_map/ppermute | solution.py:225
  21.3 16.1 %collective-permute-start.2 = (f32[16,1152]{1,0:T(8,128)S(1)}, f32[16,1152]{1,0:T(8,128)S(1)}, u32[]{:S(2)}, u32[]{:S(2)}) collective-permute-start(f32[16,1152]{1,0:T(8,128)S(1)} %collective-permute-done.1.refs_2_.after), channel_id=1, source_target_pairs={{0,4},{4,0},{8,12},{12,8},{16,20},{20,16},{24,28},{28,24},{1,5},{5... | collective-permute-start | bytes 221192 | tf_op jit(solution)/shard_map/ppermute | solution.py:225
  34.3 4.4 %collective-permute-start.4 = (f32[16,1152]{1,0:T(8,128)S(1)}, f32[16,1152]{1,0:T(8,128)S(1)}, u32[]{:S(2)}, u32[]{:S(2)}) collective-permute-start(f32[16,1152]{1,0:T(8,128)S(1)} %collective-permute-done.3.refs_4_), channel_id=1, source_target_pairs={{0,4},{4,0},{8,12},{12,8},{16,20},{20,16},{24,28},{28,24},{1,5},{5... | collective-permute-start | bytes 221192 | tf_op jit(solution)/shard_map/ppermute | solution.py:225
  35.8 4.4 %collective-permute-start.6 = (f32[16,1152]{1,0:T(8,128)S(1)}, f32[16,1152]{1,0:T(8,128)S(1)}, u32[]{:S(2)}, u32[]{:S(2)}) collective-permute-start(f32[16,1152]{1,0:T(8,128)S(1)} %collective-permute-done.5.refs_6_), channel_id=1, source_target_pairs={{0,4},{4,0},{8,12},{12,8},{16,20},{20,16},{24,28},{28,24},{1,5},{5... | collective-permute-start | bytes 221192 | tf_op jit(solution)/shard_map/ppermute | solution.py:225
  40.9 10.4 %collective-permute-start.8 = (f32[1056,128]{1,0:T(8,128)S(1)}, f32[1056,128]{1,0:T(8,128)S(1)}, u32[]{:S(2)}, u32[]{:S(2)}) collective-permute-start(f32[1056,128]{1,0:T(8,128)S(1)} %shard_map.75.own), channel_id=1, source_target_pairs={{0,2},{1,3},{2,0},{3,1},{4,6},{5,7},{6,4},{7,5},{8,10},{9,11},{10,... | collective-permute-start | bytes 1622024 | tf_op jit(solution)/shard_map/ppermute | solution.py:281
  43.9 15.3 %all-to-all-start.1 = ((f32[8,2,16,512]{3,2,1,0:T(8,128)}), f32[8,2,16,512]{3,2,1,0:T(8,128)S(1)}, u32[]{:S(2)}, u32[]{:S(2)}) async-start(f32[8,2,16,512]{3,2,1,0:T(8,128)} %shard_map.78), calls=%async_computation.1 | async-start | bytes 1048576 | tf_op jit(solution)/shard_map/all_to_all | solution.py:292
  47.4 4.0 %collective-permute-start.7 = (f32[1056,128]{1,0:T(8,128)S(1)}, f32[1056,128]{1,0:T(8,128)S(1)}, u32[]{:S(2)}, u32[]{:S(2)}) collective-permute-start(f32[1056,128]{1,0:T(8,128)S(1)} %shard_map.75.own), channel_id=1, source_target_pairs={{0,1},{1,0},{2,3},{3,2},{4,5},{5,4},{6,7},{7,6},{8,9},{9,8},{10,11... | collective-permute-start | bytes 1622024 | tf_op jit(solution)/shard_map/ppermute | solution.py:282
  51.3 1.9 %collective-permute-start.9 = (f32[1056,128]{1,0:T(8,128)S(1)}, f32[1056,128]{1,0:T(8,128)S(1)}, u32[]{:S(2)}, u32[]{:S(2)}) collective-permute-start(f32[1056,128]{1,0:T(8,128)S(1)} %collective-permute-done.8.far), channel_id=1, source_target_pairs={{0,1},{1,0},{2,3},{3,2},{4,5},{5,4},{6,7},{7,6},{8,9},{9,8},{10,11... | collective-permute-start | bytes 1622024 | tf_op jit(solution)/shard_map/ppermute | solution.py:283

commit v4 on v3

--- a/solution.py
+++ b/solution.py
@@ -82,7 +82,7 @@
         out[row : row + 1, block : block + LANES] = ancestors[b].astype(F32)
 
 
-def retile_kernel(shape, prior, after, out):
+def retile_kernel(shape, prior, out):
     n, slab, depth, block_cells = shape
     for r in range(n):
         for level in range(depth):
@@ -120,7 +120,7 @@
     steps[NB] = turned.T
 
 
-def turn_kernel(shape, owner, rows, *refs):
+def turn_kernel(shape, owner, rows, ahead, *refs):
     n, slab, width = shape
     pieces, out, held = refs[:-2], refs[-2], refs[-1]
     members = n * slab
@@ -140,16 +140,16 @@
         out[width + PARENT + i : width + PARENT + i + 1, :] = held[owner[b], line : line + 1, lane : lane + LANES]
 
 
-def mix_kernel(shape, steps, fields, out):
+def mix_kernel(shape, steps, pull, fields, out):
     n, slab, depth, block_cells = shape
+    blend = steps[NB] + pull[0:1, :]
     for level in range(depth):
         value = fields[:, level].reshape(n * slab, block_cells)
-        out[:, level] = high_dot(steps[NB], value).reshape(n, slab, block_cells)
-
-
-def chain_kernel(shape, own, near, far, cross, steps, fields, out):
-    n, slab, depth, block_cells, groups, count = shape
-    members = n * slab
+        out[:, level] = high_dot(blend, value).reshape(n, slab, block_cells)
+
+
+def chain_kernel(shape, own, near, far, cross, steps, out):
+    members, groups, count = shape
     width = groups * count
     base = NB * width
     group = lax.axis_index("lev")
@@ -199,19 +199,14 @@
     pull = jnp.zeros((8, members), F32)
     for b in range(NB):
         pull = pull + high_dot(jnp.broadcast_to(pulled[b], (8, members)), steps[b])
-    for level in range(depth):
-        value = fields[:, level].reshape(members, block_cells)
-        shift = high_dot(pull, value)[0:1]
-        for d in range(n):
-            out[d, level : level + 1, :] = shift
-
-
-def final_kernel(shape, moved, shift, out):
+    out[...] = pull
+
+
+def final_kernel(shape, moved, out):
     n, slab, depth, block_cells = shape
     for r in range(n):
         for level in range(depth):
-            value = moved[r, level] + shift[r, level : level + 1, :]
-            out[:, level, r * block_cells : (r + 1) * block_cells] = value
+            out[:, level, r * block_cells : (r + 1) * block_cells] = moved[r, level]
 
 
 def gather_pieces(piece, n):
@@ -259,9 +254,9 @@
     send = call(
         functools.partial(retile_kernel, (n, slab, depth, block_cells)),
         shape((n, depth, slab, block_cells), F32),
-        [VMEM, PLACE],
-        moved=10**6,
-    )(prior, pieces[min(2, len(pieces) - 1)])
+        [VMEM],
+        moved=10**6,
+    )(prior)
     fields = lax.all_to_all(send, "grid", 0, 0, tiled=True)
 
     rows, steps = call(
@@ -274,39 +269,36 @@
     own = call(
         functools.partial(turn_kernel, (n, slab, width)),
         shape((width + SPARE, members), F32),
-        [SMEM] + [VMEM] * (1 + len(pieces)),
+        [SMEM, VMEM, PLACE] + [VMEM] * len(pieces),
         scratch=[pltpu.VMEM((n, slab, wide), F32)],
         moved=10**6,
-    )(obs_owner, rows, *pieces)
+    )(obs_owner, rows, send, *pieces)
     far = lax.ppermute(own, "lev", [(j, j ^ 2) for j in range(lev)])
     near = lax.ppermute(own, "lev", [(j, j ^ 1) for j in range(lev)])
     cross = lax.ppermute(far, "lev", [(j, j ^ 1) for j in range(lev)])
 
+    pull = call(
+        functools.partial(chain_kernel, (members, groups, count)),
+        shape((8, members), F32),
+        [VMEM] * 5,
+        moved=10**5,
+    )(own, near, far, cross, steps)
+
     send = call(
         functools.partial(mix_kernel, (n, slab, depth, block_cells)),
         shape((n, depth, slab, block_cells), F32),
-        [VMEM, VMEM],
+        [VMEM] * 3,
         flops=10**8,
         moved=10**6,
-    )(steps, fields)
+    )(steps, pull, fields)
     moved = lax.all_to_all(send, "grid", 0, 0, tiled=True)
-
-    send = call(
-        functools.partial(chain_kernel, (n, slab, depth, block_cells, groups, count)),
-        shape((n, depth, block_cells), F32),
-        [VMEM] * 6,
-        flops=10**9,
-        moved=10**7,
-    )(own, near, far, cross, steps, fields)
-    send, moved = lax.optimization_barrier((send, moved))
-    shift = lax.all_to_all(send, "grid", 0, 0, tiled=True)
 
     return call(
         functools.partial(final_kernel, (n, slab, depth, block_cells)),
         shape((slab, depth, cells), F32),
-        [VMEM, VMEM],
-        moved=10**6,
-    )(moved, shift)
+        [VMEM],
+        moved=10**6,
+    )(moved)
 
 
 def solution(mesh):

time: 70.6 us -> 58.6 us (0.83)
  waiting for transfers between devices: 26.3 us -> 14.5 us
  blocking collectives: 10.2 us -> 17.2 us
  starting transfers between devices: 23.1 us -> 17.1 us
  Pallas kernels: 10.6 us -> 9.33 us
    ppermute x3, waiting for transfers between devices: 15 us -> 2.27 us  [gather_pieces(): pieces.append(lax.ppermute(piece, 'grid', [(j, j ^ far) for j in range(n)]))]
    all_to_all x1, blocking collectives: 10.2 us -> 17.2 us  [body(): moved = lax.all_to_all(send, 'grid', 0, 0, tiled=True)]
    ppermute x1, waiting for transfers between devices: 3.86 us -> 7.69 us  [body(): far = lax.ppermute(own, 'lev', [(j, j ^ 2) for j in range(lev)])]
    all_to_all x1 -> x0, starting transfers between devices: 3.49 us -> none  [body(): moved = lax.all_to_all(send, 'grid', 0, 0, tiled=True)]
    all_to_all x1 -> x0, waiting for transfers between devices: 2.8 us -> none  [body(): moved = lax.all_to_all(send, 'grid', 0, 0, tiled=True)]
    all_to_all x1, starting transfers between devices: 6.42 us -> 4.22 us  [body(): fields = lax.all_to_all(send, 'grid', 0, 0, tiled=True)]
    ppermute x3, starting transfers between devices: 7.47 us -> 5.76 us  [gather_pieces(): pieces.append(lax.ppermute(piece, 'grid', [(j, j ^ far) for j in range(n)]))]
    ppermute x4, starting transfers between devices: 4.05 us -> 5.55 us  [gather_pieces(): result += [part, lax.ppermute(part, 'grid', [(j, j ^ 1) for j in range(n)])]]
  transfers between devices with their start and end apart: 12 -> 11, of which waited for: 7 -> 7; matrix products, arithmetic and copies ran while one was open for 0% -> 0% of each run, Pallas kernels for 9% -> 8%
where the time goes in v4:
time: 58.6 us; the launch traced here: 58.3 us
  blocking collectives  17.2 us (29%)
  starting transfers between devices  17.1 us (29%)
  waiting for transfers between devices  14.5 us (25%)
  Pallas kernels  9.33 us (16%)
    all_to_all x1, blocking collectives, body(): moved = lax.all_to_all(send, 'grid', 0, 0, tiled=True)  17.2 us
    ppermute x1, waiting for transfers between devices, body(): far = lax.ppermute(own, 'lev', [(j, j ^ 2) for j in range(lev)])  7.69 us
    ppermute x3, starting transfers between devices, gather_pieces(): pieces.append(lax.ppermute(piece, 'grid', [(j, j ^ far) for j in range(n)]))  5.76 us
    ppermute x4, starting transfers between devices, gather_pieces(): result += [part, lax.ppermute(part, 'grid', [(j, j ^ 1) for j in range(n)])]  5.55 us
    all_to_all x1, starting transfers between devices, body(): fields = lax.all_to_all(send, 'grid', 0, 0, tiled=True)  4.22 us
    pallas_call x1, Pallas kernels, body(): call(functools.partial(chain_kernel, (members, groups, count)), shape((8,...  2.73 us
    pallas_call x1, Pallas kernels, body(): call(functools.partial(pick_kernel, (slab, depth, block_cells, groups, co...  2.46 us
    ppermute x3, waiting for transfers between devices, gather_pieces(): pieces.append(lax.ppermute(piece, 'grid', [(j, j ^ far) for j in range(n)]))  2.27 us
  transfers between devices with their start and end apart: 11, of which 7 were waited for; matrix products, arithmetic and copies ran while one was open for 0% of the time, Pallas kernels for 8%

profile of v4, /device:TPU:0, one launch (start us, length us, event | category | flops | bytes accessed | tf_op | source)
XLA Modules:
  0.0 58.3 jit_solution(9438205363125181950)
XLA Ops:
  0.0 0.0 copy-start
  0.0 2.5 %shard_map.75.refs_0_ = f32[16,1152]{1,0:T(8,128)} custom-call(s32[4]{0:T(128)} %owner.3, f32[2,4]{1,0:T(2,128)} %refs_1_.1, s32[4,4,64]{2,1,0:T(4,128)} %refs_2_.1, s32[4,1,128]{2,1,0:T(1,128)} %bitcast.1, f32[16,2,4096]{2,1,0:T(2,128)} %refs_4_.1), custom_call_target="tpu_custom_call" | custom-call | bytes 1000000 | tf_op jit(solution)/shard_map/pallas_call | solution.py:237
  2.5 0.0 copy-start.2
  2.5 0.0 copy-start.3
  2.5 0.0 copy-start.4
  2.5 0.0 copy-start.5
  2.5 0.0 copy-start.6
  2.5 0.0 copy-start.1
  2.5 5.1 %collective-permute-start.5 = (f32[16,1152]{1,0:T(8,128)}, f32[16,1152]{1,0:T(8,128)S(1)}, u32[]{:S(2)}, u32[]{:S(2)}) collective-permute-start(f32[16,1152]{1,0:T(8,128)} %shard_map.75.refs_0_), channel_id=1, source_target_pairs={{0,24},{4,28},{8,16},{12,20},{16,8},{20,12},{24,0},{28,4},{1,25},{... | collective-permute-start | bytes 221192 | tf_op jit(solution)/shard_map/ppermute | solution.py:217
  7.7 0.0 collective-permute-start.3
  7.7 0.6 %collective-permute-start.1 = (f32[16,1152]{1,0:T(8,128)}, f32[16,1152]{1,0:T(8,128)S(1)}, u32[]{:S(2)}, u32[]{:S(2)}) collective-permute-start(f32[16,1152]{1,0:T(8,128)} %shard_map.75.refs_0_), channel_id=1, source_target_pairs={{0,8},{4,12},{8,0},{12,4},{16,24},{20,28},{24,16},{28,20},{1,9},{5... | collective-permute-start | bytes 221192 | tf_op jit(solution)/shard_map/ppermute | solution.py:217
  8.3 1.7 %collective-permute-start = (f32[16,1152]{1,0:T(8,128)}, f32[16,1152]{1,0:T(8,128)S(1)}, u32[]{:S(2)}, u32[]{:S(2)}) collective-permute-start(f32[16,1152]{1,0:T(8,128)} %shard_map.75.refs_0_), channel_id=1, source_target_pairs={{0,4},{4,0},{8,12},{12,8},{16,20},{20,16},{24,28},{28,24},{1,5},{5... | collective-permute-start | bytes 221192 | tf_op jit(solution)/shard_map/ppermute | solution.py:220
  10.0 0.7 %collective-permute-done.5.refs_6_ = f32[16,1152]{1,0:T(8,128)S(1)} collective-permute-done((f32[16,1152]{1,0:T(8,128)}, f32[16,1152]{1,0:T(8,128)S(1)}, u32[]{:S(2)}, u32[]{:S(2)}) %collective-permute-start.5) | collective-permute-done | bytes 73760 | tf_op jit(solution)/shard_map/ppermute | solution.py:217
  10.6 1.9 %collective-permute-start.6 = (f32[16,1152]{1,0:T(8,128)S(1)}, f32[16,1152]{1,0:T(8,128)S(1)}, u32[]{:S(2)}, u32[]{:S(2)}) collective-permute-start(f32[16,1152]{1,0:T(8,128)S(1)} %collective-permute-done.5.refs_6_), channel_id=1, source_target_pairs={{0,4},{4,0},{8,12},{12,8},{16,20},{20,16},{24,28},{28,24},{1,5},{5... | collective-permute-start | bytes 221192 | tf_op jit(solution)/shard_map/ppermute | solution.py:220
  12.5 1.6 %collective-permute-done.3.refs_4_ = f32[16,1152]{1,0:T(8,128)S(1)} collective-permute-done((f32[16,1152]{1,0:T(8,128)}, f32[16,1152]{1,0:T(8,128)S(1)}, u32[]{:S(2)}, u32[]{:S(2)}) %collective-permute-start.3) | collective-permute-done | bytes 73760 | tf_op jit(solution)/shard_map/ppermute | solution.py:217
  14.1 1.5 %collective-permute-start.4 = (f32[16,1152]{1,0:T(8,128)S(1)}, f32[16,1152]{1,0:T(8,128)S(1)}, u32[]{:S(2)}, u32[]{:S(2)}) collective-permute-start(f32[16,1152]{1,0:T(8,128)S(1)} %collective-permute-done.3.refs_4_), channel_id=1, source_target_pairs={{0,4},{4,0},{8,12},{12,8},{16,20},{20,16},{24,28},{28,24},{1,5},{5... | collective-permute-start | bytes 221192 | tf_op jit(solution)/shard_map/ppermute | solution.py:220
  15.6 0.0 collective-permute-done.1.refs_2_
  15.6 0.5 collective-permute-start.2
  16.1 0.0 copy-done
  16.1 0.9 %shard_map.74.ahead = f32[8,2,16,512]{3,2,1,0:T(8,128)} custom-call(f32[16,2,4096]{2,1,0:T(2,128)S(1)} %copy-done), custom_call_target="tpu_custom_call" | custom-call | bytes 1000000 | tf_op jit(solution)/shard_map/pallas_call | solution.py:254
  17.0 0.0 copy-done.2
  17.0 0.0 copy-done.3
  17.0 0.0 copy-done.4
  17.0 0.0 copy-done.5
  17.0 0.0 copy-done.6
  17.0 1.0 %shard_map.73 = (f32[32,128]{1,0:T(8,128)S(1)}, f32[5,128,128]{2,1,0:T(8,128)S(1)}) custom-call(s32[4]{0:T(128)S(1)} %copy-done.4, s32[4,4,64]{2,1,0:T(4,128)S(1)} %copy-done.2, f32[4,1,64]{2,1,0:T(1,128)S(1)} %copy-done.5, f32[4,1,64]{2,1,0:T(1,128)S(1)} %copy-done.6, s32[4,1,128]{2,1,0:T(1,128)S(1)} %bitcast.2), custom_call_target="tpu_custom_call" | custom-call | bytes 1000000 | tf_op jit(solution)/shard_map/pallas_call | solution.py:262
  18.0 0.0 collective-permute-done.refs_1_
  18.0 0.0 collective-permute-done.6.refs_7_
  18.1 1.1 %collective-permute-done.4.refs_5_ = f32[16,1152]{1,0:T(8,128)S(1)} collective-permute-done((f32[16,1152]{1,0:T(8,128)S(1)}, f32[16,1152]{1,0:T(8,128)S(1)}, u32[]{:S(2)}, u32[]{:S(2)}) %collective-permute-start.4) | collective-permute-done | bytes 73760 | tf_op jit(solution)/shard_map/ppermute | solution.py:220
  19.2 0.8 %collective-permute-done.2.refs_3_ = f32[16,1152]{1,0:T(8,128)S(1)} collective-permute-done((f32[16,1152]{1,0:T(8,128)S(1)}, f32[16,1152]{1,0:T(8,128)S(1)}, u32[]{:S(2)}, u32[]{:S(2)}) %collective-permute-start.2) | collective-permute-done | bytes 73760 | tf_op jit(solution)/shard_map/ppermute | solution.py:220
  20.0 0.0 copy-done.1
  20.0 0.8 %shard_map.76.own = f32[1056,128]{1,0:T(8,128)S(1)} custom-call(s32[4]{0:T(128)S(1)} %copy-done.4, f32[32,128]{1,0:T(8,128)S(1)} %get-tuple-element.8.rows, f32[8,2,16,512]{3,2,1,0:T(8,128)} %shard_map.74.ahead, f32[16,1152]{1,0:T(8,128)S(1)} %copy-done.1, f32[16,1152]{1,0:T(8,128)S(1)} %collective-permute-done.refs_1_, ...), custom_call_target="tpu_custom_call" | custom-call | bytes 1000000 | tf_op jit(solution)/shard_map/pallas_call | solution.py:269
  20.8 1.6 %collective-permute-start.8 = (f32[1056,128]{1,0:T(8,128)S(1)}, f32[1056,128]{1,0:T(8,128)S(1)}, u32[]{:S(2)}, u32[]{:S(2)}) collective-permute-start(f32[1056,128]{1,0:T(8,128)S(1)} %shard_map.76.own), channel_id=1, source_target_pairs={{0,2},{1,3},{2,0},{3,1},{4,6},{5,7},{6,4},{7,5},{8,10},{9,11},{10,... | collective-permute-start | bytes 1622024 | tf_op jit(solution)/shard_map/ppermute | solution.py:276
  22.3 4.2 %all-to-all-start = ((f32[8,2,16,512]{3,2,1,0:T(8,128)}), f32[8,2,16,512]{3,2,1,0:T(8,128)S(1)}, u32[]{:S(2)}, u32[]{:S(2)}) async-start(f32[8,2,16,512]{3,2,1,0:T(8,128)} %shard_map.74.ahead), calls=%async_computation | async-start | bytes 1048576 | tf_op jit(solution)/shard_map/all_to_all | solution.py:260
  26.5 0.0 collective-permute-start.7
  26.5 7.7 %collective-permute-done.8.far = f32[1056,128]{1,0:T(8,128)S(1)} collective-permute-done((f32[1056,128]{1,0:T(8,128)S(1)}, f32[1056,128]{1,0:T(8,128)S(1)}, u32[]{:S(2)}, u32[]{:S(2)}) %collective-permute-start.8) | collective-permute-done | bytes 540704 | tf_op jit(solution)/shard_map/ppermute | solution.py:276
  34.2 0.0 collective-permute-start.9
  34.2 0.0 collective-permute-done.7.near
  34.2 1.9 %collective-permute-done.9.cross = f32[1056,128]{1,0:T(8,128)S(1)} collective-permute-done((f32[1056,128]{1,0:T(8,128)S(1)}, f32[1056,128]{1,0:T(8,128)S(1)}, u32[]{:S(2)}, u32[]{:S(2)}) %collective-permute-start.9) | collective-permute-done | bytes 540704 | tf_op jit(solution)/shard_map/ppermute | solution.py:278
  36.2 2.7 %shard_map.77.pull = f32[8,128]{1,0:T(8,128)S(1)} custom-call(f32[1056,128]{1,0:T(8,128)S(1)} %shard_map.76.own, f32[1056,128]{1,0:T(8,128)S(1)} %collective-permute-done.7.near, f32[1056,128]{1,0:T(8,128)S(1)} %collective-permute-done.8.far, f32[1056,128]{1,0:T(8,128)S(1)} %collective-permute-done.9.cross, f32[5,128,128]{2,1,0:T(8,128)S(1)} %get-tuple-element.7.steps), custom_call_target="tpu_custom_call" | custom-call | bytes 100000 | tf_op jit(solution)/shard_map/pallas_call | solution.py:280
  38.9 0.7 %all-to-all-done.fields = f32[8,2,16,512]{3,2,1,0:T(8,128)S(1)} async-done(((f32[8,2,16,512]{3,2,1,0:T(8,128)}), f32[8,2,16,512]{3,2,1,0:T(8,128)S(1)}, u32[]{:S(2)}, u32[]{:S(2)}) %all-to-all-start) | async-done | bytes 524320 | tf_op jit(solution)/shard_map/all_to_all | solution.py:260
  39.6 0.6 shard_map.78
  40.2 17.2 %all_to_all.10.moved = f32[8,2,16,512]{3,2,1,0:T(8,128)S(1)} all-to-all(f32[8,2,16,512]{3,2,1,0:T(8,128)S(1)} %shard_map.78), channel_id=1, replica_groups=mesh['grid'=8,'lev'=4] {'grid'}, dimensions={0} | all-to-all | bytes 1048576 | tf_op jit(solution)/shard_map/all_to_all | solution.py:294
  57.4 0.9 %shard_map.79 = f32[16,2,4096]{2,1,0:T(2,128)} custom-call(f32[8,2,16,512]{3,2,1,0:T(8,128)S(1)} %all_to_all.10.moved), custom_call_target="tpu_custom_call" | custom-call | bytes 1000000 | tf_op jit(solution)/shard_map/pallas_call | solution.py:296
Async XLA Ops:
  0.0 16.1 %copy-start = (f32[16,2,4096]{2,1,0:T(2,128)S(1)}, f32[16,2,4096]{2,1,0:T(2,128)}, u32[]{:S(2)}) copy-start(f32[16,2,4096]{2,1,0:T(2,128)} %refs_4_.1) | copy-start | bytes 1572868
  2.5 14.5 %copy-start.2 = (s32[4,4,64]{2,1,0:T(4,128)S(1)}, s32[4,4,64]{2,1,0:T(4,128)}, u32[]{:S(2)}) copy-start(s32[4,4,64]{2,1,0:T(4,128)} %refs_2_.1) | copy-start | bytes 12292
  2.5 14.5 %copy-start.3 = (s32[4,1,1,128]{3,2,1,0:T(1,128)S(1)}, s32[4,1,1,128]{3,2,1,0:T(1,128)}, u32[]{:S(2)}) copy-start(s32[4,1,1,128]{3,2,1,0:T(1,128)} %param.13) | copy-start | bytes 6148
  2.5 14.5 %copy-start.4 = (s32[4]{0:T(128)S(1)}, s32[4]{0:T(128)}, u32[]{:S(2)}) copy-start(s32[4]{0:T(128)} %owner.3) | copy-start | bytes 52
  2.5 14.5 %copy-start.5 = (f32[4,1,64]{2,1,0:T(1,128)S(1)}, f32[4,1,64]{2,1,0:T(1,128)}, u32[]{:S(2)}) copy-start(f32[4,1,64]{2,1,0:T(1,128)} %values.1) | copy-start | bytes 3076
  2.5 14.5 %copy-start.6 = (f32[4,1,64]{2,1,0:T(1,128)S(1)}, f32[4,1,64]{2,1,0:T(1,128)}, u32[]{:S(2)}) copy-start(f32[4,1,64]{2,1,0:T(1,128)} %errors.1) | copy-start | bytes 3076
  2.5 17.4 %copy-start.1 = (f32[16,1152]{1,0:T(8,128)S(1)}, f32[16,1152]{1,0:T(8,128)}, u32[]{:S(2)}) copy-start(f32[16,1152]{1,0:T(8,128)} %shard_map.75.refs_0_) | copy-start | bytes 221188
  2.5 8.1 %collective-permute-start.5 = (f32[16,1152]{1,0:T(8,128)}, f32[16,1152]{1,0:T(8,128)S(1)}, u32[]{:S(2)}, u32[]{:S(2)}) collective-permute-start(f32[16,1152]{1,0:T(8,128)} %shard_map.75.refs_0_), channel_id=1, source_target_pairs={{0,24},{4,28},{8,16},{12,20},{16,8},{20,12},{24,0},{28,4},{1,25},{... | collective-permute-start | bytes 221192 | tf_op jit(solution)/shard_map/ppermute | solution.py:217
  7.7 6.4 %collective-permute-start.3 = (f32[16,1152]{1,0:T(8,128)}, f32[16,1152]{1,0:T(8,128)S(1)}, u32[]{:S(2)}, u32[]{:S(2)}) collective-permute-start(f32[16,1152]{1,0:T(8,128)} %shard_map.75.refs_0_), channel_id=1, source_target_pairs={{0,16},{4,20},{8,24},{12,28},{16,0},{20,4},{24,8},{28,12},{1,17},{... | collective-permute-start | bytes 221192 | tf_op jit(solution)/shard_map/ppermute | solution.py:217
  7.7 7.9 %collective-permute-start.1 = (f32[16,1152]{1,0:T(8,128)}, f32[16,1152]{1,0:T(8,128)S(1)}, u32[]{:S(2)}, u32[]{:S(2)}) collective-permute-start(f32[16,1152]{1,0:T(8,128)} %shard_map.75.refs_0_), channel_id=1, source_target_pairs={{0,8},{4,12},{8,0},{12,4},{16,24},{20,28},{24,16},{28,20},{1,9},{5... | collective-permute-start | bytes 221192 | tf_op jit(solution)/shard_map/ppermute | solution.py:217
  8.3 9.7 %collective-permute-start = (f32[16,1152]{1,0:T(8,128)}, f32[16,1152]{1,0:T(8,128)S(1)}, u32[]{:S(2)}, u32[]{:S(2)}) collective-permute-start(f32[16,1152]{1,0:T(8,128)} %shard_map.75.refs_0_), channel_id=1, source_target_pairs={{0,4},{4,0},{8,12},{12,8},{16,20},{20,16},{24,28},{28,24},{1,5},{5... | collective-permute-start | bytes 221192 | tf_op jit(solution)/shard_map/ppermute | solution.py:220
  10.6 7.4 %collective-permute-start.6 = (f32[16,1152]{1,0:T(8,128)S(1)}, f32[16,1152]{1,0:T(8,128)S(1)}, u32[]{:S(2)}, u32[]{:S(2)}) collective-permute-start(f32[16,1152]{1,0:T(8,128)S(1)} %collective-permute-done.5.refs_6_), channel_id=1, source_target_pairs={{0,4},{4,0},{8,12},{12,8},{16,20},{20,16},{24,28},{28,24},{1,5},{5... | collective-permute-start | bytes 221192 | tf_op jit(solution)/shard_map/ppermute | solution.py:220
  14.1 5.1 %collective-permute-start.4 = (f32[16,1152]{1,0:T(8,128)S(1)}, f32[16,1152]{1,0:T(8,128)S(1)}, u32[]{:S(2)}, u32[]{:S(2)}) collective-permute-start(f32[16,1152]{1,0:T(8,128)S(1)} %collective-permute-done.3.refs_4_), channel_id=1, source_target_pairs={{0,4},{4,0},{8,12},{12,8},{16,20},{20,16},{24,28},{28,24},{1,5},{5... | collective-permute-start | bytes 221192 | tf_op jit(solution)/shard_map/ppermute | solution.py:220
  15.6 4.4 %collective-permute-start.2 = (f32[16,1152]{1,0:T(8,128)S(1)}, f32[16,1152]{1,0:T(8,128)S(1)}, u32[]{:S(2)}, u32[]{:S(2)}) collective-permute-start(f32[16,1152]{1,0:T(8,128)S(1)} %collective-permute-done.1.refs_2_), channel_id=1, source_target_pairs={{0,4},{4,0},{8,12},{12,8},{16,20},{20,16},{24,28},{28,24},{1,5},{5... | collective-permute-start | bytes 221192 | tf_op jit(solution)/shard_map/ppermute | solution.py:220
  20.8 13.5 %collective-permute-start.8 = (f32[1056,128]{1,0:T(8,128)S(1)}, f32[1056,128]{1,0:T(8,128)S(1)}, u32[]{:S(2)}, u32[]{:S(2)}) collective-permute-start(f32[1056,128]{1,0:T(8,128)S(1)} %shard_map.76.own), channel_id=1, source_target_pairs={{0,2},{1,3},{2,0},{3,1},{4,6},{5,7},{6,4},{7,5},{8,10},{9,11},{10,... | collective-permute-start | bytes 1622024 | tf_op jit(solution)/shard_map/ppermute | solution.py:276
  22.3 17.3 %all-to-all-start = ((f32[8,2,16,512]{3,2,1,0:T(8,128)}), f32[8,2,16,512]{3,2,1,0:T(8,128)S(1)}, u32[]{:S(2)}, u32[]{:S(2)}) async-start(f32[8,2,16,512]{3,2,1,0:T(8,128)} %shard_map.74.ahead), calls=%async_computation | async-start | bytes 1048576 | tf_op jit(solution)/shard_map/all_to_all | solution.py:260
  26.5 7.7 %collective-permute-start.7 = (f32[1056,128]{1,0:T(8,128)S(1)}, f32[1056,128]{1,0:T(8,128)S(1)}, u32[]{:S(2)}, u32[]{:S(2)}) collective-permute-start(f32[1056,128]{1,0:T(8,128)S(1)} %shard_map.76.own), channel_id=1, source_target_pairs={{0,1},{1,0},{2,3},{3,2},{4,5},{5,4},{6,7},{7,6},{8,9},{9,8},{10,11... | collective-permute-start | bytes 1622024 | tf_op jit(solution)/shard_map/ppermute | solution.py:277
  34.2 1.9 %collective-permute-start.9 = (f32[1056,128]{1,0:T(8,128)S(1)}, f32[1056,128]{1,0:T(8,128)S(1)}, u32[]{:S(2)}, u32[]{:S(2)}) collective-permute-start(f32[1056,128]{1,0:T(8,128)S(1)} %collective-permute-done.8.far), channel_id=1, source_target_pairs={{0,1},{1,0},{2,3},{3,2},{4,5},{5,4},{6,7},{7,6},{8,9},{9,8},{10,11... | collective-permute-start | bytes 1622024 | tf_op jit(solution)/shard_map/ppermute | solution.py:278

commit v5 on v4

--- a/solution.py
+++ b/solution.py
@@ -140,12 +140,23 @@
         out[width + PARENT + i : width + PARENT + i + 1, :] = held[owner[b], line : line + 1, lane : lane + LANES]
 
 
-def mix_kernel(shape, steps, pull, fields, out):
+def mix_kernel(shape, steps, pull, fields, *refs):
     n, slab, depth, block_cells = shape
-    blend = steps[NB] + pull[0:1, :]
+    outs, held = refs[:-1], refs[-1]
+    members = n * slab
+    held[...] = (steps[NB] + pull[0:1, :]).reshape(n, slab, members)
+    block = lax.axis_index("grid")
+    if len(outs) == n:
+        blend = jnp.concatenate([held[lax.bitwise_xor(block, i)] for i in range(n)], axis=0)
+    else:
+        blend = held[...].reshape(members, members)
     for level in range(depth):
-        value = fields[:, level].reshape(n * slab, block_cells)
-        out[:, level] = high_dot(blend, value).reshape(n, slab, block_cells)
+        value = high_dot(blend, fields[:, level].reshape(members, block_cells)).reshape(n, slab, block_cells)
+        if len(outs) == n:
+            for i in range(n):
+                outs[i][level] = value[i]
+        else:
+            outs[0][:, level] = value
 
 
 def chain_kernel(shape, own, near, far, cross, steps, out):
@@ -202,11 +213,15 @@
     out[...] = pull
 
 
-def final_kernel(shape, moved, out):
+def final_kernel(shape, *refs):
     n, slab, depth, block_cells = shape
-    for r in range(n):
+    pieces, out = refs[:-1], refs[-1]
+    block = lax.axis_index("grid")
+    for i in range(n):
+        region = lax.bitwise_xor(block, i) if len(pieces) == n else i
+        cells = pl.ds(pl.multiple_of(region * block_cells, LANES), block_cells)
         for level in range(depth):
-            out[:, level, r * block_cells : (r + 1) * block_cells] = moved[r, level]
+            out[:, level, cells] = pieces[i][level] if len(pieces) == n else pieces[0][i, level]
 
 
 def gather_pieces(piece, n):
@@ -219,6 +234,14 @@
     for part in pieces:
         result += [part, lax.ppermute(part, "grid", [(j, j ^ 1) for j in range(n)])]
     return result
+
+
+def exchange_pieces(pieces, n):
+    if len(pieces) == 1:
+        return [lax.all_to_all(pieces[0], "grid", 0, 0, tiled=True)]
+    return [pieces[0]] + [
+        lax.ppermute(pieces[i], "grid", [(j, j ^ i) for j in range(n)]) for i in range(1, n)
+    ]
 
 
 def body(prior, channel_weights, obs_owner, obs_offset, obs_value, obs_error, ancestors):
@@ -284,21 +307,26 @@
         moved=10**5,
     )(own, near, far, cross, steps)
 
+    if n == 8:
+        layout = [shape((depth, slab, block_cells), F32)] * n
+    else:
+        layout = [shape((n, depth, slab, block_cells), F32)]
     send = call(
         functools.partial(mix_kernel, (n, slab, depth, block_cells)),
-        shape((n, depth, slab, block_cells), F32),
+        layout,
         [VMEM] * 3,
+        scratch=[pltpu.VMEM((n, slab, members), F32)],
         flops=10**8,
         moved=10**6,
     )(steps, pull, fields)
-    moved = lax.all_to_all(send, "grid", 0, 0, tiled=True)
+    moved = exchange_pieces(send, n)
 
     return call(
         functools.partial(final_kernel, (n, slab, depth, block_cells)),
         shape((slab, depth, cells), F32),
-        [VMEM],
-        moved=10**6,
-    )(moved)
+        [VMEM] * len(moved),
+        moved=10**6,
+    )(*moved)
 
 
 def solution(mesh):

time: 58.6 us -> 57.3 us (0.978)
  blocking collectives: 17.2 us -> 0 us
  starting transfers between devices: 17.1 us -> 28.3 us
  waiting for transfers between devices: 14.5 us -> 19.3 us
    all_to_all x1 -> x0, blocking collectives: 17.2 us -> none  [body(): moved = lax.all_to_all(send, 'grid', 0, 0, tiled=True)]
    ppermute x0 -> x7, starting transfers between devices: none -> 11.2 us  [exchange_pieces(): lax.ppermute(pieces[i], 'grid', [(j, j ^ i) for j in range(n)])]
    ppermute x0 -> x7, waiting for transfers between devices: none -> 4.74 us  [exchange_pieces(): lax.ppermute(pieces[i], 'grid', [(j, j ^ i) for j in range(n)])]
  transfers between devices with their start and end apart: 11 -> 18, of which waited for: 7 -> 10; matrix products, arithmetic and copies ran while one was open for 0% -> 0% of each run, Pallas kernels for 8% -> 8%
where the time goes in v5:
time: 57.3 us; the launch traced here: 57.1 us
  starting transfers between devices  28.3 us (49%)
  waiting for transfers between devices  19.3 us (34%)
  Pallas kernels  9.34 us (16%)
    ppermute x7, starting transfers between devices, exchange_pieces(): lax.ppermute(pieces[i], 'grid', [(j, j ^ i) for j in range(n)])  11.2 us
    ppermute x1, waiting for transfers between devices, body(): far = lax.ppermute(own, 'lev', [(j, j ^ 2) for j in range(lev)])  7.69 us
    ppermute x3, starting transfers between devices, gather_pieces(): pieces.append(lax.ppermute(piece, 'grid', [(j, j ^ far) for j in range(n)]))  5.76 us
    ppermute x4, starting transfers between devices, gather_pieces(): result += [part, lax.ppermute(part, 'grid', [(j, j ^ 1) for j in range(n)])]  5.55 us
    ppermute x7, waiting for transfers between devices, exchange_pieces(): lax.ppermute(pieces[i], 'grid', [(j, j ^ i) for j in range(n)])  4.74 us
    all_to_all x1, starting transfers between devices, body(): fields = lax.all_to_all(send, 'grid', 0, 0, tiled=True)  4.22 us
    pallas_call x1, Pallas kernels, body(): call(functools.partial(chain_kernel, (members, groups, count)), shape((8,...  2.73 us
    pallas_call x1, Pallas kernels, body(): call(functools.partial(pick_kernel, (slab, depth, block_cells, groups, co...  2.45 us
  transfers between devices with their start and end apart: 18, of which 10 were waited for; matrix products, arithmetic and copies ran while one was open for 0% of the time, Pallas kernels for 8%

profile of v5, /device:TPU:0, one launch (start us, length us, event | category | flops | bytes accessed | tf_op | source)
XLA Modules:
  0.0 57.1 jit_solution(905701332689408310)
XLA Ops:
  0.0 2.5 %shard_map.75.refs_0_ = f32[16,1152]{1,0:T(8,128)} custom-call(s32[4]{0:T(128)} %owner.3, f32[2,4]{1,0:T(2,128)} %refs_1_.1, s32[4,4,64]{2,1,0:T(4,128)} %refs_2_.1, s32[4,1,128]{2,1,0:T(1,128)} %bitcast.1, f32[16,2,4096]{2,1,0:T(2,128)} %refs_4_.1), custom_call_target="tpu_custom_call" | custom-call | bytes 1000000 | tf_op jit(solution)/shard_map/pallas_call | solution.py:260
  2.5 0.0 copy-start.2
  2.5 0.0 copy-start.3
  2.5 0.0 copy-start.4
  2.5 0.0 copy-start.5
  2.5 0.0 copy-start.6
  2.5 5.1 %collective-permute-start.5 = (f32[16,1152]{1,0:T(8,128)}, f32[16,1152]{1,0:T(8,128)S(1)}, u32[]{:S(2)}, u32[]{:S(2)}) collective-permute-start(f32[16,1152]{1,0:T(8,128)} %shard_map.75.refs_0_), channel_id=1, source_target_pairs={{0,24},{4,28},{8,16},{12,20},{16,8},{20,12},{24,0},{28,4},{1,25},{... | collective-permute-start | bytes 221192 | tf_op jit(solution)/shard_map/ppermute | solution.py:232
  7.6 0.0 collective-permute-start.3
  7.7 0.6 %collective-permute-start.1 = (f32[16,1152]{1,0:T(8,128)}, f32[16,1152]{1,0:T(8,128)S(1)}, u32[]{:S(2)}, u32[]{:S(2)}) collective-permute-start(f32[16,1152]{1,0:T(8,128)} %shard_map.75.refs_0_), channel_id=1, source_target_pairs={{0,8},{4,12},{8,0},{12,4},{16,24},{20,28},{24,16},{28,20},{1,9},{5... | collective-permute-start | bytes 221192 | tf_op jit(solution)/shard_map/ppermute | solution.py:232
  8.3 1.7 %collective-permute-start = (f32[16,1152]{1,0:T(8,128)}, f32[16,1152]{1,0:T(8,128)S(1)}, u32[]{:S(2)}, u32[]{:S(2)}) collective-permute-start(f32[16,1152]{1,0:T(8,128)} %shard_map.75.refs_0_), channel_id=1, source_target_pairs={{0,4},{4,0},{8,12},{12,8},{16,20},{20,16},{24,28},{28,24},{1,5},{5... | collective-permute-start | bytes 221192 | tf_op jit(solution)/shard_map/ppermute | solution.py:235
  10.0 0.7 %collective-permute-done.5.refs_6_ = f32[16,1152]{1,0:T(8,128)S(1)} collective-permute-done((f32[16,1152]{1,0:T(8,128)}, f32[16,1152]{1,0:T(8,128)S(1)}, u32[]{:S(2)}, u32[]{:S(2)}) %collective-permute-start.5) | collective-permute-done | bytes 73760 | tf_op jit(solution)/shard_map/ppermute | solution.py:232
  10.6 1.9 %collective-permute-start.6 = (f32[16,1152]{1,0:T(8,128)S(1)}, f32[16,1152]{1,0:T(8,128)S(1)}, u32[]{:S(2)}, u32[]{:S(2)}) collective-permute-start(f32[16,1152]{1,0:T(8,128)S(1)} %collective-permute-done.5.refs_6_), channel_id=1, source_target_pairs={{0,4},{4,0},{8,12},{12,8},{16,20},{20,16},{24,28},{28,24},{1,5},{5... | collective-permute-start | bytes 221192 | tf_op jit(solution)/shard_map/ppermute | solution.py:235
  12.5 1.6 %collective-permute-done.3.refs_4_ = f32[16,1152]{1,0:T(8,128)S(1)} collective-permute-done((f32[16,1152]{1,0:T(8,128)}, f32[16,1152]{1,0:T(8,128)S(1)}, u32[]{:S(2)}, u32[]{:S(2)}) %collective-permute-start.3) | collective-permute-done | bytes 73760 | tf_op jit(solution)/shard_map/ppermute | solution.py:232
  14.1 1.5 %collective-permute-start.4 = (f32[16,1152]{1,0:T(8,128)S(1)}, f32[16,1152]{1,0:T(8,128)S(1)}, u32[]{:S(2)}, u32[]{:S(2)}) collective-permute-start(f32[16,1152]{1,0:T(8,128)S(1)} %collective-permute-done.3.refs_4_), channel_id=1, source_target_pairs={{0,4},{4,0},{8,12},{12,8},{16,20},{20,16},{24,28},{28,24},{1,5},{5... | collective-permute-start | bytes 221192 | tf_op jit(solution)/shard_map/ppermute | solution.py:235
  15.6 0.0 collective-permute-done.1.refs_2_
  15.6 0.5 collective-permute-start.2
  16.1 0.9 %shard_map.74.ahead = f32[8,2,16,512]{3,2,1,0:T(8,128)} custom-call(f32[16,2,4096]{2,1,0:T(2,128)S(1)} %copy-done), custom_call_target="tpu_custom_call" | custom-call | bytes 1000000 | tf_op jit(solution)/shard_map/pallas_call | solution.py:277
  17.0 1.0 %shard_map.73 = (f32[32,128]{1,0:T(8,128)S(1)}, f32[5,128,128]{2,1,0:T(8,128)S(1)}) custom-call(s32[4]{0:T(128)S(1)} %copy-done.4, s32[4,4,64]{2,1,0:T(4,128)S(1)} %copy-done.2, f32[4,1,64]{2,1,0:T(1,128)S(1)} %copy-done.5, f32[4,1,64]{2,1,0:T(1,128)S(1)} %copy-done.6, s32[4,1,128]{2,1,0:T(1,128)S(1)} %bitcast.2), custom_call_target="tpu_custom_call" | custom-call | bytes 1000000 | tf_op jit(solution)/shard_map/pallas_call | solution.py:285
  18.0 0.0 collective-permute-done.refs_1_
  18.0 0.0 collective-permute-done.6.refs_7_
  18.0 1.1 %collective-permute-done.4.refs_5_ = f32[16,1152]{1,0:T(8,128)S(1)} collective-permute-done((f32[16,1152]{1,0:T(8,128)S(1)}, f32[16,1152]{1,0:T(8,128)S(1)}, u32[]{:S(2)}, u32[]{:S(2)}) %collective-permute-start.4) | collective-permute-done | bytes 73760 | tf_op jit(solution)/shard_map/ppermute | solution.py:235
  19.1 0.8 %collective-permute-done.2.refs_3_ = f32[16,1152]{1,0:T(8,128)S(1)} collective-permute-done((f32[16,1152]{1,0:T(8,128)S(1)}, f32[16,1152]{1,0:T(8,128)S(1)}, u32[]{:S(2)}, u32[]{:S(2)}) %collective-permute-start.2) | collective-permute-done | bytes 73760 | tf_op jit(solution)/shard_map/ppermute | solution.py:235
  20.0 0.8 %shard_map.76.own = f32[1056,128]{1,0:T(8,128)S(1)} custom-call(s32[4]{0:T(128)S(1)} %copy-done.4, f32[32,128]{1,0:T(8,128)S(1)} %get-tuple-element.16.rows, f32[8,2,16,512]{3,2,1,0:T(8,128)} %shard_map.74.ahead, f32[16,1152]{1,0:T(8,128)S(1)} %copy-done.1, f32[16,1152]{1,0:T(8,128)S(1)} %collective-permute-done.refs_1_, ...), custom_call_target="tpu_custom_call" | custom-call | bytes 1000000 | tf_op jit(solution)/shard_map/pallas_call | solution.py:292
  20.7 1.6 %collective-permute-start.8 = (f32[1056,128]{1,0:T(8,128)S(1)}, f32[1056,128]{1,0:T(8,128)S(1)}, u32[]{:S(2)}, u32[]{:S(2)}) collective-permute-start(f32[1056,128]{1,0:T(8,128)S(1)} %shard_map.76.own), channel_id=1, source_target_pairs={{0,2},{1,3},{2,0},{3,1},{4,6},{5,7},{6,4},{7,5},{8,10},{9,11},{10,... | collective-permute-start | bytes 1622024 | tf_op jit(solution)/shard_map/ppermute | solution.py:299
  22.3 4.2 %all-to-all-start = ((f32[8,2,16,512]{3,2,1,0:T(8,128)}), f32[8,2,16,512]{3,2,1,0:T(8,128)S(1)}, u32[]{:S(2)}, u32[]{:S(2)}) async-start(f32[8,2,16,512]{3,2,1,0:T(8,128)} %shard_map.74.ahead), calls=%async_computation | async-start | bytes 1048576 | tf_op jit(solution)/shard_map/all_to_all | solution.py:283
  26.5 0.0 collective-permute-start.7
  26.5 7.7 %collective-permute-done.8.far = f32[1056,128]{1,0:T(8,128)S(1)} collective-permute-done((f32[1056,128]{1,0:T(8,128)S(1)}, f32[1056,128]{1,0:T(8,128)S(1)}, u32[]{:S(2)}, u32[]{:S(2)}) %collective-permute-start.8) | collective-permute-done | bytes 540704 | tf_op jit(solution)/shard_map/ppermute | solution.py:299
  34.2 0.0 collective-permute-start.9
  34.2 0.0 collective-permute-done.7.near
  34.2 1.9 %collective-permute-done.9.cross = f32[1056,128]{1,0:T(8,128)S(1)} collective-permute-done((f32[1056,128]{1,0:T(8,128)S(1)}, f32[1056,128]{1,0:T(8,128)S(1)}, u32[]{:S(2)}, u32[]{:S(2)}) %collective-permute-start.9) | collective-permute-done | bytes 540704 | tf_op jit(solution)/shard_map/ppermute | solution.py:301
  36.2 2.7 %shard_map.77.pull = f32[8,128]{1,0:T(8,128)S(1)} custom-call(f32[1056,128]{1,0:T(8,128)S(1)} %shard_map.76.own, f32[1056,128]{1,0:T(8,128)S(1)} %collective-permute-done.7.near, f32[1056,128]{1,0:T(8,128)S(1)} %collective-permute-done.8.far, f32[1056,128]{1,0:T(8,128)S(1)} %collective-permute-done.9.cross, f32[5,128,128]{2,1,0:T(8,128)S(1)} %get-tuple-element.15.steps), custom_call_target="tpu_custom_call" | custom-call | bytes 100000 | tf_op jit(solution)/shard_map/pallas_call | solution.py:303
  38.9 0.7 %all-to-all-done.fields = f32[8,2,16,512]{3,2,1,0:T(8,128)S(1)} async-done(((f32[8,2,16,512]{3,2,1,0:T(8,128)}), f32[8,2,16,512]{3,2,1,0:T(8,128)S(1)}, u32[]{:S(2)}, u32[]{:S(2)}) %all-to-all-start) | async-done | bytes 524320 | tf_op jit(solution)/shard_map/all_to_all | solution.py:283
  39.6 0.6 %shard_map.78 = (f32[2,16,512]{2,1,0:T(8,128)S(1)}, f32[2,16,512]{2,1,0:T(8,128)S(1)}, f32[2,16,512]{2,1,0:T(8,128)S(1)}, f32[2,16,512]{2,1,0:T(8,128)S(1)}, f32...) custom-call(f32[5,128,128]{2,1,0:T(8,128)S(1)} %get-tuple-element.15., ...), custom_call_target="tpu_custom_call" | custom-call | flops 100000000 | bytes 1000000 | tf_op jit(solution)/shard_map/pallas_call | solution.py:314
  40.2 1.5 %collective-permute-start.10 = (f32[2,16,512]{2,1,0:T(8,128)S(1)}, f32[2,16,512]{2,1,0:T(8,128)S(1)}, u32[]{:S(2)}, u32[]{:S(2)}) collective-permute-start(f32[2,16,512]{2,1,0:T(8,128)S(1)} %get-tuple-element.18), channel_id=1, source_target_pairs={{0,4},{4,0},{8,12},{12,8},{16,20},{20,16},{24,28},{28,24},{1,5},{5... | collective-permute-start | bytes 196616 | tf_op jit(solution)/shard_map/ppermute | solution.py:243
  41.7 0.0 collective-permute-start.11
  41.7 2.0 %collective-permute-start.12 = (f32[2,16,512]{2,1,0:T(8,128)S(1)}, f32[2,16,512]{2,1,0:T(8,128)S(1)}, u32[]{:S(2)}, u32[]{:S(2)}) collective-permute-start(f32[2,16,512]{2,1,0:T(8,128)S(1)} %get-tuple-element.20), channel_id=1, source_target_pairs={{0,12},{4,8},{8,4},{12,0},{16,28},{20,24},{24,20},{28,16},{1,13},{... | collective-permute-start | bytes 196616 | tf_op jit(solution)/shard_map/ppermute | solution.py:243
  43.7 0.8 %collective-permute-start.13 = (f32[2,16,512]{2,1,0:T(8,128)S(1)}, f32[2,16,512]{2,1,0:T(8,128)S(1)}, u32[]{:S(2)}, u32[]{:S(2)}) collective-permute-start(f32[2,16,512]{2,1,0:T(8,128)S(1)} %get-tuple-element.21), channel_id=1, source_target_pairs={{0,16},{4,20},{8,24},{12,28},{16,0},{20,4},{24,8},{28,12},{1,17},{... | collective-permute-start | bytes 196616 | tf_op jit(solution)/shard_map/ppermute | solution.py:243
  44.5 3.0 %collective-permute-start.14 = (f32[2,16,512]{2,1,0:T(8,128)S(1)}, f32[2,16,512]{2,1,0:T(8,128)S(1)}, u32[]{:S(2)}, u32[]{:S(2)}) collective-permute-start(f32[2,16,512]{2,1,0:T(8,128)S(1)} %get-tuple-element.22), channel_id=1, source_target_pairs={{0,20},{4,16},{8,28},{12,24},{16,4},{20,0},{24,12},{28,8},{1,21},{... | collective-permute-start | bytes 196616 | tf_op jit(solution)/shard_map/ppermute | solution.py:243
  47.6 0.0 collective-permute-done.10.refs_1_
  47.6 1.5 %collective-permute-start.15 = (f32[2,16,512]{2,1,0:T(8,128)S(1)}, f32[2,16,512]{2,1,0:T(8,128)S(1)}, u32[]{:S(2)}, u32[]{:S(2)}) collective-permute-start(f32[2,16,512]{2,1,0:T(8,128)S(1)} %get-tuple-element.23), channel_id=1, source_target_pairs={{0,24},{4,28},{8,16},{12,20},{16,8},{20,12},{24,0},{28,4},{1,25},{... | collective-permute-start | bytes 196616 | tf_op jit(solution)/shard_map/ppermute | solution.py:243
  49.1 0.0 collective-permute-done.11.refs_2_
  49.1 2.3 %collective-permute-start.16 = (f32[2,16,512]{2,1,0:T(8,128)S(1)}, f32[2,16,512]{2,1,0:T(8,128)S(1)}, u32[]{:S(2)}, u32[]{:S(2)}) collective-permute-start(f32[2,16,512]{2,1,0:T(8,128)S(1)} %get-tuple-element.24), channel_id=1, source_target_pairs={{0,28},{4,24},{8,20},{12,16},{16,12},{20,8},{24,4},{28,0},{1,29},{... | collective-permute-start | bytes 196616 | tf_op jit(solution)/shard_map/ppermute | solution.py:243
  51.4 0.0 collective-permute-done.12.refs_3_
  51.4 1.3 %collective-permute-done.13.refs_4_ = f32[2,16,512]{2,1,0:T(8,128)S(1)} collective-permute-done((f32[2,16,512]{2,1,0:T(8,128)S(1)}, f32[2,16,512]{2,1,0:T(8,128)S(1)}, u32[]{:S(2)}, u32[]{:S(2)}) %collective-permute-start.13) | collective-permute-done | bytes 65568 | tf_op jit(solution)/shard_map/ppermute | solution.py:243
  52.7 2.3 %collective-permute-done.14.refs_5_ = f32[2,16,512]{2,1,0:T(8,128)S(1)} collective-permute-done((f32[2,16,512]{2,1,0:T(8,128)S(1)}, f32[2,16,512]{2,1,0:T(8,128)S(1)}, u32[]{:S(2)}, u32[]{:S(2)}) %collective-permute-start.14) | collective-permute-done | bytes 65568 | tf_op jit(solution)/shard_map/ppermute | solution.py:243
  55.0 0.0 collective-permute-done.15.refs_6_
  55.0 1.1 %collective-permute-done.16.refs_7_ = f32[2,16,512]{2,1,0:T(8,128)S(1)} collective-permute-done((f32[2,16,512]{2,1,0:T(8,128)S(1)}, f32[2,16,512]{2,1,0:T(8,128)S(1)}, u32[]{:S(2)}, u32[]{:S(2)}) %collective-permute-start.16) | collective-permute-done | bytes 65568 | tf_op jit(solution)/shard_map/ppermute | solution.py:243
  56.1 0.9 %shard_map.79 = f32[16,2,4096]{2,1,0:T(2,128)} custom-call(f32[2,16,512]{2,1,0:T(8,128)S(1)} %get-tuple-element.17.refs_0_, f32[2,16,512]{2,1,0:T(8,128)S(1)} %collective-permute-done.10.refs_1_, f32[2,16,512]{2,1,0:T(8,128)S(1)} %collective-permute-done.11.refs_2_, f32[2,16,512]{2,1,0:T(8,128)S(1)} %collective-permute-done.12.refs_3_, ...), custom_call_target="tpu_custom_call" | custom-call | bytes 1000000 | tf_op jit(solution)/shard_map/pallas_call | solution.py:324
  (9 shorter events, 0.0 us)
Async XLA Ops:
  0.0 16.1 %copy-start = (f32[16,2,4096]{2,1,0:T(2,128)S(1)}, f32[16,2,4096]{2,1,0:T(2,128)}, u32[]{:S(2)}) copy-start(f32[16,2,4096]{2,1,0:T(2,128)} %refs_4_.1) | copy-start | bytes 1572868
  2.5 14.5 %copy-start.2 = (s32[4,4,64]{2,1,0:T(4,128)S(1)}, s32[4,4,64]{2,1,0:T(4,128)}, u32[]{:S(2)}) copy-start(s32[4,4,64]{2,1,0:T(4,128)} %refs_2_.1) | copy-start | bytes 12292
  2.5 14.5 %copy-start.3 = (s32[4,1,1,128]{3,2,1,0:T(1,128)S(1)}, s32[4,1,1,128]{3,2,1,0:T(1,128)}, u32[]{:S(2)}) copy-start(s32[4,1,1,128]{3,2,1,0:T(1,128)} %param.13) | copy-start | bytes 6148
  2.5 14.5 %copy-start.4 = (s32[4]{0:T(128)S(1)}, s32[4]{0:T(128)}, u32[]{:S(2)}) copy-start(s32[4]{0:T(128)} %owner.3) | copy-start | bytes 52
  2.5 14.5 %copy-start.5 = (f32[4,1,64]{2,1,0:T(1,128)S(1)}, f32[4,1,64]{2,1,0:T(1,128)}, u32[]{:S(2)}) copy-start(f32[4,1,64]{2,1,0:T(1,128)} %values.1) | copy-start | bytes 3076
  2.5 14.5 %copy-start.6 = (f32[4,1,64]{2,1,0:T(1,128)S(1)}, f32[4,1,64]{2,1,0:T(1,128)}, u32[]{:S(2)}) copy-start(f32[4,1,64]{2,1,0:T(1,128)} %errors.1) | copy-start | bytes 3076
  2.5 17.4 %copy-start.1 = (f32[16,1152]{1,0:T(8,128)S(1)}, f32[16,1152]{1,0:T(8,128)}, u32[]{:S(2)}) copy-start(f32[16,1152]{1,0:T(8,128)} %shard_map.75.refs_0_) | copy-start | bytes 221188
  2.5 8.1 %collective-permute-start.5 = (f32[16,1152]{1,0:T(8,128)}, f32[16,1152]{1,0:T(8,128)S(1)}, u32[]{:S(2)}, u32[]{:S(2)}) collective-permute-start(f32[16,1152]{1,0:T(8,128)} %shard_map.75.refs_0_), channel_id=1, source_target_pairs={{0,24},{4,28},{8,16},{12,20},{16,8},{20,12},{24,0},{28,4},{1,25},{... | collective-permute-start | bytes 221192 | tf_op jit(solution)/shard_map/ppermute | solution.py:232
  7.6 6.4 %collective-permute-start.3 = (f32[16,1152]{1,0:T(8,128)}, f32[16,1152]{1,0:T(8,128)S(1)}, u32[]{:S(2)}, u32[]{:S(2)}) collective-permute-start(f32[16,1152]{1,0:T(8,128)} %shard_map.75.refs_0_), channel_id=1, source_target_pairs={{0,16},{4,20},{8,24},{12,28},{16,0},{20,4},{24,8},{28,12},{1,17},{... | collective-permute-start | bytes 221192 | tf_op jit(solution)/shard_map/ppermute | solution.py:232
  7.7 7.9 %collective-permute-start.1 = (f32[16,1152]{1,0:T(8,128)}, f32[16,1152]{1,0:T(8,128)S(1)}, u32[]{:S(2)}, u32[]{:S(2)}) collective-permute-start(f32[16,1152]{1,0:T(8,128)} %shard_map.75.refs_0_), channel_id=1, source_target_pairs={{0,8},{4,12},{8,0},{12,4},{16,24},{20,28},{24,16},{28,20},{1,9},{5... | collective-permute-start | bytes 221192 | tf_op jit(solution)/shard_map/ppermute | solution.py:232
  8.3 9.7 %collective-permute-start = (f32[16,1152]{1,0:T(8,128)}, f32[16,1152]{1,0:T(8,128)S(1)}, u32[]{:S(2)}, u32[]{:S(2)}) collective-permute-start(f32[16,1152]{1,0:T(8,128)} %shard_map.75.refs_0_), channel_id=1, source_target_pairs={{0,4},{4,0},{8,12},{12,8},{16,20},{20,16},{24,28},{28,24},{1,5},{5... | collective-permute-start | bytes 221192 | tf_op jit(solution)/shard_map/ppermute | solution.py:235
  10.6 7.4 %collective-permute-start.6 = (f32[16,1152]{1,0:T(8,128)S(1)}, f32[16,1152]{1,0:T(8,128)S(1)}, u32[]{:S(2)}, u32[]{:S(2)}) collective-permute-start(f32[16,1152]{1,0:T(8,128)S(1)} %collective-permute-done.5.refs_6_), channel_id=1, source_target_pairs={{0,4},{4,0},{8,12},{12,8},{16,20},{20,16},{24,28},{28,24},{1,5},{5... | collective-permute-start | bytes 221192 | tf_op jit(solution)/shard_map/ppermute | solution.py:235
  14.1 5.1 %collective-permute-start.4 = (f32[16,1152]{1,0:T(8,128)S(1)}, f32[16,1152]{1,0:T(8,128)S(1)}, u32[]{:S(2)}, u32[]{:S(2)}) collective-permute-start(f32[16,1152]{1,0:T(8,128)S(1)} %collective-permute-done.3.refs_4_), channel_id=1, source_target_pairs={{0,4},{4,0},{8,12},{12,8},{16,20},{20,16},{24,28},{28,24},{1,5},{5... | collective-permute-start | bytes 221192 | tf_op jit(solution)/shard_map/ppermute | solution.py:235
  15.6 4.4 %collective-permute-start.2 = (f32[16,1152]{1,0:T(8,128)S(1)}, f32[16,1152]{1,0:T(8,128)S(1)}, u32[]{:S(2)}, u32[]{:S(2)}) collective-permute-start(f32[16,1152]{1,0:T(8,128)S(1)} %collective-permute-done.1.refs_2_), channel_id=1, source_target_pairs={{0,4},{4,0},{8,12},{12,8},{16,20},{20,16},{24,28},{28,24},{1,5},{5... | collective-permute-start | bytes 221192 | tf_op jit(solution)/shard_map/ppermute | solution.py:235
  20.7 13.5 %collective-permute-start.8 = (f32[1056,128]{1,0:T(8,128)S(1)}, f32[1056,128]{1,0:T(8,128)S(1)}, u32[]{:S(2)}, u32[]{:S(2)}) collective-permute-start(f32[1056,128]{1,0:T(8,128)S(1)} %shard_map.76.own), channel_id=1, source_target_pairs={{0,2},{1,3},{2,0},{3,1},{4,6},{5,7},{6,4},{7,5},{8,10},{9,11},{10,... | collective-permute-start | bytes 1622024 | tf_op jit(solution)/shard_map/ppermute | solution.py:299
  22.3 17.3 %all-to-all-start = ((f32[8,2,16,512]{3,2,1,0:T(8,128)}), f32[8,2,16,512]{3,2,1,0:T(8,128)S(1)}, u32[]{:S(2)}, u32[]{:S(2)}) async-start(f32[8,2,16,512]{3,2,1,0:T(8,128)} %shard_map.74.ahead), calls=%async_computation | async-start | bytes 1048576 | tf_op jit(solution)/shard_map/all_to_all | solution.py:283
  26.5 7.7 %collective-permute-start.7 = (f32[1056,128]{1,0:T(8,128)S(1)}, f32[1056,128]{1,0:T(8,128)S(1)}, u32[]{:S(2)}, u32[]{:S(2)}) collective-permute-start(f32[1056,128]{1,0:T(8,128)S(1)} %shard_map.76.own), channel_id=1, source_target_pairs={{0,1},{1,0},{2,3},{3,2},{4,5},{5,4},{6,7},{7,6},{8,9},{9,8},{10,11... | collective-permute-start | bytes 1622024 | tf_op jit(solution)/shard_map/ppermute | solution.py:300
  34.2 1.9 %collective-permute-start.9 = (f32[1056,128]{1,0:T(8,128)S(1)}, f32[1056,128]{1,0:T(8,128)S(1)}, u32[]{:S(2)}, u32[]{:S(2)}) collective-permute-start(f32[1056,128]{1,0:T(8,128)S(1)} %collective-permute-done.8.far), channel_id=1, source_target_pairs={{0,1},{1,0},{2,3},{3,2},{4,5},{5,4},{6,7},{7,6},{8,9},{9,8},{10,11... | collective-permute-start | bytes 1622024 | tf_op jit(solution)/shard_map/ppermute | solution.py:301
  40.2 7.4 %collective-permute-start.10 = (f32[2,16,512]{2,1,0:T(8,128)S(1)}, f32[2,16,512]{2,1,0:T(8,128)S(1)}, u32[]{:S(2)}, u32[]{:S(2)}) collective-permute-start(f32[2,16,512]{2,1,0:T(8,128)S(1)} %get-tuple-element.18), channel_id=1, source_target_pairs={{0,4},{4,0},{8,12},{12,8},{16,20},{20,16},{24,28},{28,24},{1,5},{5... | collective-permute-start | bytes 196616 | tf_op jit(solution)/shard_map/ppermute | solution.py:243
  41.7 7.3 %collective-permute-start.11 = (f32[2,16,512]{2,1,0:T(8,128)S(1)}, f32[2,16,512]{2,1,0:T(8,128)S(1)}, u32[]{:S(2)}, u32[]{:S(2)}) collective-permute-start(f32[2,16,512]{2,1,0:T(8,128)S(1)} %get-tuple-element.19), channel_id=1, source_target_pairs={{0,8},{4,12},{8,0},{12,4},{16,24},{20,28},{24,16},{28,20},{1,9},{5... | collective-permute-start | bytes 196616 | tf_op jit(solution)/shard_map/ppermute | solution.py:243
  41.7 9.7 %collective-permute-start.12 = (f32[2,16,512]{2,1,0:T(8,128)S(1)}, f32[2,16,512]{2,1,0:T(8,128)S(1)}, u32[]{:S(2)}, u32[]{:S(2)}) collective-permute-start(f32[2,16,512]{2,1,0:T(8,128)S(1)} %get-tuple-element.20), channel_id=1, source_target_pairs={{0,12},{4,8},{8,4},{12,0},{16,28},{20,24},{24,20},{28,16},{1,13},{... | collective-permute-start | bytes 196616 | tf_op jit(solution)/shard_map/ppermute | solution.py:243
  43.7 9.0 %collective-permute-start.13 = (f32[2,16,512]{2,1,0:T(8,128)S(1)}, f32[2,16,512]{2,1,0:T(8,128)S(1)}, u32[]{:S(2)}, u32[]{:S(2)}) collective-permute-start(f32[2,16,512]{2,1,0:T(8,128)S(1)} %get-tuple-element.21), channel_id=1, source_target_pairs={{0,16},{4,20},{8,24},{12,28},{16,0},{20,4},{24,8},{28,12},{1,17},{... | collective-permute-start | bytes 196616 | tf_op jit(solution)/shard_map/ppermute | solution.py:243
  44.5 10.5 %collective-permute-start.14 = (f32[2,16,512]{2,1,0:T(8,128)S(1)}, f32[2,16,512]{2,1,0:T(8,128)S(1)}, u32[]{:S(2)}, u32[]{:S(2)}) collective-permute-start(f32[2,16,512]{2,1,0:T(8,128)S(1)} %get-tuple-element.22), channel_id=1, source_target_pairs={{0,20},{4,16},{8,28},{12,24},{16,4},{20,0},{24,12},{28,8},{1,21},{... | collective-permute-start | bytes 196616 | tf_op jit(solution)/shard_map/ppermute | solution.py:243
  47.6 7.4 %collective-permute-start.15 = (f32[2,16,512]{2,1,0:T(8,128)S(1)}, f32[2,16,512]{2,1,0:T(8,128)S(1)}, u32[]{:S(2)}, u32[]{:S(2)}) collective-permute-start(f32[2,16,512]{2,1,0:T(8,128)S(1)} %get-tuple-element.23), channel_id=1, source_target_pairs={{0,24},{4,28},{8,16},{12,20},{16,8},{20,12},{24,0},{28,4},{1,25},{... | collective-permute-start | bytes 196616 | tf_op jit(solution)/shard_map/ppermute | solution.py:243
  49.1 7.1 %collective-permute-start.16 = (f32[2,16,512]{2,1,0:T(8,128)S(1)}, f32[2,16,512]{2,1,0:T(8,128)S(1)}, u32[]{:S(2)}, u32[]{:S(2)}) collective-permute-start(f32[2,16,512]{2,1,0:T(8,128)S(1)} %get-tuple-element.24), channel_id=1, source_target_pairs={{0,28},{4,24},{8,20},{12,16},{16,12},{20,8},{24,4},{28,0},{1,29},{... | collective-permute-start | bytes 196616 | tf_op jit(solution)/shard_map/ppermute | solution.py:243

commit v6 on v5

--- a/solution.py
+++ b/solution.py
@@ -16,6 +16,7 @@
 PLACE = pl.BlockSpec(memory_space=pl.ANY)
 LIMIT = 48 * 1024 * 1024
 
+ORDER = (0, 6, 4, 7, 5, 2, 3, 1)
 PAIRS = [(e, b) for b in range(1, NB) for e in range(b)]
 PARENT, ALPHA, LATER, VALUE, OWN, SPARE = 0, 6, 12, 18, 22, 32
 
@@ -73,13 +74,17 @@
                     axis=1,
                 )
                 total = total + found * row
-            lane = b * width + c * LANES
-            out[:, lane : lane + LANES] = total
-    lane = NB * width
-    out[:, lane:] = jnp.zeros((slab, out.shape[1] - lane), F32)
-    for b in range(NB):
-        row, block = b % slab, lane + (b // slab) * LANES
-        out[row : row + 1, block : block + LANES] = ancestors[b].astype(F32)
+            line = (b * width // LANES + c) * slab
+            out[line : line + slab, :] = total
+    line = NB * width // LANES * slab
+    out[line:, :] = jnp.zeros((out.shape[0] - line, LANES), F32)
+    for b in range(NB):
+        out[line + b : line + b + 1, :] = ancestors[b].astype(F32)
+
+
+def join_kernel(own, far, out):
+    out[0] = own[...]
+    out[1] = far[...]
 
 
 def retile_kernel(shape, prior, out):
@@ -120,24 +125,24 @@
     steps[NB] = turned.T
 
 
-def turn_kernel(shape, owner, rows, ahead, *refs):
+def turn_kernel(shape, owner, rows, far_rows, ahead, *refs):
     n, slab, width = shape
     pieces, out, held = refs[:-2], refs[-2], refs[-1]
     members = n * slab
-    if len(pieces) == 1:
-        held[...] = pieces[0][...]
-    else:
-        block = lax.axis_index("grid")
-        for i, piece in enumerate(pieces):
-            held[lax.bitwise_xor(block, i)] = piece[...]
-    for i in range(width // LANES):
-        lanes = slice(i * LANES, (i + 1) * LANES)
-        out[lanes, :] = held[:, :, lanes].reshape(members, LANES).T
-    out[width:, :] = rows[...]
-    for i, (e, b) in enumerate(PAIRS):
-        lane = width + (e // slab) * LANES
-        line = e % slab
-        out[width + PARENT + i : width + PARENT + i + 1, :] = held[owner[b], line : line + 1, lane : lane + LANES]
+    block = lax.axis_index("grid")
+    for i in range(n):
+        if len(pieces) == n:
+            held[lax.bitwise_xor(block, i)] = pieces[i][...]
+        else:
+            held[i] = pieces[0][i]
+    for part, extra in enumerate((rows, far_rows)):
+        for i in range(width // LANES):
+            value = held[:, part, i * slab : (i + 1) * slab, :].reshape(members, LANES)
+            out[part, i * LANES : (i + 1) * LANES, :] = value.T
+        out[part, width:, :] = extra[...]
+        line = width // LANES * slab
+        for i, (e, b) in enumerate(PAIRS):
+            out[part, width + PARENT + i : width + PARENT + i + 1, :] = held[owner[b], part, line + e : line + e + 1, :]
 
 
 def mix_kernel(shape, steps, pull, fields, *refs):
@@ -159,12 +164,12 @@
             outs[0][:, level] = value
 
 
-def chain_kernel(shape, own, near, far, cross, steps, out):
+def chain_kernel(shape, own, near, steps, out):
     members, groups, count = shape
     width = groups * count
     base = NB * width
     group = lax.axis_index("lev")
-    sources = [own, near, far, cross]
+    sources = [own.at[0], near.at[0], own.at[1], near.at[1]]
     columns = [source[base : base + SPARE, :].T for source in sources]
     parents, alphas = [], []
     for source in sources:
@@ -218,7 +223,7 @@
     pieces, out = refs[:-1], refs[-1]
     block = lax.axis_index("grid")
     for i in range(n):
-        region = lax.bitwise_xor(block, i) if len(pieces) == n else i
+        region = lax.bitwise_xor(block, ORDER[i]) if len(pieces) == n else i
         cells = pl.ds(pl.multiple_of(region * block_cells, LANES), block_cells)
         for level in range(depth):
             out[:, level, cells] = pieces[i][level] if len(pieces) == n else pieces[0][i, level]
@@ -228,19 +233,19 @@
     if n != 8:
         return [lax.all_to_all(jnp.broadcast_to(piece[None], (n,) + piece.shape), "grid", 0, 0, tiled=True)]
     pieces = [piece]
-    for far in (2, 4, 6):
-        pieces.append(lax.ppermute(piece, "grid", [(j, j ^ far) for j in range(n)]))
-    result = []
-    for part in pieces:
-        result += [part, lax.ppermute(part, "grid", [(j, j ^ 1) for j in range(n)])]
-    return result
+    pieces = {0: piece}
+    for i in (6, 4, 2):
+        pieces[i] = lax.ppermute(piece, "grid", [(j, j ^ i) for j in range(n)])
+    for i in (0, 2, 4, 6):
+        pieces[i + 1] = lax.ppermute(pieces[i], "grid", [(j, j ^ 1) for j in range(n)])
+    return [pieces[i] for i in range(n)]
 
 
 def exchange_pieces(pieces, n):
     if len(pieces) == 1:
         return [lax.all_to_all(pieces[0], "grid", 0, 0, tiled=True)]
     return [pieces[0]] + [
-        lax.ppermute(pieces[i], "grid", [(j, j ^ i) for j in range(n)]) for i in range(1, n)
+        lax.ppermute(pieces[i], "grid", [(j, j ^ i) for j in range(n)]) for i in ORDER[1:]
     ]
 
 
@@ -255,11 +260,11 @@
     scale = n / 2.0
     shape = jax.ShapeDtypeStruct
     parents = ancestors[:, 0]
-    wide = width + -(-NB // slab) * LANES
+    tall = width // LANES * slab + 8
 
     piece = call(
         functools.partial(pick_kernel, (slab, depth, block_cells, groups, count)),
-        shape((slab, wide), F32),
+        shape((tall, LANES), F32),
         [PLACE] * 5,
         scratch=[
             pltpu.SMEM(obs_owner.shape, jnp.int32),
@@ -272,7 +277,9 @@
         moved=10**6,
         limit=None,
     )(obs_owner, channel_weights, obs_offset, parents, prior)
-    pieces = gather_pieces(piece, n)
+    far = lax.ppermute(piece, "lev", [(j, j ^ 2) for j in range(lev)])
+    both = call(join_kernel, shape((2, tall, LANES), F32), [VMEM] * 2, moved=10**5)(piece, far)
+    pieces = gather_pieces(both, n)
 
     send = call(
         functools.partial(retile_kernel, (n, slab, depth, block_cells)),
@@ -289,23 +296,23 @@
         moved=10**6,
     )(obs_owner, obs_offset, obs_value, obs_error, parents)
 
+    far_rows = lax.ppermute(rows, "lev", [(j, j ^ 2) for j in range(lev)])
+
     own = call(
         functools.partial(turn_kernel, (n, slab, width)),
-        shape((width + SPARE, members), F32),
-        [SMEM, VMEM, PLACE] + [VMEM] * len(pieces),
-        scratch=[pltpu.VMEM((n, slab, wide), F32)],
-        moved=10**6,
-    )(obs_owner, rows, send, *pieces)
-    far = lax.ppermute(own, "lev", [(j, j ^ 2) for j in range(lev)])
+        shape((2, width + SPARE, members), F32),
+        [SMEM, VMEM, VMEM, PLACE] + [VMEM] * len(pieces),
+        scratch=[pltpu.VMEM((n, 2, tall, LANES), F32)],
+        moved=10**6,
+    )(obs_owner, rows, far_rows, send, *pieces)
     near = lax.ppermute(own, "lev", [(j, j ^ 1) for j in range(lev)])
-    cross = lax.ppermute(far, "lev", [(j, j ^ 1) for j in range(lev)])
 
     pull = call(
         functools.partial(chain_kernel, (members, groups, count)),
         shape((8, members), F32),
-        [VMEM] * 5,
+        [VMEM] * 3,
         moved=10**5,
-    )(own, near, far, cross, steps)
+    )(own, near, steps)
 
     if n == 8:
         layout = [shape((depth, slab, block_cells), F32)] * n

time: 57.3 us -> 72.9 us (1.27)
  waiting for transfers between devices: 19.3 us -> 29 us
  local copies, waits for them, and re-layouts: 0.04 us -> 4.28 us
  starting transfers between devices: 28.3 us -> 29.7 us
    all_to_all x1, waiting for transfers between devices: 0.72 us -> 12.4 us  [body(): fields = lax.all_to_all(send, 'grid', 0, 0, tiled=True)]
    unnamed x14 -> x16, local copies, waits for them, and re-layouts: 0.04 us -> 4.28 us
    ppermute x9, waiting for transfers between devices: 13.8 us -> 10.4 us  [the longest x3 6.59 us: gather_pieces(): pieces[i] = lax.ppermute(piece, 'grid', [(j, j ^ i) for j in range(n)])]
    ppermute x9, starting transfers between devices: 12.9 us -> 14.8 us  [the longest x4 5.42 us: gather_pieces(): lax.ppermute(pieces[i], 'grid', [(j, j ^ 1) for j in range(n)])]
    ppermute x7, waiting for transfers between devices: 4.74 us -> 6.12 us  [exchange_pieces(): lax.ppermute(pieces[i], 'grid', [(j, j ^ i) for j in range(n)])]
    ppermute x7, starting transfers between devices: 11.2 us -> 10 us  [exchange_pieces(): lax.ppermute(pieces[i], 'grid', [(j, j ^ i) for j in range(n)])]
  transfers between devices with their start and end apart: 18 -> 18, of which waited for: 10 -> 8; matrix products, arithmetic and copies ran while one was open for 0% -> 0% of each run, Pallas kernels for 8% -> 6%
where the time goes in v6:
time: 72.9 us; the launch traced here: 72.5 us
  starting transfers between devices  29.7 us (41%)
  waiting for transfers between devices  29 us (40%)
  Pallas kernels  9.53 us (13%)
  local copies, waits for them, and re-layouts  4.28 us (6%)
    all_to_all x1, waiting for transfers between devices, body(): fields = lax.all_to_all(send, 'grid', 0, 0, tiled=True)  12.4 us
    ppermute x7, starting transfers between devices, exchange_pieces(): lax.ppermute(pieces[i], 'grid', [(j, j ^ i) for j in range(n)])  10 us
    ppermute x3, waiting for transfers between devices, gather_pieces(): pieces[i] = lax.ppermute(piece, 'grid', [(j, j ^ i) for j in range(n)])  6.59 us
    ppermute x7, waiting for transfers between devices, exchange_pieces(): lax.ppermute(pieces[i], 'grid', [(j, j ^ i) for j in range(n)])  6.12 us
    ppermute x4, starting transfers between devices, gather_pieces(): lax.ppermute(pieces[i], 'grid', [(j, j ^ 1) for j in range(n)])  5.42 us
    ppermute x3, starting transfers between devices, gather_pieces(): pieces[i] = lax.ppermute(piece, 'grid', [(j, j ^ i) for j in range(n)])  4.84 us
    all_to_all x1, starting transfers between devices, body(): fields = lax.all_to_all(send, 'grid', 0, 0, tiled=True)  4.72 us
    unnamed x16, local copies, waits for them, and re-layouts  4.28 us
  transfers between devices with their start and end apart: 18, of which 8 were waited for; matrix products, arithmetic and copies ran while one was open for 0% of the time, Pallas kernels for 6%

profile of v6, /device:TPU:0, one launch (start us, length us, event | category | flops | bytes accessed | tf_op | source)
XLA Modules:
  0.0 72.5 jit_solution(14479889873097692994)
XLA Ops:
  0.0 2.5 %shard_map.75.own = f32[136,128]{1,0:T(8,128)} custom-call(s32[4]{0:T(128)} %owner.3, f32[2,4]{1,0:T(2,128)} %refs_1_.1, s32[4,4,64]{2,1,0:T(4,128)} %refs_2_.1, s32[4,1,128]{2,1,0:T(1,128)} %bitcast.1, f32[16,2,4096]{2,1,0:T(2,128)} %refs_4_.1), custom_call_target="tpu_custom_call" | custom-call | bytes 1000000 | tf_op jit(solution)/shard_map/pallas_call | solution.py:265
  2.5 3.0 %collective-permute-start.1 = (f32[136,128]{1,0:T(8,128)}, f32[136,128]{1,0:T(8,128)S(1)}, u32[]{:S(2)}, u32[]{:S(2)}) collective-permute-start(f32[136,128]{1,0:T(8,128)} %shard_map.75.own), channel_id=1, source_target_pairs={{0,2},{1,3},{2,0},{3,1},{4,6},{5,7},{6,4},{7,5},{8,10},{9,11},{10,... | collective-permute-start | bytes 208904 | tf_op jit(solution)/shard_map/ppermute | solution.py:280
  5.5 2.5 %collective-permute-done.1.far = f32[136,128]{1,0:T(8,128)S(1)} collective-permute-done((f32[136,128]{1,0:T(8,128)}, f32[136,128]{1,0:T(8,128)S(1)}, u32[]{:S(2)}, u32[]{:S(2)}) %collective-permute-start.1) | collective-permute-done | bytes 69664 | tf_op jit(solution)/shard_map/ppermute | solution.py:280
  8.0 0.9 %copy-done.1 = f32[136,128]{1,0:T(8,128)S(1)} copy-done((f32[136,128]{1,0:T(8,128)S(1)}, f32[136,128]{1,0:T(8,128)}, u32[]{:S(2)}) %copy-start.1) | copy-done | bytes 69656
  8.9 4.2 %collective-permute-start.7 = (f32[2,136,128]{2,1,0:T(8,128)S(1)}, f32[2,136,128]{2,1,0:T(8,128)S(1)}, u32[]{:S(2)}, u32[]{:S(2)}) collective-permute-start(f32[2,136,128]{2,1,0:T(8,128)S(1)} %shard_map.76.refs_0_), channel_id=1, source_target_pairs={{0,24},{4,28},{8,16},{12,20},{16,8},{20,12},{24,0},{28,4},{1,25},{... | collective-permute-start | bytes 417800 | tf_op jit(solution)/shard_map/ppermute | solution.py:238
  13.1 0.0 collective-permute-start.5
  13.1 0.6 collective-permute-start.3
  13.7 1.7 %collective-permute-start.2 = (f32[2,136,128]{2,1,0:T(8,128)S(1)}, f32[2,136,128]{2,1,0:T(8,128)S(1)}, u32[]{:S(2)}, u32[]{:S(2)}) collective-permute-start(f32[2,136,128]{2,1,0:T(8,128)S(1)} %shard_map.76.refs_0_), channel_id=1, source_target_pairs={{0,4},{4,0},{8,12},{12,8},{16,20},{20,16},{24,28},{28,24},{1,5},{5... | collective-permute-start | bytes 417800 | tf_op jit(solution)/shard_map/ppermute | solution.py:240
  15.4 2.3 %collective-permute-done.7.refs_6_ = f32[2,136,128]{2,1,0:T(8,128)S(1)} collective-permute-done((f32[2,136,128]{2,1,0:T(8,128)S(1)}, f32[2,136,128]{2,1,0:T(8,128)S(1)}, u32[]{:S(2)}, u32[]{:S(2)}) %collective-permute-start.7) | collective-permute-done | bytes 139296 | tf_op jit(solution)/shard_map/ppermute | solution.py:238
  17.7 1.7 %collective-permute-start.8 = (f32[2,136,128]{2,1,0:T(8,128)S(1)}, f32[2,136,128]{2,1,0:T(8,128)S(1)}, u32[]{:S(2)}, u32[]{:S(2)}) collective-permute-start(f32[2,136,128]{2,1,0:T(8,128)S(1)} %collective-permute-done.7.refs_6_), channel_id=1, source_target_pairs={{0,4},{4,0},{8,12},{12,8},{16,20},{20,16},{24,28},{28,24},{1,5},{5... | collective-permute-start | bytes 417800 | tf_op jit(solution)/shard_map/ppermute | solution.py:240
  19.4 4.3 %collective-permute-done.5.refs_4_ = f32[2,136,128]{2,1,0:T(8,128)S(1)} collective-permute-done((f32[2,136,128]{2,1,0:T(8,128)S(1)}, f32[2,136,128]{2,1,0:T(8,128)S(1)}, u32[]{:S(2)}, u32[]{:S(2)}) %collective-permute-start.5) | collective-permute-done | bytes 139296 | tf_op jit(solution)/shard_map/ppermute | solution.py:238
  23.7 1.5 %collective-permute-start.6 = (f32[2,136,128]{2,1,0:T(8,128)S(1)}, f32[2,136,128]{2,1,0:T(8,128)S(1)}, u32[]{:S(2)}, u32[]{:S(2)}) collective-permute-start(f32[2,136,128]{2,1,0:T(8,128)S(1)} %collective-permute-done.5.refs_4_), channel_id=1, source_target_pairs={{0,4},{4,0},{8,12},{12,8},{16,20},{20,16},{24,28},{28,24},{1,5},{5... | collective-permute-start | bytes 417800 | tf_op jit(solution)/shard_map/ppermute | solution.py:240
  25.2 0.0 collective-permute-done.3.refs_2_
  25.2 0.5 collective-permute-start.4
  25.7 0.7 copy-done.2
  26.4 0.7 copy-done.3
  27.1 0.7 copy-done.4
  27.8 0.7 copy-done.6
  28.5 0.7 copy-done.7
  29.1 1.0 %shard_map.73 = (f32[32,128]{1,0:T(8,128)S(1)}, f32[5,128,128]{2,1,0:T(8,128)S(1)}) custom-call(s32[4]{0:T(128)S(1)} %copy-done.4, s32[4,4,64]{2,1,0:T(4,128)S(1)} %copy-done.2, f32[4,1,64]{2,1,0:T(1,128)S(1)} %copy-done.6, f32[4,1,64]{2,1,0:T(1,128)S(1)} %copy-done.7, s32[4,1,128]{2,1,0:T(1,128)S(1)} %bitcast.2), custom_call_target="tpu_custom_call" | custom-call | bytes 1000000 | tf_op jit(solution)/shard_map/pallas_call | solution.py:292
  30.1 1.6 %collective-permute-start = (f32[32,128]{1,0:T(8,128)S(1)}, f32[32,128]{1,0:T(8,128)S(1)}, u32[]{:S(2)}, u32[]{:S(2)}) collective-permute-start(f32[32,128]{1,0:T(8,128)S(1)} %get-tuple-element.16.rows), channel_id=1, source_target_pairs={{0,2},{1,3},{2,0},{3,1},{4,6},{5,7},{6,4},{7,5},{8,10},{9,11},{10,... | collective-permute-start | bytes 49160 | tf_op jit(solution)/shard_map/ppermute | solution.py:299
  31.7 0.9 %shard_map.74.ahead = f32[8,2,16,512]{3,2,1,0:T(8,128)} custom-call(f32[16,2,4096]{2,1,0:T(2,128)S(1)} %copy-done), custom_call_target="tpu_custom_call" | custom-call | bytes 1000000 | tf_op jit(solution)/shard_map/pallas_call | solution.py:284
  32.6 1.4 %collective-permute-done.far_rows = f32[32,128]{1,0:T(8,128)S(1)} collective-permute-done((f32[32,128]{1,0:T(8,128)S(1)}, f32[32,128]{1,0:T(8,128)S(1)}, u32[]{:S(2)}, u32[]{:S(2)}) %collective-permute-start) | collective-permute-done | bytes 16416 | tf_op jit(solution)/shard_map/ppermute | solution.py:299
  33.9 0.0 collective-permute-done.2.refs_1_
  33.9 0.0 collective-permute-done.8.refs_7_
  33.9 0.0 collective-permute-done.6.refs_5_
  33.9 0.0 collective-permute-done.4.refs_3_
  34.0 1.0 %shard_map.77.own = f32[2,1056,128]{2,1,0:T(8,128)S(1)} custom-call(s32[4]{0:T(128)S(1)} %copy-done.5, f32[32,128]{1,0:T(8,128)S(1)} %get-tuple-element.16.rows, f32[32,128]{1,0:T(8,128)S(1)} %collective-permute-done.far_rows, f32[8,2,16,512]{3,2,1,0:T(8,128)} %shard_map.74.ahead, f32[2,136,128]{2,1,0:T(8,128)S(1)} %shard_map.76.refs_0_, ...), custom_call_target="tpu_custom_call" | custom-call | bytes 1000000 | tf_op jit(solution)/shard_map/pallas_call | solution.py:301
  34.9 0.1 collective-permute-start.9
  35.0 4.7 %all-to-all-start = ((f32[8,2,16,512]{3,2,1,0:T(8,128)}), f32[8,2,16,512]{3,2,1,0:T(8,128)S(1)}, u32[]{:S(2)}, u32[]{:S(2)}) async-start(f32[8,2,16,512]{3,2,1,0:T(8,128)} %shard_map.74.ahead), calls=%async_computation | async-start | bytes 1048576 | tf_op jit(solution)/shard_map/all_to_all | solution.py:290
  39.7 0.0 collective-permute-done.9.near
  39.7 2.7 %shard_map.78.pull = f32[8,128]{1,0:T(8,128)S(1)} custom-call(f32[2,1056,128]{2,1,0:T(8,128)S(1)} %shard_map.77.own, f32[2,1056,128]{2,1,0:T(8,128)S(1)} %collective-permute-done.9.near, f32[5,128,128]{2,1,0:T(8,128)S(1)} %get-tuple-element.15.steps), custom_call_target="tpu_custom_call" | custom-call | bytes 100000 | tf_op jit(solution)/shard_map/pallas_call | solution.py:310
  42.5 12.4 %all-to-all-done.fields = f32[8,2,16,512]{3,2,1,0:T(8,128)S(1)} async-done(((f32[8,2,16,512]{3,2,1,0:T(8,128)}), f32[8,2,16,512]{3,2,1,0:T(8,128)S(1)}, u32[]{:S(2)}, u32[]{:S(2)}) %all-to-all-start) | async-done | bytes 524320 | tf_op jit(solution)/shard_map/all_to_all | solution.py:290
  54.9 0.6 shard_map.79
  55.4 1.2 %collective-permute-start.10 = (f32[2,16,512]{2,1,0:T(8,128)S(1)}, f32[2,16,512]{2,1,0:T(8,128)S(1)}, u32[]{:S(2)}, u32[]{:S(2)}) collective-permute-start(f32[2,16,512]{2,1,0:T(8,128)S(1)} %get-tuple-element.18), channel_id=1, source_target_pairs={{0,24},{4,28},{8,16},{12,20},{16,8},{20,12},{24,0},{28,4},{1,25},{... | collective-permute-start | bytes 196616 | tf_op jit(solution)/shard_map/ppermute | solution.py:248
  56.7 1.0 %collective-permute-start.11 = (f32[2,16,512]{2,1,0:T(8,128)S(1)}, f32[2,16,512]{2,1,0:T(8,128)S(1)}, u32[]{:S(2)}, u32[]{:S(2)}) collective-permute-start(f32[2,16,512]{2,1,0:T(8,128)S(1)} %get-tuple-element.19), channel_id=1, source_target_pairs={{0,16},{4,20},{8,24},{12,28},{16,0},{20,4},{24,8},{28,12},{1,17},{... | collective-permute-start | bytes 196616 | tf_op jit(solution)/shard_map/ppermute | solution.py:248
  57.7 2.5 %collective-permute-start.12 = (f32[2,16,512]{2,1,0:T(8,128)S(1)}, f32[2,16,512]{2,1,0:T(8,128)S(1)}, u32[]{:S(2)}, u32[]{:S(2)}) collective-permute-start(f32[2,16,512]{2,1,0:T(8,128)S(1)} %get-tuple-element.20), channel_id=1, source_target_pairs={{0,28},{4,24},{8,20},{12,16},{16,12},{20,8},{24,4},{28,0},{1,29},{... | collective-permute-start | bytes 196616 | tf_op jit(solution)/shard_map/ppermute | solution.py:248
  60.2 2.0 %collective-permute-start.13 = (f32[2,16,512]{2,1,0:T(8,128)S(1)}, f32[2,16,512]{2,1,0:T(8,128)S(1)}, u32[]{:S(2)}, u32[]{:S(2)}) collective-permute-start(f32[2,16,512]{2,1,0:T(8,128)S(1)} %get-tuple-element.21), channel_id=1, source_target_pairs={{0,20},{4,16},{8,28},{12,24},{16,4},{20,0},{24,12},{28,8},{1,21},{... | collective-permute-start | bytes 196616 | tf_op jit(solution)/shard_map/ppermute | solution.py:248
  62.3 0.8 %collective-permute-start.14 = (f32[2,16,512]{2,1,0:T(8,128)S(1)}, f32[2,16,512]{2,1,0:T(8,128)S(1)}, u32[]{:S(2)}, u32[]{:S(2)}) collective-permute-start(f32[2,16,512]{2,1,0:T(8,128)S(1)} %get-tuple-element.22), channel_id=1, source_target_pairs={{0,8},{4,12},{8,0},{12,4},{16,24},{20,28},{24,16},{28,20},{1,9},{5... | collective-permute-start | bytes 196616 | tf_op jit(solution)/shard_map/ppermute | solution.py:248
  63.0 0.0 collective-permute-done.10.refs_1_
  63.0 2.2 %collective-permute-start.15 = (f32[2,16,512]{2,1,0:T(8,128)S(1)}, f32[2,16,512]{2,1,0:T(8,128)S(1)}, u32[]{:S(2)}, u32[]{:S(2)}) collective-permute-start(f32[2,16,512]{2,1,0:T(8,128)S(1)} %get-tuple-element.23), channel_id=1, source_target_pairs={{0,12},{4,8},{8,4},{12,0},{16,28},{20,24},{24,20},{28,16},{1,13},{... | collective-permute-start | bytes 196616 | tf_op jit(solution)/shard_map/ppermute | solution.py:248
  65.2 2.2 %collective-permute-done.11.refs_2_ = f32[2,16,512]{2,1,0:T(8,128)S(1)} collective-permute-done((f32[2,16,512]{2,1,0:T(8,128)S(1)}, f32[2,16,512]{2,1,0:T(8,128)S(1)}, u32[]{:S(2)}, u32[]{:S(2)}) %collective-permute-start.11) | collective-permute-done | bytes 65568 | tf_op jit(solution)/shard_map/ppermute | solution.py:248
  67.4 0.3 collective-permute-start.16
  67.7 0.0 collective-permute-done.12.refs_3_
  67.7 2.5 %collective-permute-done.13.refs_4_ = f32[2,16,512]{2,1,0:T(8,128)S(1)} collective-permute-done((f32[2,16,512]{2,1,0:T(8,128)S(1)}, f32[2,16,512]{2,1,0:T(8,128)S(1)}, u32[]{:S(2)}, u32[]{:S(2)}) %collective-permute-start.13) | collective-permute-done | bytes 65568 | tf_op jit(solution)/shard_map/ppermute | solution.py:248
  70.1 0.0 collective-permute-done.14.refs_5_
  70.1 1.5 %collective-permute-done.16.refs_7_ = f32[2,16,512]{2,1,0:T(8,128)S(1)} collective-permute-done((f32[2,16,512]{2,1,0:T(8,128)S(1)}, f32[2,16,512]{2,1,0:T(8,128)S(1)}, u32[]{:S(2)}, u32[]{:S(2)}) %collective-permute-start.16) | collective-permute-done | bytes 65568 | tf_op jit(solution)/shard_map/ppermute | solution.py:248
  71.6 0.9 %shard_map.80 = f32[16,2,4096]{2,1,0:T(2,128)} custom-call(f32[2,16,512]{2,1,0:T(8,128)S(1)} %get-tuple-element.17.refs_0_, f32[2,16,512]{2,1,0:T(8,128)S(1)} %collective-permute-done.10.refs_1_, f32[2,16,512]{2,1,0:T(8,128)S(1)} %collective-permute-done.11.refs_2_, f32[2,16,512]{2,1,0:T(8,128)S(1)} %collective-permute-done.12.refs_3_, ...), custom_call_target="tpu_custom_call" | custom-call | bytes 1000000 | tf_op jit(solution)/shard_map/pallas_call | solution.py:331
  (12 shorter events, 0.0 us)
Async XLA Ops:
  0.0 34.0 %copy-start.5 = (s32[4]{0:T(128)S(1)}, s32[4]{0:T(128)}, u32[]{:S(2)}) copy-start(s32[4]{0:T(128)} %owner.3) | copy-start | bytes 52
  0.0 31.7 %copy-start = (f32[16,2,4096]{2,1,0:T(2,128)S(1)}, f32[16,2,4096]{2,1,0:T(2,128)}, u32[]{:S(2)}) copy-start(f32[16,2,4096]{2,1,0:T(2,128)} %refs_4_.1) | copy-start | bytes 1572868
  2.5 5.5 %collective-permute-start.1 = (f32[136,128]{1,0:T(8,128)}, f32[136,128]{1,0:T(8,128)S(1)}, u32[]{:S(2)}, u32[]{:S(2)}) collective-permute-start(f32[136,128]{1,0:T(8,128)} %shard_map.75.own), channel_id=1, source_target_pairs={{0,2},{1,3},{2,0},{3,1},{4,6},{5,7},{6,4},{7,5},{8,10},{9,11},{10,... | collective-permute-start | bytes 208904 | tf_op jit(solution)/shard_map/ppermute | solution.py:280
  8.0 0.9 %copy-start.1 = (f32[136,128]{1,0:T(8,128)S(1)}, f32[136,128]{1,0:T(8,128)}, u32[]{:S(2)}) copy-start(f32[136,128]{1,0:T(8,128)} %shard_map.75.own) | copy-start | bytes 208900
  8.9 8.8 %collective-permute-start.7 = (f32[2,136,128]{2,1,0:T(8,128)S(1)}, f32[2,136,128]{2,1,0:T(8,128)S(1)}, u32[]{:S(2)}, u32[]{:S(2)}) collective-permute-start(f32[2,136,128]{2,1,0:T(8,128)S(1)} %shard_map.76.refs_0_), channel_id=1, source_target_pairs={{0,24},{4,28},{8,16},{12,20},{16,8},{20,12},{24,0},{28,4},{1,25},{... | collective-permute-start | bytes 417800 | tf_op jit(solution)/shard_map/ppermute | solution.py:238
  13.1 10.6 %collective-permute-start.5 = (f32[2,136,128]{2,1,0:T(8,128)S(1)}, f32[2,136,128]{2,1,0:T(8,128)S(1)}, u32[]{:S(2)}, u32[]{:S(2)}) collective-permute-start(f32[2,136,128]{2,1,0:T(8,128)S(1)} %shard_map.76.refs_0_), channel_id=1, source_target_pairs={{0,16},{4,20},{8,24},{12,28},{16,0},{20,4},{24,8},{28,12},{1,17},{... | collective-permute-start | bytes 417800 | tf_op jit(solution)/shard_map/ppermute | solution.py:238
  13.1 12.1 %collective-permute-start.3 = (f32[2,136,128]{2,1,0:T(8,128)S(1)}, f32[2,136,128]{2,1,0:T(8,128)S(1)}, u32[]{:S(2)}, u32[]{:S(2)}) collective-permute-start(f32[2,136,128]{2,1,0:T(8,128)S(1)} %shard_map.76.refs_0_), channel_id=1, source_target_pairs={{0,8},{4,12},{8,0},{12,4},{16,24},{20,28},{24,16},{28,20},{1,9},{5... | collective-permute-start | bytes 417800 | tf_op jit(solution)/shard_map/ppermute | solution.py:238
  13.7 20.2 %collective-permute-start.2 = (f32[2,136,128]{2,1,0:T(8,128)S(1)}, f32[2,136,128]{2,1,0:T(8,128)S(1)}, u32[]{:S(2)}, u32[]{:S(2)}) collective-permute-start(f32[2,136,128]{2,1,0:T(8,128)S(1)} %shard_map.76.refs_0_), channel_id=1, source_target_pairs={{0,4},{4,0},{8,12},{12,8},{16,20},{20,16},{24,28},{28,24},{1,5},{5... | collective-permute-start | bytes 417800 | tf_op jit(solution)/shard_map/ppermute | solution.py:240
  17.7 16.3 %collective-permute-start.8 = (f32[2,136,128]{2,1,0:T(8,128)S(1)}, f32[2,136,128]{2,1,0:T(8,128)S(1)}, u32[]{:S(2)}, u32[]{:S(2)}) collective-permute-start(f32[2,136,128]{2,1,0:T(8,128)S(1)} %collective-permute-done.7.refs_6_), channel_id=1, source_target_pairs={{0,4},{4,0},{8,12},{12,8},{16,20},{20,16},{24,28},{28,24},{1,5},{5... | collective-permute-start | bytes 417800 | tf_op jit(solution)/shard_map/ppermute | solution.py:240
  23.7 10.2 %collective-permute-start.6 = (f32[2,136,128]{2,1,0:T(8,128)S(1)}, f32[2,136,128]{2,1,0:T(8,128)S(1)}, u32[]{:S(2)}, u32[]{:S(2)}) collective-permute-start(f32[2,136,128]{2,1,0:T(8,128)S(1)} %collective-permute-done.5.refs_4_), channel_id=1, source_target_pairs={{0,4},{4,0},{8,12},{12,8},{16,20},{20,16},{24,28},{28,24},{1,5},{5... | collective-permute-start | bytes 417800 | tf_op jit(solution)/shard_map/ppermute | solution.py:240
  25.2 8.7 %collective-permute-start.4 = (f32[2,136,128]{2,1,0:T(8,128)S(1)}, f32[2,136,128]{2,1,0:T(8,128)S(1)}, u32[]{:S(2)}, u32[]{:S(2)}) collective-permute-start(f32[2,136,128]{2,1,0:T(8,128)S(1)} %collective-permute-done.3.refs_2_), channel_id=1, source_target_pairs={{0,4},{4,0},{8,12},{12,8},{16,20},{20,16},{24,28},{28,24},{1,5},{5... | collective-permute-start | bytes 417800 | tf_op jit(solution)/shard_map/ppermute | solution.py:240
  25.7 0.7 copy-start.2
  26.4 0.7 copy-start.3
  27.1 0.7 copy-start.4
  27.8 0.7 copy-start.6
  28.4 0.7 copy-start.7
  30.1 3.8 %collective-permute-start = (f32[32,128]{1,0:T(8,128)S(1)}, f32[32,128]{1,0:T(8,128)S(1)}, u32[]{:S(2)}, u32[]{:S(2)}) collective-permute-start(f32[32,128]{1,0:T(8,128)S(1)} %get-tuple-element.16.rows), channel_id=1, source_target_pairs={{0,2},{1,3},{2,0},{3,1},{4,6},{5,7},{6,4},{7,5},{8,10},{9,11},{10,... | collective-permute-start | bytes 49160 | tf_op jit(solution)/shard_map/ppermute | solution.py:299
  34.9 4.8 %collective-permute-start.9 = (f32[2,1056,128]{2,1,0:T(8,128)S(1)}, f32[2,1056,128]{2,1,0:T(8,128)S(1)}, u32[]{:S(2)}, u32[]{:S(2)}) collective-permute-start(f32[2,1056,128]{2,1,0:T(8,128)S(1)} %shard_map.77.own), channel_id=1, source_target_pairs={{0,1},{1,0},{2,3},{3,2},{4,5},{5,4},{6,7},{7,6},{8,9},{9,8},{10,11... | collective-permute-start | bytes 3244040 | tf_op jit(solution)/shard_map/ppermute | solution.py:308
  35.0 19.9 %all-to-all-start = ((f32[8,2,16,512]{3,2,1,0:T(8,128)}), f32[8,2,16,512]{3,2,1,0:T(8,128)S(1)}, u32[]{:S(2)}, u32[]{:S(2)}) async-start(f32[8,2,16,512]{3,2,1,0:T(8,128)} %shard_map.74.ahead), calls=%async_computation | async-start | bytes 1048576 | tf_op jit(solution)/shard_map/all_to_all | solution.py:290
  55.4 7.6 %collective-permute-start.10 = (f32[2,16,512]{2,1,0:T(8,128)S(1)}, f32[2,16,512]{2,1,0:T(8,128)S(1)}, u32[]{:S(2)}, u32[]{:S(2)}) collective-permute-start(f32[2,16,512]{2,1,0:T(8,128)S(1)} %get-tuple-element.18), channel_id=1, source_target_pairs={{0,24},{4,28},{8,16},{12,20},{16,8},{20,12},{24,0},{28,4},{1,25},{... | collective-permute-start | bytes 196616 | tf_op jit(solution)/shard_map/ppermute | solution.py:248
  56.7 10.7 %collective-permute-start.11 = (f32[2,16,512]{2,1,0:T(8,128)S(1)}, f32[2,16,512]{2,1,0:T(8,128)S(1)}, u32[]{:S(2)}, u32[]{:S(2)}) collective-permute-start(f32[2,16,512]{2,1,0:T(8,128)S(1)} %get-tuple-element.19), channel_id=1, source_target_pairs={{0,16},{4,20},{8,24},{12,28},{16,0},{20,4},{24,8},{28,12},{1,17},{... | collective-permute-start | bytes 196616 | tf_op jit(solution)/shard_map/ppermute | solution.py:248
  57.7 9.9 %collective-permute-start.12 = (f32[2,16,512]{2,1,0:T(8,128)S(1)}, f32[2,16,512]{2,1,0:T(8,128)S(1)}, u32[]{:S(2)}, u32[]{:S(2)}) collective-permute-start(f32[2,16,512]{2,1,0:T(8,128)S(1)} %get-tuple-element.20), channel_id=1, source_target_pairs={{0,28},{4,24},{8,20},{12,16},{16,12},{20,8},{24,4},{28,0},{1,29},{... | collective-permute-start | bytes 196616 | tf_op jit(solution)/shard_map/ppermute | solution.py:248
  60.2 9.9 %collective-permute-start.13 = (f32[2,16,512]{2,1,0:T(8,128)S(1)}, f32[2,16,512]{2,1,0:T(8,128)S(1)}, u32[]{:S(2)}, u32[]{:S(2)}) collective-permute-start(f32[2,16,512]{2,1,0:T(8,128)S(1)} %get-tuple-element.21), channel_id=1, source_target_pairs={{0,20},{4,16},{8,28},{12,24},{16,4},{20,0},{24,12},{28,8},{1,21},{... | collective-permute-start | bytes 196616 | tf_op jit(solution)/shard_map/ppermute | solution.py:248
  62.3 7.9 %collective-permute-start.14 = (f32[2,16,512]{2,1,0:T(8,128)S(1)}, f32[2,16,512]{2,1,0:T(8,128)S(1)}, u32[]{:S(2)}, u32[]{:S(2)}) collective-permute-start(f32[2,16,512]{2,1,0:T(8,128)S(1)} %get-tuple-element.22), channel_id=1, source_target_pairs={{0,8},{4,12},{8,0},{12,4},{16,24},{20,28},{24,16},{28,20},{1,9},{5... | collective-permute-start | bytes 196616 | tf_op jit(solution)/shard_map/ppermute | solution.py:248
  63.0 7.1 %collective-permute-start.15 = (f32[2,16,512]{2,1,0:T(8,128)S(1)}, f32[2,16,512]{2,1,0:T(8,128)S(1)}, u32[]{:S(2)}, u32[]{:S(2)}) collective-permute-start(f32[2,16,512]{2,1,0:T(8,128)S(1)} %get-tuple-element.23), channel_id=1, source_target_pairs={{0,12},{4,8},{8,4},{12,0},{16,28},{20,24},{24,20},{28,16},{1,13},{... | collective-permute-start | bytes 196616 | tf_op jit(solution)/shard_map/ppermute | solution.py:248
  67.4 4.3 %collective-permute-start.16 = (f32[2,16,512]{2,1,0:T(8,128)S(1)}, f32[2,16,512]{2,1,0:T(8,128)S(1)}, u32[]{:S(2)}, u32[]{:S(2)}) collective-permute-start(f32[2,16,512]{2,1,0:T(8,128)S(1)} %get-tuple-element.24), channel_id=1, source_target_pairs={{0,4},{4,0},{8,12},{12,8},{16,20},{20,16},{24,28},{28,24},{1,5},{5... | collective-permute-start | bytes 196616 | tf_op jit(solution)/shard_map/ppermute | solution.py:248

commit v7 on v3

--- a/solution.py
+++ b/solution.py
@@ -73,20 +73,19 @@
                     axis=1,
                 )
                 total = total + found * row
-            lane = b * width + c * LANES
-            out[:, lane : lane + LANES] = total
-    lane = NB * width
-    out[:, lane:] = jnp.zeros((slab, out.shape[1] - lane), F32)
-    for b in range(NB):
-        row, block = b % slab, lane + (b // slab) * LANES
-        out[row : row + 1, block : block + LANES] = ancestors[b].astype(F32)
-
-
-def retile_kernel(shape, prior, after, out):
+            line = (b * width // LANES + c) * slab
+            out[line : line + slab, :] = total
+    line = NB * width // LANES * slab
+    out[line:, :] = jnp.zeros((out.shape[0] - line, LANES), F32)
+    for b in range(NB):
+        out[line + b : line + b + 1, :] = ancestors[b].astype(F32)
+
+
+def retile_kernel(shape, prior, out):
     n, slab, depth, block_cells = shape
-    for r in range(n):
+    for i in range(n):
         for level in range(depth):
-            out[r, level] = prior[:, level, r * block_cells : (r + 1) * block_cells]
+            out[i, level] = prior[:, level, i * block_cells : (i + 1) * block_cells]
 
 
 def prep_kernel(shape, owner, offsets, values, errors, ancestors, rows, steps):
@@ -121,23 +120,32 @@
 
 
 def turn_kernel(shape, owner, rows, *refs):
-    n, slab, width = shape
-    pieces, out, held = refs[:-2], refs[-2], refs[-1]
+    n, slab, width, count = shape
+    pieces, out, slim, held = refs[:-3], refs[-3], refs[-2], refs[-1]
     members = n * slab
+    block, group = lax.axis_index("grid"), lax.axis_index("lev")
     if len(pieces) == 1:
         held[...] = pieces[0][...]
     else:
-        block = lax.axis_index("grid")
         for i, piece in enumerate(pieces):
             held[lax.bitwise_xor(block, i)] = piece[...]
+    common = width // NB * (NB - 1)
     for i in range(width // LANES):
-        lanes = slice(i * LANES, (i + 1) * LANES)
-        out[lanes, :] = held[:, :, lanes].reshape(members, LANES).T
+        value = held[:, i * slab : (i + 1) * slab, :].reshape(members, LANES).T
+        out[i * LANES : (i + 1) * LANES, :] = value
+        if (i + 1) * LANES <= common:
+            slim[i * LANES : (i + 1) * LANES, :] = value
+    for i in range(2):
+        start = pl.multiple_of(common + lax.bitwise_xor(group, 2 + i) * count, count)
+        slim[common + i * count : common + (i + 1) * count, :] = out[pl.ds(start, count), :]
+    low = common + 2 * count
     out[width:, :] = rows[...]
+    slim[low:, :] = rows[...]
+    line = width // LANES * slab
     for i, (e, b) in enumerate(PAIRS):
-        lane = width + (e // slab) * LANES
-        line = e % slab
-        out[width + PARENT + i : width + PARENT + i + 1, :] = held[owner[b], line : line + 1, lane : lane + LANES]
+        value = held[owner[b], line + e : line + e + 1, :]
+        out[width + PARENT + i : width + PARENT + i + 1, :] = value
+        slim[low + PARENT + i : low + PARENT + i + 1, :] = value
 
 
 def mix_kernel(shape, steps, fields, out):
@@ -148,15 +156,14 @@
 
 
 def chain_kernel(shape, own, near, far, cross, steps, fields, out):
-    n, slab, depth, block_cells, groups, count = shape
-    members = n * slab
+    members, groups, count, depth, block_cells = shape
     width = groups * count
-    base = NB * width
     group = lax.axis_index("lev")
     sources = [own, near, far, cross]
-    columns = [source[base : base + SPARE, :].T for source in sources]
+    bases = [NB * width, NB * width, (NB - 1) * width + 2 * count, (NB - 1) * width + 2 * count]
+    columns = [source[base : base + SPARE, :].T for source, base in zip(sources, bases)]
     parents, alphas = [], []
-    for source in sources:
+    for source, base in zip(sources, bases):
         parents.append(source[base + PARENT : base + PARENT + 8, :].astype(jnp.int32))
         alphas.append(source[base + ALPHA : base + ALPHA + 6, :])
     tilts = {}
@@ -171,7 +178,10 @@
             total = jnp.zeros((count, members), F32)
             tilted = jnp.zeros((count, members), F32)
             for p, source in enumerate(sources):
-                value = source[pl.ds(start, count), :]
+                if b == NB - 1 and p > 1:
+                    value = source[b * width + (p - 2) * count : b * width + (p - 1) * count, :]
+                else:
+                    value = source[pl.ds(start, count), :]
                 for e in range(b):
                     i = PAIRS.index((e, b))
                     tilted = tilted + value * tilts[e, p, b]
@@ -201,29 +211,37 @@
         pull = pull + high_dot(jnp.broadcast_to(pulled[b], (8, members)), steps[b])
     for level in range(depth):
         value = fields[:, level].reshape(members, block_cells)
-        shift = high_dot(pull, value)[0:1]
-        for d in range(n):
-            out[d, level : level + 1, :] = shift
-
-
-def final_kernel(shape, moved, shift, out):
+        out[level : level + 1, :] = high_dot(pull, value)[0:1]
+
+
+def final_kernel(shape, moved, *refs):
     n, slab, depth, block_cells = shape
-    for r in range(n):
+    shifts, out = refs[:-1], refs[-1]
+    block = lax.axis_index("grid")
+    for i in range(n):
+        region = i if len(shifts) == 1 else lax.bitwise_xor(block, i)
+        cells = pl.ds(pl.multiple_of(region * block_cells, LANES), block_cells)
         for level in range(depth):
-            value = moved[r, level] + shift[r, level : level + 1, :]
-            out[:, level, r * block_cells : (r + 1) * block_cells] = value
+            if len(shifts) == 1:
+                shift = shifts[0][i, level : level + 1, :]
+            else:
+                shift = shifts[i][level : level + 1, :]
+            out[:, level, cells] = moved[region, level] + shift
+
+
+def hop(value, distance, n):
+    return lax.ppermute(value, "grid", [(j, j ^ distance) for j in range(n)])
 
 
 def gather_pieces(piece, n):
     if n != 8:
         return [lax.all_to_all(jnp.broadcast_to(piece[None], (n,) + piece.shape), "grid", 0, 0, tiled=True)]
-    pieces = [piece]
-    for far in (2, 4, 6):
-        pieces.append(lax.ppermute(piece, "grid", [(j, j ^ far) for j in range(n)]))
-    result = []
-    for part in pieces:
-        result += [part, lax.ppermute(part, "grid", [(j, j ^ 1) for j in range(n)])]
-    return result
+    pieces = {0: piece}
+    for i in (6, 4, 2):
+        pieces[i] = hop(piece, i, n)
+    for i in (0, 2, 4, 6):
+        pieces[i + 1] = hop(pieces[i], 1, n)
+    return [pieces[i] for i in range(n)]
 
 
 def body(prior, channel_weights, obs_owner, obs_offset, obs_value, obs_error, ancestors):
@@ -237,11 +255,11 @@
     scale = n / 2.0
     shape = jax.ShapeDtypeStruct
     parents = ancestors[:, 0]
-    wide = width + -(-NB // slab) * LANES
+    tall = width // LANES * slab + 8
 
     piece = call(
         functools.partial(pick_kernel, (slab, depth, block_cells, groups, count)),
-        shape((slab, wide), F32),
+        shape((tall, LANES), F32),
         [PLACE] * 5,
         scratch=[
             pltpu.SMEM(obs_owner.shape, jnp.int32),
@@ -255,13 +273,13 @@
         limit=None,
     )(obs_owner, channel_weights, obs_offset, parents, prior)
     pieces = gather_pieces(piece, n)
-
     send = call(
         functools.partial(retile_kernel, (n, slab, depth, block_cells)),
         shape((n, depth, slab, block_cells), F32),
-        [VMEM, PLACE],
-        moved=10**6,
-    )(prior, pieces[min(2, len(pieces) - 1)])
+        [VMEM],
+        moved=10**6,
+    )(prior)
+    send, *_ = lax.optimization_barrier((send, *pieces[2::2]))
     fields = lax.all_to_all(send, "grid", 0, 0, tiled=True)
 
     rows, steps = call(
@@ -271,42 +289,41 @@
         moved=10**6,
     )(obs_owner, obs_offset, obs_value, obs_error, parents)
 
-    own = call(
-        functools.partial(turn_kernel, (n, slab, width)),
-        shape((width + SPARE, members), F32),
-        [SMEM] + [VMEM] * (1 + len(pieces)),
-        scratch=[pltpu.VMEM((n, slab, wide), F32)],
+    slim_height = (NB - 1) * groups * count + 2 * count + SPARE
+    own, slim = call(
+        functools.partial(turn_kernel, (n, slab, width, count)),
+        [shape((width + SPARE, members), F32), shape((slim_height, members), F32)],
+        [SMEM, VMEM] + [VMEM] * len(pieces),
+        scratch=[pltpu.VMEM((n, tall, LANES), F32)],
         moved=10**6,
     )(obs_owner, rows, *pieces)
-    far = lax.ppermute(own, "lev", [(j, j ^ 2) for j in range(lev)])
+    far = lax.ppermute(slim, "lev", [(j, j ^ 2) for j in range(lev)])
     near = lax.ppermute(own, "lev", [(j, j ^ 1) for j in range(lev)])
     cross = lax.ppermute(far, "lev", [(j, j ^ 1) for j in range(lev)])
 
     send = call(
         functools.partial(mix_kernel, (n, slab, depth, block_cells)),
         shape((n, depth, slab, block_cells), F32),
-        [VMEM, VMEM],
+        [VMEM] * 2,
         flops=10**8,
         moved=10**6,
     )(steps, fields)
     moved = lax.all_to_all(send, "grid", 0, 0, tiled=True)
 
-    send = call(
-        functools.partial(chain_kernel, (n, slab, depth, block_cells, groups, count)),
-        shape((n, depth, block_cells), F32),
+    shift = call(
+        functools.partial(chain_kernel, (members, groups, count, depth, block_cells)),
+        shape((depth, block_cells), F32),
         [VMEM] * 6,
-        flops=10**9,
-        moved=10**7,
+        moved=10**5,
     )(own, near, far, cross, steps, fields)
-    send, moved = lax.optimization_barrier((send, moved))
-    shift = lax.all_to_all(send, "grid", 0, 0, tiled=True)
+    shifts = gather_pieces(shift, n)
 
     return call(
         functools.partial(final_kernel, (n, slab, depth, block_cells)),
         shape((slab, depth, cells), F32),
-        [VMEM, VMEM],
-        moved=10**6,
-    )(moved, shift)
+        [VMEM] * (1 + len(shifts)),
+        moved=10**6,
+    )(moved, *shifts)
 
 
 def solution(mesh):

time: 70.6 us -> 61.1 us (0.87)
  blocking collectives: 10.2 us -> 0 us
  starting transfers between devices: 23.1 us -> 29.7 us
  waiting for transfers between devices: 26.3 us -> 20.4 us
    all_to_all x1 -> x0, blocking collectives: 10.2 us -> none  [body(): shift = lax.all_to_all(send, 'grid', 0, 0, tiled=True)]
    ppermute x8 -> x15, starting transfers between devices: 13.1 us -> 20.2 us  [the longest x14 18.6 us: hop(): return lax.ppermute(value, 'grid', [(j, j ^ distance) for j in range(n)])]
    ppermute x8 -> x15, waiting for transfers between devices: 21.6 us -> 18.5 us  [the longest x14 15.7 us: hop(): return lax.ppermute(value, 'grid', [(j, j ^ distance) for j in range(n)])]
    all_to_all x1, waiting for transfers between devices: 2.8 us -> 0.01 us  [body(): moved = lax.all_to_all(send, 'grid', 0, 0, tiled=True)]
    all_to_all x1, starting transfers between devices: 6.42 us -> 4.95 us  [body(): fields = lax.all_to_all(send, 'grid', 0, 0, tiled=True)]
    all_to_all x1, starting transfers between devices: 3.49 us -> 4.58 us  [body(): moved = lax.all_to_all(send, 'grid', 0, 0, tiled=True)]
  transfers between devices with their start and end apart: 12 -> 19, of which waited for: 7 -> 11; matrix products, arithmetic and copies ran while one was open for 0% -> 0% of each run, Pallas kernels for 9% -> 12%
where the time goes in v7:
time: 61.1 us; the launch traced here: 60.8 us
  starting transfers between devices  29.7 us (49%)
  waiting for transfers between devices  20.4 us (33%)
  Pallas kernels  10.6 us (17%)
    ppermute x14, starting transfers between devices, hop(): return lax.ppermute(value, 'grid', [(j, j ^ distance) for j in range(n)])  18.6 us
    ppermute x14, waiting for transfers between devices, hop(): return lax.ppermute(value, 'grid', [(j, j ^ distance) for j in range(n)])  15.7 us
    all_to_all x1, starting transfers between devices, body(): fields = lax.all_to_all(send, 'grid', 0, 0, tiled=True)  4.95 us
    all_to_all x1, starting transfers between devices, body(): moved = lax.all_to_all(send, 'grid', 0, 0, tiled=True)  4.58 us
    pallas_call x1, Pallas kernels, body(): call(functools.partial(chain_kernel, (members, groups, count, depth, bloc...  3.07 us
    ppermute x1, waiting for transfers between devices, body(): far = lax.ppermute(slim, 'lev', [(j, j ^ 2) for j in range(lev)])  2.86 us
    pallas_call x1, Pallas kernels, body(): call(functools.partial(pick_kernel, (slab, depth, block_cells, groups, co...  2.46 us
    ppermute x1, waiting for transfers between devices, body(): cross = lax.ppermute(far, 'lev', [(j, j ^ 1) for j in range(lev)])  1.83 us
  transfers between devices with their start and end apart: 19, of which 11 were waited for; matrix products, arithmetic and copies ran while one was open for 0% of the time, Pallas kernels for 12%

profile of v7, /device:TPU:0, one launch (start us, length us, event | category | flops | bytes accessed | tf_op | source)
XLA Modules:
  0.0 60.8 jit_solution(14458875105758199010)
XLA Ops:
  0.0 2.5 %shard_map.75.refs_0_ = f32[136,128]{1,0:T(8,128)} custom-call(s32[4]{0:T(128)} %owner.3, f32[2,4]{1,0:T(2,128)} %refs_1_.1, s32[4,4,64]{2,1,0:T(4,128)} %refs_2_.1, s32[4,1,128]{2,1,0:T(1,128)} %bitcast.1, f32[16,2,4096]{2,1,0:T(2,128)} %refs_4_.1), custom_call_target="tpu_custom_call" | custom-call | bytes 1000000 | tf_op jit(solution)/shard_map/pallas_call | solution.py:260
  2.5 5.1 %collective-permute-start.2 = (f32[136,128]{1,0:T(8,128)}, f32[136,128]{1,0:T(8,128)S(1)}, u32[]{:S(2)}, u32[]{:S(2)}) collective-permute-start(f32[136,128]{1,0:T(8,128)} %shard_map.75.refs_0_), channel_id=1, source_target_pairs={{0,24},{4,28},{8,16},{12,20},{16,8},{20,12},{24,0},{28,4},{1,25},{... | collective-permute-start | bytes 208904 | tf_op jit(solution)/shard_map/ppermute | solution.py:233
  7.6 0.0 collective-permute-start.1
  7.6 0.6 %collective-permute-start = (f32[136,128]{1,0:T(8,128)}, f32[136,128]{1,0:T(8,128)S(1)}, u32[]{:S(2)}, u32[]{:S(2)}) collective-permute-start(f32[136,128]{1,0:T(8,128)} %shard_map.75.refs_0_), channel_id=1, source_target_pairs={{0,8},{4,12},{8,0},{12,4},{16,24},{20,28},{24,16},{28,20},{1,9},{5... | collective-permute-start | bytes 208904 | tf_op jit(solution)/shard_map/ppermute | solution.py:233
  8.2 0.9 %shard_map.74 = f32[8,2,16,512]{3,2,1,0:T(8,128)} custom-call(f32[16,2,4096]{2,1,0:T(2,128)S(1)} %copy-done), custom_call_target="tpu_custom_call" | custom-call | bytes 1000000 | tf_op jit(solution)/shard_map/pallas_call | solution.py:276
  9.1 0.0 copy-start.5
  9.1 0.0 copy-start.6
  9.2 1.3 %collective-permute-done.2.refs_6_ = f32[136,128]{1,0:T(8,128)S(1)} collective-permute-done((f32[136,128]{1,0:T(8,128)}, f32[136,128]{1,0:T(8,128)S(1)}, u32[]{:S(2)}, u32[]{:S(2)}) %collective-permute-start.2) | collective-permute-done | bytes 69664 | tf_op jit(solution)/shard_map/ppermute | solution.py:233
  10.5 3.2 %collective-permute-done.1.refs_4_ = f32[136,128]{1,0:T(8,128)S(1)} collective-permute-done((f32[136,128]{1,0:T(8,128)}, f32[136,128]{1,0:T(8,128)S(1)}, u32[]{:S(2)}, u32[]{:S(2)}) %collective-permute-start.1) | collective-permute-done | bytes 69664 | tf_op jit(solution)/shard_map/ppermute | solution.py:233
  13.7 0.0 collective-permute-done.refs_2_
  13.7 5.0 %all-to-all-start = ((f32[8,2,16,512]{3,2,1,0:T(8,128)}), f32[8,2,16,512]{3,2,1,0:T(8,128)S(1)}, u32[]{:S(2)}, u32[]{:S(2)}) async-start(f32[8,2,16,512]{3,2,1,0:T(8,128)} %shard_map.74), calls=%async_computation | async-start | bytes 1048576 | tf_op jit(solution)/shard_map/all_to_all | solution.py:283
  18.7 2.0 %collective-permute-start.3 = (f32[136,128]{1,0:T(8,128)S(1)}, f32[136,128]{1,0:T(8,128)S(1)}, u32[]{:S(2)}, u32[]{:S(2)}) collective-permute-start(f32[136,128]{1,0:T(8,128)S(1)} %copy-done.1), channel_id=1, source_target_pairs={{0,4},{4,0},{8,12},{12,8},{16,20},{20,16},{24,28},{28,24},{1,5},{5... | collective-permute-start | bytes 208904 | tf_op jit(solution)/shard_map/ppermute | solution.py:233
  20.7 0.1 collective-permute-start.6
  20.8 2.0 %collective-permute-start.5 = (f32[136,128]{1,0:T(8,128)S(1)}, f32[136,128]{1,0:T(8,128)S(1)}, u32[]{:S(2)}, u32[]{:S(2)}) collective-permute-start(f32[136,128]{1,0:T(8,128)S(1)} %collective-permute-done.1.refs_4_), channel_id=1, source_target_pairs={{0,4},{4,0},{8,12},{12,8},{16,20},{20,16},{24,28},{28,24},{1,5},{5... | collective-permute-start | bytes 208904 | tf_op jit(solution)/shard_map/ppermute | solution.py:233
  22.7 0.1 collective-permute-start.4
  22.8 0.0 copy-done.5
  22.8 1.0 %shard_map.73 = (f32[32,128]{1,0:T(8,128)S(1)}, f32[5,128,128]{2,1,0:T(8,128)S(1)}) custom-call(s32[4]{0:T(128)S(1)} %copy-done.4, s32[4,4,64]{2,1,0:T(4,128)S(1)} %copy-done.2, f32[4,1,64]{2,1,0:T(1,128)S(1)} %copy-done.5, f32[4,1,64]{2,1,0:T(1,128)S(1)} %copy-done.6, s32[4,1,128]{2,1,0:T(1,128)S(1)} %bitcast.2), custom_call_target="tpu_custom_call" | custom-call | bytes 1000000 | tf_op jit(solution)/shard_map/pallas_call | solution.py:285
  23.8 3.9 %collective-permute-done.3.refs_1_ = f32[136,128]{1,0:T(8,128)S(1)} collective-permute-done((f32[136,128]{1,0:T(8,128)S(1)}, f32[136,128]{1,0:T(8,128)S(1)}, u32[]{:S(2)}, u32[]{:S(2)}) %collective-permute-start.3) | collective-permute-done | bytes 69664 | tf_op jit(solution)/shard_map/ppermute | solution.py:233
  27.7 1.4 %collective-permute-done.6.refs_7_ = f32[136,128]{1,0:T(8,128)S(1)} collective-permute-done((f32[136,128]{1,0:T(8,128)S(1)}, f32[136,128]{1,0:T(8,128)S(1)}, u32[]{:S(2)}, u32[]{:S(2)}) %collective-permute-start.6) | collective-permute-done | bytes 69664 | tf_op jit(solution)/shard_map/ppermute | solution.py:233
  29.1 1.4 %collective-permute-done.5.refs_5_ = f32[136,128]{1,0:T(8,128)S(1)} collective-permute-done((f32[136,128]{1,0:T(8,128)S(1)}, f32[136,128]{1,0:T(8,128)S(1)}, u32[]{:S(2)}, u32[]{:S(2)}) %collective-permute-start.5) | collective-permute-done | bytes 69664 | tf_op jit(solution)/shard_map/ppermute | solution.py:233
  30.5 0.7 %collective-permute-done.4.refs_3_ = f32[136,128]{1,0:T(8,128)S(1)} collective-permute-done((f32[136,128]{1,0:T(8,128)S(1)}, f32[136,128]{1,0:T(8,128)S(1)}, u32[]{:S(2)}, u32[]{:S(2)}) %collective-permute-start.4) | collective-permute-done | bytes 69664 | tf_op jit(solution)/shard_map/ppermute | solution.py:233
  31.3 0.8 %shard_map.77 = (f32[1056,128]{1,0:T(8,128)S(1)}, f32[928,128]{1,0:T(8,128)S(1)}) custom-call(s32[4]{0:T(128)S(1)} %copy-done.4, f32[32,128]{1,0:T(8,128)S(1)} %get-tuple-element.12.rows, f32[136,128]{1,0:T(8,128)S(1)} %copy-done.1, f32[136,128]{1,0:T(8,128)S(1)} %collective-permute-done.3.refs_1_, f32[136,128]{1,0:T(8,128)S(1)} %collective-permute-done.refs_2_, ...), custom_call_target="tpu_custom_call" | custom-call | bytes 1000000 | tf_op jit(solution)/shard_map/pallas_call | solution.py:293
  32.1 1.6 %collective-permute-start.8 = (f32[928,128]{1,0:T(8,128)S(1)}, f32[928,128]{1,0:T(8,128)S(1)}, u32[]{:S(2)}, u32[]{:S(2)}) collective-permute-start(f32[928,128]{1,0:T(8,128)S(1)} %get-tuple-element.14), channel_id=1, source_target_pairs={{0,2},{1,3},{2,0},{3,1},{4,6},{5,7},{6,4},{7,5},{8,10},{9,11},{10,... | collective-permute-start | bytes 1425416 | tf_op jit(solution)/shard_map/ppermute | solution.py:300
  33.7 0.0 all-to-all-done.fields
  33.7 1.4 %shard_map.76 = f32[8,2,16,512]{3,2,1,0:T(8,128)} custom-call(f32[5,128,128]{2,1,0:T(8,128)S(1)} %get-tuple-element.10.steps, f32[8,2,16,512]{3,2,1,0:T(8,128)S(1)} %all-to-all-done.fields), custom_call_target="tpu_custom_call" | custom-call | flops 100000000 | bytes 1000000 | tf_op jit(solution)/shard_map/pallas_call | solution.py:304
  35.0 4.6 %all-to-all-start.1 = ((f32[8,2,16,512]{3,2,1,0:T(8,128)}), f32[8,2,16,512]{3,2,1,0:T(8,128)S(1)}, u32[]{:S(2)}, u32[]{:S(2)}) async-start(f32[8,2,16,512]{3,2,1,0:T(8,128)} %shard_map.76), calls=%async_computation.1 | async-start | bytes 1048576 | tf_op jit(solution)/shard_map/all_to_all | solution.py:311
  39.6 0.0 collective-permute-start.7
  39.6 2.9 %collective-permute-done.8.far = f32[928,128]{1,0:T(8,128)S(1)} collective-permute-done((f32[928,128]{1,0:T(8,128)S(1)}, f32[928,128]{1,0:T(8,128)S(1)}, u32[]{:S(2)}, u32[]{:S(2)}) %collective-permute-start.8) | collective-permute-done | bytes 475168 | tf_op jit(solution)/shard_map/ppermute | solution.py:300
  42.5 0.0 collective-permute-start.9
  42.5 0.0 collective-permute-done.7.near
  42.5 1.8 %collective-permute-done.9.cross = f32[928,128]{1,0:T(8,128)S(1)} collective-permute-done((f32[928,128]{1,0:T(8,128)S(1)}, f32[928,128]{1,0:T(8,128)S(1)}, u32[]{:S(2)}, u32[]{:S(2)}) %collective-permute-start.9) | collective-permute-done | bytes 475168 | tf_op jit(solution)/shard_map/ppermute | solution.py:302
  44.3 3.1 %shard_map.78.refs_0_ = f32[2,512]{1,0:T(2,128)S(1)} custom-call(f32[1056,128]{1,0:T(8,128)S(1)} %get-tuple-element.13.own, f32[1056,128]{1,0:T(8,128)S(1)} %collective-permute-done.7.near, f32[928,128]{1,0:T(8,128)S(1)} %collective-permute-done.8.far, f32[928,128]{1,0:T(8,128)S(1)} %collective-permute-done.9.cross, ...), custom_call_target="tpu_custom_call" | custom-call | bytes 100000 | tf_op jit(solution)/shard_map/pallas_call | solution.py:313
  47.4 4.2 %collective-permute-start.15 = (f32[2,512]{1,0:T(2,128)S(1)}, f32[2,512]{1,0:T(2,128)S(1)}, u32[]{:S(2)}, u32[]{:S(2)}) collective-permute-start(f32[2,512]{1,0:T(2,128)S(1)} %shard_map.78.refs_0_), channel_id=1, source_target_pairs={{0,24},{4,28},{8,16},{12,20},{16,8},{20,12},{24,0},{28,4},{1,25},{... | collective-permute-start | bytes 12296 | tf_op jit(solution)/shard_map/ppermute | solution.py:233
  51.6 0.0 collective-permute-start.13
  51.6 0.6 collective-permute-start.11
  52.2 0.8 %collective-permute-start.10 = (f32[2,512]{1,0:T(2,128)S(1)}, f32[2,512]{1,0:T(2,128)S(1)}, u32[]{:S(2)}, u32[]{:S(2)}) collective-permute-start(f32[2,512]{1,0:T(2,128)S(1)} %shard_map.78.refs_0_), channel_id=1, source_target_pairs={{0,4},{4,0},{8,12},{12,8},{16,20},{20,16},{24,28},{28,24},{1,5},{5... | collective-permute-start | bytes 12296 | tf_op jit(solution)/shard_map/ppermute | solution.py:233
  53.1 0.2 collective-permute-done.15.refs_6_
  53.2 1.0 %collective-permute-start.16 = (f32[2,512]{1,0:T(2,128)S(1)}, f32[2,512]{1,0:T(2,128)S(1)}, u32[]{:S(2)}, u32[]{:S(2)}) collective-permute-start(f32[2,512]{1,0:T(2,128)S(1)} %collective-permute-done.15.refs_6_), channel_id=1, source_target_pairs={{0,4},{4,0},{8,12},{12,8},{16,20},{20,16},{24,28},{28,24},{1,5},{5... | collective-permute-start | bytes 12296 | tf_op jit(solution)/shard_map/ppermute | solution.py:233
  54.3 1.9 %collective-permute-done.13.refs_4_ = f32[2,512]{1,0:T(2,128)S(1)} collective-permute-done((f32[2,512]{1,0:T(2,128)S(1)}, f32[2,512]{1,0:T(2,128)S(1)}, u32[]{:S(2)}, u32[]{:S(2)}) %collective-permute-start.13) | collective-permute-done | bytes 4128 | tf_op jit(solution)/shard_map/ppermute | solution.py:233
  56.1 0.0 collective-permute-start.14
  56.1 0.0 collective-permute-done.11.refs_2_
  56.1 2.0 %collective-permute-start.12 = (f32[2,512]{1,0:T(2,128)S(1)}, f32[2,512]{1,0:T(2,128)S(1)}, u32[]{:S(2)}, u32[]{:S(2)}) collective-permute-start(f32[2,512]{1,0:T(2,128)S(1)} %collective-permute-done.11.refs_2_), channel_id=1, source_target_pairs={{0,4},{4,0},{8,12},{12,8},{16,20},{20,16},{24,28},{28,24},{1,5},{5... | collective-permute-start | bytes 12296 | tf_op jit(solution)/shard_map/ppermute | solution.py:233
  58.2 0.0 collective-permute-done.10.refs_1_
  58.2 0.0 collective-permute-done.16.refs_7_
  58.2 1.6 %collective-permute-done.14.refs_5_ = f32[2,512]{1,0:T(2,128)S(1)} collective-permute-done((f32[2,512]{1,0:T(2,128)S(1)}, f32[2,512]{1,0:T(2,128)S(1)}, u32[]{:S(2)}, u32[]{:S(2)}) %collective-permute-start.14) | collective-permute-done | bytes 4128 | tf_op jit(solution)/shard_map/ppermute | solution.py:233
  59.7 0.0 collective-permute-done.12.refs_3_
  59.8 0.0 all-to-all-done.1.moved
  59.8 1.0 %shard_map.79 = f32[16,2,4096]{2,1,0:T(2,128)} custom-call(f32[8,2,16,512]{3,2,1,0:T(8,128)S(1)} %all-to-all-done.1.moved, f32[2,512]{1,0:T(2,128)S(1)} %shard_map.78.refs_0_, f32[2,512]{1,0:T(2,128)S(1)} %collective-permute-done.10.refs_1_, f32[2,512]{1,0:T(2,128)S(1)} %collective-permute-done.11.refs_2_, f32[2,512]{1,0:T(2,128)S(1)} %collective-permute-done.12.refs_3_, ...), custom_call_target="tpu_custom_call" | custom-call | bytes 1000000 | tf_op jit(solution)/shard_map/pallas_call | solution.py:321
  (11 shorter events, 0.0 us)
Async XLA Ops:
  0.0 8.2 %copy-start = (f32[16,2,4096]{2,1,0:T(2,128)S(1)}, f32[16,2,4096]{2,1,0:T(2,128)}, u32[]{:S(2)}) copy-start(f32[16,2,4096]{2,1,0:T(2,128)} %refs_4_.1) | copy-start | bytes 1572868
  2.5 8.0 %collective-permute-start.2 = (f32[136,128]{1,0:T(8,128)}, f32[136,128]{1,0:T(8,128)S(1)}, u32[]{:S(2)}, u32[]{:S(2)}) collective-permute-start(f32[136,128]{1,0:T(8,128)} %shard_map.75.refs_0_), channel_id=1, source_target_pairs={{0,24},{4,28},{8,16},{12,20},{16,8},{20,12},{24,0},{28,4},{1,25},{... | collective-permute-start | bytes 208904 | tf_op jit(solution)/shard_map/ppermute | solution.py:233
  7.6 6.1 %collective-permute-start.1 = (f32[136,128]{1,0:T(8,128)}, f32[136,128]{1,0:T(8,128)S(1)}, u32[]{:S(2)}, u32[]{:S(2)}) collective-permute-start(f32[136,128]{1,0:T(8,128)} %shard_map.75.refs_0_), channel_id=1, source_target_pairs={{0,16},{4,20},{8,24},{12,28},{16,0},{20,4},{24,8},{28,12},{1,17},{... | collective-permute-start | bytes 208904 | tf_op jit(solution)/shard_map/ppermute | solution.py:233
  7.6 6.1 %collective-permute-start = (f32[136,128]{1,0:T(8,128)}, f32[136,128]{1,0:T(8,128)S(1)}, u32[]{:S(2)}, u32[]{:S(2)}) collective-permute-start(f32[136,128]{1,0:T(8,128)} %shard_map.75.refs_0_), channel_id=1, source_target_pairs={{0,8},{4,12},{8,0},{12,4},{16,24},{20,28},{24,16},{28,20},{1,9},{5... | collective-permute-start | bytes 208904 | tf_op jit(solution)/shard_map/ppermute | solution.py:233
  9.1 9.5 %copy-start.1 = (f32[136,128]{1,0:T(8,128)S(1)}, f32[136,128]{1,0:T(8,128)}, u32[]{:S(2)}) copy-start(f32[136,128]{1,0:T(8,128)} %shard_map.75.refs_0_) | copy-start | bytes 208900
  9.1 13.7 %copy-start.2 = (s32[4,4,64]{2,1,0:T(4,128)S(1)}, s32[4,4,64]{2,1,0:T(4,128)}, u32[]{:S(2)}) copy-start(s32[4,4,64]{2,1,0:T(4,128)} %refs_2_.1) | copy-start | bytes 12292
  9.1 13.7 %copy-start.3 = (s32[4,1,1,128]{3,2,1,0:T(1,128)S(1)}, s32[4,1,1,128]{3,2,1,0:T(1,128)}, u32[]{:S(2)}) copy-start(s32[4,1,1,128]{3,2,1,0:T(1,128)} %param.13) | copy-start | bytes 6148
  9.1 13.7 %copy-start.4 = (s32[4]{0:T(128)S(1)}, s32[4]{0:T(128)}, u32[]{:S(2)}) copy-start(s32[4]{0:T(128)} %owner.3) | copy-start | bytes 52
  9.1 13.7 %copy-start.5 = (f32[4,1,64]{2,1,0:T(1,128)S(1)}, f32[4,1,64]{2,1,0:T(1,128)}, u32[]{:S(2)}) copy-start(f32[4,1,64]{2,1,0:T(1,128)} %values.1) | copy-start | bytes 3076
  9.1 13.7 %copy-start.6 = (f32[4,1,64]{2,1,0:T(1,128)S(1)}, f32[4,1,64]{2,1,0:T(1,128)}, u32[]{:S(2)}) copy-start(f32[4,1,64]{2,1,0:T(1,128)} %errors.1) | copy-start | bytes 3076
  13.7 20.0 %all-to-all-start = ((f32[8,2,16,512]{3,2,1,0:T(8,128)}), f32[8,2,16,512]{3,2,1,0:T(8,128)S(1)}, u32[]{:S(2)}, u32[]{:S(2)}) async-start(f32[8,2,16,512]{3,2,1,0:T(8,128)} %shard_map.74), calls=%async_computation | async-start | bytes 1048576 | tf_op jit(solution)/shard_map/all_to_all | solution.py:283
  18.7 9.0 %collective-permute-start.3 = (f32[136,128]{1,0:T(8,128)S(1)}, f32[136,128]{1,0:T(8,128)S(1)}, u32[]{:S(2)}, u32[]{:S(2)}) collective-permute-start(f32[136,128]{1,0:T(8,128)S(1)} %copy-done.1), channel_id=1, source_target_pairs={{0,4},{4,0},{8,12},{12,8},{16,20},{20,16},{24,28},{28,24},{1,5},{5... | collective-permute-start | bytes 208904 | tf_op jit(solution)/shard_map/ppermute | solution.py:233
  20.7 8.4 %collective-permute-start.6 = (f32[136,128]{1,0:T(8,128)S(1)}, f32[136,128]{1,0:T(8,128)S(1)}, u32[]{:S(2)}, u32[]{:S(2)}) collective-permute-start(f32[136,128]{1,0:T(8,128)S(1)} %collective-permute-done.2.refs_6_), channel_id=1, source_target_pairs={{0,4},{4,0},{8,12},{12,8},{16,20},{20,16},{24,28},{28,24},{1,5},{5... | collective-permute-start | bytes 208904 | tf_op jit(solution)/shard_map/ppermute | solution.py:233
  20.8 9.8 %collective-permute-start.5 = (f32[136,128]{1,0:T(8,128)S(1)}, f32[136,128]{1,0:T(8,128)S(1)}, u32[]{:S(2)}, u32[]{:S(2)}) collective-permute-start(f32[136,128]{1,0:T(8,128)S(1)} %collective-permute-done.1.refs_4_), channel_id=1, source_target_pairs={{0,4},{4,0},{8,12},{12,8},{16,20},{20,16},{24,28},{28,24},{1,5},{5... | collective-permute-start | bytes 208904 | tf_op jit(solution)/shard_map/ppermute | solution.py:233
  22.7 8.5 %collective-permute-start.4 = (f32[136,128]{1,0:T(8,128)S(1)}, f32[136,128]{1,0:T(8,128)S(1)}, u32[]{:S(2)}, u32[]{:S(2)}) collective-permute-start(f32[136,128]{1,0:T(8,128)S(1)} %collective-permute-done.refs_2_), channel_id=1, source_target_pairs={{0,4},{4,0},{8,12},{12,8},{16,20},{20,16},{24,28},{28,24},{1,5},{5... | collective-permute-start | bytes 208904 | tf_op jit(solution)/shard_map/ppermute | solution.py:233
  32.1 10.4 %collective-permute-start.8 = (f32[928,128]{1,0:T(8,128)S(1)}, f32[928,128]{1,0:T(8,128)S(1)}, u32[]{:S(2)}, u32[]{:S(2)}) collective-permute-start(f32[928,128]{1,0:T(8,128)S(1)} %get-tuple-element.14), channel_id=1, source_target_pairs={{0,2},{1,3},{2,0},{3,1},{4,6},{5,7},{6,4},{7,5},{8,10},{9,11},{10,... | collective-permute-start | bytes 1425416 | tf_op jit(solution)/shard_map/ppermute | solution.py:300
  35.0 24.8 %all-to-all-start.1 = ((f32[8,2,16,512]{3,2,1,0:T(8,128)}), f32[8,2,16,512]{3,2,1,0:T(8,128)S(1)}, u32[]{:S(2)}, u32[]{:S(2)}) async-start(f32[8,2,16,512]{3,2,1,0:T(8,128)} %shard_map.76), calls=%async_computation.1 | async-start | bytes 1048576 | tf_op jit(solution)/shard_map/all_to_all | solution.py:311
  39.6 2.9 %collective-permute-start.7 = (f32[1056,128]{1,0:T(8,128)S(1)}, f32[1056,128]{1,0:T(8,128)S(1)}, u32[]{:S(2)}, u32[]{:S(2)}) collective-permute-start(f32[1056,128]{1,0:T(8,128)S(1)} %get-tuple-element.13.own), channel_id=1, source_target_pairs={{0,1},{1,0},{2,3},{3,2},{4,5},{5,4},{6,7},{7,6},{8,9},{9,8},{10,11... | collective-permute-start | bytes 1622024 | tf_op jit(solution)/shard_map/ppermute | solution.py:301
  42.5 1.8 %collective-permute-start.9 = (f32[928,128]{1,0:T(8,128)S(1)}, f32[928,128]{1,0:T(8,128)S(1)}, u32[]{:S(2)}, u32[]{:S(2)}) collective-permute-start(f32[928,128]{1,0:T(8,128)S(1)} %collective-permute-done.8.far), channel_id=1, source_target_pairs={{0,1},{1,0},{2,3},{3,2},{4,5},{5,4},{6,7},{7,6},{8,9},{9,8},{10,11... | collective-permute-start | bytes 1425416 | tf_op jit(solution)/shard_map/ppermute | solution.py:302
  47.4 5.8 %collective-permute-start.15 = (f32[2,512]{1,0:T(2,128)S(1)}, f32[2,512]{1,0:T(2,128)S(1)}, u32[]{:S(2)}, u32[]{:S(2)}) collective-permute-start(f32[2,512]{1,0:T(2,128)S(1)} %shard_map.78.refs_0_), channel_id=1, source_target_pairs={{0,24},{4,28},{8,16},{12,20},{16,8},{20,12},{24,0},{28,4},{1,25},{... | collective-permute-start | bytes 12296 | tf_op jit(solution)/shard_map/ppermute | solution.py:233
  51.6 4.5 %collective-permute-start.13 = (f32[2,512]{1,0:T(2,128)S(1)}, f32[2,512]{1,0:T(2,128)S(1)}, u32[]{:S(2)}, u32[]{:S(2)}) collective-permute-start(f32[2,512]{1,0:T(2,128)S(1)} %shard_map.78.refs_0_), channel_id=1, source_target_pairs={{0,16},{4,20},{8,24},{12,28},{16,0},{20,4},{24,8},{28,12},{1,17},{... | collective-permute-start | bytes 12296 | tf_op jit(solution)/shard_map/ppermute | solution.py:233
  51.6 4.5 %collective-permute-start.11 = (f32[2,512]{1,0:T(2,128)S(1)}, f32[2,512]{1,0:T(2,128)S(1)}, u32[]{:S(2)}, u32[]{:S(2)}) collective-permute-start(f32[2,512]{1,0:T(2,128)S(1)} %shard_map.78.refs_0_), channel_id=1, source_target_pairs={{0,8},{4,12},{8,0},{12,4},{16,24},{20,28},{24,16},{28,20},{1,9},{5... | collective-permute-start | bytes 12296 | tf_op jit(solution)/shard_map/ppermute | solution.py:233
  52.2 5.9 %collective-permute-start.10 = (f32[2,512]{1,0:T(2,128)S(1)}, f32[2,512]{1,0:T(2,128)S(1)}, u32[]{:S(2)}, u32[]{:S(2)}) collective-permute-start(f32[2,512]{1,0:T(2,128)S(1)} %shard_map.78.refs_0_), channel_id=1, source_target_pairs={{0,4},{4,0},{8,12},{12,8},{16,20},{20,16},{24,28},{28,24},{1,5},{5... | collective-permute-start | bytes 12296 | tf_op jit(solution)/shard_map/ppermute | solution.py:233
  53.2 5.0 %collective-permute-start.16 = (f32[2,512]{1,0:T(2,128)S(1)}, f32[2,512]{1,0:T(2,128)S(1)}, u32[]{:S(2)}, u32[]{:S(2)}) collective-permute-start(f32[2,512]{1,0:T(2,128)S(1)} %collective-permute-done.15.refs_6_), channel_id=1, source_target_pairs={{0,4},{4,0},{8,12},{12,8},{16,20},{20,16},{24,28},{28,24},{1,5},{5... | collective-permute-start | bytes 12296 | tf_op jit(solution)/shard_map/ppermute | solution.py:233
  56.1 3.6 %collective-permute-start.14 = (f32[2,512]{1,0:T(2,128)S(1)}, f32[2,512]{1,0:T(2,128)S(1)}, u32[]{:S(2)}, u32[]{:S(2)}) collective-permute-start(f32[2,512]{1,0:T(2,128)S(1)} %collective-permute-done.13.refs_4_), channel_id=1, source_target_pairs={{0,4},{4,0},{8,12},{12,8},{16,20},{20,16},{24,28},{28,24},{1,5},{5... | collective-permute-start | bytes 12296 | tf_op jit(solution)/shard_map/ppermute | solution.py:233
  56.1 3.6 %collective-permute-start.12 = (f32[2,512]{1,0:T(2,128)S(1)}, f32[2,512]{1,0:T(2,128)S(1)}, u32[]{:S(2)}, u32[]{:S(2)}) collective-permute-start(f32[2,512]{1,0:T(2,128)S(1)} %collective-permute-done.11.refs_2_), channel_id=1, source_target_pairs={{0,4},{4,0},{8,12},{12,8},{16,20},{20,16},{24,28},{28,24},{1,5},{5... | collective-permute-start | bytes 12296 | tf_op jit(solution)/shard_map/ppermute | solution.py:233

commit v8 on v7

--- a/solution.py
+++ b/solution.py
@@ -16,6 +16,8 @@
 PLACE = pl.BlockSpec(memory_space=pl.ANY)
 LIMIT = 48 * 1024 * 1024
 
+PARTS = ((0,), (6, 7), (4,), (5,), (2, 3), (1,))
+ORDER = (0, 6, 4, 5, 2, 1, 3, 7)
 PAIRS = [(e, b) for b in range(1, NB) for e in range(b)]
 PARENT, ALPHA, LATER, VALUE, OWN, SPARE = 0, 6, 12, 18, 22, 32
 
@@ -119,7 +121,7 @@
     steps[NB] = turned.T
 
 
-def turn_kernel(shape, owner, rows, *refs):
+def turn_kernel(shape, owner, rows, ahead, *refs):
     n, slab, width, count = shape
     pieces, out, slim, held = refs[:-3], refs[-3], refs[-2], refs[-1]
     members = n * slab
@@ -148,15 +150,28 @@
         slim[low + PARENT + i : low + PARENT + i + 1, :] = value
 
 
-def mix_kernel(shape, steps, fields, out):
+def mix_kernel(shape, steps, pull, fields, *refs):
     n, slab, depth, block_cells = shape
+    outs, held = refs[:-1], refs[-1]
+    members = n * slab
+    held[...] = (steps[NB] + pull[0:1, :]).reshape(n, slab, members)
+    block = lax.axis_index("grid")
+    if len(outs) == 1:
+        blend = held[...].reshape(members, members)
+    else:
+        blend = jnp.concatenate([held[lax.bitwise_xor(block, i)] for i in range(n)], axis=0)
     for level in range(depth):
-        value = fields[:, level].reshape(n * slab, block_cells)
-        out[:, level] = high_dot(steps[NB], value).reshape(n, slab, block_cells)
-
-
-def chain_kernel(shape, own, near, far, cross, steps, fields, out):
-    members, groups, count, depth, block_cells = shape
+        value = high_dot(blend, fields[:, level].reshape(members, block_cells)).reshape(n, slab, block_cells)
+        if len(outs) == 1:
+            outs[0][:, level] = value
+        else:
+            for out, part in zip(outs, PARTS):
+                for i, distance in enumerate(part):
+                    out[i, level] = value[distance]
+
+
+def chain_kernel(shape, own, near, far, cross, steps, out):
+    members, groups, count = shape
     width = groups * count
     group = lax.axis_index("lev")
     sources = [own, near, far, cross]
@@ -209,24 +224,18 @@
     pull = jnp.zeros((8, members), F32)
     for b in range(NB):
         pull = pull + high_dot(jnp.broadcast_to(pulled[b], (8, members)), steps[b])
-    for level in range(depth):
-        value = fields[:, level].reshape(members, block_cells)
-        out[level : level + 1, :] = high_dot(pull, value)[0:1]
-
-
-def final_kernel(shape, moved, *refs):
+    out[...] = pull
+
+
+def final_kernel(shape, *refs):
     n, slab, depth, block_cells = shape
-    shifts, out = refs[:-1], refs[-1]
+    pieces, out = refs[:-1], refs[-1]
     block = lax.axis_index("grid")
     for i in range(n):
-        region = i if len(shifts) == 1 else lax.bitwise_xor(block, i)
+        region = i if len(pieces) == 1 else lax.bitwise_xor(block, ORDER[i])
         cells = pl.ds(pl.multiple_of(region * block_cells, LANES), block_cells)
         for level in range(depth):
-            if len(shifts) == 1:
-                shift = shifts[0][i, level : level + 1, :]
-            else:
-                shift = shifts[i][level : level + 1, :]
-            out[:, level, cells] = moved[region, level] + shift
+            out[:, level, cells] = pieces[0][i, level] if len(pieces) == 1 else pieces[i][0, level]
 
 
 def hop(value, distance, n):
@@ -242,6 +251,17 @@
     for i in (0, 2, 4, 6):
         pieces[i + 1] = hop(pieces[i], 1, n)
     return [pieces[i] for i in range(n)]
+
+
+def exchange_parts(parts, n):
+    if len(parts) == 1:
+        return [lax.all_to_all(parts[0], "grid", 0, 0, tiled=True)]
+    pieces = {0: parts[0]}
+    for part, distances in zip(parts[1:], PARTS[1:]):
+        pieces[distances[0]] = hop(part, distances[0], n)
+        if len(distances) == 2:
+            pieces[distances[1]] = hop(pieces[distances[0]][1:], 1, n)
+    return [pieces[i] for i in ORDER]
 
 
 def body(prior, channel_weights, obs_owner, obs_offset, obs_value, obs_error, ancestors):
@@ -279,7 +299,6 @@
         [VMEM],
         moved=10**6,
     )(prior)
-    send, *_ = lax.optimization_barrier((send, *pieces[2::2]))
     fields = lax.all_to_all(send, "grid", 0, 0, tiled=True)
 
     rows, steps = call(
@@ -293,37 +312,41 @@
     own, slim = call(
         functools.partial(turn_kernel, (n, slab, width, count)),
         [shape((width + SPARE, members), F32), shape((slim_height, members), F32)],
-        [SMEM, VMEM] + [VMEM] * len(pieces),
+        [SMEM, VMEM, PLACE] + [VMEM] * len(pieces),
         scratch=[pltpu.VMEM((n, tall, LANES), F32)],
         moved=10**6,
-    )(obs_owner, rows, *pieces)
+    )(obs_owner, rows, send, *pieces)
     far = lax.ppermute(slim, "lev", [(j, j ^ 2) for j in range(lev)])
     near = lax.ppermute(own, "lev", [(j, j ^ 1) for j in range(lev)])
     cross = lax.ppermute(far, "lev", [(j, j ^ 1) for j in range(lev)])
 
+    pull = call(
+        functools.partial(chain_kernel, (members, groups, count)),
+        shape((8, members), F32),
+        [VMEM] * 5,
+        moved=10**5,
+    )(own, near, far, cross, steps)
+
+    if n == 8:
+        layout = [shape((len(part), depth, slab, block_cells), F32) for part in PARTS]
+    else:
+        layout = [shape((n, depth, slab, block_cells), F32)]
     send = call(
         functools.partial(mix_kernel, (n, slab, depth, block_cells)),
-        shape((n, depth, slab, block_cells), F32),
-        [VMEM] * 2,
+        layout,
+        [VMEM] * 3,
+        scratch=[pltpu.VMEM((n, slab, members), F32)],
         flops=10**8,
         moved=10**6,
-    )(steps, fields)
-    moved = lax.all_to_all(send, "grid", 0, 0, tiled=True)
-
-    shift = call(
-        functools.partial(chain_kernel, (members, groups, count, depth, block_cells)),
-        shape((depth, block_cells), F32),
-        [VMEM] * 6,
-        moved=10**5,
-    )(own, near, far, cross, steps, fields)
-    shifts = gather_pieces(shift, n)
+    )(steps, pull, fields)
+    moved = exchange_parts(send, n)
 
     return call(
         functools.partial(final_kernel, (n, slab, depth, block_cells)),
         shape((slab, depth, cells), F32),
-        [VMEM] * (1 + len(shifts)),
-        moved=10**6,
-    )(moved, *shifts)
+        [VMEM] * len(moved),
+        moved=10**6,
+    )(*moved)
 
 
 def solution(mesh):

time: 61.1 us -> 53.5 us (0.88)
  waiting for transfers between devices: 20.4 us -> 17 us
  starting transfers between devices: 29.7 us -> 26.7 us
  Pallas kernels: 10.6 us -> 9.36 us
    ppermute x14, waiting for transfers between devices: 15.7 us -> 8.31 us  [hop(): return lax.ppermute(value, 'grid', [(j, j ^ distance) for j in range(n)])]
    all_to_all x1 -> x0, starting transfers between devices: 4.58 us -> none  [body(): moved = lax.all_to_all(send, 'grid', 0, 0, tiled=True)]
    all_to_all x1, waiting for transfers between devices: 0.01 us -> 3.59 us  [body(): fields = lax.all_to_all(send, 'grid', 0, 0, tiled=True)]
    ppermute x14, starting transfers between devices: 18.6 us -> 20.5 us  [hop(): return lax.ppermute(value, 'grid', [(j, j ^ distance) for j in range(n)])]
    pallas_call x2, Pallas kernels: 4.43 us -> 3.3 us  [the longest x1 2.72 us: body(): call(functools.partial(chain_kernel, (members, groups, count)), shape((8,...]
  transfers between devices with their start and end apart: 19 -> 18, of which waited for: 11 -> 7; matrix products, arithmetic and copies ran while one was open for 0% -> 0% of each run, Pallas kernels for 12% -> 9%
where the time goes in v8:
time: 53.5 us; the launch traced here: 53.3 us
  starting transfers between devices  26.7 us (50%)
  waiting for transfers between devices  17 us (32%)
  Pallas kernels  9.36 us (17%)
    ppermute x14, starting transfers between devices, hop(): return lax.ppermute(value, 'grid', [(j, j ^ distance) for j in range(n)])  20.5 us
    ppermute x14, waiting for transfers between devices, hop(): return lax.ppermute(value, 'grid', [(j, j ^ distance) for j in range(n)])  8.31 us
    all_to_all x1, starting transfers between devices, body(): fields = lax.all_to_all(send, 'grid', 0, 0, tiled=True)  4.66 us
    all_to_all x1, waiting for transfers between devices, body(): fields = lax.all_to_all(send, 'grid', 0, 0, tiled=True)  3.59 us
    ppermute x1, waiting for transfers between devices, body(): far = lax.ppermute(slim, 'lev', [(j, j ^ 2) for j in range(lev)])  3.28 us
    pallas_call x1, Pallas kernels, body(): call(functools.partial(chain_kernel, (members, groups, count)), shape((8,...  2.72 us
    pallas_call x1, Pallas kernels, body(): call(functools.partial(pick_kernel, (slab, depth, block_cells, groups, co...  2.46 us
    ppermute x1, waiting for transfers between devices, body(): cross = lax.ppermute(far, 'lev', [(j, j ^ 1) for j in range(lev)])  1.83 us
  transfers between devices with their start and end apart: 18, of which 7 were waited for; matrix products, arithmetic and copies ran while one was open for 0% of the time, Pallas kernels for 9%

profile of v8, /device:TPU:0, one launch (start us, length us, event | category | flops | bytes accessed | tf_op | source)
XLA Modules:
  0.0 53.3 jit_solution(8999473934465454447)
XLA Ops:
  0.0 2.5 %shard_map.75.refs_0_ = f32[136,128]{1,0:T(8,128)} custom-call(s32[4]{0:T(128)} %owner.3, f32[2,4]{1,0:T(2,128)} %refs_1_.1, s32[4,4,64]{2,1,0:T(4,128)} %refs_2_.1, s32[4,1,128]{2,1,0:T(1,128)} %bitcast.1, f32[16,2,4096]{2,1,0:T(2,128)} %refs_4_.1), custom_call_target="tpu_custom_call" | custom-call | bytes 1000000 | tf_op jit(solution)/shard_map/pallas_call | solution.py:280
  2.5 0.0 copy-start.2
  2.5 0.0 copy-start.3
  2.5 0.0 copy-start.4
  2.5 0.0 copy-start.5
  2.5 0.0 copy-start.6
  2.5 3.1 %collective-permute-start.1 = (f32[136,128]{1,0:T(8,128)}, f32[136,128]{1,0:T(8,128)S(1)}, u32[]{:S(2)}, u32[]{:S(2)}) collective-permute-start(f32[136,128]{1,0:T(8,128)} %shard_map.75.refs_0_), channel_id=1, source_target_pairs={{0,8},{4,12},{8,0},{12,4},{16,24},{20,28},{24,16},{28,20},{1,9},{5... | collective-permute-start | bytes 208904 | tf_op jit(solution)/shard_map/ppermute | solution.py:242
  5.6 2.6 %collective-permute-start.3 = (f32[136,128]{1,0:T(8,128)}, f32[136,128]{1,0:T(8,128)S(1)}, u32[]{:S(2)}, u32[]{:S(2)}) collective-permute-start(f32[136,128]{1,0:T(8,128)} %shard_map.75.refs_0_), channel_id=1, source_target_pairs={{0,16},{4,20},{8,24},{12,28},{16,0},{20,4},{24,8},{28,12},{1,17},{... | collective-permute-start | bytes 208904 | tf_op jit(solution)/shard_map/ppermute | solution.py:242
  8.2 0.0 collective-permute-start.5
  8.2 1.7 %collective-permute-start = (f32[136,128]{1,0:T(8,128)}, f32[136,128]{1,0:T(8,128)S(1)}, u32[]{:S(2)}, u32[]{:S(2)}) collective-permute-start(f32[136,128]{1,0:T(8,128)} %shard_map.75.refs_0_), channel_id=1, source_target_pairs={{0,4},{4,0},{8,12},{12,8},{16,20},{20,16},{24,28},{28,24},{1,5},{5... | collective-permute-start | bytes 208904 | tf_op jit(solution)/shard_map/ppermute | solution.py:242
  10.0 0.0 collective-permute-done.1.refs_2_
  10.0 0.3 collective-permute-start.2
  10.2 3.1 %collective-permute-done.3.refs_4_ = f32[136,128]{1,0:T(8,128)S(1)} collective-permute-done((f32[136,128]{1,0:T(8,128)}, f32[136,128]{1,0:T(8,128)S(1)}, u32[]{:S(2)}, u32[]{:S(2)}) %collective-permute-start.3) | collective-permute-done | bytes 69664 | tf_op jit(solution)/shard_map/ppermute | solution.py:242
  13.4 1.5 %collective-permute-start.4 = (f32[136,128]{1,0:T(8,128)S(1)}, f32[136,128]{1,0:T(8,128)S(1)}, u32[]{:S(2)}, u32[]{:S(2)}) collective-permute-start(f32[136,128]{1,0:T(8,128)S(1)} %collective-permute-done.3.refs_4_), channel_id=1, source_target_pairs={{0,4},{4,0},{8,12},{12,8},{16,20},{20,16},{24,28},{28,24},{1,5},{5... | collective-permute-start | bytes 208904 | tf_op jit(solution)/shard_map/ppermute | solution.py:242
  14.9 0.0 collective-permute-done.5.refs_6_
  14.9 1.3 %collective-permute-start.6 = (f32[136,128]{1,0:T(8,128)S(1)}, f32[136,128]{1,0:T(8,128)S(1)}, u32[]{:S(2)}, u32[]{:S(2)}) collective-permute-start(f32[136,128]{1,0:T(8,128)S(1)} %collective-permute-done.5.refs_6_), channel_id=1, source_target_pairs={{0,4},{4,0},{8,12},{12,8},{16,20},{20,16},{24,28},{28,24},{1,5},{5... | collective-permute-start | bytes 208904 | tf_op jit(solution)/shard_map/ppermute | solution.py:242
  16.2 0.9 %shard_map.74.ahead = f32[8,2,16,512]{3,2,1,0:T(8,128)} custom-call(f32[16,2,4096]{2,1,0:T(2,128)S(1)} %copy-done), custom_call_target="tpu_custom_call" | custom-call | bytes 1000000 | tf_op jit(solution)/shard_map/pallas_call | solution.py:296
  17.1 1.0 %shard_map.73 = (f32[32,128]{1,0:T(8,128)S(1)}, f32[5,128,128]{2,1,0:T(8,128)S(1)}) custom-call(s32[4]{0:T(128)S(1)} %copy-done.4, s32[4,4,64]{2,1,0:T(4,128)S(1)} %copy-done.2, f32[4,1,64]{2,1,0:T(1,128)S(1)} %copy-done.5, f32[4,1,64]{2,1,0:T(1,128)S(1)} %copy-done.6, s32[4,1,128]{2,1,0:T(1,128)S(1)} %bitcast.2), custom_call_target="tpu_custom_call" | custom-call | bytes 1000000 | tf_op jit(solution)/shard_map/pallas_call | solution.py:304
  18.1 0.0 collective-permute-done.refs_1_
  18.1 0.0 collective-permute-done.2.refs_3_
  18.1 0.0 collective-permute-done.4.refs_5_
  18.1 1.1 %collective-permute-done.6.refs_7_ = f32[136,128]{1,0:T(8,128)S(1)} collective-permute-done((f32[136,128]{1,0:T(8,128)S(1)}, f32[136,128]{1,0:T(8,128)S(1)}, u32[]{:S(2)}, u32[]{:S(2)}) %collective-permute-start.6) | collective-permute-done | bytes 69664 | tf_op jit(solution)/shard_map/ppermute | solution.py:242
  19.2 0.8 %shard_map.76 = (f32[1056,128]{1,0:T(8,128)S(1)}, f32[928,128]{1,0:T(8,128)S(1)}) custom-call(s32[4]{0:T(128)S(1)} %copy-done.4, f32[32,128]{1,0:T(8,128)S(1)} %get-tuple-element.16.rows, f32[8,2,16,512]{3,2,1,0:T(8,128)} %shard_map.74.ahead, f32[136,128]{1,0:T(8,128)S(1)} %copy-done.1, f32[136,128]{1,0:T(8,128)S(1)} %collective-permute-done.refs_1_, ...), custom_call_target="tpu_custom_call" | custom-call | bytes 1000000 | tf_op jit(solution)/shard_map/pallas_call | solution.py:312
  20.0 1.6 %collective-permute-start.8 = (f32[928,128]{1,0:T(8,128)S(1)}, f32[928,128]{1,0:T(8,128)S(1)}, u32[]{:S(2)}, u32[]{:S(2)}) collective-permute-start(f32[928,128]{1,0:T(8,128)S(1)} %get-tuple-element.18), channel_id=1, source_target_pairs={{0,2},{1,3},{2,0},{3,1},{4,6},{5,7},{6,4},{7,5},{8,10},{9,11},{10,... | collective-permute-start | bytes 1425416 | tf_op jit(solution)/shard_map/ppermute | solution.py:319
  21.6 4.7 %all-to-all-start = ((f32[8,2,16,512]{3,2,1,0:T(8,128)}), f32[8,2,16,512]{3,2,1,0:T(8,128)S(1)}, u32[]{:S(2)}, u32[]{:S(2)}) async-start(f32[8,2,16,512]{3,2,1,0:T(8,128)} %shard_map.74.ahead), calls=%async_computation | async-start | bytes 1048576 | tf_op jit(solution)/shard_map/all_to_all | solution.py:302
  26.2 0.0 collective-permute-start.7
  26.2 3.3 %collective-permute-done.8.far = f32[928,128]{1,0:T(8,128)S(1)} collective-permute-done((f32[928,128]{1,0:T(8,128)S(1)}, f32[928,128]{1,0:T(8,128)S(1)}, u32[]{:S(2)}, u32[]{:S(2)}) %collective-permute-start.8) | collective-permute-done | bytes 475168 | tf_op jit(solution)/shard_map/ppermute | solution.py:319
  29.5 0.0 collective-permute-start.9
  29.5 0.0 collective-permute-done.7.near
  29.5 1.8 %collective-permute-done.9.cross = f32[928,128]{1,0:T(8,128)S(1)} collective-permute-done((f32[928,128]{1,0:T(8,128)S(1)}, f32[928,128]{1,0:T(8,128)S(1)}, u32[]{:S(2)}, u32[]{:S(2)}) %collective-permute-start.9) | collective-permute-done | bytes 475168 | tf_op jit(solution)/shard_map/ppermute | solution.py:321
  31.4 2.7 %shard_map.77.pull = f32[8,128]{1,0:T(8,128)S(1)} custom-call(f32[1056,128]{1,0:T(8,128)S(1)} %get-tuple-element.17.own, f32[1056,128]{1,0:T(8,128)S(1)} %collective-permute-done.7.near, f32[928,128]{1,0:T(8,128)S(1)} %collective-permute-done.8.far, f32[928,128]{1,0:T(8,128)S(1)} %collective-permute-done.9.cross, f32[5,128,128]{2,1,0:T(8,128)S(1)} %get-tuple-element.15.steps), custom_call_target="tpu_custom_call" | custom-call | bytes 100000 | tf_op jit(solution)/shard_map/pallas_call | solution.py:323
  34.1 3.6 %all-to-all-done.fields = f32[8,2,16,512]{3,2,1,0:T(8,128)S(1)} async-done(((f32[8,2,16,512]{3,2,1,0:T(8,128)}), f32[8,2,16,512]{3,2,1,0:T(8,128)S(1)}, u32[]{:S(2)}, u32[]{:S(2)}) %all-to-all-start) | async-done | bytes 524320 | tf_op jit(solution)/shard_map/all_to_all | solution.py:302
  37.7 0.6 %shard_map.78 = (f32[1,2,16,512]{3,2,1,0:T(8,128)S(1)}, f32[2,2,16,512]{3,2,1,0:T(8,128)S(1)}, f32[1,2,16,512]{3,2,1,0:T(8,128)S(1)}, f32[1,2,16,512]{3,2,1,0:T(...) custom-call(f32[5,128,128]{2,1,0:T(8,128)S(1)} %get-tuple-element.15.steps, ...), custom_call_target="tpu_custom_call" | custom-call | flops 100000000 | bytes 1000000 | tf_op jit(solution)/shard_map/pallas_call | solution.py:334
  38.3 0.8 %collective-permute-start.13 = (f32[2,2,16,512]{3,2,1,0:T(8,128)S(1)}, f32[2,2,16,512]{3,2,1,0:T(8,128)S(1)}, u32[]{:S(2)}, u32[]{:S(2)}) collective-permute-start(f32[2,2,16,512]{3,2,1,0:T(8,128)S(1)} %get-tuple-element.23), channel_id=1, source_target_pairs={{0,8},{4,12},{8,0},{12,4},{16,24},{20,28},{24,16},{28,20},{1,9},{5... | collective-permute-start | bytes 393224 | tf_op jit(solution)/shard_map/ppermute | solution.py:242
  39.1 1.5 %collective-permute-start.10 = (f32[2,2,16,512]{3,2,1,0:T(8,128)S(1)}, f32[2,2,16,512]{3,2,1,0:T(8,128)S(1)}, u32[]{:S(2)}, u32[]{:S(2)}) collective-permute-start(f32[2,2,16,512]{3,2,1,0:T(8,128)S(1)} %get-tuple-element.20), channel_id=1, source_target_pairs={{0,24},{4,28},{8,16},{12,20},{16,8},{20,12},{24,0},{28,4},{1,25},{... | collective-permute-start | bytes 393224 | tf_op jit(solution)/shard_map/ppermute | solution.py:242
  40.6 1.2 %collective-permute-start.11 = (f32[1,2,16,512]{3,2,1,0:T(8,128)S(1)}, f32[1,2,16,512]{3,2,1,0:T(8,128)S(1)}, u32[]{:S(2)}, u32[]{:S(2)}) collective-permute-start(f32[1,2,16,512]{3,2,1,0:T(8,128)S(1)} %get-tuple-element.21), channel_id=1, source_target_pairs={{0,16},{4,20},{8,24},{12,28},{16,0},{20,4},{24,8},{28,12},{1,17},{... | collective-permute-start | bytes 196616 | tf_op jit(solution)/shard_map/ppermute | solution.py:242
  41.8 1.9 %collective-permute-start.12 = (f32[1,2,16,512]{3,2,1,0:T(8,128)S(1)}, f32[1,2,16,512]{3,2,1,0:T(8,128)S(1)}, u32[]{:S(2)}, u32[]{:S(2)}) collective-permute-start(f32[1,2,16,512]{3,2,1,0:T(8,128)S(1)} %get-tuple-element.22), channel_id=1, source_target_pairs={{0,20},{4,16},{8,28},{12,24},{16,4},{20,0},{24,12},{28,8},{1,21},{... | collective-permute-start | bytes 196616 | tf_op jit(solution)/shard_map/ppermute | solution.py:242
  43.7 1.2 %collective-permute-start.14 = (f32[1,2,16,512]{3,2,1,0:T(8,128)S(1)}, f32[1,2,16,512]{3,2,1,0:T(8,128)S(1)}, u32[]{:S(2)}, u32[]{:S(2)}) collective-permute-start(f32[1,2,16,512]{3,2,1,0:T(8,128)S(1)} %get-tuple-element.24), channel_id=1, source_target_pairs={{0,4},{4,0},{8,12},{12,8},{16,20},{20,16},{24,28},{28,24},{1,5},{5... | collective-permute-start | bytes 196616 | tf_op jit(solution)/shard_map/ppermute | solution.py:242
  45.0 0.0 collective-permute-done.13.refs_4_
  45.0 2.3 %collective-permute-start.15 = (f32[1,2,16,512]{3,2,1,0:T(8,128)S(1)}, f32[1,2,16,512]{3,2,1,0:T(8,128)S(1)}, u32[]{:S(2)}, u32[]{:S(2)}) collective-permute-start(f32[1,2,16,512]{3,2,1,0:T(8,128)S(1)} %slice.8), channel_id=1, source_target_pairs={{0,4},{4,0},{8,12},{12,8},{16,20},{20,16},{24,28},{28,24},{1,5},{5... | collective-permute-start | bytes 196616 | tf_op jit(solution)/shard_map/ppermute | solution.py:242
  47.3 0.0 collective-permute-done.10.refs_1_
  47.3 1.0 %collective-permute-start.16 = (f32[1,2,16,512]{3,2,1,0:T(8,128)S(1)}, f32[1,2,16,512]{3,2,1,0:T(8,128)S(1)}, u32[]{:S(2)}, u32[]{:S(2)}) collective-permute-start(f32[1,2,16,512]{3,2,1,0:T(8,128)S(1)} %slice.9), channel_id=1, source_target_pairs={{0,4},{4,0},{8,12},{12,8},{16,20},{20,16},{24,28},{28,24},{1,5},{5... | collective-permute-start | bytes 196616 | tf_op jit(solution)/shard_map/ppermute | solution.py:242
  48.3 2.0 %collective-permute-done.11.refs_2_ = f32[1,2,16,512]{3,2,1,0:T(8,128)S(1)} collective-permute-done((f32[1,2,16,512]{3,2,1,0:T(8,128)S(1)}, f32[1,2,16,512]{3,2,1,0:T(8,128)S(1)}, u32[]{:S(2)}, u32[]{:S(2)}) %collective-permute-start.11) | collective-permute-done | bytes 65568 | tf_op jit(solution)/shard_map/ppermute | solution.py:242
  50.3 2.1 %collective-permute-done.12.refs_3_ = f32[1,2,16,512]{3,2,1,0:T(8,128)S(1)} collective-permute-done((f32[1,2,16,512]{3,2,1,0:T(8,128)S(1)}, f32[1,2,16,512]{3,2,1,0:T(8,128)S(1)}, u32[]{:S(2)}, u32[]{:S(2)}) %collective-permute-start.12) | collective-permute-done | bytes 65568 | tf_op jit(solution)/shard_map/ppermute | solution.py:242
  52.3 0.0 collective-permute-done.14.refs_5_
  52.3 0.0 collective-permute-done.15.refs_6_
  52.3 0.0 collective-permute-done.16.refs_7_
  52.4 0.9 %shard_map.79 = f32[16,2,4096]{2,1,0:T(2,128)} custom-call(f32[1,2,16,512]{3,2,1,0:T(8,128)S(1)} %get-tuple-element.19.refs_0_, f32[2,2,16,512]{3,2,1,0:T(8,128)S(1)} %collective-permute-done.10.refs_1_, f32[1,2,16,512]{3,2,1,0:T(8,128)S(1)} %collective-permute-done.11.refs_2_, f32[1,2,16,512]{3,2,1,0:T(8,128)S(1)} %collective-permute-done.12.refs_3_, ...), custom_call_target="tpu_custom_call" | custom-call | bytes 1000000 | tf_op jit(solution)/shard_map/pallas_call | solution.py:344
  (11 shorter events, 0.0 us)
Async XLA Ops:
  0.0 16.2 %copy-start = (f32[16,2,4096]{2,1,0:T(2,128)S(1)}, f32[16,2,4096]{2,1,0:T(2,128)}, u32[]{:S(2)}) copy-start(f32[16,2,4096]{2,1,0:T(2,128)} %refs_4_.1) | copy-start | bytes 1572868
  2.5 14.6 %copy-start.2 = (s32[4,4,64]{2,1,0:T(4,128)S(1)}, s32[4,4,64]{2,1,0:T(4,128)}, u32[]{:S(2)}) copy-start(s32[4,4,64]{2,1,0:T(4,128)} %refs_2_.1) | copy-start | bytes 12292
  2.5 14.6 %copy-start.3 = (s32[4,1,1,128]{3,2,1,0:T(1,128)S(1)}, s32[4,1,1,128]{3,2,1,0:T(1,128)}, u32[]{:S(2)}) copy-start(s32[4,1,1,128]{3,2,1,0:T(1,128)} %param.13) | copy-start | bytes 6148
  2.5 14.6 %copy-start.4 = (s32[4]{0:T(128)S(1)}, s32[4]{0:T(128)}, u32[]{:S(2)}) copy-start(s32[4]{0:T(128)} %owner.3) | copy-start | bytes 52
  2.5 14.6 %copy-start.5 = (f32[4,1,64]{2,1,0:T(1,128)S(1)}, f32[4,1,64]{2,1,0:T(1,128)}, u32[]{:S(2)}) copy-start(f32[4,1,64]{2,1,0:T(1,128)} %values.1) | copy-start | bytes 3076
  2.5 14.6 %copy-start.6 = (f32[4,1,64]{2,1,0:T(1,128)S(1)}, f32[4,1,64]{2,1,0:T(1,128)}, u32[]{:S(2)}) copy-start(f32[4,1,64]{2,1,0:T(1,128)} %errors.1) | copy-start | bytes 3076
  2.5 16.7 %copy-start.1 = (f32[136,128]{1,0:T(8,128)S(1)}, f32[136,128]{1,0:T(8,128)}, u32[]{:S(2)}) copy-start(f32[136,128]{1,0:T(8,128)} %shard_map.75.refs_0_) | copy-start | bytes 208900
  2.5 7.4 %collective-permute-start.1 = (f32[136,128]{1,0:T(8,128)}, f32[136,128]{1,0:T(8,128)S(1)}, u32[]{:S(2)}, u32[]{:S(2)}) collective-permute-start(f32[136,128]{1,0:T(8,128)} %shard_map.75.refs_0_), channel_id=1, source_target_pairs={{0,8},{4,12},{8,0},{12,4},{16,24},{20,28},{24,16},{28,20},{1,9},{5... | collective-permute-start | bytes 208904 | tf_op jit(solution)/shard_map/ppermute | solution.py:242
  5.6 7.8 %collective-permute-start.3 = (f32[136,128]{1,0:T(8,128)}, f32[136,128]{1,0:T(8,128)S(1)}, u32[]{:S(2)}, u32[]{:S(2)}) collective-permute-start(f32[136,128]{1,0:T(8,128)} %shard_map.75.refs_0_), channel_id=1, source_target_pairs={{0,16},{4,20},{8,24},{12,28},{16,0},{20,4},{24,8},{28,12},{1,17},{... | collective-permute-start | bytes 208904 | tf_op jit(solution)/shard_map/ppermute | solution.py:242
  8.2 6.7 %collective-permute-start.5 = (f32[136,128]{1,0:T(8,128)}, f32[136,128]{1,0:T(8,128)S(1)}, u32[]{:S(2)}, u32[]{:S(2)}) collective-permute-start(f32[136,128]{1,0:T(8,128)} %shard_map.75.refs_0_), channel_id=1, source_target_pairs={{0,24},{4,28},{8,16},{12,20},{16,8},{20,12},{24,0},{28,4},{1,25},{... | collective-permute-start | bytes 208904 | tf_op jit(solution)/shard_map/ppermute | solution.py:242
  8.2 9.9 %collective-permute-start = (f32[136,128]{1,0:T(8,128)}, f32[136,128]{1,0:T(8,128)S(1)}, u32[]{:S(2)}, u32[]{:S(2)}) collective-permute-start(f32[136,128]{1,0:T(8,128)} %shard_map.75.refs_0_), channel_id=1, source_target_pairs={{0,4},{4,0},{8,12},{12,8},{16,20},{20,16},{24,28},{28,24},{1,5},{5... | collective-permute-start | bytes 208904 | tf_op jit(solution)/shard_map/ppermute | solution.py:242
  10.0 8.1 %collective-permute-start.2 = (f32[136,128]{1,0:T(8,128)S(1)}, f32[136,128]{1,0:T(8,128)S(1)}, u32[]{:S(2)}, u32[]{:S(2)}) collective-permute-start(f32[136,128]{1,0:T(8,128)S(1)} %collective-permute-done.1.refs_2_), channel_id=1, source_target_pairs={{0,4},{4,0},{8,12},{12,8},{16,20},{20,16},{24,28},{28,24},{1,5},{5... | collective-permute-start | bytes 208904 | tf_op jit(solution)/shard_map/ppermute | solution.py:242
  13.4 4.7 %collective-permute-start.4 = (f32[136,128]{1,0:T(8,128)S(1)}, f32[136,128]{1,0:T(8,128)S(1)}, u32[]{:S(2)}, u32[]{:S(2)}) collective-permute-start(f32[136,128]{1,0:T(8,128)S(1)} %collective-permute-done.3.refs_4_), channel_id=1, source_target_pairs={{0,4},{4,0},{8,12},{12,8},{16,20},{20,16},{24,28},{28,24},{1,5},{5... | collective-permute-start | bytes 208904 | tf_op jit(solution)/shard_map/ppermute | solution.py:242
  14.9 4.3 %collective-permute-start.6 = (f32[136,128]{1,0:T(8,128)S(1)}, f32[136,128]{1,0:T(8,128)S(1)}, u32[]{:S(2)}, u32[]{:S(2)}) collective-permute-start(f32[136,128]{1,0:T(8,128)S(1)} %collective-permute-done.5.refs_6_), channel_id=1, source_target_pairs={{0,4},{4,0},{8,12},{12,8},{16,20},{20,16},{24,28},{28,24},{1,5},{5... | collective-permute-start | bytes 208904 | tf_op jit(solution)/shard_map/ppermute | solution.py:242
  20.0 9.5 %collective-permute-start.8 = (f32[928,128]{1,0:T(8,128)S(1)}, f32[928,128]{1,0:T(8,128)S(1)}, u32[]{:S(2)}, u32[]{:S(2)}) collective-permute-start(f32[928,128]{1,0:T(8,128)S(1)} %get-tuple-element.18), channel_id=1, source_target_pairs={{0,2},{1,3},{2,0},{3,1},{4,6},{5,7},{6,4},{7,5},{8,10},{9,11},{10,... | collective-permute-start | bytes 1425416 | tf_op jit(solution)/shard_map/ppermute | solution.py:319
  21.6 16.1 %all-to-all-start = ((f32[8,2,16,512]{3,2,1,0:T(8,128)}), f32[8,2,16,512]{3,2,1,0:T(8,128)S(1)}, u32[]{:S(2)}, u32[]{:S(2)}) async-start(f32[8,2,16,512]{3,2,1,0:T(8,128)} %shard_map.74.ahead), calls=%async_computation | async-start | bytes 1048576 | tf_op jit(solution)/shard_map/all_to_all | solution.py:302
  26.2 3.3 %collective-permute-start.7 = (f32[1056,128]{1,0:T(8,128)S(1)}, f32[1056,128]{1,0:T(8,128)S(1)}, u32[]{:S(2)}, u32[]{:S(2)}) collective-permute-start(f32[1056,128]{1,0:T(8,128)S(1)} %get-tuple-element.17.own), channel_id=1, source_target_pairs={{0,1},{1,0},{2,3},{3,2},{4,5},{5,4},{6,7},{7,6},{8,9},{9,8},{10,11... | collective-permute-start | bytes 1622024 | tf_op jit(solution)/shard_map/ppermute | solution.py:320
  29.5 1.8 %collective-permute-start.9 = (f32[928,128]{1,0:T(8,128)S(1)}, f32[928,128]{1,0:T(8,128)S(1)}, u32[]{:S(2)}, u32[]{:S(2)}) collective-permute-start(f32[928,128]{1,0:T(8,128)S(1)} %collective-permute-done.8.far), channel_id=1, source_target_pairs={{0,1},{1,0},{2,3},{3,2},{4,5},{5,4},{6,7},{7,6},{8,9},{9,8},{10,11... | collective-permute-start | bytes 1425416 | tf_op jit(solution)/shard_map/ppermute | solution.py:321
  38.3 6.7 %collective-permute-start.13 = (f32[2,2,16,512]{3,2,1,0:T(8,128)S(1)}, f32[2,2,16,512]{3,2,1,0:T(8,128)S(1)}, u32[]{:S(2)}, u32[]{:S(2)}) collective-permute-start(f32[2,2,16,512]{3,2,1,0:T(8,128)S(1)} %get-tuple-element.23), channel_id=1, source_target_pairs={{0,8},{4,12},{8,0},{12,4},{16,24},{20,28},{24,16},{28,20},{1,9},{5... | collective-permute-start | bytes 393224 | tf_op jit(solution)/shard_map/ppermute | solution.py:242
  39.1 8.2 %collective-permute-start.10 = (f32[2,2,16,512]{3,2,1,0:T(8,128)S(1)}, f32[2,2,16,512]{3,2,1,0:T(8,128)S(1)}, u32[]{:S(2)}, u32[]{:S(2)}) collective-permute-start(f32[2,2,16,512]{3,2,1,0:T(8,128)S(1)} %get-tuple-element.20), channel_id=1, source_target_pairs={{0,24},{4,28},{8,16},{12,20},{16,8},{20,12},{24,0},{28,4},{1,25},{... | collective-permute-start | bytes 393224 | tf_op jit(solution)/shard_map/ppermute | solution.py:242
  40.6 9.7 %collective-permute-start.11 = (f32[1,2,16,512]{3,2,1,0:T(8,128)S(1)}, f32[1,2,16,512]{3,2,1,0:T(8,128)S(1)}, u32[]{:S(2)}, u32[]{:S(2)}) collective-permute-start(f32[1,2,16,512]{3,2,1,0:T(8,128)S(1)} %get-tuple-element.21), channel_id=1, source_target_pairs={{0,16},{4,20},{8,24},{12,28},{16,0},{20,4},{24,8},{28,12},{1,17},{... | collective-permute-start | bytes 196616 | tf_op jit(solution)/shard_map/ppermute | solution.py:242
  41.8 10.5 %collective-permute-start.12 = (f32[1,2,16,512]{3,2,1,0:T(8,128)S(1)}, f32[1,2,16,512]{3,2,1,0:T(8,128)S(1)}, u32[]{:S(2)}, u32[]{:S(2)}) collective-permute-start(f32[1,2,16,512]{3,2,1,0:T(8,128)S(1)} %get-tuple-element.22), channel_id=1, source_target_pairs={{0,20},{4,16},{8,28},{12,24},{16,4},{20,0},{24,12},{28,8},{1,21},{... | collective-permute-start | bytes 196616 | tf_op jit(solution)/shard_map/ppermute | solution.py:242
  43.7 8.6 %collective-permute-start.14 = (f32[1,2,16,512]{3,2,1,0:T(8,128)S(1)}, f32[1,2,16,512]{3,2,1,0:T(8,128)S(1)}, u32[]{:S(2)}, u32[]{:S(2)}) collective-permute-start(f32[1,2,16,512]{3,2,1,0:T(8,128)S(1)} %get-tuple-element.24), channel_id=1, source_target_pairs={{0,4},{4,0},{8,12},{12,8},{16,20},{20,16},{24,28},{28,24},{1,5},{5... | collective-permute-start | bytes 196616 | tf_op jit(solution)/shard_map/ppermute | solution.py:242
  45.0 7.4 %collective-permute-start.15 = (f32[1,2,16,512]{3,2,1,0:T(8,128)S(1)}, f32[1,2,16,512]{3,2,1,0:T(8,128)S(1)}, u32[]{:S(2)}, u32[]{:S(2)}) collective-permute-start(f32[1,2,16,512]{3,2,1,0:T(8,128)S(1)} %slice.8), channel_id=1, source_target_pairs={{0,4},{4,0},{8,12},{12,8},{16,20},{20,16},{24,28},{28,24},{1,5},{5... | collective-permute-start | bytes 196616 | tf_op jit(solution)/shard_map/ppermute | solution.py:242
  47.3 5.0 %collective-permute-start.16 = (f32[1,2,16,512]{3,2,1,0:T(8,128)S(1)}, f32[1,2,16,512]{3,2,1,0:T(8,128)S(1)}, u32[]{:S(2)}, u32[]{:S(2)}) collective-permute-start(f32[1,2,16,512]{3,2,1,0:T(8,128)S(1)} %slice.9), channel_id=1, source_target_pairs={{0,4},{4,0},{8,12},{12,8},{16,20},{20,16},{24,28},{28,24},{1,5},{5... | collective-permute-start | bytes 196616 | tf_op jit(solution)/shard_map/ppermute | solution.py:242

commit v9 on v8

--- a/solution.py
+++ b/solution.py
@@ -318,7 +318,8 @@
     )(obs_owner, rows, send, *pieces)
     far = lax.ppermute(slim, "lev", [(j, j ^ 2) for j in range(lev)])
     near = lax.ppermute(own, "lev", [(j, j ^ 1) for j in range(lev)])
-    cross = lax.ppermute(far, "lev", [(j, j ^ 1) for j in range(lev)])
+    passed, fields = lax.optimization_barrier((far, fields))
+    cross = lax.ppermute(passed, "lev", [(j, j ^ 1) for j in range(lev)])
 
     pull = call(
         functools.partial(chain_kernel, (members, groups, count)),

time: 53.5 us -> 69 us (1.29)
  waiting for transfers between devices: 17 us -> 27.3 us
  starting transfers between devices: 26.7 us -> 30 us
  local copies, waits for them, and re-layouts: 0.05 us -> 1.96 us
    ppermute x14, waiting for transfers between devices: 8.31 us -> 17.3 us  [hop(): return lax.ppermute(value, 'grid', [(j, j ^ distance) for j in range(n)])]
    ppermute x1, waiting for transfers between devices: 3.28 us -> 8.16 us  [body(): far = lax.ppermute(slim, 'lev', [(j, j ^ 2) for j in range(lev)])]
    all_to_all x1, waiting for transfers between devices: 3.59 us -> 0.01 us  [body(): fields = lax.all_to_all(send, 'grid', 0, 0, tiled=True)]
    all_to_all x1, starting transfers between devices: 4.66 us -> 7.28 us  [body(): fields = lax.all_to_all(send, 'grid', 0, 0, tiled=True)]
    unnamed x14, local copies, waits for them, and re-layouts: 0.04 us -> 1.95 us
  transfers between devices with their start and end apart: 18 -> 18, of which waited for: 7 -> 10; matrix products, arithmetic and copies ran while one was open for 0% -> 0% of each run, Pallas kernels for 9% -> 6%
where the time goes in v9:
time: 69 us; the launch traced here: 68.7 us
  starting transfers between devices  30 us (43%)
  waiting for transfers between devices  27.3 us (40%)
  Pallas kernels  9.34 us (14%)
  local copies, waits for them, and re-layouts  1.96 us (3%)
    ppermute x14, starting transfers between devices, hop(): return lax.ppermute(value, 'grid', [(j, j ^ distance) for j in range(n)])  21.1 us
    ppermute x14, waiting for transfers between devices, hop(): return lax.ppermute(value, 'grid', [(j, j ^ distance) for j in range(n)])  17.3 us
    ppermute x1, waiting for transfers between devices, body(): far = lax.ppermute(slim, 'lev', [(j, j ^ 2) for j in range(lev)])  8.16 us
    all_to_all x1, starting transfers between devices, body(): fields = lax.all_to_all(send, 'grid', 0, 0, tiled=True)  7.28 us
    pallas_call x1, Pallas kernels, body(): call(functools.partial(chain_kernel, (members, groups, count)), shape((8,...  2.72 us
    pallas_call x1, Pallas kernels, body(): call(functools.partial(pick_kernel, (slab, depth, block_cells, groups, co...  2.42 us
    unnamed x14, local copies, waits for them, and re-layouts  1.95 us
    ppermute x1, waiting for transfers between devices, body(): cross = lax.ppermute(passed, 'lev', [(j, j ^ 1) for j in range(lev)])  1.83 us
  transfers between devices with their start and end apart: 18, of which 10 were waited for; matrix products, arithmetic and copies ran while one was open for 0% of the time, Pallas kernels for 6%

profile of v9, /device:TPU:0, one launch (start us, length us, event | category | flops | bytes accessed | tf_op | source)
XLA Modules:
  0.0 68.7 jit_solution(7022023287295046062)
XLA Ops:
  0.0 1.0 %copy-done = f32[16,2,4096]{2,1,0:T(2,128)S(1)} copy-done((f32[16,2,4096]{2,1,0:T(2,128)S(1)}, f32[16,2,4096]{2,1,0:T(2,128)}, u32[]{:S(2)}) %copy-start) | copy-done | bytes 524312
  1.0 0.9 %shard_map.74.ahead = f32[8,2,16,512]{3,2,1,0:T(8,128)} custom-call(f32[16,2,4096]{2,1,0:T(2,128)S(1)} %copy-done), custom_call_target="tpu_custom_call" | custom-call | bytes 1000000 | tf_op jit(solution)/shard_map/pallas_call | solution.py:296
  1.9 7.3 %all-to-all-start = ((f32[8,2,16,512]{3,2,1,0:T(8,128)}), f32[8,2,16,512]{3,2,1,0:T(8,128)S(1)}, u32[]{:S(2)}, u32[]{:S(2)}) async-start(f32[8,2,16,512]{3,2,1,0:T(8,128)} %shard_map.74.ahead), calls=%async_computation | async-start | bytes 1048576 | tf_op jit(solution)/shard_map/all_to_all | solution.py:302
  9.2 0.0 copy-start.3
  9.2 0.0 copy-start.4
  9.2 0.0 copy-start.5
  9.3 0.0 copy-start.6
  9.3 2.4 %shard_map.75.refs_0_ = f32[136,128]{1,0:T(8,128)} custom-call(s32[4]{0:T(128)} %owner.3, f32[2,4]{1,0:T(2,128)} %refs_1_.1, s32[4,4,64]{2,1,0:T(4,128)} %refs_2_.1, s32[4,1,128]{2,1,0:T(1,128)} %bitcast.1, f32[16,2,4096]{2,1,0:T(2,128)} %refs_4_.1), custom_call_target="tpu_custom_call" | custom-call | bytes 1000000 | tf_op jit(solution)/shard_map/pallas_call | solution.py:280
  11.7 2.1 %collective-permute-start.1 = (f32[136,128]{1,0:T(8,128)}, f32[136,128]{1,0:T(8,128)S(1)}, u32[]{:S(2)}, u32[]{:S(2)}) collective-permute-start(f32[136,128]{1,0:T(8,128)} %shard_map.75.refs_0_), channel_id=1, source_target_pairs={{0,8},{4,12},{8,0},{12,4},{16,24},{20,28},{24,16},{28,20},{1,9},{5... | collective-permute-start | bytes 208904 | tf_op jit(solution)/shard_map/ppermute | solution.py:242
  13.8 2.4 %collective-permute-start.3 = (f32[136,128]{1,0:T(8,128)}, f32[136,128]{1,0:T(8,128)S(1)}, u32[]{:S(2)}, u32[]{:S(2)}) collective-permute-start(f32[136,128]{1,0:T(8,128)} %shard_map.75.refs_0_), channel_id=1, source_target_pairs={{0,16},{4,20},{8,24},{12,28},{16,0},{20,4},{24,8},{28,12},{1,17},{... | collective-permute-start | bytes 208904 | tf_op jit(solution)/shard_map/ppermute | solution.py:242
  16.2 0.1 collective-permute-start.5
  16.2 1.9 %collective-permute-start = (f32[136,128]{1,0:T(8,128)}, f32[136,128]{1,0:T(8,128)S(1)}, u32[]{:S(2)}, u32[]{:S(2)}) collective-permute-start(f32[136,128]{1,0:T(8,128)} %shard_map.75.refs_0_), channel_id=1, source_target_pairs={{0,4},{4,0},{8,12},{12,8},{16,20},{20,16},{24,28},{28,24},{1,5},{5... | collective-permute-start | bytes 208904 | tf_op jit(solution)/shard_map/ppermute | solution.py:242
  18.2 2.4 %collective-permute-done.1.refs_2_ = f32[136,128]{1,0:T(8,128)S(1)} collective-permute-done((f32[136,128]{1,0:T(8,128)}, f32[136,128]{1,0:T(8,128)S(1)}, u32[]{:S(2)}, u32[]{:S(2)}) %collective-permute-start.1) | collective-permute-done | bytes 69664 | tf_op jit(solution)/shard_map/ppermute | solution.py:242
  20.5 2.1 %collective-permute-start.2 = (f32[136,128]{1,0:T(8,128)S(1)}, f32[136,128]{1,0:T(8,128)S(1)}, u32[]{:S(2)}, u32[]{:S(2)}) collective-permute-start(f32[136,128]{1,0:T(8,128)S(1)} %collective-permute-done.1.refs_2_), channel_id=1, source_target_pairs={{0,4},{4,0},{8,12},{12,8},{16,20},{20,16},{24,28},{28,24},{1,5},{5... | collective-permute-start | bytes 208904 | tf_op jit(solution)/shard_map/ppermute | solution.py:242
  22.7 6.2 %collective-permute-done.3.refs_4_ = f32[136,128]{1,0:T(8,128)S(1)} collective-permute-done((f32[136,128]{1,0:T(8,128)}, f32[136,128]{1,0:T(8,128)S(1)}, u32[]{:S(2)}, u32[]{:S(2)}) %collective-permute-start.3) | collective-permute-done | bytes 69664 | tf_op jit(solution)/shard_map/ppermute | solution.py:242
  28.9 1.5 %collective-permute-start.4 = (f32[136,128]{1,0:T(8,128)S(1)}, f32[136,128]{1,0:T(8,128)S(1)}, u32[]{:S(2)}, u32[]{:S(2)}) collective-permute-start(f32[136,128]{1,0:T(8,128)S(1)} %collective-permute-done.3.refs_4_), channel_id=1, source_target_pairs={{0,4},{4,0},{8,12},{12,8},{16,20},{20,16},{24,28},{28,24},{1,5},{5... | collective-permute-start | bytes 208904 | tf_op jit(solution)/shard_map/ppermute | solution.py:242
  30.4 0.0 collective-permute-done.5.refs_6_
  30.4 0.6 collective-permute-start.6
  31.0 1.0 %shard_map.73 = (f32[32,128]{1,0:T(8,128)S(1)}, f32[5,128,128]{2,1,0:T(8,128)S(1)}) custom-call(s32[4]{0:T(128)S(1)} %copy-done.4, s32[4,4,64]{2,1,0:T(4,128)S(1)} %copy-done.2, f32[4,1,64]{2,1,0:T(1,128)S(1)} %copy-done.5, f32[4,1,64]{2,1,0:T(1,128)S(1)} %copy-done.6, s32[4,1,128]{2,1,0:T(1,128)S(1)} %bitcast.2), custom_call_target="tpu_custom_call" | custom-call | bytes 1000000 | tf_op jit(solution)/shard_map/pallas_call | solution.py:304
  32.0 0.0 collective-permute-done.refs_1_
  32.0 0.0 collective-permute-done.2.refs_3_
  32.0 1.2 %collective-permute-done.4.refs_5_ = f32[136,128]{1,0:T(8,128)S(1)} collective-permute-done((f32[136,128]{1,0:T(8,128)S(1)}, f32[136,128]{1,0:T(8,128)S(1)}, u32[]{:S(2)}, u32[]{:S(2)}) %collective-permute-start.4) | collective-permute-done | bytes 69664 | tf_op jit(solution)/shard_map/ppermute | solution.py:242
  33.2 1.5 %collective-permute-done.6.refs_7_ = f32[136,128]{1,0:T(8,128)S(1)} collective-permute-done((f32[136,128]{1,0:T(8,128)S(1)}, f32[136,128]{1,0:T(8,128)S(1)}, u32[]{:S(2)}, u32[]{:S(2)}) %collective-permute-start.6) | collective-permute-done | bytes 69664 | tf_op jit(solution)/shard_map/ppermute | solution.py:242
  34.7 0.9 %copy-done.1 = f32[136,128]{1,0:T(8,128)S(1)} copy-done((f32[136,128]{1,0:T(8,128)S(1)}, f32[136,128]{1,0:T(8,128)}, u32[]{:S(2)}) %copy-start.1) | copy-done | bytes 69656
  35.6 0.8 %shard_map.76 = (f32[1056,128]{1,0:T(8,128)S(1)}, f32[928,128]{1,0:T(8,128)S(1)}) custom-call(s32[4]{0:T(128)S(1)} %copy-done.4, f32[32,128]{1,0:T(8,128)S(1)} %get-tuple-element.18.rows, f32[8,2,16,512]{3,2,1,0:T(8,128)} %shard_map.74.ahead, f32[136,128]{1,0:T(8,128)S(1)} %copy-done.1, f32[136,128]{1,0:T(8,128)S(1)} %collective-permute-done.refs_1_, ...), custom_call_target="tpu_custom_call" | custom-call | bytes 1000000 | tf_op jit(solution)/shard_map/pallas_call | solution.py:312
  36.4 1.6 %collective-permute-start.8 = (f32[928,128]{1,0:T(8,128)S(1)}, f32[928,128]{1,0:T(8,128)S(1)}, u32[]{:S(2)}, u32[]{:S(2)}) collective-permute-start(f32[928,128]{1,0:T(8,128)S(1)} %get-tuple-element.20), channel_id=1, source_target_pairs={{0,2},{1,3},{2,0},{3,1},{4,6},{5,7},{6,4},{7,5},{8,10},{9,11},{10,... | collective-permute-start | bytes 1425416 | tf_op jit(solution)/shard_map/ppermute | solution.py:319
  37.9 0.0 collective-permute-start.7
  37.9 8.2 %collective-permute-done.8.far = f32[928,128]{1,0:T(8,128)S(1)} collective-permute-done((f32[928,128]{1,0:T(8,128)S(1)}, f32[928,128]{1,0:T(8,128)S(1)}, u32[]{:S(2)}, u32[]{:S(2)}) %collective-permute-start.8) | collective-permute-done | bytes 475168 | tf_op jit(solution)/shard_map/ppermute | solution.py:319
  46.1 0.0 all-to-all-done.fields
  46.1 0.0 collective-permute-start.9
  46.1 0.0 collective-permute-done.7.near
  46.1 1.8 %collective-permute-done.9.cross = f32[928,128]{1,0:T(8,128)S(1)} collective-permute-done((f32[928,128]{1,0:T(8,128)S(1)}, f32[928,128]{1,0:T(8,128)S(1)}, u32[]{:S(2)}, u32[]{:S(2)}) %collective-permute-start.9) | collective-permute-done | bytes 475168 | tf_op jit(solution)/shard_map/ppermute | solution.py:322
  48.0 2.7 %shard_map.77.pull = f32[8,128]{1,0:T(8,128)S(1)} custom-call(f32[1056,128]{1,0:T(8,128)S(1)} %get-tuple-element.19.own, f32[1056,128]{1,0:T(8,128)S(1)} %collective-permute-done.7.near, f32[928,128]{1,0:T(8,128)S(1)} %collective-permute-done.8.far, f32[928,128]{1,0:T(8,128)S(1)} %collective-permute-done.9.cross, f32[5,128,128]{2,1,0:T(8,128)S(1)} %get-tuple-element.17.steps), custom_call_target="tpu_custom_call" | custom-call | bytes 100000 | tf_op jit(solution)/shard_map/pallas_call | solution.py:324
  50.7 0.6 shard_map.78
  51.3 0.8 %collective-permute-start.13 = (f32[2,2,16,512]{3,2,1,0:T(8,128)S(1)}, f32[2,2,16,512]{3,2,1,0:T(8,128)S(1)}, u32[]{:S(2)}, u32[]{:S(2)}) collective-permute-start(f32[2,2,16,512]{3,2,1,0:T(8,128)S(1)} %get-tuple-element.27), channel_id=1, source_target_pairs={{0,8},{4,12},{8,0},{12,4},{16,24},{20,28},{24,16},{28,20},{1,9},{5... | collective-permute-start | bytes 393224 | tf_op jit(solution)/shard_map/ppermute | solution.py:242
  52.1 2.9 %collective-permute-start.10 = (f32[2,2,16,512]{3,2,1,0:T(8,128)S(1)}, f32[2,2,16,512]{3,2,1,0:T(8,128)S(1)}, u32[]{:S(2)}, u32[]{:S(2)}) collective-permute-start(f32[2,2,16,512]{3,2,1,0:T(8,128)S(1)} %get-tuple-element.24), channel_id=1, source_target_pairs={{0,24},{4,28},{8,16},{12,20},{16,8},{20,12},{24,0},{28,4},{1,25},{... | collective-permute-start | bytes 393224 | tf_op jit(solution)/shard_map/ppermute | solution.py:242
  55.0 0.2 collective-permute-start.11
  55.1 3.4 %collective-permute-start.12 = (f32[1,2,16,512]{3,2,1,0:T(8,128)S(1)}, f32[1,2,16,512]{3,2,1,0:T(8,128)S(1)}, u32[]{:S(2)}, u32[]{:S(2)}) collective-permute-start(f32[1,2,16,512]{3,2,1,0:T(8,128)S(1)} %get-tuple-element.26), channel_id=1, source_target_pairs={{0,20},{4,16},{8,28},{12,24},{16,4},{20,0},{24,12},{28,8},{1,21},{... | collective-permute-start | bytes 196616 | tf_op jit(solution)/shard_map/ppermute | solution.py:242
  58.5 0.9 %collective-permute-start.14 = (f32[1,2,16,512]{3,2,1,0:T(8,128)S(1)}, f32[1,2,16,512]{3,2,1,0:T(8,128)S(1)}, u32[]{:S(2)}, u32[]{:S(2)}) collective-permute-start(f32[1,2,16,512]{3,2,1,0:T(8,128)S(1)} %get-tuple-element.28), channel_id=1, source_target_pairs={{0,4},{4,0},{8,12},{12,8},{16,20},{20,16},{24,28},{28,24},{1,5},{5... | collective-permute-start | bytes 196616 | tf_op jit(solution)/shard_map/ppermute | solution.py:242
  59.4 1.2 %collective-permute-start.15 = (f32[1,2,16,512]{3,2,1,0:T(8,128)S(1)}, f32[1,2,16,512]{3,2,1,0:T(8,128)S(1)}, u32[]{:S(2)}, u32[]{:S(2)}) collective-permute-start(f32[1,2,16,512]{3,2,1,0:T(8,128)S(1)} %slice.8), channel_id=1, source_target_pairs={{0,4},{4,0},{8,12},{12,8},{16,20},{20,16},{24,28},{28,24},{1,5},{5... | collective-permute-start | bytes 196616 | tf_op jit(solution)/shard_map/ppermute | solution.py:242
  60.6 1.6 %collective-permute-done.10.refs_1_ = f32[2,2,16,512]{3,2,1,0:T(8,128)S(1)} collective-permute-done((f32[2,2,16,512]{3,2,1,0:T(8,128)S(1)}, f32[2,2,16,512]{3,2,1,0:T(8,128)S(1)}, u32[]{:S(2)}, u32[]{:S(2)}) %collective-permute-start.10) | collective-permute-done | bytes 131104 | tf_op jit(solution)/shard_map/ppermute | solution.py:242
  62.2 1.2 %collective-permute-start.16 = (f32[1,2,16,512]{3,2,1,0:T(8,128)S(1)}, f32[1,2,16,512]{3,2,1,0:T(8,128)S(1)}, u32[]{:S(2)}, u32[]{:S(2)}) collective-permute-start(f32[1,2,16,512]{3,2,1,0:T(8,128)S(1)} %slice.9), channel_id=1, source_target_pairs={{0,4},{4,0},{8,12},{12,8},{16,20},{20,16},{24,28},{28,24},{1,5},{5... | collective-permute-start | bytes 196616 | tf_op jit(solution)/shard_map/ppermute | solution.py:242
  63.4 3.0 %collective-permute-done.11.refs_2_ = f32[1,2,16,512]{3,2,1,0:T(8,128)S(1)} collective-permute-done((f32[1,2,16,512]{3,2,1,0:T(8,128)S(1)}, f32[1,2,16,512]{3,2,1,0:T(8,128)S(1)}, u32[]{:S(2)}, u32[]{:S(2)}) %collective-permute-start.11) | collective-permute-done | bytes 65568 | tf_op jit(solution)/shard_map/ppermute | solution.py:242
  66.4 1.2 %collective-permute-done.12.refs_3_ = f32[1,2,16,512]{3,2,1,0:T(8,128)S(1)} collective-permute-done((f32[1,2,16,512]{3,2,1,0:T(8,128)S(1)}, f32[1,2,16,512]{3,2,1,0:T(8,128)S(1)}, u32[]{:S(2)}, u32[]{:S(2)}) %collective-permute-start.12) | collective-permute-done | bytes 65568 | tf_op jit(solution)/shard_map/ppermute | solution.py:242
  67.6 0.0 collective-permute-done.14.refs_5_
  67.6 0.0 collective-permute-done.15.refs_6_
  67.6 0.2 collective-permute-done.16.refs_7_
  67.8 0.9 %shard_map.79 = f32[16,2,4096]{2,1,0:T(2,128)} custom-call(f32[1,2,16,512]{3,2,1,0:T(8,128)S(1)} %get-tuple-element.23.refs_0_, f32[2,2,16,512]{3,2,1,0:T(8,128)S(1)} %collective-permute-done.10.refs_1_, f32[1,2,16,512]{3,2,1,0:T(8,128)S(1)} %collective-permute-done.11.refs_2_, f32[1,2,16,512]{3,2,1,0:T(8,128)S(1)} %collective-permute-done.12.refs_3_, ...), custom_call_target="tpu_custom_call" | custom-call | bytes 1000000 | tf_op jit(solution)/shard_map/pallas_call | solution.py:345
  (11 shorter events, 0.0 us)
Async XLA Ops:
  0.0 1.0 %copy-start = (f32[16,2,4096]{2,1,0:T(2,128)S(1)}, f32[16,2,4096]{2,1,0:T(2,128)}, u32[]{:S(2)}) copy-start(f32[16,2,4096]{2,1,0:T(2,128)} %refs_4_.1) | copy-start | bytes 1572868
  1.9 44.2 %all-to-all-start = ((f32[8,2,16,512]{3,2,1,0:T(8,128)}), f32[8,2,16,512]{3,2,1,0:T(8,128)S(1)}, u32[]{:S(2)}, u32[]{:S(2)}) async-start(f32[8,2,16,512]{3,2,1,0:T(8,128)} %shard_map.74.ahead), calls=%async_computation | async-start | bytes 1048576 | tf_op jit(solution)/shard_map/all_to_all | solution.py:302
  9.2 21.7 %copy-start.2 = (s32[4,4,64]{2,1,0:T(4,128)S(1)}, s32[4,4,64]{2,1,0:T(4,128)}, u32[]{:S(2)}) copy-start(s32[4,4,64]{2,1,0:T(4,128)} %refs_2_.1) | copy-start | bytes 12292
  9.2 21.7 %copy-start.3 = (s32[4,1,1,128]{3,2,1,0:T(1,128)S(1)}, s32[4,1,1,128]{3,2,1,0:T(1,128)}, u32[]{:S(2)}) copy-start(s32[4,1,1,128]{3,2,1,0:T(1,128)} %param.13) | copy-start | bytes 6148
  9.2 21.7 %copy-start.4 = (s32[4]{0:T(128)S(1)}, s32[4]{0:T(128)}, u32[]{:S(2)}) copy-start(s32[4]{0:T(128)} %owner.3) | copy-start | bytes 52
  9.2 21.7 %copy-start.5 = (f32[4,1,64]{2,1,0:T(1,128)S(1)}, f32[4,1,64]{2,1,0:T(1,128)}, u32[]{:S(2)}) copy-start(f32[4,1,64]{2,1,0:T(1,128)} %values.1) | copy-start | bytes 3076
  9.3 21.7 %copy-start.6 = (f32[4,1,64]{2,1,0:T(1,128)S(1)}, f32[4,1,64]{2,1,0:T(1,128)}, u32[]{:S(2)}) copy-start(f32[4,1,64]{2,1,0:T(1,128)} %errors.1) | copy-start | bytes 3076
  11.7 8.8 %collective-permute-start.1 = (f32[136,128]{1,0:T(8,128)}, f32[136,128]{1,0:T(8,128)S(1)}, u32[]{:S(2)}, u32[]{:S(2)}) collective-permute-start(f32[136,128]{1,0:T(8,128)} %shard_map.75.refs_0_), channel_id=1, source_target_pairs={{0,8},{4,12},{8,0},{12,4},{16,24},{20,28},{24,16},{28,20},{1,9},{5... | collective-permute-start | bytes 208904 | tf_op jit(solution)/shard_map/ppermute | solution.py:242
  13.8 15.1 %collective-permute-start.3 = (f32[136,128]{1,0:T(8,128)}, f32[136,128]{1,0:T(8,128)S(1)}, u32[]{:S(2)}, u32[]{:S(2)}) collective-permute-start(f32[136,128]{1,0:T(8,128)} %shard_map.75.refs_0_), channel_id=1, source_target_pairs={{0,16},{4,20},{8,24},{12,28},{16,0},{20,4},{24,8},{28,12},{1,17},{... | collective-permute-start | bytes 208904 | tf_op jit(solution)/shard_map/ppermute | solution.py:242
  16.2 14.2 %collective-permute-start.5 = (f32[136,128]{1,0:T(8,128)}, f32[136,128]{1,0:T(8,128)S(1)}, u32[]{:S(2)}, u32[]{:S(2)}) collective-permute-start(f32[136,128]{1,0:T(8,128)} %shard_map.75.refs_0_), channel_id=1, source_target_pairs={{0,24},{4,28},{8,16},{12,20},{16,8},{20,12},{24,0},{28,4},{1,25},{... | collective-permute-start | bytes 208904 | tf_op jit(solution)/shard_map/ppermute | solution.py:242
  16.2 15.8 %collective-permute-start = (f32[136,128]{1,0:T(8,128)}, f32[136,128]{1,0:T(8,128)S(1)}, u32[]{:S(2)}, u32[]{:S(2)}) collective-permute-start(f32[136,128]{1,0:T(8,128)} %shard_map.75.refs_0_), channel_id=1, source_target_pairs={{0,4},{4,0},{8,12},{12,8},{16,20},{20,16},{24,28},{28,24},{1,5},{5... | collective-permute-start | bytes 208904 | tf_op jit(solution)/shard_map/ppermute | solution.py:242
  20.5 11.5 %collective-permute-start.2 = (f32[136,128]{1,0:T(8,128)S(1)}, f32[136,128]{1,0:T(8,128)S(1)}, u32[]{:S(2)}, u32[]{:S(2)}) collective-permute-start(f32[136,128]{1,0:T(8,128)S(1)} %collective-permute-done.1.refs_2_), channel_id=1, source_target_pairs={{0,4},{4,0},{8,12},{12,8},{16,20},{20,16},{24,28},{28,24},{1,5},{5... | collective-permute-start | bytes 208904 | tf_op jit(solution)/shard_map/ppermute | solution.py:242
  28.9 4.3 %collective-permute-start.4 = (f32[136,128]{1,0:T(8,128)S(1)}, f32[136,128]{1,0:T(8,128)S(1)}, u32[]{:S(2)}, u32[]{:S(2)}) collective-permute-start(f32[136,128]{1,0:T(8,128)S(1)} %collective-permute-done.3.refs_4_), channel_id=1, source_target_pairs={{0,4},{4,0},{8,12},{12,8},{16,20},{20,16},{24,28},{28,24},{1,5},{5... | collective-permute-start | bytes 208904 | tf_op jit(solution)/shard_map/ppermute | solution.py:242
  30.4 4.3 %collective-permute-start.6 = (f32[136,128]{1,0:T(8,128)S(1)}, f32[136,128]{1,0:T(8,128)S(1)}, u32[]{:S(2)}, u32[]{:S(2)}) collective-permute-start(f32[136,128]{1,0:T(8,128)S(1)} %collective-permute-done.5.refs_6_), channel_id=1, source_target_pairs={{0,4},{4,0},{8,12},{12,8},{16,20},{20,16},{24,28},{28,24},{1,5},{5... | collective-permute-start | bytes 208904 | tf_op jit(solution)/shard_map/ppermute | solution.py:242
  34.7 0.9 %copy-start.1 = (f32[136,128]{1,0:T(8,128)S(1)}, f32[136,128]{1,0:T(8,128)}, u32[]{:S(2)}) copy-start(f32[136,128]{1,0:T(8,128)} %shard_map.75.refs_0_) | copy-start | bytes 208900
  36.4 9.7 %collective-permute-start.8 = (f32[928,128]{1,0:T(8,128)S(1)}, f32[928,128]{1,0:T(8,128)S(1)}, u32[]{:S(2)}, u32[]{:S(2)}) collective-permute-start(f32[928,128]{1,0:T(8,128)S(1)} %get-tuple-element.20), channel_id=1, source_target_pairs={{0,2},{1,3},{2,0},{3,1},{4,6},{5,7},{6,4},{7,5},{8,10},{9,11},{10,... | collective-permute-start | bytes 1425416 | tf_op jit(solution)/shard_map/ppermute | solution.py:319
  37.9 8.2 %collective-permute-start.7 = (f32[1056,128]{1,0:T(8,128)S(1)}, f32[1056,128]{1,0:T(8,128)S(1)}, u32[]{:S(2)}, u32[]{:S(2)}) collective-permute-start(f32[1056,128]{1,0:T(8,128)S(1)} %get-tuple-element.19.own), channel_id=1, source_target_pairs={{0,1},{1,0},{2,3},{3,2},{4,5},{5,4},{6,7},{7,6},{8,9},{9,8},{10,11... | collective-permute-start | bytes 1622024 | tf_op jit(solution)/shard_map/ppermute | solution.py:320
  46.1 1.8 %collective-permute-start.9 = (f32[928,128]{1,0:T(8,128)S(1)}, f32[928,128]{1,0:T(8,128)S(1)}, u32[]{:S(2)}, u32[]{:S(2)}) collective-permute-start(f32[928,128]{1,0:T(8,128)S(1)} %collective-permute-done.8.far), channel_id=1, source_target_pairs={{0,1},{1,0},{2,3},{3,2},{4,5},{5,4},{6,7},{7,6},{8,9},{9,8},{10,11... | collective-permute-start | bytes 1425416 | tf_op jit(solution)/shard_map/ppermute | solution.py:322
  51.3 8.1 %collective-permute-start.13 = (f32[2,2,16,512]{3,2,1,0:T(8,128)S(1)}, f32[2,2,16,512]{3,2,1,0:T(8,128)S(1)}, u32[]{:S(2)}, u32[]{:S(2)}) collective-permute-start(f32[2,2,16,512]{3,2,1,0:T(8,128)S(1)} %get-tuple-element.27), channel_id=1, source_target_pairs={{0,8},{4,12},{8,0},{12,4},{16,24},{20,28},{24,16},{28,20},{1,9},{5... | collective-permute-start | bytes 393224 | tf_op jit(solution)/shard_map/ppermute | solution.py:242
  52.1 10.1 %collective-permute-start.10 = (f32[2,2,16,512]{3,2,1,0:T(8,128)S(1)}, f32[2,2,16,512]{3,2,1,0:T(8,128)S(1)}, u32[]{:S(2)}, u32[]{:S(2)}) collective-permute-start(f32[2,2,16,512]{3,2,1,0:T(8,128)S(1)} %get-tuple-element.24), channel_id=1, source_target_pairs={{0,24},{4,28},{8,16},{12,20},{16,8},{20,12},{24,0},{28,4},{1,25},{... | collective-permute-start | bytes 393224 | tf_op jit(solution)/shard_map/ppermute | solution.py:242
  55.0 11.4 %collective-permute-start.11 = (f32[1,2,16,512]{3,2,1,0:T(8,128)S(1)}, f32[1,2,16,512]{3,2,1,0:T(8,128)S(1)}, u32[]{:S(2)}, u32[]{:S(2)}) collective-permute-start(f32[1,2,16,512]{3,2,1,0:T(8,128)S(1)} %get-tuple-element.25), channel_id=1, source_target_pairs={{0,16},{4,20},{8,24},{12,28},{16,0},{20,4},{24,8},{28,12},{1,17},{... | collective-permute-start | bytes 196616 | tf_op jit(solution)/shard_map/ppermute | solution.py:242
  55.1 12.4 %collective-permute-start.12 = (f32[1,2,16,512]{3,2,1,0:T(8,128)S(1)}, f32[1,2,16,512]{3,2,1,0:T(8,128)S(1)}, u32[]{:S(2)}, u32[]{:S(2)}) collective-permute-start(f32[1,2,16,512]{3,2,1,0:T(8,128)S(1)} %get-tuple-element.26), channel_id=1, source_target_pairs={{0,20},{4,16},{8,28},{12,24},{16,4},{20,0},{24,12},{28,8},{1,21},{... | collective-permute-start | bytes 196616 | tf_op jit(solution)/shard_map/ppermute | solution.py:242
  58.5 9.1 %collective-permute-start.14 = (f32[1,2,16,512]{3,2,1,0:T(8,128)S(1)}, f32[1,2,16,512]{3,2,1,0:T(8,128)S(1)}, u32[]{:S(2)}, u32[]{:S(2)}) collective-permute-start(f32[1,2,16,512]{3,2,1,0:T(8,128)S(1)} %get-tuple-element.28), channel_id=1, source_target_pairs={{0,4},{4,0},{8,12},{12,8},{16,20},{20,16},{24,28},{28,24},{1,5},{5... | collective-permute-start | bytes 196616 | tf_op jit(solution)/shard_map/ppermute | solution.py:242
  59.4 8.2 %collective-permute-start.15 = (f32[1,2,16,512]{3,2,1,0:T(8,128)S(1)}, f32[1,2,16,512]{3,2,1,0:T(8,128)S(1)}, u32[]{:S(2)}, u32[]{:S(2)}) collective-permute-start(f32[1,2,16,512]{3,2,1,0:T(8,128)S(1)} %slice.8), channel_id=1, source_target_pairs={{0,4},{4,0},{8,12},{12,8},{16,20},{20,16},{24,28},{28,24},{1,5},{5... | collective-permute-start | bytes 196616 | tf_op jit(solution)/shard_map/ppermute | solution.py:242
  62.2 5.6 %collective-permute-start.16 = (f32[1,2,16,512]{3,2,1,0:T(8,128)S(1)}, f32[1,2,16,512]{3,2,1,0:T(8,128)S(1)}, u32[]{:S(2)}, u32[]{:S(2)}) collective-permute-start(f32[1,2,16,512]{3,2,1,0:T(8,128)S(1)} %slice.9), channel_id=1, source_target_pairs={{0,4},{4,0},{8,12},{12,8},{16,20},{20,16},{24,28},{28,24},{1,5},{5... | collective-permute-start | bytes 196616 | tf_op jit(solution)/shard_map/ppermute | solution.py:242

commit v10 on v8

--- a/solution.py
+++ b/solution.py
@@ -16,8 +16,8 @@
 PLACE = pl.BlockSpec(memory_space=pl.ANY)
 LIMIT = 48 * 1024 * 1024
 
-PARTS = ((0,), (6, 7), (4,), (5,), (2, 3), (1,))
-ORDER = (0, 6, 4, 5, 2, 1, 3, 7)
+PARTS = ((0,), (6, 7), (4,), (5,), (2,), (3,), (1,))
+ORDER = (0, 6, 4, 5, 2, 3, 1, 7)
 PAIRS = [(e, b) for b in range(1, NB) for e in range(b)]
 PARENT, ALPHA, LATER, VALUE, OWN, SPARE = 0, 6, 12, 18, 22, 32
 
@@ -121,28 +121,37 @@
     steps[NB] = turned.T
 
 
-def turn_kernel(shape, owner, rows, ahead, *refs):
-    n, slab, width, count = shape
-    pieces, out, slim, held = refs[:-3], refs[-3], refs[-2], refs[-1]
+def join_kernel(shape, rows, ahead, *refs):
+    tall, out = shape[0], refs[-1]
+    for i, piece in enumerate(refs[:-1]):
+        out[i * tall : (i + 1) * tall, :] = piece[...]
+    out[(len(refs) - 1) * tall :, :] = rows[...]
+
+
+def turn_kernel(shape, owner, *refs):
+    n, slab, width, count, tall = shape
+    gathered, out, slim, held = refs[:-3], refs[-3], refs[-2], refs[-1]
     members = n * slab
     block, group = lax.axis_index("grid"), lax.axis_index("lev")
-    if len(pieces) == 1:
-        held[...] = pieces[0][...]
+    if n == 8:
+        for y, part in enumerate(gathered):
+            for i in range(n // 2):
+                held[lax.bitwise_xor(block, 2 * i + y)] = part[i * tall : (i + 1) * tall, :]
+        rows = gathered[0][n // 2 * tall :, :]
     else:
-        for i, piece in enumerate(pieces):
-            held[lax.bitwise_xor(block, i)] = piece[...]
+        held[...] = gathered[0][...]
+        rows = gathered[1][...]
     common = width // NB * (NB - 1)
     for i in range(width // LANES):
         value = held[:, i * slab : (i + 1) * slab, :].reshape(members, LANES).T
         out[i * LANES : (i + 1) * LANES, :] = value
         if (i + 1) * LANES <= common:
             slim[i * LANES : (i + 1) * LANES, :] = value
-    for i in range(2):
-        start = pl.multiple_of(common + lax.bitwise_xor(group, 2 + i) * count, count)
-        slim[common + i * count : common + (i + 1) * count, :] = out[pl.ds(start, count), :]
-    low = common + 2 * count
-    out[width:, :] = rows[...]
-    slim[low:, :] = rows[...]
+    start = pl.multiple_of(common + lax.bitwise_xor(group, 1) * count, count)
+    slim[common : common + count, :] = out[pl.ds(start, count), :]
+    low = common + count
+    out[width:, :] = rows
+    slim[low:, :] = rows
     line = width // LANES * slab
     for i, (e, b) in enumerate(PAIRS):
         value = held[owner[b], line + e : line + e + 1, :]
@@ -175,7 +184,7 @@
     width = groups * count
     group = lax.axis_index("lev")
     sources = [own, near, far, cross]
-    bases = [NB * width, NB * width, (NB - 1) * width + 2 * count, (NB - 1) * width + 2 * count]
+    bases = [NB * width, (NB - 1) * width + count, NB * width, (NB - 1) * width + count]
     columns = [source[base : base + SPARE, :].T for source, base in zip(sources, bases)]
     parents, alphas = [], []
     for source, base in zip(sources, bases):
@@ -193,8 +202,8 @@
             total = jnp.zeros((count, members), F32)
             tilted = jnp.zeros((count, members), F32)
             for p, source in enumerate(sources):
-                if b == NB - 1 and p > 1:
-                    value = source[b * width + (p - 2) * count : b * width + (p - 1) * count, :]
+                if b == NB - 1 and p % 2 == 1:
+                    value = source[b * width : b * width + count, :]
                 else:
                     value = source[pl.ds(start, count), :]
                 for e in range(b):
@@ -242,17 +251,6 @@
     return lax.ppermute(value, "grid", [(j, j ^ distance) for j in range(n)])
 
 
-def gather_pieces(piece, n):
-    if n != 8:
-        return [lax.all_to_all(jnp.broadcast_to(piece[None], (n,) + piece.shape), "grid", 0, 0, tiled=True)]
-    pieces = {0: piece}
-    for i in (6, 4, 2):
-        pieces[i] = hop(piece, i, n)
-    for i in (0, 2, 4, 6):
-        pieces[i + 1] = hop(pieces[i], 1, n)
-    return [pieces[i] for i in range(n)]
-
-
 def exchange_parts(parts, n):
     if len(parts) == 1:
         return [lax.all_to_all(parts[0], "grid", 0, 0, tiled=True)]
@@ -292,7 +290,7 @@
         moved=10**6,
         limit=None,
     )(obs_owner, channel_weights, obs_offset, parents, prior)
-    pieces = gather_pieces(piece, n)
+
     send = call(
         functools.partial(retile_kernel, (n, slab, depth, block_cells)),
         shape((n, depth, slab, block_cells), F32),
@@ -308,17 +306,38 @@
         moved=10**6,
     )(obs_owner, obs_offset, obs_value, obs_error, parents)
 
-    slim_height = (NB - 1) * groups * count + 2 * count + SPARE
-    own, slim = call(
-        functools.partial(turn_kernel, (n, slab, width, count)),
-        [shape((width + SPARE, members), F32), shape((slim_height, members), F32)],
-        [SMEM, VMEM, PLACE] + [VMEM] * len(pieces),
-        scratch=[pltpu.VMEM((n, tall, LANES), F32)],
-        moved=10**6,
-    )(obs_owner, rows, send, *pieces)
-    far = lax.ppermute(slim, "lev", [(j, j ^ 2) for j in range(lev)])
-    near = lax.ppermute(own, "lev", [(j, j ^ 1) for j in range(lev)])
-    cross = lax.ppermute(far, "lev", [(j, j ^ 1) for j in range(lev)])
+    across = [(j, j ^ 2) for j in range(lev)]
+    beside = [(j, j ^ 1) for j in range(lev)]
+    if n == 8:
+        pieces = [piece] + [hop(piece, i, n) for i in (2, 4, 6)]
+        here = call(
+            functools.partial(join_kernel, (tall,)),
+            shape((len(pieces) * tall + SPARE, LANES), F32),
+            [VMEM, PLACE] + [VMEM] * len(pieces),
+            moved=10**5,
+        )(rows, send, *pieces)
+        gathered = [here, hop(here, 1, n)]
+    else:
+        every = jnp.broadcast_to(piece[None], (n,) + piece.shape)
+        gathered = [lax.all_to_all(every, "grid", 0, 0, tiled=True), rows]
+
+    def turn(parts):
+        return call(
+            functools.partial(turn_kernel, (n, slab, width, count, tall)),
+            [
+                shape((width + SPARE, members), F32),
+                shape((width // NB * (NB - 1) + count + SPARE, members), F32),
+            ],
+            [SMEM] + [VMEM] * len(parts),
+            scratch=[pltpu.VMEM((n, tall, LANES), F32)],
+            moved=10**6,
+        )(obs_owner, *parts)
+
+    arriving = [lax.ppermute(part, "lev", across) for part in gathered]
+    own, slim = turn(gathered)
+    near = lax.ppermute(slim, "lev", beside)
+    far, slim = turn(arriving)
+    cross = lax.ppermute(slim, "lev", beside)
 
     pull = call(
         functools.partial(chain_kernel, (members, groups, count)),

time: 53.5 us -> 59.5 us (1.11)
  waiting for transfers between devices: 17 us -> 22.2 us
  Pallas kernels: 9.36 us -> 10.2 us
    ppermute x14 -> x11, waiting for transfers between devices: 8.31 us -> 14.3 us  [hop(): return lax.ppermute(value, 'grid', [(j, j ^ distance) for j in range(n)])]
    all_to_all x1, waiting for transfers between devices: 3.59 us -> 0.01 us  [body(): fields = lax.all_to_all(send, 'grid', 0, 0, tiled=True)]
    ppermute x3 -> x4, waiting for transfers between devices: 5.11 us -> 7.95 us  [the longest x2 6.18 us: body(): arriving = [lax.ppermute(part, 'lev', across) for part in gathered]]
    ppermute x3 -> x4, starting transfers between devices: 1.56 us -> 3.12 us  [the longest x2 2.98 us: body(): arriving = [lax.ppermute(part, 'lev', across) for part in gathered]]
    ppermute x14 -> x11, starting transfers between devices: 20.5 us -> 19.6 us  [hop(): return lax.ppermute(value, 'grid', [(j, j ^ distance) for j in range(n)])]
    pallas_call x1 -> x3, Pallas kernels: 0.8 us -> 1.61 us  [the longest x2 1.59 us: turn(): call(functools.partial(turn_kernel, (n, slab, width, count, tall)), [shap...]
    all_to_all x1, starting transfers between devices: 4.66 us -> 3.99 us  [body(): fields = lax.all_to_all(send, 'grid', 0, 0, tiled=True)]
  transfers between devices with their start and end apart: 18 -> 16, of which waited for: 7 -> 9; matrix products, arithmetic and copies ran while one was open for 0% -> 0% of each run, Pallas kernels for 9% -> 10%
where the time goes in v10:
time: 59.5 us; the launch traced here: 59.3 us
  starting transfers between devices  26.7 us (45%)
  waiting for transfers between devices  22.2 us (37%)
  Pallas kernels  10.2 us (17%)
    ppermute x11, starting transfers between devices, hop(): return lax.ppermute(value, 'grid', [(j, j ^ distance) for j in range(n)])  19.6 us
    ppermute x11, waiting for transfers between devices, hop(): return lax.ppermute(value, 'grid', [(j, j ^ distance) for j in range(n)])  14.3 us
    ppermute x2, waiting for transfers between devices, body(): arriving = [lax.ppermute(part, 'lev', across) for part in gathered]  6.18 us
    all_to_all x1, starting transfers between devices, body(): fields = lax.all_to_all(send, 'grid', 0, 0, tiled=True)  3.99 us
    ppermute x2, starting transfers between devices, body(): arriving = [lax.ppermute(part, 'lev', across) for part in gathered]  2.98 us
    pallas_call x1, Pallas kernels, body(): call(functools.partial(chain_kernel, (members, groups, count)), shape((8,...  2.72 us
    pallas_call x1, Pallas kernels, body(): call(functools.partial(pick_kernel, (slab, depth, block_cells, groups, co...  2.45 us
    ppermute x1, waiting for transfers between devices, body(): cross = lax.ppermute(slim, 'lev', beside)  1.77 us
  transfers between devices with their start and end apart: 16, of which 9 were waited for; matrix products, arithmetic and copies ran while one was open for 0% of the time, Pallas kernels for 10%

profile of v10, /device:TPU:0, one launch (start us, length us, event | category | flops | bytes accessed | tf_op | source)
XLA Modules:
  0.0 59.3 jit_solution(10790327129315362225)
XLA Ops:
  0.0 2.5 %shard_map.75.refs_0_ = f32[136,128]{1,0:T(8,128)} custom-call(s32[4]{0:T(128)} %owner.5, f32[2,4]{1,0:T(2,128)} %refs_1_.1, s32[4,4,64]{2,1,0:T(4,128)} %refs_2_.1, s32[4,1,128]{2,1,0:T(1,128)} %bitcast.1, f32[16,2,4096]{2,1,0:T(2,128)} %refs_4_.1), custom_call_target="tpu_custom_call" | custom-call | bytes 1000000 | tf_op jit(solution)/shard_map/pallas_call | solution.py:278
  2.5 0.0 copy-start.2
  2.5 0.0 copy-start.3
  2.5 0.0 copy-start.4
  2.5 0.0 copy-start.5
  2.5 0.0 copy-start.6
  2.5 0.0 copy-start.1
  2.5 5.1 %collective-permute-start.2 = (f32[136,128]{1,0:T(8,128)}, f32[136,128]{1,0:T(8,128)S(1)}, u32[]{:S(2)}, u32[]{:S(2)}) collective-permute-start(f32[136,128]{1,0:T(8,128)} %shard_map.75.refs_0_), channel_id=1, source_target_pairs={{0,24},{4,28},{8,16},{12,20},{16,8},{20,12},{24,0},{28,4},{1,25},{... | collective-permute-start | bytes 208904 | tf_op jit(solution)/shard_map/ppermute | solution.py:251
  7.6 0.0 collective-permute-start.1
  7.7 0.6 %collective-permute-start = (f32[136,128]{1,0:T(8,128)}, f32[136,128]{1,0:T(8,128)S(1)}, u32[]{:S(2)}, u32[]{:S(2)}) collective-permute-start(f32[136,128]{1,0:T(8,128)} %shard_map.75.refs_0_), channel_id=1, source_target_pairs={{0,8},{4,12},{8,0},{12,4},{16,24},{20,28},{24,16},{28,20},{1,9},{5... | collective-permute-start | bytes 208904 | tf_op jit(solution)/shard_map/ppermute | solution.py:251
  8.3 0.9 %shard_map.74.ahead = f32[8,2,16,512]{3,2,1,0:T(8,128)} custom-call(f32[16,2,4096]{2,1,0:T(2,128)S(1)} %copy-done), custom_call_target="tpu_custom_call" | custom-call | bytes 1000000 | tf_op jit(solution)/shard_map/pallas_call | solution.py:294
  9.2 0.0 copy-done.2
  9.2 0.0 copy-done.6
  9.2 1.0 %shard_map.73 = (f32[32,128]{1,0:T(8,128)S(1)}, f32[5,128,128]{2,1,0:T(8,128)S(1)}) custom-call(s32[4]{0:T(128)S(1)} %copy-done.4, s32[4,4,64]{2,1,0:T(4,128)S(1)} %copy-done.2, f32[4,1,64]{2,1,0:T(1,128)S(1)} %copy-done.5, f32[4,1,64]{2,1,0:T(1,128)S(1)} %copy-done.6, s32[4,1,128]{2,1,0:T(1,128)S(1)} %bitcast.2), custom_call_target="tpu_custom_call" | custom-call | bytes 1000000 | tf_op jit(solution)/shard_map/pallas_call | solution.py:302
  10.2 0.3 collective-permute-done.2.refs_3_
  10.6 3.2 %collective-permute-done.1.refs_2_ = f32[136,128]{1,0:T(8,128)S(1)} collective-permute-done((f32[136,128]{1,0:T(8,128)}, f32[136,128]{1,0:T(8,128)S(1)}, u32[]{:S(2)}, u32[]{:S(2)}) %collective-permute-start.1) | collective-permute-done | bytes 69664 | tf_op jit(solution)/shard_map/ppermute | solution.py:251
  13.8 0.0 collective-permute-done.refs_1_
  13.8 1.6 %collective-permute-start.3 = (f32[576,128]{1,0:T(8,128)S(1)}, f32[576,128]{1,0:T(8,128)S(1)}, u32[]{:S(2)}, u32[]{:S(2)}) collective-permute-start(f32[576,128]{1,0:T(8,128)S(1)} %shard_map.76.refs_0_), channel_id=1, source_target_pairs={{0,4},{4,0},{8,12},{12,8},{16,20},{20,16},{24,28},{28,24},{1,5},{5... | collective-permute-start | bytes 884744 | tf_op jit(solution)/shard_map/ppermute | solution.py:251
  15.4 4.0 %all-to-all-start = ((f32[8,2,16,512]{3,2,1,0:T(8,128)}), f32[8,2,16,512]{3,2,1,0:T(8,128)S(1)}, u32[]{:S(2)}, u32[]{:S(2)}) async-start(f32[8,2,16,512]{3,2,1,0:T(8,128)} %shard_map.74.ahead), calls=%async_computation | async-start | bytes 1048576 | tf_op jit(solution)/shard_map/all_to_all | solution.py:300
  19.4 1.5 %collective-permute-start.5 = (f32[576,128]{1,0:T(8,128)S(1)}, f32[576,128]{1,0:T(8,128)S(1)}, u32[]{:S(2)}, u32[]{:S(2)}) collective-permute-start(f32[576,128]{1,0:T(8,128)S(1)} %shard_map.76.refs_0_), channel_id=1, source_target_pairs={{0,2},{1,3},{2,0},{3,1},{4,6},{5,7},{6,4},{7,5},{8,10},{9,11},{10,... | collective-permute-start | bytes 884744 | tf_op jit(solution)/shard_map/ppermute | solution.py:336
  20.9 4.3 %collective-permute-done.3.refs_1_ = f32[576,128]{1,0:T(8,128)S(1)} collective-permute-done((f32[576,128]{1,0:T(8,128)S(1)}, f32[576,128]{1,0:T(8,128)S(1)}, u32[]{:S(2)}, u32[]{:S(2)}) %collective-permute-start.3) | collective-permute-done | bytes 294944 | tf_op jit(solution)/shard_map/ppermute | solution.py:251
  25.2 1.5 %collective-permute-start.6 = (f32[576,128]{1,0:T(8,128)S(1)}, f32[576,128]{1,0:T(8,128)S(1)}, u32[]{:S(2)}, u32[]{:S(2)}) collective-permute-start(f32[576,128]{1,0:T(8,128)S(1)} %collective-permute-done.3.refs_1_), channel_id=1, source_target_pairs={{0,2},{1,3},{2,0},{3,1},{4,6},{5,7},{6,4},{7,5},{8,10},{9,11},{10,... | collective-permute-start | bytes 884744 | tf_op jit(solution)/shard_map/ppermute | solution.py:336
  26.7 0.8 %shard_map.77 = (f32[1056,128]{1,0:T(8,128)S(1)}, f32[864,128]{1,0:T(8,128)S(1)}) custom-call(s32[4]{0:T(128)S(1)} %copy-done.4, f32[576,128]{1,0:T(8,128)S(1)} %shard_map.76.refs_0_, f32[576,128]{1,0:T(8,128)S(1)} %collective-permute-done.3.refs_1_), custom_call_target="tpu_custom_call" | custom-call | bytes 1000000 | tf_op jit(solution)/shard_map/pallas_call | solution.py:325
  27.5 0.1 collective-permute-start.4
  27.5 1.8 %collective-permute-done.5.refs_0_ = f32[576,128]{1,0:T(8,128)S(1)} collective-permute-done((f32[576,128]{1,0:T(8,128)S(1)}, f32[576,128]{1,0:T(8,128)S(1)}, u32[]{:S(2)}, u32[]{:S(2)}) %collective-permute-start.5) | collective-permute-done | bytes 294944 | tf_op jit(solution)/shard_map/ppermute | solution.py:336
  29.3 4.4 %collective-permute-done.6.refs_1_ = f32[576,128]{1,0:T(8,128)S(1)} collective-permute-done((f32[576,128]{1,0:T(8,128)S(1)}, f32[576,128]{1,0:T(8,128)S(1)}, u32[]{:S(2)}, u32[]{:S(2)}) %collective-permute-start.6) | collective-permute-done | bytes 294944 | tf_op jit(solution)/shard_map/ppermute | solution.py:336
  33.7 0.8 %shard_map.78 = (f32[1056,128]{1,0:T(8,128)S(1)}, f32[864,128]{1,0:T(8,128)S(1)}) custom-call(s32[4]{0:T(128)S(1)} %copy-done.4, f32[576,128]{1,0:T(8,128)S(1)} %collective-permute-done.5.refs_0_, f32[576,128]{1,0:T(8,128)S(1)} %collective-permute-done.6.refs_1_), custom_call_target="tpu_custom_call" | custom-call | bytes 1000000 | tf_op jit(solution)/shard_map/pallas_call | solution.py:325
  34.5 0.1 collective-permute-start.7
  34.6 0.0 collective-permute-done.4.near
  34.6 1.8 %collective-permute-done.7.cross = f32[864,128]{1,0:T(8,128)S(1)} collective-permute-done((f32[864,128]{1,0:T(8,128)S(1)}, f32[864,128]{1,0:T(8,128)S(1)}, u32[]{:S(2)}, u32[]{:S(2)}) %collective-permute-start.7) | collective-permute-done | bytes 442400 | tf_op jit(solution)/shard_map/ppermute | solution.py:340
  36.4 2.7 %shard_map.79.pull = f32[8,128]{1,0:T(8,128)S(1)} custom-call(f32[1056,128]{1,0:T(8,128)S(1)} %get-tuple-element.20.own, f32[864,128]{1,0:T(8,128)S(1)} %collective-permute-done.4.near, f32[1056,128]{1,0:T(8,128)S(1)} %get-tuple-element.22.far, f32[864,128]{1,0:T(8,128)S(1)} %collective-permute-done.7.cross, f32[5,128,128]{2,1,0:T(8,128)S(1)} %get-tuple-element.18.steps), custom_call_target="tpu_custom_call" | custom-call | bytes 100000 | tf_op jit(solution)/shard_map/pallas_call | solution.py:342
  39.1 0.0 all-to-all-done.fields
  39.1 0.6 shard_map.80
  39.7 3.5 %collective-permute-start.8 = (f32[2,2,16,512]{3,2,1,0:T(8,128)S(1)}, f32[2,2,16,512]{3,2,1,0:T(8,128)S(1)}, u32[]{:S(2)}, u32[]{:S(2)}) collective-permute-start(f32[2,2,16,512]{3,2,1,0:T(8,128)S(1)} %get-tuple-element.25), channel_id=1, source_target_pairs={{0,24},{4,28},{8,16},{12,20},{16,8},{20,12},{24,0},{28,4},{1,25},{... | collective-permute-start | bytes 393224 | tf_op jit(solution)/shard_map/ppermute | solution.py:251
  43.2 0.0 collective-permute-start.9
  43.2 3.8 %collective-permute-start.10 = (f32[1,2,16,512]{3,2,1,0:T(8,128)S(1)}, f32[1,2,16,512]{3,2,1,0:T(8,128)S(1)}, u32[]{:S(2)}, u32[]{:S(2)}) collective-permute-start(f32[1,2,16,512]{3,2,1,0:T(8,128)S(1)} %get-tuple-element.27), channel_id=1, source_target_pairs={{0,20},{4,16},{8,28},{12,24},{16,4},{20,0},{24,12},{28,8},{1,21},{... | collective-permute-start | bytes 196616 | tf_op jit(solution)/shard_map/ppermute | solution.py:251
  47.0 0.0 collective-permute-start.11
  47.0 2.0 %collective-permute-start.12 = (f32[1,2,16,512]{3,2,1,0:T(8,128)S(1)}, f32[1,2,16,512]{3,2,1,0:T(8,128)S(1)}, u32[]{:S(2)}, u32[]{:S(2)}) collective-permute-start(f32[1,2,16,512]{3,2,1,0:T(8,128)S(1)} %get-tuple-element.29), channel_id=1, source_target_pairs={{0,12},{4,8},{8,4},{12,0},{16,28},{20,24},{24,20},{28,16},{1,13},{... | collective-permute-start | bytes 196616 | tf_op jit(solution)/shard_map/ppermute | solution.py:251
  49.0 0.0 collective-permute-done.8.refs_1_
  49.0 1.5 %collective-permute-start.13 = (f32[1,2,16,512]{3,2,1,0:T(8,128)S(1)}, f32[1,2,16,512]{3,2,1,0:T(8,128)S(1)}, u32[]{:S(2)}, u32[]{:S(2)}) collective-permute-start(f32[1,2,16,512]{3,2,1,0:T(8,128)S(1)} %get-tuple-element.30), channel_id=1, source_target_pairs={{0,4},{4,0},{8,12},{12,8},{16,20},{20,16},{24,28},{28,24},{1,5},{5... | collective-permute-start | bytes 196616 | tf_op jit(solution)/shard_map/ppermute | solution.py:251
  50.5 3.6 %collective-permute-done.9.refs_2_ = f32[1,2,16,512]{3,2,1,0:T(8,128)S(1)} collective-permute-done((f32[1,2,16,512]{3,2,1,0:T(8,128)S(1)}, f32[1,2,16,512]{3,2,1,0:T(8,128)S(1)}, u32[]{:S(2)}, u32[]{:S(2)}) %collective-permute-start.9) | collective-permute-done | bytes 65568 | tf_op jit(solution)/shard_map/ppermute | solution.py:251
  54.1 1.4 %collective-permute-start.14 = (f32[1,2,16,512]{3,2,1,0:T(8,128)S(1)}, f32[1,2,16,512]{3,2,1,0:T(8,128)S(1)}, u32[]{:S(2)}, u32[]{:S(2)}) collective-permute-start(f32[1,2,16,512]{3,2,1,0:T(8,128)S(1)} %slice.4), channel_id=1, source_target_pairs={{0,4},{4,0},{8,12},{12,8},{16,20},{20,16},{24,28},{28,24},{1,5},{5... | collective-permute-start | bytes 196616 | tf_op jit(solution)/shard_map/ppermute | solution.py:251
  55.5 0.2 collective-permute-done.10.refs_3_
  55.7 0.0 collective-permute-done.11.refs_4_
  55.7 0.0 collective-permute-done.12.refs_5_
  55.7 0.0 collective-permute-done.13.refs_6_
  55.7 2.6 %collective-permute-done.14.refs_7_ = f32[1,2,16,512]{3,2,1,0:T(8,128)S(1)} collective-permute-done((f32[1,2,16,512]{3,2,1,0:T(8,128)S(1)}, f32[1,2,16,512]{3,2,1,0:T(8,128)S(1)}, u32[]{:S(2)}, u32[]{:S(2)}) %collective-permute-start.14) | collective-permute-done | bytes 65568 | tf_op jit(solution)/shard_map/ppermute | solution.py:251
  58.3 0.9 %shard_map.81 = f32[16,2,4096]{2,1,0:T(2,128)} custom-call(f32[1,2,16,512]{3,2,1,0:T(8,128)S(1)} %get-tuple-element.24.refs_0_, f32[2,2,16,512]{3,2,1,0:T(8,128)S(1)} %collective-permute-done.8.refs_1_, f32[1,2,16,512]{3,2,1,0:T(8,128)S(1)} %collective-permute-done.9.refs_2_, f32[1,2,16,512]{3,2,1,0:T(8,128)S(1)} %collective-permute-done.10.refs_3_, ...), custom_call_target="tpu_custom_call" | custom-call | bytes 1000000 | tf_op jit(solution)/shard_map/pallas_call | solution.py:363
  (8 shorter events, 0.0 us)
Async XLA Ops:
  0.0 8.3 %copy-start = (f32[16,2,4096]{2,1,0:T(2,128)S(1)}, f32[16,2,4096]{2,1,0:T(2,128)}, u32[]{:S(2)}) copy-start(f32[16,2,4096]{2,1,0:T(2,128)} %refs_4_.1) | copy-start | bytes 1572868
  2.5 6.7 %copy-start.2 = (s32[4,4,64]{2,1,0:T(4,128)S(1)}, s32[4,4,64]{2,1,0:T(4,128)}, u32[]{:S(2)}) copy-start(s32[4,4,64]{2,1,0:T(4,128)} %refs_2_.1) | copy-start | bytes 12292
  2.5 6.7 %copy-start.3 = (s32[4,1,1,128]{3,2,1,0:T(1,128)S(1)}, s32[4,1,1,128]{3,2,1,0:T(1,128)}, u32[]{:S(2)}) copy-start(s32[4,1,1,128]{3,2,1,0:T(1,128)} %param.13) | copy-start | bytes 6148
  2.5 6.7 %copy-start.4 = (s32[4]{0:T(128)S(1)}, s32[4]{0:T(128)}, u32[]{:S(2)}) copy-start(s32[4]{0:T(128)} %owner.5) | copy-start | bytes 52
  2.5 6.7 %copy-start.5 = (f32[4,1,64]{2,1,0:T(1,128)S(1)}, f32[4,1,64]{2,1,0:T(1,128)}, u32[]{:S(2)}) copy-start(f32[4,1,64]{2,1,0:T(1,128)} %values.1) | copy-start | bytes 3076
  2.5 6.7 %copy-start.6 = (f32[4,1,64]{2,1,0:T(1,128)S(1)}, f32[4,1,64]{2,1,0:T(1,128)}, u32[]{:S(2)}) copy-start(f32[4,1,64]{2,1,0:T(1,128)} %errors.1) | copy-start | bytes 3076
  2.5 11.3 %copy-start.1 = (f32[136,128]{1,0:T(8,128)S(1)}, f32[136,128]{1,0:T(8,128)}, u32[]{:S(2)}) copy-start(f32[136,128]{1,0:T(8,128)} %shard_map.75.refs_0_) | copy-start | bytes 208900
  2.5 8.0 %collective-permute-start.2 = (f32[136,128]{1,0:T(8,128)}, f32[136,128]{1,0:T(8,128)S(1)}, u32[]{:S(2)}, u32[]{:S(2)}) collective-permute-start(f32[136,128]{1,0:T(8,128)} %shard_map.75.refs_0_), channel_id=1, source_target_pairs={{0,24},{4,28},{8,16},{12,20},{16,8},{20,12},{24,0},{28,4},{1,25},{... | collective-permute-start | bytes 208904 | tf_op jit(solution)/shard_map/ppermute | solution.py:251
  7.6 6.1 %collective-permute-start.1 = (f32[136,128]{1,0:T(8,128)}, f32[136,128]{1,0:T(8,128)S(1)}, u32[]{:S(2)}, u32[]{:S(2)}) collective-permute-start(f32[136,128]{1,0:T(8,128)} %shard_map.75.refs_0_), channel_id=1, source_target_pairs={{0,16},{4,20},{8,24},{12,28},{16,0},{20,4},{24,8},{28,12},{1,17},{... | collective-permute-start | bytes 208904 | tf_op jit(solution)/shard_map/ppermute | solution.py:251
  7.7 6.1 %collective-permute-start = (f32[136,128]{1,0:T(8,128)}, f32[136,128]{1,0:T(8,128)S(1)}, u32[]{:S(2)}, u32[]{:S(2)}) collective-permute-start(f32[136,128]{1,0:T(8,128)} %shard_map.75.refs_0_), channel_id=1, source_target_pairs={{0,8},{4,12},{8,0},{12,4},{16,24},{20,28},{24,16},{28,20},{1,9},{5... | collective-permute-start | bytes 208904 | tf_op jit(solution)/shard_map/ppermute | solution.py:251
  13.8 11.4 %collective-permute-start.3 = (f32[576,128]{1,0:T(8,128)S(1)}, f32[576,128]{1,0:T(8,128)S(1)}, u32[]{:S(2)}, u32[]{:S(2)}) collective-permute-start(f32[576,128]{1,0:T(8,128)S(1)} %shard_map.76.refs_0_), channel_id=1, source_target_pairs={{0,4},{4,0},{8,12},{12,8},{16,20},{20,16},{24,28},{28,24},{1,5},{5... | collective-permute-start | bytes 884744 | tf_op jit(solution)/shard_map/ppermute | solution.py:251
  15.4 23.7 %all-to-all-start = ((f32[8,2,16,512]{3,2,1,0:T(8,128)}), f32[8,2,16,512]{3,2,1,0:T(8,128)S(1)}, u32[]{:S(2)}, u32[]{:S(2)}) async-start(f32[8,2,16,512]{3,2,1,0:T(8,128)} %shard_map.74.ahead), calls=%async_computation | async-start | bytes 1048576 | tf_op jit(solution)/shard_map/all_to_all | solution.py:300
  19.4 9.9 %collective-permute-start.5 = (f32[576,128]{1,0:T(8,128)S(1)}, f32[576,128]{1,0:T(8,128)S(1)}, u32[]{:S(2)}, u32[]{:S(2)}) collective-permute-start(f32[576,128]{1,0:T(8,128)S(1)} %shard_map.76.refs_0_), channel_id=1, source_target_pairs={{0,2},{1,3},{2,0},{3,1},{4,6},{5,7},{6,4},{7,5},{8,10},{9,11},{10,... | collective-permute-start | bytes 884744 | tf_op jit(solution)/shard_map/ppermute | solution.py:336
  25.2 8.5 %collective-permute-start.6 = (f32[576,128]{1,0:T(8,128)S(1)}, f32[576,128]{1,0:T(8,128)S(1)}, u32[]{:S(2)}, u32[]{:S(2)}) collective-permute-start(f32[576,128]{1,0:T(8,128)S(1)} %collective-permute-done.3.refs_1_), channel_id=1, source_target_pairs={{0,2},{1,3},{2,0},{3,1},{4,6},{5,7},{6,4},{7,5},{8,10},{9,11},{10,... | collective-permute-start | bytes 884744 | tf_op jit(solution)/shard_map/ppermute | solution.py:336
  27.5 7.1 %collective-permute-start.4 = (f32[864,128]{1,0:T(8,128)S(1)}, f32[864,128]{1,0:T(8,128)S(1)}, u32[]{:S(2)}, u32[]{:S(2)}) collective-permute-start(f32[864,128]{1,0:T(8,128)S(1)} %get-tuple-element.21), channel_id=1, source_target_pairs={{0,1},{1,0},{2,3},{3,2},{4,5},{5,4},{6,7},{7,6},{8,9},{9,8},{10,11... | collective-permute-start | bytes 1327112 | tf_op jit(solution)/shard_map/ppermute | solution.py:338
  34.5 1.9 %collective-permute-start.7 = (f32[864,128]{1,0:T(8,128)S(1)}, f32[864,128]{1,0:T(8,128)S(1)}, u32[]{:S(2)}, u32[]{:S(2)}) collective-permute-start(f32[864,128]{1,0:T(8,128)S(1)} %get-tuple-element.23), channel_id=1, source_target_pairs={{0,1},{1,0},{2,3},{3,2},{4,5},{5,4},{6,7},{7,6},{8,9},{9,8},{10,11... | collective-permute-start | bytes 1327112 | tf_op jit(solution)/shard_map/ppermute | solution.py:340
  39.7 9.3 %collective-permute-start.8 = (f32[2,2,16,512]{3,2,1,0:T(8,128)S(1)}, f32[2,2,16,512]{3,2,1,0:T(8,128)S(1)}, u32[]{:S(2)}, u32[]{:S(2)}) collective-permute-start(f32[2,2,16,512]{3,2,1,0:T(8,128)S(1)} %get-tuple-element.25), channel_id=1, source_target_pairs={{0,24},{4,28},{8,16},{12,20},{16,8},{20,12},{24,0},{28,4},{1,25},{... | collective-permute-start | bytes 393224 | tf_op jit(solution)/shard_map/ppermute | solution.py:251
  43.2 10.9 %collective-permute-start.9 = (f32[1,2,16,512]{3,2,1,0:T(8,128)S(1)}, f32[1,2,16,512]{3,2,1,0:T(8,128)S(1)}, u32[]{:S(2)}, u32[]{:S(2)}) collective-permute-start(f32[1,2,16,512]{3,2,1,0:T(8,128)S(1)} %get-tuple-element.26), channel_id=1, source_target_pairs={{0,16},{4,20},{8,24},{12,28},{16,0},{20,4},{24,8},{28,12},{1,17},{... | collective-permute-start | bytes 196616 | tf_op jit(solution)/shard_map/ppermute | solution.py:251
  43.2 12.5 %collective-permute-start.10 = (f32[1,2,16,512]{3,2,1,0:T(8,128)S(1)}, f32[1,2,16,512]{3,2,1,0:T(8,128)S(1)}, u32[]{:S(2)}, u32[]{:S(2)}) collective-permute-start(f32[1,2,16,512]{3,2,1,0:T(8,128)S(1)} %get-tuple-element.27), channel_id=1, source_target_pairs={{0,20},{4,16},{8,28},{12,24},{16,4},{20,0},{24,12},{28,8},{1,21},{... | collective-permute-start | bytes 196616 | tf_op jit(solution)/shard_map/ppermute | solution.py:251
  47.0 8.7 %collective-permute-start.11 = (f32[1,2,16,512]{3,2,1,0:T(8,128)S(1)}, f32[1,2,16,512]{3,2,1,0:T(8,128)S(1)}, u32[]{:S(2)}, u32[]{:S(2)}) collective-permute-start(f32[1,2,16,512]{3,2,1,0:T(8,128)S(1)} %get-tuple-element.28), channel_id=1, source_target_pairs={{0,8},{4,12},{8,0},{12,4},{16,24},{20,28},{24,16},{28,20},{1,9},{5... | collective-permute-start | bytes 196616 | tf_op jit(solution)/shard_map/ppermute | solution.py:251
  47.0 8.7 %collective-permute-start.12 = (f32[1,2,16,512]{3,2,1,0:T(8,128)S(1)}, f32[1,2,16,512]{3,2,1,0:T(8,128)S(1)}, u32[]{:S(2)}, u32[]{:S(2)}) collective-permute-start(f32[1,2,16,512]{3,2,1,0:T(8,128)S(1)} %get-tuple-element.29), channel_id=1, source_target_pairs={{0,12},{4,8},{8,4},{12,0},{16,28},{20,24},{24,20},{28,16},{1,13},{... | collective-permute-start | bytes 196616 | tf_op jit(solution)/shard_map/ppermute | solution.py:251
  49.0 6.7 %collective-permute-start.13 = (f32[1,2,16,512]{3,2,1,0:T(8,128)S(1)}, f32[1,2,16,512]{3,2,1,0:T(8,128)S(1)}, u32[]{:S(2)}, u32[]{:S(2)}) collective-permute-start(f32[1,2,16,512]{3,2,1,0:T(8,128)S(1)} %get-tuple-element.30), channel_id=1, source_target_pairs={{0,4},{4,0},{8,12},{12,8},{16,20},{20,16},{24,28},{28,24},{1,5},{5... | collective-permute-start | bytes 196616 | tf_op jit(solution)/shard_map/ppermute | solution.py:251
  54.1 4.3 %collective-permute-start.14 = (f32[1,2,16,512]{3,2,1,0:T(8,128)S(1)}, f32[1,2,16,512]{3,2,1,0:T(8,128)S(1)}, u32[]{:S(2)}, u32[]{:S(2)}) collective-permute-start(f32[1,2,16,512]{3,2,1,0:T(8,128)S(1)} %slice.4), channel_id=1, source_target_pairs={{0,4},{4,0},{8,12},{12,8},{16,20},{20,16},{24,28},{28,24},{1,5},{5... | collective-permute-start | bytes 196616 | tf_op jit(solution)/shard_map/ppermute | solution.py:251

commit v11 on v10

--- a/solution.py
+++ b/solution.py
@@ -16,8 +16,8 @@
 PLACE = pl.BlockSpec(memory_space=pl.ANY)
 LIMIT = 48 * 1024 * 1024
 
-PARTS = ((0,), (6, 7), (4,), (5,), (2,), (3,), (1,))
-ORDER = (0, 6, 4, 5, 2, 3, 1, 7)
+PARTS = ((0,), (6, 7), (4,), (5,), (2, 3), (1,))
+ORDER = (0, 6, 4, 5, 2, 1, 3, 7)
 PAIRS = [(e, b) for b in range(1, NB) for e in range(b)]
 PARENT, ALPHA, LATER, VALUE, OWN, SPARE = 0, 6, 12, 18, 22, 32
 
@@ -333,7 +333,11 @@
             moved=10**6,
         )(obs_owner, *parts)
 
-    arriving = [lax.ppermute(part, "lev", across) for part in gathered]
+    arriving = []
+    for part in gathered:
+        if arriving:
+            part, arriving[0] = lax.optimization_barrier((part, arriving[0]))
+        arriving.append(lax.ppermute(part, "lev", across))
     own, slim = turn(gathered)
     near = lax.ppermute(slim, "lev", beside)
     far, slim = turn(arriving)

time: 59.5 us -> 57 us (0.958)
  waiting for transfers between devices: 22.2 us -> 19.7 us
    ppermute x11, waiting for transfers between devices: 14.3 us -> 11.2 us  [hop(): return lax.ppermute(value, 'grid', [(j, j ^ distance) for j in range(n)])]
    ppermute x2, starting transfers between devices: 2.98 us -> 2.09 us  [body(): arriving.append(lax.ppermute(part, 'lev', across))]
    ppermute x11, starting transfers between devices: 19.6 us -> 20.4 us  [hop(): return lax.ppermute(value, 'grid', [(j, j ^ distance) for j in range(n)])]
    ppermute x2, waiting for transfers between devices: 6.18 us -> 6.78 us  [body(): arriving.append(lax.ppermute(part, 'lev', across))]
  transfers between devices with their start and end apart: 16 -> 16, of which waited for: 9 -> 9; matrix products, arithmetic and copies ran while one was open for 0% -> 0% of each run, Pallas kernels for 10% -> 11%
where the time goes in v11:
time: 57 us; the launch traced here: 56.8 us
  starting transfers between devices  26.7 us (47%)
  waiting for transfers between devices  19.7 us (35%)
  Pallas kernels  10.2 us (18%)
    ppermute x11, starting transfers between devices, hop(): return lax.ppermute(value, 'grid', [(j, j ^ distance) for j in range(n)])  20.4 us
    ppermute x11, waiting for transfers between devices, hop(): return lax.ppermute(value, 'grid', [(j, j ^ distance) for j in range(n)])  11.2 us
    ppermute x2, waiting for transfers between devices, body(): arriving.append(lax.ppermute(part, 'lev', across))  6.78 us
    all_to_all x1, starting transfers between devices, body(): fields = lax.all_to_all(send, 'grid', 0, 0, tiled=True)  3.99 us
    pallas_call x1, Pallas kernels, body(): call(functools.partial(chain_kernel, (members, groups, count)), shape((8,...  2.72 us
    pallas_call x1, Pallas kernels, body(): call(functools.partial(pick_kernel, (slab, depth, block_cells, groups, co...  2.45 us
    ppermute x2, starting transfers between devices, body(): arriving.append(lax.ppermute(part, 'lev', across))  2.09 us
    ppermute x1, waiting for transfers between devices, body(): cross = lax.ppermute(slim, 'lev', beside)  1.77 us
  transfers between devices with their start and end apart: 16, of which 9 were waited for; matrix products, arithmetic and copies ran while one was open for 0% of the time, Pallas kernels for 11%

profile of v11, /device:TPU:0, one launch (start us, length us, event | category | flops | bytes accessed | tf_op | source)
XLA Modules:
  0.0 56.8 jit_solution(14884987467181384669)
XLA Ops:
  0.0 2.5 %shard_map.75.refs_0_ = f32[136,128]{1,0:T(8,128)} custom-call(s32[4]{0:T(128)} %owner.5, f32[2,4]{1,0:T(2,128)} %refs_1_.1, s32[4,4,64]{2,1,0:T(4,128)} %refs_2_.1, s32[4,1,128]{2,1,0:T(1,128)} %bitcast.1, f32[16,2,4096]{2,1,0:T(2,128)} %refs_4_.1), custom_call_target="tpu_custom_call" | custom-call | bytes 1000000 | tf_op jit(solution)/shard_map/pallas_call | solution.py:278
  2.5 0.0 copy-start.2
  2.5 0.0 copy-start.3
  2.5 0.0 copy-start.4
  2.5 0.0 copy-start.5
  2.5 0.0 copy-start.6
  2.5 0.0 copy-start.1
  2.5 5.1 %collective-permute-start.2 = (f32[136,128]{1,0:T(8,128)}, f32[136,128]{1,0:T(8,128)S(1)}, u32[]{:S(2)}, u32[]{:S(2)}) collective-permute-start(f32[136,128]{1,0:T(8,128)} %shard_map.75.refs_0_), channel_id=1, source_target_pairs={{0,24},{4,28},{8,16},{12,20},{16,8},{20,12},{24,0},{28,4},{1,25},{... | collective-permute-start | bytes 208904 | tf_op jit(solution)/shard_map/ppermute | solution.py:251
  7.6 0.0 collective-permute-start.1
  7.7 0.6 %collective-permute-start = (f32[136,128]{1,0:T(8,128)}, f32[136,128]{1,0:T(8,128)S(1)}, u32[]{:S(2)}, u32[]{:S(2)}) collective-permute-start(f32[136,128]{1,0:T(8,128)} %shard_map.75.refs_0_), channel_id=1, source_target_pairs={{0,8},{4,12},{8,0},{12,4},{16,24},{20,28},{24,16},{28,20},{1,9},{5... | collective-permute-start | bytes 208904 | tf_op jit(solution)/shard_map/ppermute | solution.py:251
  8.3 0.0 copy-done
  8.3 0.9 %shard_map.74.ahead = f32[8,2,16,512]{3,2,1,0:T(8,128)} custom-call(f32[16,2,4096]{2,1,0:T(2,128)S(1)} %copy-done), custom_call_target="tpu_custom_call" | custom-call | bytes 1000000 | tf_op jit(solution)/shard_map/pallas_call | solution.py:294
  9.2 0.0 copy-done.3
  9.2 1.0 %shard_map.73 = (f32[32,128]{1,0:T(8,128)S(1)}, f32[5,128,128]{2,1,0:T(8,128)S(1)}) custom-call(s32[4]{0:T(128)S(1)} %copy-done.4, s32[4,4,64]{2,1,0:T(4,128)S(1)} %copy-done.2, f32[4,1,64]{2,1,0:T(1,128)S(1)} %copy-done.5, f32[4,1,64]{2,1,0:T(1,128)S(1)} %copy-done.6, s32[4,1,128]{2,1,0:T(1,128)S(1)} %bitcast.2), custom_call_target="tpu_custom_call" | custom-call | bytes 1000000 | tf_op jit(solution)/shard_map/pallas_call | solution.py:302
  10.2 0.3 collective-permute-done.2.refs_3_
  10.6 3.2 %collective-permute-done.1.refs_2_ = f32[136,128]{1,0:T(8,128)S(1)} collective-permute-done((f32[136,128]{1,0:T(8,128)}, f32[136,128]{1,0:T(8,128)S(1)}, u32[]{:S(2)}, u32[]{:S(2)}) %collective-permute-start.1) | collective-permute-done | bytes 69664 | tf_op jit(solution)/shard_map/ppermute | solution.py:251
  13.8 0.0 collective-permute-done.refs_1_
  13.8 1.6 %collective-permute-start.5 = (f32[576,128]{1,0:T(8,128)S(1)}, f32[576,128]{1,0:T(8,128)S(1)}, u32[]{:S(2)}, u32[]{:S(2)}) collective-permute-start(f32[576,128]{1,0:T(8,128)S(1)} %shard_map.76.refs_0_), channel_id=1, source_target_pairs={{0,2},{1,3},{2,0},{3,1},{4,6},{5,7},{6,4},{7,5},{8,10},{9,11},{10,... | collective-permute-start | bytes 884744 | tf_op jit(solution)/shard_map/ppermute | solution.py:340
  15.4 1.5 %collective-permute-start.3 = (f32[576,128]{1,0:T(8,128)S(1)}, f32[576,128]{1,0:T(8,128)S(1)}, u32[]{:S(2)}, u32[]{:S(2)}) collective-permute-start(f32[576,128]{1,0:T(8,128)S(1)} %shard_map.76.refs_0_), channel_id=1, source_target_pairs={{0,4},{4,0},{8,12},{12,8},{16,20},{20,16},{24,28},{28,24},{1,5},{5... | collective-permute-start | bytes 884744 | tf_op jit(solution)/shard_map/ppermute | solution.py:251
  16.9 4.0 %all-to-all-start = ((f32[8,2,16,512]{3,2,1,0:T(8,128)}), f32[8,2,16,512]{3,2,1,0:T(8,128)S(1)}, u32[]{:S(2)}, u32[]{:S(2)}) async-start(f32[8,2,16,512]{3,2,1,0:T(8,128)} %shard_map.74.ahead), calls=%async_computation | async-start | bytes 1048576 | tf_op jit(solution)/shard_map/all_to_all | solution.py:300
  20.9 1.5 %collective-permute-done.5.refs_0_ = f32[576,128]{1,0:T(8,128)S(1)} collective-permute-done((f32[576,128]{1,0:T(8,128)S(1)}, f32[576,128]{1,0:T(8,128)S(1)}, u32[]{:S(2)}, u32[]{:S(2)}) %collective-permute-start.5) | collective-permute-done | bytes 294944 | tf_op jit(solution)/shard_map/ppermute | solution.py:340
  22.3 3.7 %collective-permute-done.3.refs_1_ = f32[576,128]{1,0:T(8,128)S(1)} collective-permute-done((f32[576,128]{1,0:T(8,128)S(1)}, f32[576,128]{1,0:T(8,128)S(1)}, u32[]{:S(2)}, u32[]{:S(2)}) %collective-permute-start.3) | collective-permute-done | bytes 294944 | tf_op jit(solution)/shard_map/ppermute | solution.py:251
  26.0 0.5 collective-permute-start.6
  26.5 0.8 %shard_map.77 = (f32[1056,128]{1,0:T(8,128)S(1)}, f32[864,128]{1,0:T(8,128)S(1)}) custom-call(s32[4]{0:T(128)S(1)} %copy-done.4, f32[576,128]{1,0:T(8,128)S(1)} %shard_map.76.refs_0_, f32[576,128]{1,0:T(8,128)S(1)} %collective-permute-done.3.refs_1_), custom_call_target="tpu_custom_call" | custom-call | bytes 1000000 | tf_op jit(solution)/shard_map/pallas_call | solution.py:325
  27.3 0.1 collective-permute-start.4
  27.4 5.3 %collective-permute-done.6.refs_1_ = f32[576,128]{1,0:T(8,128)S(1)} collective-permute-done((f32[576,128]{1,0:T(8,128)S(1)}, f32[576,128]{1,0:T(8,128)S(1)}, u32[]{:S(2)}, u32[]{:S(2)}) %collective-permute-start.6) | collective-permute-done | bytes 294944 | tf_op jit(solution)/shard_map/ppermute | solution.py:340
  32.7 0.8 %shard_map.78 = (f32[1056,128]{1,0:T(8,128)S(1)}, f32[864,128]{1,0:T(8,128)S(1)}) custom-call(s32[4]{0:T(128)S(1)} %copy-done.4, f32[576,128]{1,0:T(8,128)S(1)} %collective-permute-done.5.refs_0_, f32[576,128]{1,0:T(8,128)S(1)} %collective-permute-done.6.refs_1_), custom_call_target="tpu_custom_call" | custom-call | bytes 1000000 | tf_op jit(solution)/shard_map/pallas_call | solution.py:325
  33.5 0.1 collective-permute-start.7
  33.6 0.0 collective-permute-done.4.near
  33.6 1.8 %collective-permute-done.7.cross = f32[864,128]{1,0:T(8,128)S(1)} collective-permute-done((f32[864,128]{1,0:T(8,128)S(1)}, f32[864,128]{1,0:T(8,128)S(1)}, u32[]{:S(2)}, u32[]{:S(2)}) %collective-permute-start.7) | collective-permute-done | bytes 442400 | tf_op jit(solution)/shard_map/ppermute | solution.py:344
  35.4 2.7 %shard_map.79.pull = f32[8,128]{1,0:T(8,128)S(1)} custom-call(f32[1056,128]{1,0:T(8,128)S(1)} %get-tuple-element.21.own, f32[864,128]{1,0:T(8,128)S(1)} %collective-permute-done.4.near, f32[1056,128]{1,0:T(8,128)S(1)} %get-tuple-element.25.far, f32[864,128]{1,0:T(8,128)S(1)} %collective-permute-done.7.cross, f32[5,128,128]{2,1,0:T(8,128)S(1)} %get-tuple-element.19.steps), custom_call_target="tpu_custom_call" | custom-call | bytes 100000 | tf_op jit(solution)/shard_map/pallas_call | solution.py:346
  38.1 0.0 all-to-all-done.fields
  38.1 0.6 %shard_map.80 = (f32[1,2,16,512]{3,2,1,0:T(8,128)S(1)}, f32[2,2,16,512]{3,2,1,0:T(8,128)S(1)}, f32[1,2,16,512]{3,2,1,0:T(8,128)S(1)}, f32[1,2,16,512]{3,2,1,0:T(...) custom-call(f32[5,128,128]{2,1,0:T(8,128)S(1)} %get-tuple-element.19.steps, ...), custom_call_target="tpu_custom_call" | custom-call | flops 100000000 | bytes 1000000 | tf_op jit(solution)/shard_map/pallas_call | solution.py:357
  38.7 0.9 %collective-permute-start.8 = (f32[2,2,16,512]{3,2,1,0:T(8,128)S(1)}, f32[2,2,16,512]{3,2,1,0:T(8,128)S(1)}, u32[]{:S(2)}, u32[]{:S(2)}) collective-permute-start(f32[2,2,16,512]{3,2,1,0:T(8,128)S(1)} %get-tuple-element.28), channel_id=1, source_target_pairs={{0,24},{4,28},{8,16},{12,20},{16,8},{20,12},{24,0},{28,4},{1,25},{... | collective-permute-start | bytes 393224 | tf_op jit(solution)/shard_map/ppermute | solution.py:251
  39.6 0.0 collective-permute-start.11
  39.6 3.6 %collective-permute-start.9 = (f32[1,2,16,512]{3,2,1,0:T(8,128)S(1)}, f32[1,2,16,512]{3,2,1,0:T(8,128)S(1)}, u32[]{:S(2)}, u32[]{:S(2)}) collective-permute-start(f32[1,2,16,512]{3,2,1,0:T(8,128)S(1)} %get-tuple-element.29), channel_id=1, source_target_pairs={{0,16},{4,20},{8,24},{12,28},{16,0},{20,4},{24,8},{28,12},{1,17},{... | collective-permute-start | bytes 196616 | tf_op jit(solution)/shard_map/ppermute | solution.py:251
  43.2 1.9 %collective-permute-start.10 = (f32[1,2,16,512]{3,2,1,0:T(8,128)S(1)}, f32[1,2,16,512]{3,2,1,0:T(8,128)S(1)}, u32[]{:S(2)}, u32[]{:S(2)}) collective-permute-start(f32[1,2,16,512]{3,2,1,0:T(8,128)S(1)} %get-tuple-element.30), channel_id=1, source_target_pairs={{0,20},{4,16},{8,28},{12,24},{16,4},{20,0},{24,12},{28,8},{1,21},{... | collective-permute-start | bytes 196616 | tf_op jit(solution)/shard_map/ppermute | solution.py:251
  45.1 0.6 collective-permute-start.12
  45.7 1.4 %collective-permute-done.8.refs_1_ = f32[2,2,16,512]{3,2,1,0:T(8,128)S(1)} collective-permute-done((f32[2,2,16,512]{3,2,1,0:T(8,128)S(1)}, f32[2,2,16,512]{3,2,1,0:T(8,128)S(1)}, u32[]{:S(2)}, u32[]{:S(2)}) %collective-permute-start.8) | collective-permute-done | bytes 131104 | tf_op jit(solution)/shard_map/ppermute | solution.py:251
  47.1 2.5 %collective-permute-start.14 = (f32[1,2,16,512]{3,2,1,0:T(8,128)S(1)}, f32[1,2,16,512]{3,2,1,0:T(8,128)S(1)}, u32[]{:S(2)}, u32[]{:S(2)}) collective-permute-start(f32[1,2,16,512]{3,2,1,0:T(8,128)S(1)} %slice.9), channel_id=1, source_target_pairs={{0,4},{4,0},{8,12},{12,8},{16,20},{20,16},{24,28},{28,24},{1,5},{5... | collective-permute-start | bytes 196616 | tf_op jit(solution)/shard_map/ppermute | solution.py:251
  49.6 0.3 collective-permute-done.11.refs_4_
  49.9 3.7 %collective-permute-start.13 = (f32[1,2,16,512]{3,2,1,0:T(8,128)S(1)}, f32[1,2,16,512]{3,2,1,0:T(8,128)S(1)}, u32[]{:S(2)}, u32[]{:S(2)}) collective-permute-start(f32[1,2,16,512]{3,2,1,0:T(8,128)S(1)} %slice.8), channel_id=1, source_target_pairs={{0,4},{4,0},{8,12},{12,8},{16,20},{20,16},{24,28},{28,24},{1,5},{5... | collective-permute-start | bytes 196616 | tf_op jit(solution)/shard_map/ppermute | solution.py:251
  53.6 0.0 collective-permute-done.9.refs_2_
  53.6 0.0 collective-permute-done.10.refs_3_
  53.6 0.0 collective-permute-done.12.refs_5_
  53.6 0.0 collective-permute-done.14.refs_7_
  53.6 2.2 %collective-permute-done.13.refs_6_ = f32[1,2,16,512]{3,2,1,0:T(8,128)S(1)} collective-permute-done((f32[1,2,16,512]{3,2,1,0:T(8,128)S(1)}, f32[1,2,16,512]{3,2,1,0:T(8,128)S(1)}, u32[]{:S(2)}, u32[]{:S(2)}) %collective-permute-start.13) | collective-permute-done | bytes 65568 | tf_op jit(solution)/shard_map/ppermute | solution.py:251
  55.8 0.9 %shard_map.81 = f32[16,2,4096]{2,1,0:T(2,128)} custom-call(f32[1,2,16,512]{3,2,1,0:T(8,128)S(1)} %get-tuple-element.27.refs_0_, f32[2,2,16,512]{3,2,1,0:T(8,128)S(1)} %collective-permute-done.8.refs_1_, f32[1,2,16,512]{3,2,1,0:T(8,128)S(1)} %collective-permute-done.9.refs_2_, f32[1,2,16,512]{3,2,1,0:T(8,128)S(1)} %collective-permute-done.10.refs_3_, ...), custom_call_target="tpu_custom_call" | custom-call | bytes 1000000 | tf_op jit(solution)/shard_map/pallas_call | solution.py:367
  (9 shorter events, 0.0 us)
Async XLA Ops:
  0.0 8.3 %copy-start = (f32[16,2,4096]{2,1,0:T(2,128)S(1)}, f32[16,2,4096]{2,1,0:T(2,128)}, u32[]{:S(2)}) copy-start(f32[16,2,4096]{2,1,0:T(2,128)} %refs_4_.1) | copy-start | bytes 1572868
  2.5 6.7 %copy-start.2 = (s32[4,4,64]{2,1,0:T(4,128)S(1)}, s32[4,4,64]{2,1,0:T(4,128)}, u32[]{:S(2)}) copy-start(s32[4,4,64]{2,1,0:T(4,128)} %refs_2_.1) | copy-start | bytes 12292
  2.5 6.7 %copy-start.3 = (s32[4,1,1,128]{3,2,1,0:T(1,128)S(1)}, s32[4,1,1,128]{3,2,1,0:T(1,128)}, u32[]{:S(2)}) copy-start(s32[4,1,1,128]{3,2,1,0:T(1,128)} %param.13) | copy-start | bytes 6148
  2.5 6.7 %copy-start.4 = (s32[4]{0:T(128)S(1)}, s32[4]{0:T(128)}, u32[]{:S(2)}) copy-start(s32[4]{0:T(128)} %owner.5) | copy-start | bytes 52
  2.5 6.7 %copy-start.5 = (f32[4,1,64]{2,1,0:T(1,128)S(1)}, f32[4,1,64]{2,1,0:T(1,128)}, u32[]{:S(2)}) copy-start(f32[4,1,64]{2,1,0:T(1,128)} %values.1) | copy-start | bytes 3076
  2.5 6.7 %copy-start.6 = (f32[4,1,64]{2,1,0:T(1,128)S(1)}, f32[4,1,64]{2,1,0:T(1,128)}, u32[]{:S(2)}) copy-start(f32[4,1,64]{2,1,0:T(1,128)} %errors.1) | copy-start | bytes 3076
  2.5 11.3 %copy-start.1 = (f32[136,128]{1,0:T(8,128)S(1)}, f32[136,128]{1,0:T(8,128)}, u32[]{:S(2)}) copy-start(f32[136,128]{1,0:T(8,128)} %shard_map.75.refs_0_) | copy-start | bytes 208900
  2.5 8.0 %collective-permute-start.2 = (f32[136,128]{1,0:T(8,128)}, f32[136,128]{1,0:T(8,128)S(1)}, u32[]{:S(2)}, u32[]{:S(2)}) collective-permute-start(f32[136,128]{1,0:T(8,128)} %shard_map.75.refs_0_), channel_id=1, source_target_pairs={{0,24},{4,28},{8,16},{12,20},{16,8},{20,12},{24,0},{28,4},{1,25},{... | collective-permute-start | bytes 208904 | tf_op jit(solution)/shard_map/ppermute | solution.py:251
  7.6 6.1 %collective-permute-start.1 = (f32[136,128]{1,0:T(8,128)}, f32[136,128]{1,0:T(8,128)S(1)}, u32[]{:S(2)}, u32[]{:S(2)}) collective-permute-start(f32[136,128]{1,0:T(8,128)} %shard_map.75.refs_0_), channel_id=1, source_target_pairs={{0,16},{4,20},{8,24},{12,28},{16,0},{20,4},{24,8},{28,12},{1,17},{... | collective-permute-start | bytes 208904 | tf_op jit(solution)/shard_map/ppermute | solution.py:251
  7.7 6.1 %collective-permute-start = (f32[136,128]{1,0:T(8,128)}, f32[136,128]{1,0:T(8,128)S(1)}, u32[]{:S(2)}, u32[]{:S(2)}) collective-permute-start(f32[136,128]{1,0:T(8,128)} %shard_map.75.refs_0_), channel_id=1, source_target_pairs={{0,8},{4,12},{8,0},{12,4},{16,24},{20,28},{24,16},{28,20},{1,9},{5... | collective-permute-start | bytes 208904 | tf_op jit(solution)/shard_map/ppermute | solution.py:251
  13.8 8.5 %collective-permute-start.5 = (f32[576,128]{1,0:T(8,128)S(1)}, f32[576,128]{1,0:T(8,128)S(1)}, u32[]{:S(2)}, u32[]{:S(2)}) collective-permute-start(f32[576,128]{1,0:T(8,128)S(1)} %shard_map.76.refs_0_), channel_id=1, source_target_pairs={{0,2},{1,3},{2,0},{3,1},{4,6},{5,7},{6,4},{7,5},{8,10},{9,11},{10,... | collective-permute-start | bytes 884744 | tf_op jit(solution)/shard_map/ppermute | solution.py:340
  15.4 10.7 %collective-permute-start.3 = (f32[576,128]{1,0:T(8,128)S(1)}, f32[576,128]{1,0:T(8,128)S(1)}, u32[]{:S(2)}, u32[]{:S(2)}) collective-permute-start(f32[576,128]{1,0:T(8,128)S(1)} %shard_map.76.refs_0_), channel_id=1, source_target_pairs={{0,4},{4,0},{8,12},{12,8},{16,20},{20,16},{24,28},{28,24},{1,5},{5... | collective-permute-start | bytes 884744 | tf_op jit(solution)/shard_map/ppermute | solution.py:251
  16.9 21.2 %all-to-all-start = ((f32[8,2,16,512]{3,2,1,0:T(8,128)}), f32[8,2,16,512]{3,2,1,0:T(8,128)S(1)}, u32[]{:S(2)}, u32[]{:S(2)}) async-start(f32[8,2,16,512]{3,2,1,0:T(8,128)} %shard_map.74.ahead), calls=%async_computation | async-start | bytes 1048576 | tf_op jit(solution)/shard_map/all_to_all | solution.py:300
  26.0 6.7 %collective-permute-start.6 = (f32[576,128]{1,0:T(8,128)S(1)}, f32[576,128]{1,0:T(8,128)S(1)}, u32[]{:S(2)}, u32[]{:S(2)}) collective-permute-start(f32[576,128]{1,0:T(8,128)S(1)} %collective-permute-done.3.refs_1_), channel_id=1, source_target_pairs={{0,2},{1,3},{2,0},{3,1},{4,6},{5,7},{6,4},{7,5},{8,10},{9,11},{10,... | collective-permute-start | bytes 884744 | tf_op jit(solution)/shard_map/ppermute | solution.py:340
  27.3 6.3 %collective-permute-start.4 = (f32[864,128]{1,0:T(8,128)S(1)}, f32[864,128]{1,0:T(8,128)S(1)}, u32[]{:S(2)}, u32[]{:S(2)}) collective-permute-start(f32[864,128]{1,0:T(8,128)S(1)} %get-tuple-element.22), channel_id=1, source_target_pairs={{0,1},{1,0},{2,3},{3,2},{4,5},{5,4},{6,7},{7,6},{8,9},{9,8},{10,11... | collective-permute-start | bytes 1327112 | tf_op jit(solution)/shard_map/ppermute | solution.py:342
  33.5 1.9 %collective-permute-start.7 = (f32[864,128]{1,0:T(8,128)S(1)}, f32[864,128]{1,0:T(8,128)S(1)}, u32[]{:S(2)}, u32[]{:S(2)}) collective-permute-start(f32[864,128]{1,0:T(8,128)S(1)} %get-tuple-element.26), channel_id=1, source_target_pairs={{0,1},{1,0},{2,3},{3,2},{4,5},{5,4},{6,7},{7,6},{8,9},{9,8},{10,11... | collective-permute-start | bytes 1327112 | tf_op jit(solution)/shard_map/ppermute | solution.py:344
  38.7 8.3 %collective-permute-start.8 = (f32[2,2,16,512]{3,2,1,0:T(8,128)S(1)}, f32[2,2,16,512]{3,2,1,0:T(8,128)S(1)}, u32[]{:S(2)}, u32[]{:S(2)}) collective-permute-start(f32[2,2,16,512]{3,2,1,0:T(8,128)S(1)} %get-tuple-element.28), channel_id=1, source_target_pairs={{0,24},{4,28},{8,16},{12,20},{16,8},{20,12},{24,0},{28,4},{1,25},{... | collective-permute-start | bytes 393224 | tf_op jit(solution)/shard_map/ppermute | solution.py:251
  39.6 10.3 %collective-permute-start.11 = (f32[2,2,16,512]{3,2,1,0:T(8,128)S(1)}, f32[2,2,16,512]{3,2,1,0:T(8,128)S(1)}, u32[]{:S(2)}, u32[]{:S(2)}) collective-permute-start(f32[2,2,16,512]{3,2,1,0:T(8,128)S(1)} %get-tuple-element.31), channel_id=1, source_target_pairs={{0,8},{4,12},{8,0},{12,4},{16,24},{20,28},{24,16},{28,20},{1,9},{5... | collective-permute-start | bytes 393224 | tf_op jit(solution)/shard_map/ppermute | solution.py:251
  39.6 14.0 %collective-permute-start.9 = (f32[1,2,16,512]{3,2,1,0:T(8,128)S(1)}, f32[1,2,16,512]{3,2,1,0:T(8,128)S(1)}, u32[]{:S(2)}, u32[]{:S(2)}) collective-permute-start(f32[1,2,16,512]{3,2,1,0:T(8,128)S(1)} %get-tuple-element.29), channel_id=1, source_target_pairs={{0,16},{4,20},{8,24},{12,28},{16,0},{20,4},{24,8},{28,12},{1,17},{... | collective-permute-start | bytes 196616 | tf_op jit(solution)/shard_map/ppermute | solution.py:251
  43.2 10.4 %collective-permute-start.10 = (f32[1,2,16,512]{3,2,1,0:T(8,128)S(1)}, f32[1,2,16,512]{3,2,1,0:T(8,128)S(1)}, u32[]{:S(2)}, u32[]{:S(2)}) collective-permute-start(f32[1,2,16,512]{3,2,1,0:T(8,128)S(1)} %get-tuple-element.30), channel_id=1, source_target_pairs={{0,20},{4,16},{8,28},{12,24},{16,4},{20,0},{24,12},{28,8},{1,21},{... | collective-permute-start | bytes 196616 | tf_op jit(solution)/shard_map/ppermute | solution.py:251
  45.1 8.5 %collective-permute-start.12 = (f32[1,2,16,512]{3,2,1,0:T(8,128)S(1)}, f32[1,2,16,512]{3,2,1,0:T(8,128)S(1)}, u32[]{:S(2)}, u32[]{:S(2)}) collective-permute-start(f32[1,2,16,512]{3,2,1,0:T(8,128)S(1)} %get-tuple-element.32), channel_id=1, source_target_pairs={{0,4},{4,0},{8,12},{12,8},{16,20},{20,16},{24,28},{28,24},{1,5},{5... | collective-permute-start | bytes 196616 | tf_op jit(solution)/shard_map/ppermute | solution.py:251
  47.1 6.6 %collective-permute-start.14 = (f32[1,2,16,512]{3,2,1,0:T(8,128)S(1)}, f32[1,2,16,512]{3,2,1,0:T(8,128)S(1)}, u32[]{:S(2)}, u32[]{:S(2)}) collective-permute-start(f32[1,2,16,512]{3,2,1,0:T(8,128)S(1)} %slice.9), channel_id=1, source_target_pairs={{0,4},{4,0},{8,12},{12,8},{16,20},{20,16},{24,28},{28,24},{1,5},{5... | collective-permute-start | bytes 196616 | tf_op jit(solution)/shard_map/ppermute | solution.py:251
  49.9 5.9 %collective-permute-start.13 = (f32[1,2,16,512]{3,2,1,0:T(8,128)S(1)}, f32[1,2,16,512]{3,2,1,0:T(8,128)S(1)}, u32[]{:S(2)}, u32[]{:S(2)}) collective-permute-start(f32[1,2,16,512]{3,2,1,0:T(8,128)S(1)} %slice.8), channel_id=1, source_target_pairs={{0,4},{4,0},{8,12},{12,8},{16,20},{20,16},{24,28},{28,24},{1,5},{5... | collective-permute-start | bytes 196616 | tf_op jit(solution)/shard_map/ppermute | solution.py:251

commit v12 on v10

--- a/solution.py
+++ b/solution.py
@@ -16,8 +16,8 @@
 PLACE = pl.BlockSpec(memory_space=pl.ANY)
 LIMIT = 48 * 1024 * 1024
 
-PARTS = ((0,), (6, 7), (4,), (5,), (2,), (3,), (1,))
-ORDER = (0, 6, 4, 5, 2, 3, 1, 7)
+PARTS = ((0,), (2, 3), (6, 7), (4,), (5,), (1,))
+ARRIVING = ((0,), (2,), (6,), (4,), (5,), (1, 3), (7,))
 PAIRS = [(e, b) for b in range(1, NB) for e in range(b)]
 PARENT, ALPHA, LATER, VALUE, OWN, SPARE = 0, 6, 12, 18, 22, 32
 
@@ -238,13 +238,20 @@
 
 def final_kernel(shape, *refs):
     n, slab, depth, block_cells = shape
-    pieces, out = refs[:-1], refs[-1]
+    arrived, out = refs[:-1], refs[-1]
     block = lax.axis_index("grid")
-    for i in range(n):
-        region = i if len(pieces) == 1 else lax.bitwise_xor(block, ORDER[i])
+    if len(arrived) == 1:
+        places = [(i, 0, i) for i in range(n)]
+    else:
+        places = [
+            (lax.bitwise_xor(block, distance), i, j)
+            for i, distances in enumerate(ARRIVING)
+            for j, distance in enumerate(distances)
+        ]
+    for region, i, j in places:
         cells = pl.ds(pl.multiple_of(region * block_cells, LANES), block_cells)
         for level in range(depth):
-            out[:, level, cells] = pieces[0][i, level] if len(pieces) == 1 else pieces[i][0, level]
+            out[:, level, cells] = arrived[i][j, level]
 
 
 def hop(value, distance, n):
@@ -254,12 +261,11 @@
 def exchange_parts(parts, n):
     if len(parts) == 1:
         return [lax.all_to_all(parts[0], "grid", 0, 0, tiled=True)]
-    pieces = {0: parts[0]}
-    for part, distances in zip(parts[1:], PARTS[1:]):
-        pieces[distances[0]] = hop(part, distances[0], n)
-        if len(distances) == 2:
-            pieces[distances[1]] = hop(pieces[distances[0]][1:], 1, n)
-    return [pieces[i] for i in ORDER]
+    arrived = [parts[0]]
+    for part, distances in zip(parts[1:-1], PARTS[1:-1]):
+        arrived.append(hop(part, distances[0], n))
+    last = jnp.concatenate([parts[-1], arrived[1][1:]], axis=0)
+    return arrived + [hop(last, 1, n), hop(arrived[2][1:], 1, n)]
 
 
 def body(prior, channel_weights, obs_owner, obs_offset, obs_value, obs_error, ancestors):
@@ -334,6 +340,7 @@
         )(obs_owner, *parts)
 
     arriving = [lax.ppermute(part, "lev", across) for part in gathered]
+    gathered[0], arriving[0] = lax.optimization_barrier((gathered[0], arriving[0]))
     own, slim = turn(gathered)
     near = lax.ppermute(slim, "lev", beside)
     far, slim = turn(arriving)

time: 59.5 us -> 57.4 us (0.965)
  starting transfers between devices: 26.7 us -> 25.2 us
  waiting for transfers between devices: 22.2 us -> 21.5 us
    ppermute x11 -> x10, starting transfers between devices: 19.6 us -> 18.1 us  [hop(): return lax.ppermute(value, 'grid', [(j, j ^ distance) for j in range(n)])]
    ppermute x11 -> x10, waiting for transfers between devices: 14.3 us -> 13.6 us  [hop(): return lax.ppermute(value, 'grid', [(j, j ^ distance) for j in range(n)])]
  transfers between devices with their start and end apart: 16 -> 15, of which waited for: 9 -> 9; matrix products, arithmetic and copies ran while one was open for 0% -> 0% of each run, Pallas kernels for 10% -> 11%
where the time goes in v12:
time: 57.4 us; the launch traced here: 57.2 us
  starting transfers between devices  25.2 us (44%)
  waiting for transfers between devices  21.5 us (37%)
  Pallas kernels  10.2 us (18%)
    ppermute x10, starting transfers between devices, hop(): return lax.ppermute(value, 'grid', [(j, j ^ distance) for j in range(n)])  18.1 us
    ppermute x10, waiting for transfers between devices, hop(): return lax.ppermute(value, 'grid', [(j, j ^ distance) for j in range(n)])  13.6 us
    ppermute x2, waiting for transfers between devices, body(): arriving = [lax.ppermute(part, 'lev', across) for part in gathered]  6.18 us
    all_to_all x1, starting transfers between devices, body(): fields = lax.all_to_all(send, 'grid', 0, 0, tiled=True)  3.99 us
    ppermute x2, starting transfers between devices, body(): arriving = [lax.ppermute(part, 'lev', across) for part in gathered]  2.98 us
    pallas_call x1, Pallas kernels, body(): call(functools.partial(chain_kernel, (members, groups, count)), shape((8,...  2.72 us
    pallas_call x1, Pallas kernels, body(): call(functools.partial(pick_kernel, (slab, depth, block_cells, groups, co...  2.46 us
    ppermute x1, waiting for transfers between devices, body(): cross = lax.ppermute(slim, 'lev', beside)  1.77 us
  transfers between devices with their start and end apart: 15, of which 9 were waited for; matrix products, arithmetic and copies ran while one was open for 0% of the time, Pallas kernels for 11%

profile of v12, /device:TPU:0, one launch (start us, length us, event | category | flops | bytes accessed | tf_op | source)
XLA Modules:
  0.0 57.2 jit_solution(4919631749628585049)
XLA Ops:
  0.0 2.5 %shard_map.75.refs_0_ = f32[136,128]{1,0:T(8,128)} custom-call(s32[4]{0:T(128)} %owner.5, f32[2,4]{1,0:T(2,128)} %refs_1_.1, s32[4,4,64]{2,1,0:T(4,128)} %refs_2_.1, s32[4,1,128]{2,1,0:T(1,128)} %bitcast.1, f32[16,2,4096]{2,1,0:T(2,128)} %refs_4_.1), custom_call_target="tpu_custom_call" | custom-call | bytes 1000000 | tf_op jit(solution)/shard_map/pallas_call | solution.py:284
  2.5 0.0 copy-start.2
  2.5 0.0 copy-start.3
  2.5 0.0 copy-start.4
  2.5 0.0 copy-start.5
  2.5 0.0 copy-start.6
  2.5 0.0 copy-start.1
  2.5 5.1 %collective-permute-start.2 = (f32[136,128]{1,0:T(8,128)}, f32[136,128]{1,0:T(8,128)S(1)}, u32[]{:S(2)}, u32[]{:S(2)}) collective-permute-start(f32[136,128]{1,0:T(8,128)} %shard_map.75.refs_0_), channel_id=1, source_target_pairs={{0,24},{4,28},{8,16},{12,20},{16,8},{20,12},{24,0},{28,4},{1,25},{... | collective-permute-start | bytes 208904 | tf_op jit(solution)/shard_map/ppermute | solution.py:258
  7.7 0.0 collective-permute-start.1
  7.7 0.6 %collective-permute-start = (f32[136,128]{1,0:T(8,128)}, f32[136,128]{1,0:T(8,128)S(1)}, u32[]{:S(2)}, u32[]{:S(2)}) collective-permute-start(f32[136,128]{1,0:T(8,128)} %shard_map.75.refs_0_), channel_id=1, source_target_pairs={{0,8},{4,12},{8,0},{12,4},{16,24},{20,28},{24,16},{28,20},{1,9},{5... | collective-permute-start | bytes 208904 | tf_op jit(solution)/shard_map/ppermute | solution.py:258
  8.3 0.0 copy-done
  8.3 0.9 %shard_map.74.ahead = f32[8,2,16,512]{3,2,1,0:T(8,128)} custom-call(f32[16,2,4096]{2,1,0:T(2,128)S(1)} %copy-done), custom_call_target="tpu_custom_call" | custom-call | bytes 1000000 | tf_op jit(solution)/shard_map/pallas_call | solution.py:300
  9.2 0.0 copy-done.2
  9.2 0.0 copy-done.3
  9.2 0.0 copy-done.6
  9.2 1.0 %shard_map.73 = (f32[32,128]{1,0:T(8,128)S(1)}, f32[5,128,128]{2,1,0:T(8,128)S(1)}) custom-call(s32[4]{0:T(128)S(1)} %copy-done.4, s32[4,4,64]{2,1,0:T(4,128)S(1)} %copy-done.2, f32[4,1,64]{2,1,0:T(1,128)S(1)} %copy-done.5, f32[4,1,64]{2,1,0:T(1,128)S(1)} %copy-done.6, s32[4,1,128]{2,1,0:T(1,128)S(1)} %bitcast.2), custom_call_target="tpu_custom_call" | custom-call | bytes 1000000 | tf_op jit(solution)/shard_map/pallas_call | solution.py:308
  10.2 0.3 collective-permute-done.2.refs_3_
  10.6 3.2 %collective-permute-done.1.refs_2_ = f32[136,128]{1,0:T(8,128)S(1)} collective-permute-done((f32[136,128]{1,0:T(8,128)}, f32[136,128]{1,0:T(8,128)S(1)}, u32[]{:S(2)}, u32[]{:S(2)}) %collective-permute-start.1) | collective-permute-done | bytes 69664 | tf_op jit(solution)/shard_map/ppermute | solution.py:258
  13.8 0.0 collective-permute-done.refs_1_
  13.8 1.6 %collective-permute-start.4 = (f32[576,128]{1,0:T(8,128)S(1)}, f32[576,128]{1,0:T(8,128)S(1)}, u32[]{:S(2)}, u32[]{:S(2)}) collective-permute-start(f32[576,128]{1,0:T(8,128)S(1)} %shard_map.76.refs_0_), channel_id=1, source_target_pairs={{0,4},{4,0},{8,12},{12,8},{16,20},{20,16},{24,28},{28,24},{1,5},{5... | collective-permute-start | bytes 884744 | tf_op jit(solution)/shard_map/ppermute | solution.py:258
  15.4 4.0 %all-to-all-start = ((f32[8,2,16,512]{3,2,1,0:T(8,128)}), f32[8,2,16,512]{3,2,1,0:T(8,128)S(1)}, u32[]{:S(2)}, u32[]{:S(2)}) async-start(f32[8,2,16,512]{3,2,1,0:T(8,128)} %shard_map.74.ahead), calls=%async_computation | async-start | bytes 1048576 | tf_op jit(solution)/shard_map/all_to_all | solution.py:306
  19.4 1.5 %collective-permute-start.3 = (f32[576,128]{1,0:T(8,128)S(1)}, f32[576,128]{1,0:T(8,128)S(1)}, u32[]{:S(2)}, u32[]{:S(2)}) collective-permute-start(f32[576,128]{1,0:T(8,128)S(1)} %shard_map.76.refs_0_), channel_id=1, source_target_pairs={{0,2},{1,3},{2,0},{3,1},{4,6},{5,7},{6,4},{7,5},{8,10},{9,11},{10,... | collective-permute-start | bytes 884744 | tf_op jit(solution)/shard_map/ppermute | solution.py:342
  20.9 4.3 %collective-permute-done.4.refs_1_ = f32[576,128]{1,0:T(8,128)S(1)} collective-permute-done((f32[576,128]{1,0:T(8,128)S(1)}, f32[576,128]{1,0:T(8,128)S(1)}, u32[]{:S(2)}, u32[]{:S(2)}) %collective-permute-start.4) | collective-permute-done | bytes 294944 | tf_op jit(solution)/shard_map/ppermute | solution.py:258
  25.2 1.5 %collective-permute-start.6 = (f32[576,128]{1,0:T(8,128)S(1)}, f32[576,128]{1,0:T(8,128)S(1)}, u32[]{:S(2)}, u32[]{:S(2)}) collective-permute-start(f32[576,128]{1,0:T(8,128)S(1)} %collective-permute-done.4.refs_1_), channel_id=1, source_target_pairs={{0,2},{1,3},{2,0},{3,1},{4,6},{5,7},{6,4},{7,5},{8,10},{9,11},{10,... | collective-permute-start | bytes 884744 | tf_op jit(solution)/shard_map/ppermute | solution.py:342
  26.7 2.7 %collective-permute-done.3.refs_0_ = f32[576,128]{1,0:T(8,128)S(1)} collective-permute-done((f32[576,128]{1,0:T(8,128)S(1)}, f32[576,128]{1,0:T(8,128)S(1)}, u32[]{:S(2)}, u32[]{:S(2)}) %collective-permute-start.3) | collective-permute-done | bytes 294944 | tf_op jit(solution)/shard_map/ppermute | solution.py:342
  29.3 0.8 %shard_map.77 = (f32[1056,128]{1,0:T(8,128)S(1)}, f32[864,128]{1,0:T(8,128)S(1)}) custom-call(s32[4]{0:T(128)S(1)} %copy-done.4, f32[576,128]{1,0:T(8,128)S(1)} %shard_map.76.refs_0_, f32[576,128]{1,0:T(8,128)S(1)} %collective-permute-done.4.refs_1_), custom_call_target="tpu_custom_call" | custom-call | bytes 1000000 | tf_op jit(solution)/shard_map/pallas_call | solution.py:331
  30.1 0.1 collective-permute-start.5
  30.2 3.5 %collective-permute-done.6.refs_1_ = f32[576,128]{1,0:T(8,128)S(1)} collective-permute-done((f32[576,128]{1,0:T(8,128)S(1)}, f32[576,128]{1,0:T(8,128)S(1)}, u32[]{:S(2)}, u32[]{:S(2)}) %collective-permute-start.6) | collective-permute-done | bytes 294944 | tf_op jit(solution)/shard_map/ppermute | solution.py:342
  33.7 0.8 %shard_map.78 = (f32[1056,128]{1,0:T(8,128)S(1)}, f32[864,128]{1,0:T(8,128)S(1)}) custom-call(s32[4]{0:T(128)S(1)} %copy-done.4, f32[576,128]{1,0:T(8,128)S(1)} %collective-permute-done.3.refs_0_, f32[576,128]{1,0:T(8,128)S(1)} %collective-permute-done.6.refs_1_), custom_call_target="tpu_custom_call" | custom-call | bytes 1000000 | tf_op jit(solution)/shard_map/pallas_call | solution.py:331
  34.5 0.1 collective-permute-start.7
  34.6 0.0 collective-permute-done.5.near
  34.6 1.8 %collective-permute-done.7.cross = f32[864,128]{1,0:T(8,128)S(1)} collective-permute-done((f32[864,128]{1,0:T(8,128)S(1)}, f32[864,128]{1,0:T(8,128)S(1)}, u32[]{:S(2)}, u32[]{:S(2)}) %collective-permute-start.7) | collective-permute-done | bytes 442400 | tf_op jit(solution)/shard_map/ppermute | solution.py:347
  36.4 2.7 %shard_map.79.pull = f32[8,128]{1,0:T(8,128)S(1)} custom-call(f32[1056,128]{1,0:T(8,128)S(1)} %get-tuple-element.22.own, f32[864,128]{1,0:T(8,128)S(1)} %collective-permute-done.5.near, f32[1056,128]{1,0:T(8,128)S(1)} %get-tuple-element.25.far, f32[864,128]{1,0:T(8,128)S(1)} %collective-permute-done.7.cross, f32[5,128,128]{2,1,0:T(8,128)S(1)} %get-tuple-element.19.steps), custom_call_target="tpu_custom_call" | custom-call | bytes 100000 | tf_op jit(solution)/shard_map/pallas_call | solution.py:349
  39.1 0.0 all-to-all-done.fields
  39.1 0.6 %shard_map.80 = (f32[1,2,16,512]{3,2,1,0:T(8,128)S(1)}, f32[2,2,16,512]{3,2,1,0:T(8,128)S(1)}, f32[2,2,16,512]{3,2,1,0:T(8,128)S(1)}, f32[1,2,16,512]{3,2,1,0:T(...) custom-call(f32[5,128,128]{2,1,0:T(8,128)S(1)} %get-tuple-element.19.steps, ...), custom_call_target="tpu_custom_call" | custom-call | flops 100000000 | bytes 1000000 | tf_op jit(solution)/shard_map/pallas_call | solution.py:360
  39.7 1.6 %collective-permute-start.8 = (f32[2,2,16,512]{3,2,1,0:T(8,128)S(1)}, f32[2,2,16,512]{3,2,1,0:T(8,128)S(1)}, u32[]{:S(2)}, u32[]{:S(2)}) collective-permute-start(f32[2,2,16,512]{3,2,1,0:T(8,128)S(1)} %get-tuple-element.28), channel_id=1, source_target_pairs={{0,8},{4,12},{8,0},{12,4},{16,24},{20,28},{24,16},{28,20},{1,9},{5... | collective-permute-start | bytes 393224 | tf_op jit(solution)/shard_map/ppermute | solution.py:258
  41.4 2.4 %collective-permute-start.9 = (f32[2,2,16,512]{3,2,1,0:T(8,128)S(1)}, f32[2,2,16,512]{3,2,1,0:T(8,128)S(1)}, u32[]{:S(2)}, u32[]{:S(2)}) collective-permute-start(f32[2,2,16,512]{3,2,1,0:T(8,128)S(1)} %get-tuple-element.29), channel_id=1, source_target_pairs={{0,24},{4,28},{8,16},{12,20},{16,8},{20,12},{24,0},{28,4},{1,25},{... | collective-permute-start | bytes 393224 | tf_op jit(solution)/shard_map/ppermute | solution.py:258
  43.7 1.6 %collective-permute-done.8.refs_1_ = f32[2,2,16,512]{3,2,1,0:T(8,128)S(1)} collective-permute-done((f32[2,2,16,512]{3,2,1,0:T(8,128)S(1)}, f32[2,2,16,512]{3,2,1,0:T(8,128)S(1)}, u32[]{:S(2)}, u32[]{:S(2)}) %collective-permute-start.8) | collective-permute-done | bytes 131104 | tf_op jit(solution)/shard_map/ppermute | solution.py:258
  45.3 1.6 %collective-permute-start.12 = (f32[2,2,16,512]{3,2,1,0:T(8,128)S(1)}, f32[2,2,16,512]{3,2,1,0:T(8,128)S(1)}, u32[]{:S(2)}, u32[]{:S(2)}) collective-permute-start(f32[2,2,16,512]{3,2,1,0:T(8,128)S(1)} %pad_maximum_fusion), channel_id=1, source_target_pairs={{0,4},{4,0},{8,12},{12,8},{16,20},{20,16},{24,28},{28,24},{1,5},{5... | collective-permute-start | bytes 393224 | tf_op jit(solution)/shard_map/ppermute | solution.py:258
  47.0 3.2 %collective-permute-start.10 = (f32[1,2,16,512]{3,2,1,0:T(8,128)S(1)}, f32[1,2,16,512]{3,2,1,0:T(8,128)S(1)}, u32[]{:S(2)}, u32[]{:S(2)}) collective-permute-start(f32[1,2,16,512]{3,2,1,0:T(8,128)S(1)} %get-tuple-element.30), channel_id=1, source_target_pairs={{0,16},{4,20},{8,24},{12,28},{16,0},{20,4},{24,8},{28,12},{1,17},{... | collective-permute-start | bytes 196616 | tf_op jit(solution)/shard_map/ppermute | solution.py:258
  50.2 0.0 collective-permute-start.11
  50.2 0.0 collective-permute-done.9.refs_2_
  50.2 1.9 %collective-permute-start.13 = (f32[1,2,16,512]{3,2,1,0:T(8,128)S(1)}, f32[1,2,16,512]{3,2,1,0:T(8,128)S(1)}, u32[]{:S(2)}, u32[]{:S(2)}) collective-permute-start(f32[1,2,16,512]{3,2,1,0:T(8,128)S(1)} %slice.9), channel_id=1, source_target_pairs={{0,4},{4,0},{8,12},{12,8},{16,20},{20,16},{24,28},{28,24},{1,5},{5... | collective-permute-start | bytes 196616 | tf_op jit(solution)/shard_map/ppermute | solution.py:258
  52.1 2.3 %collective-permute-done.10.refs_3_ = f32[1,2,16,512]{3,2,1,0:T(8,128)S(1)} collective-permute-done((f32[1,2,16,512]{3,2,1,0:T(8,128)S(1)}, f32[1,2,16,512]{3,2,1,0:T(8,128)S(1)}, u32[]{:S(2)}, u32[]{:S(2)}) %collective-permute-start.10) | collective-permute-done | bytes 65568 | tf_op jit(solution)/shard_map/ppermute | solution.py:258
  54.4 1.8 %collective-permute-done.11.refs_4_ = f32[1,2,16,512]{3,2,1,0:T(8,128)S(1)} collective-permute-done((f32[1,2,16,512]{3,2,1,0:T(8,128)S(1)}, f32[1,2,16,512]{3,2,1,0:T(8,128)S(1)}, u32[]{:S(2)}, u32[]{:S(2)}) %collective-permute-start.11) | collective-permute-done | bytes 65568 | tf_op jit(solution)/shard_map/ppermute | solution.py:258
  56.2 0.0 collective-permute-done.13.refs_6_
  56.2 0.0 collective-permute-done.12.refs_5_
  56.2 0.9 %shard_map.81 = f32[16,2,4096]{2,1,0:T(2,128)} custom-call(f32[1,2,16,512]{3,2,1,0:T(8,128)S(1)} %get-tuple-element.27.refs_0_, f32[2,2,16,512]{3,2,1,0:T(8,128)S(1)} %collective-permute-done.8.refs_1_, f32[2,2,16,512]{3,2,1,0:T(8,128)S(1)} %collective-permute-done.9.refs_2_, f32[1,2,16,512]{3,2,1,0:T(8,128)S(1)} %collective-permute-done.10.refs_3_, ...), custom_call_target="tpu_custom_call" | custom-call | bytes 1000000 | tf_op jit(solution)/shard_map/pallas_call | solution.py:370
  (8 shorter events, 0.0 us)
Async XLA Ops:
  0.0 8.3 %copy-start = (f32[16,2,4096]{2,1,0:T(2,128)S(1)}, f32[16,2,4096]{2,1,0:T(2,128)}, u32[]{:S(2)}) copy-start(f32[16,2,4096]{2,1,0:T(2,128)} %refs_4_.1) | copy-start | bytes 1572868
  2.5 6.7 %copy-start.2 = (s32[4,4,64]{2,1,0:T(4,128)S(1)}, s32[4,4,64]{2,1,0:T(4,128)}, u32[]{:S(2)}) copy-start(s32[4,4,64]{2,1,0:T(4,128)} %refs_2_.1) | copy-start | bytes 12292
  2.5 6.7 %copy-start.3 = (s32[4,1,1,128]{3,2,1,0:T(1,128)S(1)}, s32[4,1,1,128]{3,2,1,0:T(1,128)}, u32[]{:S(2)}) copy-start(s32[4,1,1,128]{3,2,1,0:T(1,128)} %param.13) | copy-start | bytes 6148
  2.5 6.7 %copy-start.4 = (s32[4]{0:T(128)S(1)}, s32[4]{0:T(128)}, u32[]{:S(2)}) copy-start(s32[4]{0:T(128)} %owner.5) | copy-start | bytes 52
  2.5 6.7 %copy-start.5 = (f32[4,1,64]{2,1,0:T(1,128)S(1)}, f32[4,1,64]{2,1,0:T(1,128)}, u32[]{:S(2)}) copy-start(f32[4,1,64]{2,1,0:T(1,128)} %values.1) | copy-start | bytes 3076
  2.5 6.7 %copy-start.6 = (f32[4,1,64]{2,1,0:T(1,128)S(1)}, f32[4,1,64]{2,1,0:T(1,128)}, u32[]{:S(2)}) copy-start(f32[4,1,64]{2,1,0:T(1,128)} %errors.1) | copy-start | bytes 3076
  2.5 11.3 %copy-start.1 = (f32[136,128]{1,0:T(8,128)S(1)}, f32[136,128]{1,0:T(8,128)}, u32[]{:S(2)}) copy-start(f32[136,128]{1,0:T(8,128)} %shard_map.75.refs_0_) | copy-start | bytes 208900
  2.5 8.0 %collective-permute-start.2 = (f32[136,128]{1,0:T(8,128)}, f32[136,128]{1,0:T(8,128)S(1)}, u32[]{:S(2)}, u32[]{:S(2)}) collective-permute-start(f32[136,128]{1,0:T(8,128)} %shard_map.75.refs_0_), channel_id=1, source_target_pairs={{0,24},{4,28},{8,16},{12,20},{16,8},{20,12},{24,0},{28,4},{1,25},{... | collective-permute-start | bytes 208904 | tf_op jit(solution)/shard_map/ppermute | solution.py:258
  7.7 6.1 %collective-permute-start.1 = (f32[136,128]{1,0:T(8,128)}, f32[136,128]{1,0:T(8,128)S(1)}, u32[]{:S(2)}, u32[]{:S(2)}) collective-permute-start(f32[136,128]{1,0:T(8,128)} %shard_map.75.refs_0_), channel_id=1, source_target_pairs={{0,16},{4,20},{8,24},{12,28},{16,0},{20,4},{24,8},{28,12},{1,17},{... | collective-permute-start | bytes 208904 | tf_op jit(solution)/shard_map/ppermute | solution.py:258
  7.7 6.1 %collective-permute-start = (f32[136,128]{1,0:T(8,128)}, f32[136,128]{1,0:T(8,128)S(1)}, u32[]{:S(2)}, u32[]{:S(2)}) collective-permute-start(f32[136,128]{1,0:T(8,128)} %shard_map.75.refs_0_), channel_id=1, source_target_pairs={{0,8},{4,12},{8,0},{12,4},{16,24},{20,28},{24,16},{28,20},{1,9},{5... | collective-permute-start | bytes 208904 | tf_op jit(solution)/shard_map/ppermute | solution.py:258
  13.8 11.4 %collective-permute-start.4 = (f32[576,128]{1,0:T(8,128)S(1)}, f32[576,128]{1,0:T(8,128)S(1)}, u32[]{:S(2)}, u32[]{:S(2)}) collective-permute-start(f32[576,128]{1,0:T(8,128)S(1)} %shard_map.76.refs_0_), channel_id=1, source_target_pairs={{0,4},{4,0},{8,12},{12,8},{16,20},{20,16},{24,28},{28,24},{1,5},{5... | collective-permute-start | bytes 884744 | tf_op jit(solution)/shard_map/ppermute | solution.py:258
  15.4 23.7 %all-to-all-start = ((f32[8,2,16,512]{3,2,1,0:T(8,128)}), f32[8,2,16,512]{3,2,1,0:T(8,128)S(1)}, u32[]{:S(2)}, u32[]{:S(2)}) async-start(f32[8,2,16,512]{3,2,1,0:T(8,128)} %shard_map.74.ahead), calls=%async_computation | async-start | bytes 1048576 | tf_op jit(solution)/shard_map/all_to_all | solution.py:306
  19.4 9.9 %collective-permute-start.3 = (f32[576,128]{1,0:T(8,128)S(1)}, f32[576,128]{1,0:T(8,128)S(1)}, u32[]{:S(2)}, u32[]{:S(2)}) collective-permute-start(f32[576,128]{1,0:T(8,128)S(1)} %shard_map.76.refs_0_), channel_id=1, source_target_pairs={{0,2},{1,3},{2,0},{3,1},{4,6},{5,7},{6,4},{7,5},{8,10},{9,11},{10,... | collective-permute-start | bytes 884744 | tf_op jit(solution)/shard_map/ppermute | solution.py:342
  25.2 8.5 %collective-permute-start.6 = (f32[576,128]{1,0:T(8,128)S(1)}, f32[576,128]{1,0:T(8,128)S(1)}, u32[]{:S(2)}, u32[]{:S(2)}) collective-permute-start(f32[576,128]{1,0:T(8,128)S(1)} %collective-permute-done.4.refs_1_), channel_id=1, source_target_pairs={{0,2},{1,3},{2,0},{3,1},{4,6},{5,7},{6,4},{7,5},{8,10},{9,11},{10,... | collective-permute-start | bytes 884744 | tf_op jit(solution)/shard_map/ppermute | solution.py:342
  30.1 4.5 %collective-permute-start.5 = (f32[864,128]{1,0:T(8,128)S(1)}, f32[864,128]{1,0:T(8,128)S(1)}, u32[]{:S(2)}, u32[]{:S(2)}) collective-permute-start(f32[864,128]{1,0:T(8,128)S(1)} %get-tuple-element.23), channel_id=1, source_target_pairs={{0,1},{1,0},{2,3},{3,2},{4,5},{5,4},{6,7},{7,6},{8,9},{9,8},{10,11... | collective-permute-start | bytes 1327112 | tf_op jit(solution)/shard_map/ppermute | solution.py:345
  34.5 1.9 %collective-permute-start.7 = (f32[864,128]{1,0:T(8,128)S(1)}, f32[864,128]{1,0:T(8,128)S(1)}, u32[]{:S(2)}, u32[]{:S(2)}) collective-permute-start(f32[864,128]{1,0:T(8,128)S(1)} %get-tuple-element.26), channel_id=1, source_target_pairs={{0,1},{1,0},{2,3},{3,2},{4,5},{5,4},{6,7},{7,6},{8,9},{9,8},{10,11... | collective-permute-start | bytes 1327112 | tf_op jit(solution)/shard_map/ppermute | solution.py:347
  39.7 5.6 %collective-permute-start.8 = (f32[2,2,16,512]{3,2,1,0:T(8,128)S(1)}, f32[2,2,16,512]{3,2,1,0:T(8,128)S(1)}, u32[]{:S(2)}, u32[]{:S(2)}) collective-permute-start(f32[2,2,16,512]{3,2,1,0:T(8,128)S(1)} %get-tuple-element.28), channel_id=1, source_target_pairs={{0,8},{4,12},{8,0},{12,4},{16,24},{20,28},{24,16},{28,20},{1,9},{5... | collective-permute-start | bytes 393224 | tf_op jit(solution)/shard_map/ppermute | solution.py:258
  41.4 8.8 %collective-permute-start.9 = (f32[2,2,16,512]{3,2,1,0:T(8,128)S(1)}, f32[2,2,16,512]{3,2,1,0:T(8,128)S(1)}, u32[]{:S(2)}, u32[]{:S(2)}) collective-permute-start(f32[2,2,16,512]{3,2,1,0:T(8,128)S(1)} %get-tuple-element.29), channel_id=1, source_target_pairs={{0,24},{4,28},{8,16},{12,20},{16,8},{20,12},{24,0},{28,4},{1,25},{... | collective-permute-start | bytes 393224 | tf_op jit(solution)/shard_map/ppermute | solution.py:258
  45.3 10.9 %collective-permute-start.12 = (f32[2,2,16,512]{3,2,1,0:T(8,128)S(1)}, f32[2,2,16,512]{3,2,1,0:T(8,128)S(1)}, u32[]{:S(2)}, u32[]{:S(2)}) collective-permute-start(f32[2,2,16,512]{3,2,1,0:T(8,128)S(1)} %pad_maximum_fusion), channel_id=1, source_target_pairs={{0,4},{4,0},{8,12},{12,8},{16,20},{20,16},{24,28},{28,24},{1,5},{5... | collective-permute-start | bytes 393224 | tf_op jit(solution)/shard_map/ppermute | solution.py:258
  47.0 7.4 %collective-permute-start.10 = (f32[1,2,16,512]{3,2,1,0:T(8,128)S(1)}, f32[1,2,16,512]{3,2,1,0:T(8,128)S(1)}, u32[]{:S(2)}, u32[]{:S(2)}) collective-permute-start(f32[1,2,16,512]{3,2,1,0:T(8,128)S(1)} %get-tuple-element.30), channel_id=1, source_target_pairs={{0,16},{4,20},{8,24},{12,28},{16,0},{20,4},{24,8},{28,12},{1,17},{... | collective-permute-start | bytes 196616 | tf_op jit(solution)/shard_map/ppermute | solution.py:258
  50.2 6.1 %collective-permute-start.11 = (f32[1,2,16,512]{3,2,1,0:T(8,128)S(1)}, f32[1,2,16,512]{3,2,1,0:T(8,128)S(1)}, u32[]{:S(2)}, u32[]{:S(2)}) collective-permute-start(f32[1,2,16,512]{3,2,1,0:T(8,128)S(1)} %get-tuple-element.31), channel_id=1, source_target_pairs={{0,20},{4,16},{8,28},{12,24},{16,4},{20,0},{24,12},{28,8},{1,21},{... | collective-permute-start | bytes 196616 | tf_op jit(solution)/shard_map/ppermute | solution.py:258
  50.2 6.1 %collective-permute-start.13 = (f32[1,2,16,512]{3,2,1,0:T(8,128)S(1)}, f32[1,2,16,512]{3,2,1,0:T(8,128)S(1)}, u32[]{:S(2)}, u32[]{:S(2)}) collective-permute-start(f32[1,2,16,512]{3,2,1,0:T(8,128)S(1)} %slice.9), channel_id=1, source_target_pairs={{0,4},{4,0},{8,12},{12,8},{16,20},{20,16},{24,28},{28,24},{1,5},{5... | collective-permute-start | bytes 196616 | tf_op jit(solution)/shard_map/ppermute | solution.py:258

commit v13 on v8

--- a/solution.py
+++ b/solution.py
@@ -246,9 +246,9 @@
     if n != 8:
         return [lax.all_to_all(jnp.broadcast_to(piece[None], (n,) + piece.shape), "grid", 0, 0, tiled=True)]
     pieces = {0: piece}
-    for i in (6, 4, 2):
+    for i in (4, 2, 6, 7, 1):
         pieces[i] = hop(piece, i, n)
-    for i in (0, 2, 4, 6):
+    for i in (4, 2):
         pieces[i + 1] = hop(pieces[i], 1, n)
     return [pieces[i] for i in range(n)]
 

time: 53.5 us -> 53.1 us (level)
  waiting for transfers between devices: 17 us -> 15.8 us
  starting transfers between devices: 26.7 us -> 27.5 us
    all_to_all x1, waiting for transfers between devices: 3.59 us -> 2.22 us  [body(): fields = lax.all_to_all(send, 'grid', 0, 0, tiled=True)]
  transfers between devices with their start and end apart: 18 -> 18, of which waited for: 7 -> 9; matrix products, arithmetic and copies ran while one was open for 0% -> 0% of each run, Pallas kernels for 9% -> 9%
where the time goes in v13:
time: 53.1 us; the launch traced here: 52.9 us
  starting transfers between devices  27.5 us (52%)
  waiting for transfers between devices  15.8 us (30%)
  Pallas kernels  9.36 us (18%)
    ppermute x14, starting transfers between devices, hop(): return lax.ppermute(value, 'grid', [(j, j ^ distance) for j in range(n)])  21 us
    ppermute x14, waiting for transfers between devices, hop(): return lax.ppermute(value, 'grid', [(j, j ^ distance) for j in range(n)])  8.12 us
    all_to_all x1, starting transfers between devices, body(): fields = lax.all_to_all(send, 'grid', 0, 0, tiled=True)  4.95 us
    ppermute x1, waiting for transfers between devices, body(): far = lax.ppermute(slim, 'lev', [(j, j ^ 2) for j in range(lev)])  3.64 us
    pallas_call x1, Pallas kernels, body(): call(functools.partial(chain_kernel, (members, groups, count)), shape((8,...  2.72 us
    pallas_call x1, Pallas kernels, body(): call(functools.partial(pick_kernel, (slab, depth, block_cells, groups, co...  2.46 us
    all_to_all x1, waiting for transfers between devices, body(): fields = lax.all_to_all(send, 'grid', 0, 0, tiled=True)  2.22 us
    ppermute x1, waiting for transfers between devices, body(): cross = lax.ppermute(far, 'lev', [(j, j ^ 1) for j in range(lev)])  1.83 us
  transfers between devices with their start and end apart: 18, of which 9 were waited for; matrix products, arithmetic and copies ran while one was open for 0% of the time, Pallas kernels for 9%

profile of v13, /device:TPU:0, one launch (start us, length us, event | category | flops | bytes accessed | tf_op | source)
XLA Modules:
  0.0 52.9 jit_solution(12562037440960617281)
XLA Ops:
  0.0 2.5 %shard_map.75.refs_0_ = f32[136,128]{1,0:T(8,128)} custom-call(s32[4]{0:T(128)} %owner.3, f32[2,4]{1,0:T(2,128)} %refs_1_.1, s32[4,4,64]{2,1,0:T(4,128)} %refs_2_.1, s32[4,1,128]{2,1,0:T(1,128)} %bitcast.1, f32[16,2,4096]{2,1,0:T(2,128)} %refs_4_.1), custom_call_target="tpu_custom_call" | custom-call | bytes 1000000 | tf_op jit(solution)/shard_map/pallas_call | solution.py:280
  2.5 0.0 copy-start.2
  2.5 0.0 copy-start.3
  2.5 0.0 copy-start.4
  2.5 0.0 copy-start.5
  2.5 0.0 copy-start.6
  2.5 3.1 %collective-permute-start.1 = (f32[136,128]{1,0:T(8,128)}, f32[136,128]{1,0:T(8,128)S(1)}, u32[]{:S(2)}, u32[]{:S(2)}) collective-permute-start(f32[136,128]{1,0:T(8,128)} %shard_map.75.refs_0_), channel_id=1, source_target_pairs={{0,8},{4,12},{8,0},{12,4},{16,24},{20,28},{24,16},{28,20},{1,9},{5... | collective-permute-start | bytes 208904 | tf_op jit(solution)/shard_map/ppermute | solution.py:242
  5.6 2.6 %collective-permute-start.3 = (f32[136,128]{1,0:T(8,128)}, f32[136,128]{1,0:T(8,128)S(1)}, u32[]{:S(2)}, u32[]{:S(2)}) collective-permute-start(f32[136,128]{1,0:T(8,128)} %shard_map.75.refs_0_), channel_id=1, source_target_pairs={{0,16},{4,20},{8,24},{12,28},{16,0},{20,4},{24,8},{28,12},{1,17},{... | collective-permute-start | bytes 208904 | tf_op jit(solution)/shard_map/ppermute | solution.py:242
  8.2 1.5 %collective-permute-start = (f32[136,128]{1,0:T(8,128)}, f32[136,128]{1,0:T(8,128)S(1)}, u32[]{:S(2)}, u32[]{:S(2)}) collective-permute-start(f32[136,128]{1,0:T(8,128)} %shard_map.75.refs_0_), channel_id=1, source_target_pairs={{0,4},{4,0},{8,12},{12,8},{16,20},{20,16},{24,28},{28,24},{1,5},{5... | collective-permute-start | bytes 208904 | tf_op jit(solution)/shard_map/ppermute | solution.py:242
  9.7 0.2 collective-permute-start.5
  10.0 3.5 %collective-permute-start.6 = (f32[136,128]{1,0:T(8,128)}, f32[136,128]{1,0:T(8,128)S(1)}, u32[]{:S(2)}, u32[]{:S(2)}) collective-permute-start(f32[136,128]{1,0:T(8,128)} %shard_map.75.refs_0_), channel_id=1, source_target_pairs={{0,28},{4,24},{8,20},{12,16},{16,12},{20,8},{24,4},{28,0},{1,29},{... | collective-permute-start | bytes 208904 | tf_op jit(solution)/shard_map/ppermute | solution.py:242
  13.5 0.0 collective-permute-done.1.refs_2_
  13.5 1.5 %collective-permute-start.2 = (f32[136,128]{1,0:T(8,128)S(1)}, f32[136,128]{1,0:T(8,128)S(1)}, u32[]{:S(2)}, u32[]{:S(2)}) collective-permute-start(f32[136,128]{1,0:T(8,128)S(1)} %collective-permute-done.1.refs_2_), channel_id=1, source_target_pairs={{0,4},{4,0},{8,12},{12,8},{16,20},{20,16},{24,28},{28,24},{1,5},{5... | collective-permute-start | bytes 208904 | tf_op jit(solution)/shard_map/ppermute | solution.py:242
  15.0 0.0 collective-permute-done.3.refs_4_
  15.0 0.6 %collective-permute-start.4 = (f32[136,128]{1,0:T(8,128)S(1)}, f32[136,128]{1,0:T(8,128)S(1)}, u32[]{:S(2)}, u32[]{:S(2)}) collective-permute-start(f32[136,128]{1,0:T(8,128)S(1)} %collective-permute-done.3.refs_4_), channel_id=1, source_target_pairs={{0,4},{4,0},{8,12},{12,8},{16,20},{20,16},{24,28},{28,24},{1,5},{5... | collective-permute-start | bytes 208904 | tf_op jit(solution)/shard_map/ppermute | solution.py:242
  15.6 0.9 %shard_map.74.ahead = f32[8,2,16,512]{3,2,1,0:T(8,128)} custom-call(f32[16,2,4096]{2,1,0:T(2,128)S(1)} %copy-done), custom_call_target="tpu_custom_call" | custom-call | bytes 1000000 | tf_op jit(solution)/shard_map/pallas_call | solution.py:296
  16.5 1.0 %shard_map.73 = (f32[32,128]{1,0:T(8,128)S(1)}, f32[5,128,128]{2,1,0:T(8,128)S(1)}) custom-call(s32[4]{0:T(128)S(1)} %copy-done.4, s32[4,4,64]{2,1,0:T(4,128)S(1)} %copy-done.2, f32[4,1,64]{2,1,0:T(1,128)S(1)} %copy-done.5, f32[4,1,64]{2,1,0:T(1,128)S(1)} %copy-done.6, s32[4,1,128]{2,1,0:T(1,128)S(1)} %bitcast.2), custom_call_target="tpu_custom_call" | custom-call | bytes 1000000 | tf_op jit(solution)/shard_map/pallas_call | solution.py:304
  17.5 0.0 collective-permute-done.refs_1_
  17.5 0.0 collective-permute-done.5.refs_6_
  17.6 0.0 collective-permute-done.6.refs_7_
  17.6 0.4 collective-permute-done.2.refs_3_
  18.0 1.3 %collective-permute-done.4.refs_5_ = f32[136,128]{1,0:T(8,128)S(1)} collective-permute-done((f32[136,128]{1,0:T(8,128)S(1)}, f32[136,128]{1,0:T(8,128)S(1)}, u32[]{:S(2)}, u32[]{:S(2)}) %collective-permute-start.4) | collective-permute-done | bytes 69664 | tf_op jit(solution)/shard_map/ppermute | solution.py:242
  19.3 0.8 %shard_map.76 = (f32[1056,128]{1,0:T(8,128)S(1)}, f32[928,128]{1,0:T(8,128)S(1)}) custom-call(s32[4]{0:T(128)S(1)} %copy-done.4, f32[32,128]{1,0:T(8,128)S(1)} %get-tuple-element.16.rows, f32[8,2,16,512]{3,2,1,0:T(8,128)} %shard_map.74.ahead, f32[136,128]{1,0:T(8,128)S(1)} %copy-done.1, f32[136,128]{1,0:T(8,128)S(1)} %collective-permute-done.refs_1_, ...), custom_call_target="tpu_custom_call" | custom-call | bytes 1000000 | tf_op jit(solution)/shard_map/pallas_call | solution.py:312
  20.1 1.6 %collective-permute-start.8 = (f32[928,128]{1,0:T(8,128)S(1)}, f32[928,128]{1,0:T(8,128)S(1)}, u32[]{:S(2)}, u32[]{:S(2)}) collective-permute-start(f32[928,128]{1,0:T(8,128)S(1)} %get-tuple-element.18), channel_id=1, source_target_pairs={{0,2},{1,3},{2,0},{3,1},{4,6},{5,7},{6,4},{7,5},{8,10},{9,11},{10,... | collective-permute-start | bytes 1425416 | tf_op jit(solution)/shard_map/ppermute | solution.py:319
  21.7 4.9 %all-to-all-start = ((f32[8,2,16,512]{3,2,1,0:T(8,128)}), f32[8,2,16,512]{3,2,1,0:T(8,128)S(1)}, u32[]{:S(2)}, u32[]{:S(2)}) async-start(f32[8,2,16,512]{3,2,1,0:T(8,128)} %shard_map.74.ahead), calls=%async_computation | async-start | bytes 1048576 | tf_op jit(solution)/shard_map/all_to_all | solution.py:302
  26.7 0.0 collective-permute-start.7
  26.7 3.6 %collective-permute-done.8.far = f32[928,128]{1,0:T(8,128)S(1)} collective-permute-done((f32[928,128]{1,0:T(8,128)S(1)}, f32[928,128]{1,0:T(8,128)S(1)}, u32[]{:S(2)}, u32[]{:S(2)}) %collective-permute-start.8) | collective-permute-done | bytes 475168 | tf_op jit(solution)/shard_map/ppermute | solution.py:319
  30.3 0.0 collective-permute-start.9
  30.3 0.0 collective-permute-done.7.near
  30.3 1.8 %collective-permute-done.9.cross = f32[928,128]{1,0:T(8,128)S(1)} collective-permute-done((f32[928,128]{1,0:T(8,128)S(1)}, f32[928,128]{1,0:T(8,128)S(1)}, u32[]{:S(2)}, u32[]{:S(2)}) %collective-permute-start.9) | collective-permute-done | bytes 475168 | tf_op jit(solution)/shard_map/ppermute | solution.py:321
  32.1 2.7 %shard_map.77.pull = f32[8,128]{1,0:T(8,128)S(1)} custom-call(f32[1056,128]{1,0:T(8,128)S(1)} %get-tuple-element.17.own, f32[1056,128]{1,0:T(8,128)S(1)} %collective-permute-done.7.near, f32[928,128]{1,0:T(8,128)S(1)} %collective-permute-done.8.far, f32[928,128]{1,0:T(8,128)S(1)} %collective-permute-done.9.cross, f32[5,128,128]{2,1,0:T(8,128)S(1)} %get-tuple-element.15.steps), custom_call_target="tpu_custom_call" | custom-call | bytes 100000 | tf_op jit(solution)/shard_map/pallas_call | solution.py:323
  34.9 2.2 %all-to-all-done.fields = f32[8,2,16,512]{3,2,1,0:T(8,128)S(1)} async-done(((f32[8,2,16,512]{3,2,1,0:T(8,128)}), f32[8,2,16,512]{3,2,1,0:T(8,128)S(1)}, u32[]{:S(2)}, u32[]{:S(2)}) %all-to-all-start) | async-done | bytes 524320 | tf_op jit(solution)/shard_map/all_to_all | solution.py:302
  37.1 0.6 %shard_map.78 = (f32[1,2,16,512]{3,2,1,0:T(8,128)S(1)}, f32[2,2,16,512]{3,2,1,0:T(8,128)S(1)}, f32[1,2,16,512]{3,2,1,0:T(8,128)S(1)}, f32[1,2,16,512]{3,2,1,0:T(...) custom-call(f32[5,128,128]{2,1,0:T(8,128)S(1)} %get-tuple-element.15.steps, ...), custom_call_target="tpu_custom_call" | custom-call | flops 100000000 | bytes 1000000 | tf_op jit(solution)/shard_map/pallas_call | solution.py:334
  37.7 0.1 collective-permute-start.13
  37.7 2.3 %collective-permute-start.10 = (f32[2,2,16,512]{3,2,1,0:T(8,128)S(1)}, f32[2,2,16,512]{3,2,1,0:T(8,128)S(1)}, u32[]{:S(2)}, u32[]{:S(2)}) collective-permute-start(f32[2,2,16,512]{3,2,1,0:T(8,128)S(1)} %get-tuple-element.20), channel_id=1, source_target_pairs={{0,24},{4,28},{8,16},{12,20},{16,8},{20,12},{24,0},{28,4},{1,25},{... | collective-permute-start | bytes 393224 | tf_op jit(solution)/shard_map/ppermute | solution.py:242
  40.0 1.2 %collective-permute-start.11 = (f32[1,2,16,512]{3,2,1,0:T(8,128)S(1)}, f32[1,2,16,512]{3,2,1,0:T(8,128)S(1)}, u32[]{:S(2)}, u32[]{:S(2)}) collective-permute-start(f32[1,2,16,512]{3,2,1,0:T(8,128)S(1)} %get-tuple-element.21), channel_id=1, source_target_pairs={{0,16},{4,20},{8,24},{12,28},{16,0},{20,4},{24,8},{28,12},{1,17},{... | collective-permute-start | bytes 196616 | tf_op jit(solution)/shard_map/ppermute | solution.py:242
  41.2 2.0 %collective-permute-start.12 = (f32[1,2,16,512]{3,2,1,0:T(8,128)S(1)}, f32[1,2,16,512]{3,2,1,0:T(8,128)S(1)}, u32[]{:S(2)}, u32[]{:S(2)}) collective-permute-start(f32[1,2,16,512]{3,2,1,0:T(8,128)S(1)} %get-tuple-element.22), channel_id=1, source_target_pairs={{0,20},{4,16},{8,28},{12,24},{16,4},{20,0},{24,12},{28,8},{1,21},{... | collective-permute-start | bytes 196616 | tf_op jit(solution)/shard_map/ppermute | solution.py:242
  43.2 1.2 %collective-permute-start.14 = (f32[1,2,16,512]{3,2,1,0:T(8,128)S(1)}, f32[1,2,16,512]{3,2,1,0:T(8,128)S(1)}, u32[]{:S(2)}, u32[]{:S(2)}) collective-permute-start(f32[1,2,16,512]{3,2,1,0:T(8,128)S(1)} %get-tuple-element.24), channel_id=1, source_target_pairs={{0,4},{4,0},{8,12},{12,8},{16,20},{20,16},{24,28},{28,24},{1,5},{5... | collective-permute-start | bytes 196616 | tf_op jit(solution)/shard_map/ppermute | solution.py:242
  44.4 1.5 %collective-permute-done.13.refs_4_ = f32[2,2,16,512]{3,2,1,0:T(8,128)S(1)} collective-permute-done((f32[2,2,16,512]{3,2,1,0:T(8,128)S(1)}, f32[2,2,16,512]{3,2,1,0:T(8,128)S(1)}, u32[]{:S(2)}, u32[]{:S(2)}) %collective-permute-start.13) | collective-permute-done | bytes 131104 | tf_op jit(solution)/shard_map/ppermute | solution.py:242
  46.0 0.0 collective-permute-start.15
  46.0 0.9 %collective-permute-done.10.refs_1_ = f32[2,2,16,512]{3,2,1,0:T(8,128)S(1)} collective-permute-done((f32[2,2,16,512]{3,2,1,0:T(8,128)S(1)}, f32[2,2,16,512]{3,2,1,0:T(8,128)S(1)}, u32[]{:S(2)}, u32[]{:S(2)}) %collective-permute-start.10) | collective-permute-done | bytes 131104 | tf_op jit(solution)/shard_map/ppermute | solution.py:242
  46.9 1.2 %collective-permute-start.16 = (f32[1,2,16,512]{3,2,1,0:T(8,128)S(1)}, f32[1,2,16,512]{3,2,1,0:T(8,128)S(1)}, u32[]{:S(2)}, u32[]{:S(2)}) collective-permute-start(f32[1,2,16,512]{3,2,1,0:T(8,128)S(1)} %slice.9), channel_id=1, source_target_pairs={{0,4},{4,0},{8,12},{12,8},{16,20},{20,16},{24,28},{28,24},{1,5},{5... | collective-permute-start | bytes 196616 | tf_op jit(solution)/shard_map/ppermute | solution.py:242
  48.1 2.8 %collective-permute-done.11.refs_2_ = f32[1,2,16,512]{3,2,1,0:T(8,128)S(1)} collective-permute-done((f32[1,2,16,512]{3,2,1,0:T(8,128)S(1)}, f32[1,2,16,512]{3,2,1,0:T(8,128)S(1)}, u32[]{:S(2)}, u32[]{:S(2)}) %collective-permute-start.11) | collective-permute-done | bytes 65568 | tf_op jit(solution)/shard_map/ppermute | solution.py:242
  50.9 1.1 %collective-permute-done.12.refs_3_ = f32[1,2,16,512]{3,2,1,0:T(8,128)S(1)} collective-permute-done((f32[1,2,16,512]{3,2,1,0:T(8,128)S(1)}, f32[1,2,16,512]{3,2,1,0:T(8,128)S(1)}, u32[]{:S(2)}, u32[]{:S(2)}) %collective-permute-start.12) | collective-permute-done | bytes 65568 | tf_op jit(solution)/shard_map/ppermute | solution.py:242
  51.9 0.0 collective-permute-done.14.refs_5_
  51.9 0.0 collective-permute-done.15.refs_6_
  52.0 0.0 collective-permute-done.16.refs_7_
  52.0 0.9 %shard_map.79 = f32[16,2,4096]{2,1,0:T(2,128)} custom-call(f32[1,2,16,512]{3,2,1,0:T(8,128)S(1)} %get-tuple-element.19.refs_0_, f32[2,2,16,512]{3,2,1,0:T(8,128)S(1)} %collective-permute-done.10.refs_1_, f32[1,2,16,512]{3,2,1,0:T(8,128)S(1)} %collective-permute-done.11.refs_2_, f32[1,2,16,512]{3,2,1,0:T(8,128)S(1)} %collective-permute-done.12.refs_3_, ...), custom_call_target="tpu_custom_call" | custom-call | bytes 1000000 | tf_op jit(solution)/shard_map/pallas_call | solution.py:344
  (11 shorter events, 0.0 us)
Async XLA Ops:
  0.0 15.6 %copy-start = (f32[16,2,4096]{2,1,0:T(2,128)S(1)}, f32[16,2,4096]{2,1,0:T(2,128)}, u32[]{:S(2)}) copy-start(f32[16,2,4096]{2,1,0:T(2,128)} %refs_4_.1) | copy-start | bytes 1572868
  2.5 14.1 %copy-start.2 = (s32[4,4,64]{2,1,0:T(4,128)S(1)}, s32[4,4,64]{2,1,0:T(4,128)}, u32[]{:S(2)}) copy-start(s32[4,4,64]{2,1,0:T(4,128)} %refs_2_.1) | copy-start | bytes 12292
  2.5 14.0 %copy-start.3 = (s32[4,1,1,128]{3,2,1,0:T(1,128)S(1)}, s32[4,1,1,128]{3,2,1,0:T(1,128)}, u32[]{:S(2)}) copy-start(s32[4,1,1,128]{3,2,1,0:T(1,128)} %param.13) | copy-start | bytes 6148
  2.5 14.0 %copy-start.4 = (s32[4]{0:T(128)S(1)}, s32[4]{0:T(128)}, u32[]{:S(2)}) copy-start(s32[4]{0:T(128)} %owner.3) | copy-start | bytes 52
  2.5 14.0 %copy-start.5 = (f32[4,1,64]{2,1,0:T(1,128)S(1)}, f32[4,1,64]{2,1,0:T(1,128)}, u32[]{:S(2)}) copy-start(f32[4,1,64]{2,1,0:T(1,128)} %values.1) | copy-start | bytes 3076
  2.5 14.0 %copy-start.6 = (f32[4,1,64]{2,1,0:T(1,128)S(1)}, f32[4,1,64]{2,1,0:T(1,128)}, u32[]{:S(2)}) copy-start(f32[4,1,64]{2,1,0:T(1,128)} %errors.1) | copy-start | bytes 3076
  2.5 16.8 %copy-start.1 = (f32[136,128]{1,0:T(8,128)S(1)}, f32[136,128]{1,0:T(8,128)}, u32[]{:S(2)}) copy-start(f32[136,128]{1,0:T(8,128)} %shard_map.75.refs_0_) | copy-start | bytes 208900
  2.5 11.0 %collective-permute-start.1 = (f32[136,128]{1,0:T(8,128)}, f32[136,128]{1,0:T(8,128)S(1)}, u32[]{:S(2)}, u32[]{:S(2)}) collective-permute-start(f32[136,128]{1,0:T(8,128)} %shard_map.75.refs_0_), channel_id=1, source_target_pairs={{0,8},{4,12},{8,0},{12,4},{16,24},{20,28},{24,16},{28,20},{1,9},{5... | collective-permute-start | bytes 208904 | tf_op jit(solution)/shard_map/ppermute | solution.py:242
  5.6 9.4 %collective-permute-start.3 = (f32[136,128]{1,0:T(8,128)}, f32[136,128]{1,0:T(8,128)S(1)}, u32[]{:S(2)}, u32[]{:S(2)}) collective-permute-start(f32[136,128]{1,0:T(8,128)} %shard_map.75.refs_0_), channel_id=1, source_target_pairs={{0,16},{4,20},{8,24},{12,28},{16,0},{20,4},{24,8},{28,12},{1,17},{... | collective-permute-start | bytes 208904 | tf_op jit(solution)/shard_map/ppermute | solution.py:242
  8.2 9.3 %collective-permute-start = (f32[136,128]{1,0:T(8,128)}, f32[136,128]{1,0:T(8,128)S(1)}, u32[]{:S(2)}, u32[]{:S(2)}) collective-permute-start(f32[136,128]{1,0:T(8,128)} %shard_map.75.refs_0_), channel_id=1, source_target_pairs={{0,4},{4,0},{8,12},{12,8},{16,20},{20,16},{24,28},{28,24},{1,5},{5... | collective-permute-start | bytes 208904 | tf_op jit(solution)/shard_map/ppermute | solution.py:242
  9.7 7.8 %collective-permute-start.5 = (f32[136,128]{1,0:T(8,128)}, f32[136,128]{1,0:T(8,128)S(1)}, u32[]{:S(2)}, u32[]{:S(2)}) collective-permute-start(f32[136,128]{1,0:T(8,128)} %shard_map.75.refs_0_), channel_id=1, source_target_pairs={{0,24},{4,28},{8,16},{12,20},{16,8},{20,12},{24,0},{28,4},{1,25},{... | collective-permute-start | bytes 208904 | tf_op jit(solution)/shard_map/ppermute | solution.py:242
  10.0 7.6 %collective-permute-start.6 = (f32[136,128]{1,0:T(8,128)}, f32[136,128]{1,0:T(8,128)S(1)}, u32[]{:S(2)}, u32[]{:S(2)}) collective-permute-start(f32[136,128]{1,0:T(8,128)} %shard_map.75.refs_0_), channel_id=1, source_target_pairs={{0,28},{4,24},{8,20},{12,16},{16,12},{20,8},{24,4},{28,0},{1,29},{... | collective-permute-start | bytes 208904 | tf_op jit(solution)/shard_map/ppermute | solution.py:242
  13.5 4.5 %collective-permute-start.2 = (f32[136,128]{1,0:T(8,128)S(1)}, f32[136,128]{1,0:T(8,128)S(1)}, u32[]{:S(2)}, u32[]{:S(2)}) collective-permute-start(f32[136,128]{1,0:T(8,128)S(1)} %collective-permute-done.1.refs_2_), channel_id=1, source_target_pairs={{0,4},{4,0},{8,12},{12,8},{16,20},{20,16},{24,28},{28,24},{1,5},{5... | collective-permute-start | bytes 208904 | tf_op jit(solution)/shard_map/ppermute | solution.py:242
  15.0 4.3 %collective-permute-start.4 = (f32[136,128]{1,0:T(8,128)S(1)}, f32[136,128]{1,0:T(8,128)S(1)}, u32[]{:S(2)}, u32[]{:S(2)}) collective-permute-start(f32[136,128]{1,0:T(8,128)S(1)} %collective-permute-done.3.refs_4_), channel_id=1, source_target_pairs={{0,4},{4,0},{8,12},{12,8},{16,20},{20,16},{24,28},{28,24},{1,5},{5... | collective-permute-start | bytes 208904 | tf_op jit(solution)/shard_map/ppermute | solution.py:242
  20.1 10.2 %collective-permute-start.8 = (f32[928,128]{1,0:T(8,128)S(1)}, f32[928,128]{1,0:T(8,128)S(1)}, u32[]{:S(2)}, u32[]{:S(2)}) collective-permute-start(f32[928,128]{1,0:T(8,128)S(1)} %get-tuple-element.18), channel_id=1, source_target_pairs={{0,2},{1,3},{2,0},{3,1},{4,6},{5,7},{6,4},{7,5},{8,10},{9,11},{10,... | collective-permute-start | bytes 1425416 | tf_op jit(solution)/shard_map/ppermute | solution.py:319
  21.7 15.4 %all-to-all-start = ((f32[8,2,16,512]{3,2,1,0:T(8,128)}), f32[8,2,16,512]{3,2,1,0:T(8,128)S(1)}, u32[]{:S(2)}, u32[]{:S(2)}) async-start(f32[8,2,16,512]{3,2,1,0:T(8,128)} %shard_map.74.ahead), calls=%async_computation | async-start | bytes 1048576 | tf_op jit(solution)/shard_map/all_to_all | solution.py:302
  26.7 3.7 %collective-permute-start.7 = (f32[1056,128]{1,0:T(8,128)S(1)}, f32[1056,128]{1,0:T(8,128)S(1)}, u32[]{:S(2)}, u32[]{:S(2)}) collective-permute-start(f32[1056,128]{1,0:T(8,128)S(1)} %get-tuple-element.17.own), channel_id=1, source_target_pairs={{0,1},{1,0},{2,3},{3,2},{4,5},{5,4},{6,7},{7,6},{8,9},{9,8},{10,11... | collective-permute-start | bytes 1622024 | tf_op jit(solution)/shard_map/ppermute | solution.py:320
  30.3 1.8 %collective-permute-start.9 = (f32[928,128]{1,0:T(8,128)S(1)}, f32[928,128]{1,0:T(8,128)S(1)}, u32[]{:S(2)}, u32[]{:S(2)}) collective-permute-start(f32[928,128]{1,0:T(8,128)S(1)} %collective-permute-done.8.far), channel_id=1, source_target_pairs={{0,1},{1,0},{2,3},{3,2},{4,5},{5,4},{6,7},{7,6},{8,9},{9,8},{10,11... | collective-permute-start | bytes 1425416 | tf_op jit(solution)/shard_map/ppermute | solution.py:321
  37.7 8.3 %collective-permute-start.13 = (f32[2,2,16,512]{3,2,1,0:T(8,128)S(1)}, f32[2,2,16,512]{3,2,1,0:T(8,128)S(1)}, u32[]{:S(2)}, u32[]{:S(2)}) collective-permute-start(f32[2,2,16,512]{3,2,1,0:T(8,128)S(1)} %get-tuple-element.23), channel_id=1, source_target_pairs={{0,8},{4,12},{8,0},{12,4},{16,24},{20,28},{24,16},{28,20},{1,9},{5... | collective-permute-start | bytes 393224 | tf_op jit(solution)/shard_map/ppermute | solution.py:242
  37.7 9.1 %collective-permute-start.10 = (f32[2,2,16,512]{3,2,1,0:T(8,128)S(1)}, f32[2,2,16,512]{3,2,1,0:T(8,128)S(1)}, u32[]{:S(2)}, u32[]{:S(2)}) collective-permute-start(f32[2,2,16,512]{3,2,1,0:T(8,128)S(1)} %get-tuple-element.20), channel_id=1, source_target_pairs={{0,24},{4,28},{8,16},{12,20},{16,8},{20,12},{24,0},{28,4},{1,25},{... | collective-permute-start | bytes 393224 | tf_op jit(solution)/shard_map/ppermute | solution.py:242
  40.0 10.8 %collective-permute-start.11 = (f32[1,2,16,512]{3,2,1,0:T(8,128)S(1)}, f32[1,2,16,512]{3,2,1,0:T(8,128)S(1)}, u32[]{:S(2)}, u32[]{:S(2)}) collective-permute-start(f32[1,2,16,512]{3,2,1,0:T(8,128)S(1)} %get-tuple-element.21), channel_id=1, source_target_pairs={{0,16},{4,20},{8,24},{12,28},{16,0},{20,4},{24,8},{28,12},{1,17},{... | collective-permute-start | bytes 196616 | tf_op jit(solution)/shard_map/ppermute | solution.py:242
  41.2 10.7 %collective-permute-start.12 = (f32[1,2,16,512]{3,2,1,0:T(8,128)S(1)}, f32[1,2,16,512]{3,2,1,0:T(8,128)S(1)}, u32[]{:S(2)}, u32[]{:S(2)}) collective-permute-start(f32[1,2,16,512]{3,2,1,0:T(8,128)S(1)} %get-tuple-element.22), channel_id=1, source_target_pairs={{0,20},{4,16},{8,28},{12,24},{16,4},{20,0},{24,12},{28,8},{1,21},{... | collective-permute-start | bytes 196616 | tf_op jit(solution)/shard_map/ppermute | solution.py:242
  43.2 8.8 %collective-permute-start.14 = (f32[1,2,16,512]{3,2,1,0:T(8,128)S(1)}, f32[1,2,16,512]{3,2,1,0:T(8,128)S(1)}, u32[]{:S(2)}, u32[]{:S(2)}) collective-permute-start(f32[1,2,16,512]{3,2,1,0:T(8,128)S(1)} %get-tuple-element.24), channel_id=1, source_target_pairs={{0,4},{4,0},{8,12},{12,8},{16,20},{20,16},{24,28},{28,24},{1,5},{5... | collective-permute-start | bytes 196616 | tf_op jit(solution)/shard_map/ppermute | solution.py:242
  46.0 6.0 %collective-permute-start.15 = (f32[1,2,16,512]{3,2,1,0:T(8,128)S(1)}, f32[1,2,16,512]{3,2,1,0:T(8,128)S(1)}, u32[]{:S(2)}, u32[]{:S(2)}) collective-permute-start(f32[1,2,16,512]{3,2,1,0:T(8,128)S(1)} %slice.8), channel_id=1, source_target_pairs={{0,4},{4,0},{8,12},{12,8},{16,20},{20,16},{24,28},{28,24},{1,5},{5... | collective-permute-start | bytes 196616 | tf_op jit(solution)/shard_map/ppermute | solution.py:242
  46.9 5.1 %collective-permute-start.16 = (f32[1,2,16,512]{3,2,1,0:T(8,128)S(1)}, f32[1,2,16,512]{3,2,1,0:T(8,128)S(1)}, u32[]{:S(2)}, u32[]{:S(2)}) collective-permute-start(f32[1,2,16,512]{3,2,1,0:T(8,128)S(1)} %slice.9), channel_id=1, source_target_pairs={{0,4},{4,0},{8,12},{12,8},{16,20},{20,16},{24,28},{28,24},{1,5},{5... | collective-permute-start | bytes 196616 | tf_op jit(solution)/shard_map/ppermute | solution.py:242

commit v14 on v13

--- a/solution.py
+++ b/solution.py
@@ -55,28 +55,33 @@
     owner, weights, offsets, ancestors, prior = refs[6:11]
     width = groups * count
     per = LANES // count
+    blocks = width // LANES
+    level_of = lax.broadcasted_iota(jnp.int32, (slab, depth, LANES), 1)
+    gains = []
+    for c in range(blocks):
+        gain = jnp.zeros((slab, depth, LANES), F32)
+        for level in range(depth):
+            row = jnp.concatenate(
+                [
+                    jnp.broadcast_to(weights[level : level + 1, g : g + 1], (1, count))
+                    for g in range(c * per, (c + 1) * per)
+                ],
+                axis=1,
+            )
+            gain = jnp.where(level_of == level, row[None], gain)
+        gains.append(gain.reshape(slab * depth, LANES))
     for b in range(NB):
         start = pl.multiple_of(owner[b] * block_cells, LANES)
-        levels = [prior[:, level, pl.ds(start, block_cells)] for level in range(depth)]
-        for c in range(width // LANES):
+        both = prior[:, :, pl.ds(start, block_cells)].reshape(slab * depth, block_cells)
+        for c in range(blocks):
             cell = jnp.concatenate([offsets[b, g : g + 1, :] for g in range(c * per, (c + 1) * per)], axis=1)
             low, high = lax.rem(cell, LANES), lax.div(cell, LANES)
-            total = jnp.zeros((slab, LANES), F32)
-            for level in range(depth):
-                found = jnp.zeros((slab, LANES), F32)
-                for h in range(block_cells // LANES):
-                    part = lane_take(levels[level][:, h * LANES : (h + 1) * LANES], low)
-                    found = jnp.where(high == h, part, found)
-                row = jnp.concatenate(
-                    [
-                        jnp.broadcast_to(weights[level : level + 1, g : g + 1], (1, count))
-                        for g in range(c * per, (c + 1) * per)
-                    ],
-                    axis=1,
-                )
-                total = total + found * row
-            line = (b * width // LANES + c) * slab
-            out[line : line + slab, :] = total
+            found = jnp.zeros((slab * depth, LANES), F32)
+            for h in range(block_cells // LANES):
+                part = lane_take(both[:, h * LANES : (h + 1) * LANES], low)
+                found = jnp.where(high == h, part, found)
+            line = (b * blocks + c) * slab
+            out[line : line + slab, :] = jnp.sum((found * gains[c]).reshape(slab, depth, LANES), axis=1)
     line = NB * width // LANES * slab
     out[line:, :] = jnp.zeros((out.shape[0] - line, LANES), F32)
     for b in range(NB):
@@ -234,8 +239,8 @@
     for i in range(n):
         region = i if len(pieces) == 1 else lax.bitwise_xor(block, ORDER[i])
         cells = pl.ds(pl.multiple_of(region * block_cells, LANES), block_cells)
-        for level in range(depth):
-            out[:, level, cells] = pieces[0][i, level] if len(pieces) == 1 else pieces[i][0, level]
+        piece, at = (pieces[0], i) if len(pieces) == 1 else (pieces[i], 0)
+        out[:, :, cells] = jnp.stack([piece[at, level] for level in range(depth)], axis=1)
 
 
 def hop(value, distance, n):

time: 53.1 us -> 53.3 us (level)
  no operation moved by 1% of the time
where the time goes in v14:
time: 53.3 us; the launch traced here: 53.1 us
  starting transfers between devices  27.5 us (52%)
  waiting for transfers between devices  15.8 us (30%)
  Pallas kernels  9.53 us (18%)
    ppermute x14, starting transfers between devices, hop(): return lax.ppermute(value, 'grid', [(j, j ^ distance) for j in range(n)])  21 us
    ppermute x14, waiting for transfers between devices, hop(): return lax.ppermute(value, 'grid', [(j, j ^ distance) for j in range(n)])  8.13 us
    all_to_all x1, starting transfers between devices, body(): fields = lax.all_to_all(send, 'grid', 0, 0, tiled=True)  4.95 us
    ppermute x1, waiting for transfers between devices, body(): far = lax.ppermute(slim, 'lev', [(j, j ^ 2) for j in range(lev)])  3.64 us
    pallas_call x1, Pallas kernels, body(): call(functools.partial(chain_kernel, (members, groups, count)), shape((8,...  2.72 us
    pallas_call x1, Pallas kernels, body(): call(functools.partial(pick_kernel, (slab, depth, block_cells, groups, co...  2.39 us
    all_to_all x1, waiting for transfers between devices, body(): fields = lax.all_to_all(send, 'grid', 0, 0, tiled=True)  2.22 us
    ppermute x1, waiting for transfers between devices, body(): cross = lax.ppermute(far, 'lev', [(j, j ^ 1) for j in range(lev)])  1.83 us
  transfers between devices with their start and end apart: 18, of which 9 were waited for; matrix products, arithmetic and copies ran while one was open for 0% of the time, Pallas kernels for 9%

profile of v14, /device:TPU:0, one launch (start us, length us, event | category | flops | bytes accessed | tf_op | source)
XLA Modules:
  0.0 53.1 jit_solution(4111562812450354568)
XLA Ops:
  0.0 2.4 %shard_map.75.refs_0_ = f32[136,128]{1,0:T(8,128)} custom-call(s32[4]{0:T(128)} %owner.3, f32[2,4]{1,0:T(2,128)} %refs_1_.1, s32[4,4,64]{2,1,0:T(4,128)} %refs_2_.1, s32[4,1,128]{2,1,0:T(1,128)} %bitcast.1, f32[16,2,4096]{2,1,0:T(2,128)} %refs_4_.1), custom_call_target="tpu_custom_call" | custom-call | bytes 1000000 | tf_op jit(solution)/shard_map/pallas_call | solution.py:285
  2.4 0.0 copy-start.2
  2.4 0.0 copy-start.3
  2.4 0.0 copy-start.4
  2.4 0.0 copy-start.5
  2.4 0.0 copy-start.6
  2.5 3.1 %collective-permute-start.1 = (f32[136,128]{1,0:T(8,128)}, f32[136,128]{1,0:T(8,128)S(1)}, u32[]{:S(2)}, u32[]{:S(2)}) collective-permute-start(f32[136,128]{1,0:T(8,128)} %shard_map.75.refs_0_), channel_id=1, source_target_pairs={{0,8},{4,12},{8,0},{12,4},{16,24},{20,28},{24,16},{28,20},{1,9},{5... | collective-permute-start | bytes 208904 | tf_op jit(solution)/shard_map/ppermute | solution.py:247
  5.6 2.6 %collective-permute-start.3 = (f32[136,128]{1,0:T(8,128)}, f32[136,128]{1,0:T(8,128)S(1)}, u32[]{:S(2)}, u32[]{:S(2)}) collective-permute-start(f32[136,128]{1,0:T(8,128)} %shard_map.75.refs_0_), channel_id=1, source_target_pairs={{0,16},{4,20},{8,24},{12,28},{16,0},{20,4},{24,8},{28,12},{1,17},{... | collective-permute-start | bytes 208904 | tf_op jit(solution)/shard_map/ppermute | solution.py:247
  8.2 1.5 %collective-permute-start = (f32[136,128]{1,0:T(8,128)}, f32[136,128]{1,0:T(8,128)S(1)}, u32[]{:S(2)}, u32[]{:S(2)}) collective-permute-start(f32[136,128]{1,0:T(8,128)} %shard_map.75.refs_0_), channel_id=1, source_target_pairs={{0,4},{4,0},{8,12},{12,8},{16,20},{20,16},{24,28},{28,24},{1,5},{5... | collective-permute-start | bytes 208904 | tf_op jit(solution)/shard_map/ppermute | solution.py:247
  9.7 0.2 collective-permute-start.5
  9.9 3.5 %collective-permute-start.6 = (f32[136,128]{1,0:T(8,128)}, f32[136,128]{1,0:T(8,128)S(1)}, u32[]{:S(2)}, u32[]{:S(2)}) collective-permute-start(f32[136,128]{1,0:T(8,128)} %shard_map.75.refs_0_), channel_id=1, source_target_pairs={{0,28},{4,24},{8,20},{12,16},{16,12},{20,8},{24,4},{28,0},{1,29},{... | collective-permute-start | bytes 208904 | tf_op jit(solution)/shard_map/ppermute | solution.py:247
  13.4 0.0 collective-permute-done.1.refs_2_
  13.4 1.5 %collective-permute-start.2 = (f32[136,128]{1,0:T(8,128)S(1)}, f32[136,128]{1,0:T(8,128)S(1)}, u32[]{:S(2)}, u32[]{:S(2)}) collective-permute-start(f32[136,128]{1,0:T(8,128)S(1)} %collective-permute-done.1.refs_2_), channel_id=1, source_target_pairs={{0,4},{4,0},{8,12},{12,8},{16,20},{20,16},{24,28},{28,24},{1,5},{5... | collective-permute-start | bytes 208904 | tf_op jit(solution)/shard_map/ppermute | solution.py:247
  15.0 0.0 collective-permute-done.3.refs_4_
  15.0 0.6 %collective-permute-start.4 = (f32[136,128]{1,0:T(8,128)S(1)}, f32[136,128]{1,0:T(8,128)S(1)}, u32[]{:S(2)}, u32[]{:S(2)}) collective-permute-start(f32[136,128]{1,0:T(8,128)S(1)} %collective-permute-done.3.refs_4_), channel_id=1, source_target_pairs={{0,4},{4,0},{8,12},{12,8},{16,20},{20,16},{24,28},{28,24},{1,5},{5... | collective-permute-start | bytes 208904 | tf_op jit(solution)/shard_map/ppermute | solution.py:247
  15.6 0.9 %shard_map.74.ahead = f32[8,2,16,512]{3,2,1,0:T(8,128)} custom-call(f32[16,2,4096]{2,1,0:T(2,128)S(1)} %copy-done), custom_call_target="tpu_custom_call" | custom-call | bytes 1000000 | tf_op jit(solution)/shard_map/pallas_call | solution.py:301
  16.5 1.0 %shard_map.73 = (f32[32,128]{1,0:T(8,128)S(1)}, f32[5,128,128]{2,1,0:T(8,128)S(1)}) custom-call(s32[4]{0:T(128)S(1)} %copy-done.4, s32[4,4,64]{2,1,0:T(4,128)S(1)} %copy-done.2, f32[4,1,64]{2,1,0:T(1,128)S(1)} %copy-done.5, f32[4,1,64]{2,1,0:T(1,128)S(1)} %copy-done.6, s32[4,1,128]{2,1,0:T(1,128)S(1)} %bitcast.2), custom_call_target="tpu_custom_call" | custom-call | bytes 1000000 | tf_op jit(solution)/shard_map/pallas_call | solution.py:309
  17.5 0.0 collective-permute-done.refs_1_
  17.5 0.0 collective-permute-done.5.refs_6_
  17.5 0.0 collective-permute-done.6.refs_7_
  17.5 0.4 collective-permute-done.2.refs_3_
  18.0 1.3 %collective-permute-done.4.refs_5_ = f32[136,128]{1,0:T(8,128)S(1)} collective-permute-done((f32[136,128]{1,0:T(8,128)S(1)}, f32[136,128]{1,0:T(8,128)S(1)}, u32[]{:S(2)}, u32[]{:S(2)}) %collective-permute-start.4) | collective-permute-done | bytes 69664 | tf_op jit(solution)/shard_map/ppermute | solution.py:247
  19.3 0.8 %shard_map.76 = (f32[1056,128]{1,0:T(8,128)S(1)}, f32[928,128]{1,0:T(8,128)S(1)}) custom-call(s32[4]{0:T(128)S(1)} %copy-done.4, f32[32,128]{1,0:T(8,128)S(1)} %get-tuple-element.16.rows, f32[8,2,16,512]{3,2,1,0:T(8,128)} %shard_map.74.ahead, f32[136,128]{1,0:T(8,128)S(1)} %copy-done.1, f32[136,128]{1,0:T(8,128)S(1)} %collective-permute-done.refs_1_, ...), custom_call_target="tpu_custom_call" | custom-call | bytes 1000000 | tf_op jit(solution)/shard_map/pallas_call | solution.py:317
  20.1 1.6 %collective-permute-start.8 = (f32[928,128]{1,0:T(8,128)S(1)}, f32[928,128]{1,0:T(8,128)S(1)}, u32[]{:S(2)}, u32[]{:S(2)}) collective-permute-start(f32[928,128]{1,0:T(8,128)S(1)} %get-tuple-element.18), channel_id=1, source_target_pairs={{0,2},{1,3},{2,0},{3,1},{4,6},{5,7},{6,4},{7,5},{8,10},{9,11},{10,... | collective-permute-start | bytes 1425416 | tf_op jit(solution)/shard_map/ppermute | solution.py:324
  21.6 4.9 %all-to-all-start = ((f32[8,2,16,512]{3,2,1,0:T(8,128)}), f32[8,2,16,512]{3,2,1,0:T(8,128)S(1)}, u32[]{:S(2)}, u32[]{:S(2)}) async-start(f32[8,2,16,512]{3,2,1,0:T(8,128)} %shard_map.74.ahead), calls=%async_computation | async-start | bytes 1048576 | tf_op jit(solution)/shard_map/all_to_all | solution.py:307
  26.6 0.0 collective-permute-start.7
  26.6 3.6 %collective-permute-done.8.far = f32[928,128]{1,0:T(8,128)S(1)} collective-permute-done((f32[928,128]{1,0:T(8,128)S(1)}, f32[928,128]{1,0:T(8,128)S(1)}, u32[]{:S(2)}, u32[]{:S(2)}) %collective-permute-start.8) | collective-permute-done | bytes 475168 | tf_op jit(solution)/shard_map/ppermute | solution.py:324
  30.2 0.0 collective-permute-start.9
  30.2 0.0 collective-permute-done.7.near
  30.2 1.8 %collective-permute-done.9.cross = f32[928,128]{1,0:T(8,128)S(1)} collective-permute-done((f32[928,128]{1,0:T(8,128)S(1)}, f32[928,128]{1,0:T(8,128)S(1)}, u32[]{:S(2)}, u32[]{:S(2)}) %collective-permute-start.9) | collective-permute-done | bytes 475168 | tf_op jit(solution)/shard_map/ppermute | solution.py:326
  32.1 2.7 %shard_map.77.pull = f32[8,128]{1,0:T(8,128)S(1)} custom-call(f32[1056,128]{1,0:T(8,128)S(1)} %get-tuple-element.17.own, f32[1056,128]{1,0:T(8,128)S(1)} %collective-permute-done.7.near, f32[928,128]{1,0:T(8,128)S(1)} %collective-permute-done.8.far, f32[928,128]{1,0:T(8,128)S(1)} %collective-permute-done.9.cross, f32[5,128,128]{2,1,0:T(8,128)S(1)} %get-tuple-element.15.steps), custom_call_target="tpu_custom_call" | custom-call | bytes 100000 | tf_op jit(solution)/shard_map/pallas_call | solution.py:328
  34.8 2.2 %all-to-all-done.fields = f32[8,2,16,512]{3,2,1,0:T(8,128)S(1)} async-done(((f32[8,2,16,512]{3,2,1,0:T(8,128)}), f32[8,2,16,512]{3,2,1,0:T(8,128)S(1)}, u32[]{:S(2)}, u32[]{:S(2)}) %all-to-all-start) | async-done | bytes 524320 | tf_op jit(solution)/shard_map/all_to_all | solution.py:307
  37.0 0.6 %shard_map.78 = (f32[1,2,16,512]{3,2,1,0:T(8,128)S(1)}, f32[2,2,16,512]{3,2,1,0:T(8,128)S(1)}, f32[1,2,16,512]{3,2,1,0:T(8,128)S(1)}, f32[1,2,16,512]{3,2,1,0:T(...) custom-call(f32[5,128,128]{2,1,0:T(8,128)S(1)} %get-tuple-element.15.steps, ...), custom_call_target="tpu_custom_call" | custom-call | flops 100000000 | bytes 1000000 | tf_op jit(solution)/shard_map/pallas_call | solution.py:339
  37.6 0.1 collective-permute-start.13
  37.7 2.3 %collective-permute-start.10 = (f32[2,2,16,512]{3,2,1,0:T(8,128)S(1)}, f32[2,2,16,512]{3,2,1,0:T(8,128)S(1)}, u32[]{:S(2)}, u32[]{:S(2)}) collective-permute-start(f32[2,2,16,512]{3,2,1,0:T(8,128)S(1)} %get-tuple-element.20), channel_id=1, source_target_pairs={{0,24},{4,28},{8,16},{12,20},{16,8},{20,12},{24,0},{28,4},{1,25},{... | collective-permute-start | bytes 393224 | tf_op jit(solution)/shard_map/ppermute | solution.py:247
  40.0 1.2 %collective-permute-start.11 = (f32[1,2,16,512]{3,2,1,0:T(8,128)S(1)}, f32[1,2,16,512]{3,2,1,0:T(8,128)S(1)}, u32[]{:S(2)}, u32[]{:S(2)}) collective-permute-start(f32[1,2,16,512]{3,2,1,0:T(8,128)S(1)} %get-tuple-element.21), channel_id=1, source_target_pairs={{0,16},{4,20},{8,24},{12,28},{16,0},{20,4},{24,8},{28,12},{1,17},{... | collective-permute-start | bytes 196616 | tf_op jit(solution)/shard_map/ppermute | solution.py:247
  41.2 2.0 %collective-permute-start.12 = (f32[1,2,16,512]{3,2,1,0:T(8,128)S(1)}, f32[1,2,16,512]{3,2,1,0:T(8,128)S(1)}, u32[]{:S(2)}, u32[]{:S(2)}) collective-permute-start(f32[1,2,16,512]{3,2,1,0:T(8,128)S(1)} %get-tuple-element.22), channel_id=1, source_target_pairs={{0,20},{4,16},{8,28},{12,24},{16,4},{20,0},{24,12},{28,8},{1,21},{... | collective-permute-start | bytes 196616 | tf_op jit(solution)/shard_map/ppermute | solution.py:247
  43.1 1.2 %collective-permute-start.14 = (f32[1,2,16,512]{3,2,1,0:T(8,128)S(1)}, f32[1,2,16,512]{3,2,1,0:T(8,128)S(1)}, u32[]{:S(2)}, u32[]{:S(2)}) collective-permute-start(f32[1,2,16,512]{3,2,1,0:T(8,128)S(1)} %get-tuple-element.24), channel_id=1, source_target_pairs={{0,4},{4,0},{8,12},{12,8},{16,20},{20,16},{24,28},{28,24},{1,5},{5... | collective-permute-start | bytes 196616 | tf_op jit(solution)/shard_map/ppermute | solution.py:247
  44.4 1.5 %collective-permute-done.13.refs_4_ = f32[2,2,16,512]{3,2,1,0:T(8,128)S(1)} collective-permute-done((f32[2,2,16,512]{3,2,1,0:T(8,128)S(1)}, f32[2,2,16,512]{3,2,1,0:T(8,128)S(1)}, u32[]{:S(2)}, u32[]{:S(2)}) %collective-permute-start.13) | collective-permute-done | bytes 131104 | tf_op jit(solution)/shard_map/ppermute | solution.py:247
  45.9 0.0 collective-permute-start.15
  45.9 0.9 %collective-permute-done.10.refs_1_ = f32[2,2,16,512]{3,2,1,0:T(8,128)S(1)} collective-permute-done((f32[2,2,16,512]{3,2,1,0:T(8,128)S(1)}, f32[2,2,16,512]{3,2,1,0:T(8,128)S(1)}, u32[]{:S(2)}, u32[]{:S(2)}) %collective-permute-start.10) | collective-permute-done | bytes 131104 | tf_op jit(solution)/shard_map/ppermute | solution.py:247
  46.8 1.2 %collective-permute-start.16 = (f32[1,2,16,512]{3,2,1,0:T(8,128)S(1)}, f32[1,2,16,512]{3,2,1,0:T(8,128)S(1)}, u32[]{:S(2)}, u32[]{:S(2)}) collective-permute-start(f32[1,2,16,512]{3,2,1,0:T(8,128)S(1)} %slice.9), channel_id=1, source_target_pairs={{0,4},{4,0},{8,12},{12,8},{16,20},{20,16},{24,28},{28,24},{1,5},{5... | collective-permute-start | bytes 196616 | tf_op jit(solution)/shard_map/ppermute | solution.py:247
  48.0 2.8 %collective-permute-done.11.refs_2_ = f32[1,2,16,512]{3,2,1,0:T(8,128)S(1)} collective-permute-done((f32[1,2,16,512]{3,2,1,0:T(8,128)S(1)}, f32[1,2,16,512]{3,2,1,0:T(8,128)S(1)}, u32[]{:S(2)}, u32[]{:S(2)}) %collective-permute-start.11) | collective-permute-done | bytes 65568 | tf_op jit(solution)/shard_map/ppermute | solution.py:247
  50.8 1.1 %collective-permute-done.12.refs_3_ = f32[1,2,16,512]{3,2,1,0:T(8,128)S(1)} collective-permute-done((f32[1,2,16,512]{3,2,1,0:T(8,128)S(1)}, f32[1,2,16,512]{3,2,1,0:T(8,128)S(1)}, u32[]{:S(2)}, u32[]{:S(2)}) %collective-permute-start.12) | collective-permute-done | bytes 65568 | tf_op jit(solution)/shard_map/ppermute | solution.py:247
  51.9 0.0 collective-permute-done.14.refs_5_
  51.9 0.0 collective-permute-done.15.refs_6_
  51.9 0.0 collective-permute-done.16.refs_7_
  51.9 1.2 %shard_map.79 = f32[16,2,4096]{2,1,0:T(2,128)} custom-call(f32[1,2,16,512]{3,2,1,0:T(8,128)S(1)} %get-tuple-element.19.refs_0_, f32[2,2,16,512]{3,2,1,0:T(8,128)S(1)} %collective-permute-done.10.refs_1_, f32[1,2,16,512]{3,2,1,0:T(8,128)S(1)} %collective-permute-done.11.refs_2_, f32[1,2,16,512]{3,2,1,0:T(8,128)S(1)} %collective-permute-done.12.refs_3_, ...), custom_call_target="tpu_custom_call" | custom-call | bytes 1000000 | tf_op jit(solution)/shard_map/pallas_call | solution.py:349
  (11 shorter events, 0.0 us)
Async XLA Ops:
  0.0 15.6 %copy-start = (f32[16,2,4096]{2,1,0:T(2,128)S(1)}, f32[16,2,4096]{2,1,0:T(2,128)}, u32[]{:S(2)}) copy-start(f32[16,2,4096]{2,1,0:T(2,128)} %refs_4_.1) | copy-start | bytes 1572868
  2.4 14.1 %copy-start.2 = (s32[4,4,64]{2,1,0:T(4,128)S(1)}, s32[4,4,64]{2,1,0:T(4,128)}, u32[]{:S(2)}) copy-start(s32[4,4,64]{2,1,0:T(4,128)} %refs_2_.1) | copy-start | bytes 12292
  2.4 14.0 %copy-start.3 = (s32[4,1,1,128]{3,2,1,0:T(1,128)S(1)}, s32[4,1,1,128]{3,2,1,0:T(1,128)}, u32[]{:S(2)}) copy-start(s32[4,1,1,128]{3,2,1,0:T(1,128)} %param.13) | copy-start | bytes 6148
  2.4 14.0 %copy-start.4 = (s32[4]{0:T(128)S(1)}, s32[4]{0:T(128)}, u32[]{:S(2)}) copy-start(s32[4]{0:T(128)} %owner.3) | copy-start | bytes 52
  2.4 14.0 %copy-start.5 = (f32[4,1,64]{2,1,0:T(1,128)S(1)}, f32[4,1,64]{2,1,0:T(1,128)}, u32[]{:S(2)}) copy-start(f32[4,1,64]{2,1,0:T(1,128)} %values.1) | copy-start | bytes 3076
  2.4 14.0 %copy-start.6 = (f32[4,1,64]{2,1,0:T(1,128)S(1)}, f32[4,1,64]{2,1,0:T(1,128)}, u32[]{:S(2)}) copy-start(f32[4,1,64]{2,1,0:T(1,128)} %errors.1) | copy-start | bytes 3076
  2.5 16.8 %copy-start.1 = (f32[136,128]{1,0:T(8,128)S(1)}, f32[136,128]{1,0:T(8,128)}, u32[]{:S(2)}) copy-start(f32[136,128]{1,0:T(8,128)} %shard_map.75.refs_0_) | copy-start | bytes 208900
  2.5 11.0 %collective-permute-start.1 = (f32[136,128]{1,0:T(8,128)}, f32[136,128]{1,0:T(8,128)S(1)}, u32[]{:S(2)}, u32[]{:S(2)}) collective-permute-start(f32[136,128]{1,0:T(8,128)} %shard_map.75.refs_0_), channel_id=1, source_target_pairs={{0,8},{4,12},{8,0},{12,4},{16,24},{20,28},{24,16},{28,20},{1,9},{5... | collective-permute-start | bytes 208904 | tf_op jit(solution)/shard_map/ppermute | solution.py:247
  5.6 9.4 %collective-permute-start.3 = (f32[136,128]{1,0:T(8,128)}, f32[136,128]{1,0:T(8,128)S(1)}, u32[]{:S(2)}, u32[]{:S(2)}) collective-permute-start(f32[136,128]{1,0:T(8,128)} %shard_map.75.refs_0_), channel_id=1, source_target_pairs={{0,16},{4,20},{8,24},{12,28},{16,0},{20,4},{24,8},{28,12},{1,17},{... | collective-permute-start | bytes 208904 | tf_op jit(solution)/shard_map/ppermute | solution.py:247
  8.2 9.3 %collective-permute-start = (f32[136,128]{1,0:T(8,128)}, f32[136,128]{1,0:T(8,128)S(1)}, u32[]{:S(2)}, u32[]{:S(2)}) collective-permute-start(f32[136,128]{1,0:T(8,128)} %shard_map.75.refs_0_), channel_id=1, source_target_pairs={{0,4},{4,0},{8,12},{12,8},{16,20},{20,16},{24,28},{28,24},{1,5},{5... | collective-permute-start | bytes 208904 | tf_op jit(solution)/shard_map/ppermute | solution.py:247
  9.7 7.8 %collective-permute-start.5 = (f32[136,128]{1,0:T(8,128)}, f32[136,128]{1,0:T(8,128)S(1)}, u32[]{:S(2)}, u32[]{:S(2)}) collective-permute-start(f32[136,128]{1,0:T(8,128)} %shard_map.75.refs_0_), channel_id=1, source_target_pairs={{0,24},{4,28},{8,16},{12,20},{16,8},{20,12},{24,0},{28,4},{1,25},{... | collective-permute-start | bytes 208904 | tf_op jit(solution)/shard_map/ppermute | solution.py:247
  9.9 7.6 %collective-permute-start.6 = (f32[136,128]{1,0:T(8,128)}, f32[136,128]{1,0:T(8,128)S(1)}, u32[]{:S(2)}, u32[]{:S(2)}) collective-permute-start(f32[136,128]{1,0:T(8,128)} %shard_map.75.refs_0_), channel_id=1, source_target_pairs={{0,28},{4,24},{8,20},{12,16},{16,12},{20,8},{24,4},{28,0},{1,29},{... | collective-permute-start | bytes 208904 | tf_op jit(solution)/shard_map/ppermute | solution.py:247
  13.4 4.5 %collective-permute-start.2 = (f32[136,128]{1,0:T(8,128)S(1)}, f32[136,128]{1,0:T(8,128)S(1)}, u32[]{:S(2)}, u32[]{:S(2)}) collective-permute-start(f32[136,128]{1,0:T(8,128)S(1)} %collective-permute-done.1.refs_2_), channel_id=1, source_target_pairs={{0,4},{4,0},{8,12},{12,8},{16,20},{20,16},{24,28},{28,24},{1,5},{5... | collective-permute-start | bytes 208904 | tf_op jit(solution)/shard_map/ppermute | solution.py:247
  15.0 4.3 %collective-permute-start.4 = (f32[136,128]{1,0:T(8,128)S(1)}, f32[136,128]{1,0:T(8,128)S(1)}, u32[]{:S(2)}, u32[]{:S(2)}) collective-permute-start(f32[136,128]{1,0:T(8,128)S(1)} %collective-permute-done.3.refs_4_), channel_id=1, source_target_pairs={{0,4},{4,0},{8,12},{12,8},{16,20},{20,16},{24,28},{28,24},{1,5},{5... | collective-permute-start | bytes 208904 | tf_op jit(solution)/shard_map/ppermute | solution.py:247
  20.1 10.2 %collective-permute-start.8 = (f32[928,128]{1,0:T(8,128)S(1)}, f32[928,128]{1,0:T(8,128)S(1)}, u32[]{:S(2)}, u32[]{:S(2)}) collective-permute-start(f32[928,128]{1,0:T(8,128)S(1)} %get-tuple-element.18), channel_id=1, source_target_pairs={{0,2},{1,3},{2,0},{3,1},{4,6},{5,7},{6,4},{7,5},{8,10},{9,11},{10,... | collective-permute-start | bytes 1425416 | tf_op jit(solution)/shard_map/ppermute | solution.py:324
  21.6 15.4 %all-to-all-start = ((f32[8,2,16,512]{3,2,1,0:T(8,128)}), f32[8,2,16,512]{3,2,1,0:T(8,128)S(1)}, u32[]{:S(2)}, u32[]{:S(2)}) async-start(f32[8,2,16,512]{3,2,1,0:T(8,128)} %shard_map.74.ahead), calls=%async_computation | async-start | bytes 1048576 | tf_op jit(solution)/shard_map/all_to_all | solution.py:307
  26.6 3.7 %collective-permute-start.7 = (f32[1056,128]{1,0:T(8,128)S(1)}, f32[1056,128]{1,0:T(8,128)S(1)}, u32[]{:S(2)}, u32[]{:S(2)}) collective-permute-start(f32[1056,128]{1,0:T(8,128)S(1)} %get-tuple-element.17.own), channel_id=1, source_target_pairs={{0,1},{1,0},{2,3},{3,2},{4,5},{5,4},{6,7},{7,6},{8,9},{9,8},{10,11... | collective-permute-start | bytes 1622024 | tf_op jit(solution)/shard_map/ppermute | solution.py:325
  30.2 1.8 %collective-permute-start.9 = (f32[928,128]{1,0:T(8,128)S(1)}, f32[928,128]{1,0:T(8,128)S(1)}, u32[]{:S(2)}, u32[]{:S(2)}) collective-permute-start(f32[928,128]{1,0:T(8,128)S(1)} %collective-permute-done.8.far), channel_id=1, source_target_pairs={{0,1},{1,0},{2,3},{3,2},{4,5},{5,4},{6,7},{7,6},{8,9},{9,8},{10,11... | collective-permute-start | bytes 1425416 | tf_op jit(solution)/shard_map/ppermute | solution.py:326
  37.6 8.3 %collective-permute-start.13 = (f32[2,2,16,512]{3,2,1,0:T(8,128)S(1)}, f32[2,2,16,512]{3,2,1,0:T(8,128)S(1)}, u32[]{:S(2)}, u32[]{:S(2)}) collective-permute-start(f32[2,2,16,512]{3,2,1,0:T(8,128)S(1)} %get-tuple-element.23), channel_id=1, source_target_pairs={{0,8},{4,12},{8,0},{12,4},{16,24},{20,28},{24,16},{28,20},{1,9},{5... | collective-permute-start | bytes 393224 | tf_op jit(solution)/shard_map/ppermute | solution.py:247
  37.7 9.1 %collective-permute-start.10 = (f32[2,2,16,512]{3,2,1,0:T(8,128)S(1)}, f32[2,2,16,512]{3,2,1,0:T(8,128)S(1)}, u32[]{:S(2)}, u32[]{:S(2)}) collective-permute-start(f32[2,2,16,512]{3,2,1,0:T(8,128)S(1)} %get-tuple-element.20), channel_id=1, source_target_pairs={{0,24},{4,28},{8,16},{12,20},{16,8},{20,12},{24,0},{28,4},{1,25},{... | collective-permute-start | bytes 393224 | tf_op jit(solution)/shard_map/ppermute | solution.py:247
  40.0 10.8 %collective-permute-start.11 = (f32[1,2,16,512]{3,2,1,0:T(8,128)S(1)}, f32[1,2,16,512]{3,2,1,0:T(8,128)S(1)}, u32[]{:S(2)}, u32[]{:S(2)}) collective-permute-start(f32[1,2,16,512]{3,2,1,0:T(8,128)S(1)} %get-tuple-element.21), channel_id=1, source_target_pairs={{0,16},{4,20},{8,24},{12,28},{16,0},{20,4},{24,8},{28,12},{1,17},{... | collective-permute-start | bytes 196616 | tf_op jit(solution)/shard_map/ppermute | solution.py:247
  41.2 10.7 %collective-permute-start.12 = (f32[1,2,16,512]{3,2,1,0:T(8,128)S(1)}, f32[1,2,16,512]{3,2,1,0:T(8,128)S(1)}, u32[]{:S(2)}, u32[]{:S(2)}) collective-permute-start(f32[1,2,16,512]{3,2,1,0:T(8,128)S(1)} %get-tuple-element.22), channel_id=1, source_target_pairs={{0,20},{4,16},{8,28},{12,24},{16,4},{20,0},{24,12},{28,8},{1,21},{... | collective-permute-start | bytes 196616 | tf_op jit(solution)/shard_map/ppermute | solution.py:247
  43.1 8.8 %collective-permute-start.14 = (f32[1,2,16,512]{3,2,1,0:T(8,128)S(1)}, f32[1,2,16,512]{3,2,1,0:T(8,128)S(1)}, u32[]{:S(2)}, u32[]{:S(2)}) collective-permute-start(f32[1,2,16,512]{3,2,1,0:T(8,128)S(1)} %get-tuple-element.24), channel_id=1, source_target_pairs={{0,4},{4,0},{8,12},{12,8},{16,20},{20,16},{24,28},{28,24},{1,5},{5... | collective-permute-start | bytes 196616 | tf_op jit(solution)/shard_map/ppermute | solution.py:247
  45.9 6.0 %collective-permute-start.15 = (f32[1,2,16,512]{3,2,1,0:T(8,128)S(1)}, f32[1,2,16,512]{3,2,1,0:T(8,128)S(1)}, u32[]{:S(2)}, u32[]{:S(2)}) collective-permute-start(f32[1,2,16,512]{3,2,1,0:T(8,128)S(1)} %slice.8), channel_id=1, source_target_pairs={{0,4},{4,0},{8,12},{12,8},{16,20},{20,16},{24,28},{28,24},{1,5},{5... | collective-permute-start | bytes 196616 | tf_op jit(solution)/shard_map/ppermute | solution.py:247
  46.8 5.1 %collective-permute-start.16 = (f32[1,2,16,512]{3,2,1,0:T(8,128)S(1)}, f32[1,2,16,512]{3,2,1,0:T(8,128)S(1)}, u32[]{:S(2)}, u32[]{:S(2)}) collective-permute-start(f32[1,2,16,512]{3,2,1,0:T(8,128)S(1)} %slice.9), channel_id=1, source_target_pairs={{0,4},{4,0},{8,12},{12,8},{16,20},{20,16},{24,28},{28,24},{1,5},{5... | collective-permute-start | bytes 196616 | tf_op jit(solution)/shard_map/ppermute | solution.py:247

commit v15 on v14

--- a/solution.py
+++ b/solution.py
@@ -16,8 +16,8 @@
 PLACE = pl.BlockSpec(memory_space=pl.ANY)
 LIMIT = 48 * 1024 * 1024
 
-PARTS = ((0,), (6, 7), (4,), (5,), (2, 3), (1,))
-ORDER = (0, 6, 4, 5, 2, 1, 3, 7)
+PARTS = ((0,), (6,), (7,), (4,), (5,), (2, 3), (1,))
+ORDER = (0, 6, 7, 4, 5, 2, 1, 3)
 PAIRS = [(e, b) for b in range(1, NB) for e in range(b)]
 PARENT, ALPHA, LATER, VALUE, OWN, SPARE = 0, 6, 12, 18, 22, 32
 
@@ -47,7 +47,11 @@
 def pick_kernel(shape, *refs):
     slab, depth, block_cells, groups, count = shape
     out, arrivals = refs[5], refs[11]
-    copies = [pltpu.make_async_copy(refs[i], refs[6 + i], arrivals.at[i]) for i in range(5)]
+    copies = [pltpu.make_async_copy(refs[i], refs[6 + i], arrivals.at[i]) for i in range(4)]
+    parts = 4 if slab % 4 == 0 else 1
+    for i in range(parts):
+        some = pl.ds(i * (slab // parts), slab // parts)
+        copies.append(pltpu.make_async_copy(refs[4].at[some], refs[10].at[some], arrivals.at[4 + i]))
     for copy in copies:
         copy.start()
     for copy in copies:
@@ -239,8 +243,8 @@
     for i in range(n):
         region = i if len(pieces) == 1 else lax.bitwise_xor(block, ORDER[i])
         cells = pl.ds(pl.multiple_of(region * block_cells, LANES), block_cells)
-        piece, at = (pieces[0], i) if len(pieces) == 1 else (pieces[i], 0)
-        out[:, :, cells] = jnp.stack([piece[at, level] for level in range(depth)], axis=1)
+        for level in range(depth):
+            out[:, level, cells] = pieces[0][i, level] if len(pieces) == 1 else pieces[i][0, level]
 
 
 def hop(value, distance, n):
@@ -292,7 +296,7 @@
             pltpu.VMEM(obs_offset.shape, jnp.int32),
             pltpu.VMEM(parents.shape, jnp.int32),
             pltpu.VMEM(prior.shape, F32),
-            pltpu.SemaphoreType.DMA((5,)),
+            pltpu.SemaphoreType.DMA((8,)),
         ],
         moved=10**6,
         limit=None,

time: 53.3 us -> 53.8 us (level)
  starting transfers between devices: 27.5 us -> 29.5 us
  waiting for transfers between devices: 15.8 us -> 14.5 us
    ppermute x14, starting transfers between devices: 21 us -> 23 us  [hop(): return lax.ppermute(value, 'grid', [(j, j ^ distance) for j in range(n)])]
    ppermute x14, waiting for transfers between devices: 8.13 us -> 6.85 us  [hop(): return lax.ppermute(value, 'grid', [(j, j ^ distance) for j in range(n)])]
  transfers between devices with their start and end apart: 18 -> 18, of which waited for: 9 -> 7; matrix products, arithmetic and copies ran while one was open for 0% -> 0% of each run, Pallas kernels for 9% -> 9%
where the time goes in v15:
time: 53.8 us; the launch traced here: 53.6 us
  starting transfers between devices  29.5 us (55%)
  waiting for transfers between devices  14.5 us (27%)
  Pallas kernels  9.37 us (17%)
    ppermute x14, starting transfers between devices, hop(): return lax.ppermute(value, 'grid', [(j, j ^ distance) for j in range(n)])  23 us
    ppermute x14, waiting for transfers between devices, hop(): return lax.ppermute(value, 'grid', [(j, j ^ distance) for j in range(n)])  6.85 us
    all_to_all x1, starting transfers between devices, body(): fields = lax.all_to_all(send, 'grid', 0, 0, tiled=True)  4.95 us
    ppermute x1, waiting for transfers between devices, body(): far = lax.ppermute(slim, 'lev', [(j, j ^ 2) for j in range(lev)])  3.64 us
    pallas_call x1, Pallas kernels, body(): call(functools.partial(chain_kernel, (members, groups, count)), shape((8,...  2.72 us
    pallas_call x1, Pallas kernels, body(): call(functools.partial(pick_kernel, (slab, depth, block_cells, groups, co...  2.47 us
    all_to_all x1, waiting for transfers between devices, body(): fields = lax.all_to_all(send, 'grid', 0, 0, tiled=True)  2.22 us
    ppermute x1, waiting for transfers between devices, body(): cross = lax.ppermute(far, 'lev', [(j, j ^ 1) for j in range(lev)])  1.83 us
  transfers between devices with their start and end apart: 18, of which 7 were waited for; matrix products, arithmetic and copies ran while one was open for 0% of the time, Pallas kernels for 9%

profile of v15, /device:TPU:0, one launch (start us, length us, event | category | flops | bytes accessed | tf_op | source)
XLA Modules:
  0.0 53.6 jit_solution(14860129797135137205)
XLA Ops:
  0.0 2.5 %shard_map.75.refs_0_ = f32[136,128]{1,0:T(8,128)} custom-call(s32[4]{0:T(128)} %owner.3, f32[2,4]{1,0:T(2,128)} %refs_1_.1, s32[4,4,64]{2,1,0:T(4,128)} %refs_2_.1, s32[4,1,128]{2,1,0:T(1,128)} %bitcast.1, f32[16,2,4096]{2,1,0:T(2,128)} %refs_4_.1), custom_call_target="tpu_custom_call" | custom-call | bytes 1000000 | tf_op jit(solution)/shard_map/pallas_call | solution.py:289
  2.5 0.0 copy-start.2
  2.5 0.0 copy-start.3
  2.5 0.0 copy-start.4
  2.5 0.0 copy-start.5
  2.5 0.0 copy-start.6
  2.5 3.1 %collective-permute-start.1 = (f32[136,128]{1,0:T(8,128)}, f32[136,128]{1,0:T(8,128)S(1)}, u32[]{:S(2)}, u32[]{:S(2)}) collective-permute-start(f32[136,128]{1,0:T(8,128)} %shard_map.75.refs_0_), channel_id=1, source_target_pairs={{0,8},{4,12},{8,0},{12,4},{16,24},{20,28},{24,16},{28,20},{1,9},{5... | collective-permute-start | bytes 208904 | tf_op jit(solution)/shard_map/ppermute | solution.py:251
  5.6 2.6 %collective-permute-start.3 = (f32[136,128]{1,0:T(8,128)}, f32[136,128]{1,0:T(8,128)S(1)}, u32[]{:S(2)}, u32[]{:S(2)}) collective-permute-start(f32[136,128]{1,0:T(8,128)} %shard_map.75.refs_0_), channel_id=1, source_target_pairs={{0,16},{4,20},{8,24},{12,28},{16,0},{20,4},{24,8},{28,12},{1,17},{... | collective-permute-start | bytes 208904 | tf_op jit(solution)/shard_map/ppermute | solution.py:251
  8.2 1.5 %collective-permute-start = (f32[136,128]{1,0:T(8,128)}, f32[136,128]{1,0:T(8,128)S(1)}, u32[]{:S(2)}, u32[]{:S(2)}) collective-permute-start(f32[136,128]{1,0:T(8,128)} %shard_map.75.refs_0_), channel_id=1, source_target_pairs={{0,4},{4,0},{8,12},{12,8},{16,20},{20,16},{24,28},{28,24},{1,5},{5... | collective-permute-start | bytes 208904 | tf_op jit(solution)/shard_map/ppermute | solution.py:251
  9.7 0.2 collective-permute-start.5
  10.0 3.5 %collective-permute-start.6 = (f32[136,128]{1,0:T(8,128)}, f32[136,128]{1,0:T(8,128)S(1)}, u32[]{:S(2)}, u32[]{:S(2)}) collective-permute-start(f32[136,128]{1,0:T(8,128)} %shard_map.75.refs_0_), channel_id=1, source_target_pairs={{0,28},{4,24},{8,20},{12,16},{16,12},{20,8},{24,4},{28,0},{1,29},{... | collective-permute-start | bytes 208904 | tf_op jit(solution)/shard_map/ppermute | solution.py:251
  13.5 0.0 collective-permute-done.1.refs_2_
  13.5 1.5 %collective-permute-start.2 = (f32[136,128]{1,0:T(8,128)S(1)}, f32[136,128]{1,0:T(8,128)S(1)}, u32[]{:S(2)}, u32[]{:S(2)}) collective-permute-start(f32[136,128]{1,0:T(8,128)S(1)} %collective-permute-done.1.refs_2_), channel_id=1, source_target_pairs={{0,4},{4,0},{8,12},{12,8},{16,20},{20,16},{24,28},{28,24},{1,5},{5... | collective-permute-start | bytes 208904 | tf_op jit(solution)/shard_map/ppermute | solution.py:251
  15.0 0.0 collective-permute-done.3.refs_4_
  15.0 0.6 %collective-permute-start.4 = (f32[136,128]{1,0:T(8,128)S(1)}, f32[136,128]{1,0:T(8,128)S(1)}, u32[]{:S(2)}, u32[]{:S(2)}) collective-permute-start(f32[136,128]{1,0:T(8,128)S(1)} %collective-permute-done.3.refs_4_), channel_id=1, source_target_pairs={{0,4},{4,0},{8,12},{12,8},{16,20},{20,16},{24,28},{28,24},{1,5},{5... | collective-permute-start | bytes 208904 | tf_op jit(solution)/shard_map/ppermute | solution.py:251
  15.6 0.9 %shard_map.74.ahead = f32[8,2,16,512]{3,2,1,0:T(8,128)} custom-call(f32[16,2,4096]{2,1,0:T(2,128)S(1)} %copy-done), custom_call_target="tpu_custom_call" | custom-call | bytes 1000000 | tf_op jit(solution)/shard_map/pallas_call | solution.py:305
  16.5 1.0 %shard_map.73 = (f32[32,128]{1,0:T(8,128)S(1)}, f32[5,128,128]{2,1,0:T(8,128)S(1)}) custom-call(s32[4]{0:T(128)S(1)} %copy-done.4, s32[4,4,64]{2,1,0:T(4,128)S(1)} %copy-done.2, f32[4,1,64]{2,1,0:T(1,128)S(1)} %copy-done.5, f32[4,1,64]{2,1,0:T(1,128)S(1)} %copy-done.6, s32[4,1,128]{2,1,0:T(1,128)S(1)} %bitcast.2), custom_call_target="tpu_custom_call" | custom-call | bytes 1000000 | tf_op jit(solution)/shard_map/pallas_call | solution.py:313
  17.5 0.0 collective-permute-done.refs_1_
  17.6 0.0 collective-permute-done.5.refs_6_
  17.6 0.0 collective-permute-done.6.refs_7_
  17.6 0.4 collective-permute-done.2.refs_3_
  18.0 1.3 %collective-permute-done.4.refs_5_ = f32[136,128]{1,0:T(8,128)S(1)} collective-permute-done((f32[136,128]{1,0:T(8,128)S(1)}, f32[136,128]{1,0:T(8,128)S(1)}, u32[]{:S(2)}, u32[]{:S(2)}) %collective-permute-start.4) | collective-permute-done | bytes 69664 | tf_op jit(solution)/shard_map/ppermute | solution.py:251
  19.4 0.8 %shard_map.76 = (f32[1056,128]{1,0:T(8,128)S(1)}, f32[928,128]{1,0:T(8,128)S(1)}) custom-call(s32[4]{0:T(128)S(1)} %copy-done.4, f32[32,128]{1,0:T(8,128)S(1)} %get-tuple-element.17.rows, f32[8,2,16,512]{3,2,1,0:T(8,128)} %shard_map.74.ahead, f32[136,128]{1,0:T(8,128)S(1)} %copy-done.1, f32[136,128]{1,0:T(8,128)S(1)} %collective-permute-done.refs_1_, ...), custom_call_target="tpu_custom_call" | custom-call | bytes 1000000 | tf_op jit(solution)/shard_map/pallas_call | solution.py:321
  20.2 1.6 %collective-permute-start.8 = (f32[928,128]{1,0:T(8,128)S(1)}, f32[928,128]{1,0:T(8,128)S(1)}, u32[]{:S(2)}, u32[]{:S(2)}) collective-permute-start(f32[928,128]{1,0:T(8,128)S(1)} %get-tuple-element.19), channel_id=1, source_target_pairs={{0,2},{1,3},{2,0},{3,1},{4,6},{5,7},{6,4},{7,5},{8,10},{9,11},{10,... | collective-permute-start | bytes 1425416 | tf_op jit(solution)/shard_map/ppermute | solution.py:328
  21.7 4.9 %all-to-all-start = ((f32[8,2,16,512]{3,2,1,0:T(8,128)}), f32[8,2,16,512]{3,2,1,0:T(8,128)S(1)}, u32[]{:S(2)}, u32[]{:S(2)}) async-start(f32[8,2,16,512]{3,2,1,0:T(8,128)} %shard_map.74.ahead), calls=%async_computation | async-start | bytes 1048576 | tf_op jit(solution)/shard_map/all_to_all | solution.py:311
  26.7 0.0 collective-permute-start.7
  26.7 3.6 %collective-permute-done.8.far = f32[928,128]{1,0:T(8,128)S(1)} collective-permute-done((f32[928,128]{1,0:T(8,128)S(1)}, f32[928,128]{1,0:T(8,128)S(1)}, u32[]{:S(2)}, u32[]{:S(2)}) %collective-permute-start.8) | collective-permute-done | bytes 475168 | tf_op jit(solution)/shard_map/ppermute | solution.py:328
  30.3 0.0 collective-permute-start.9
  30.3 0.0 collective-permute-done.7.near
  30.3 1.8 %collective-permute-done.9.cross = f32[928,128]{1,0:T(8,128)S(1)} collective-permute-done((f32[928,128]{1,0:T(8,128)S(1)}, f32[928,128]{1,0:T(8,128)S(1)}, u32[]{:S(2)}, u32[]{:S(2)}) %collective-permute-start.9) | collective-permute-done | bytes 475168 | tf_op jit(solution)/shard_map/ppermute | solution.py:330
  32.1 2.7 %shard_map.77.pull = f32[8,128]{1,0:T(8,128)S(1)} custom-call(f32[1056,128]{1,0:T(8,128)S(1)} %get-tuple-element.18.own, f32[1056,128]{1,0:T(8,128)S(1)} %collective-permute-done.7.near, f32[928,128]{1,0:T(8,128)S(1)} %collective-permute-done.8.far, f32[928,128]{1,0:T(8,128)S(1)} %collective-permute-done.9.cross, f32[5,128,128]{2,1,0:T(8,128)S(1)} %get-tuple-element.16.steps), custom_call_target="tpu_custom_call" | custom-call | bytes 100000 | tf_op jit(solution)/shard_map/pallas_call | solution.py:332
  34.9 2.2 %all-to-all-done.fields = f32[8,2,16,512]{3,2,1,0:T(8,128)S(1)} async-done(((f32[8,2,16,512]{3,2,1,0:T(8,128)}), f32[8,2,16,512]{3,2,1,0:T(8,128)S(1)}, u32[]{:S(2)}, u32[]{:S(2)}) %all-to-all-start) | async-done | bytes 524320 | tf_op jit(solution)/shard_map/all_to_all | solution.py:311
  37.1 0.6 %shard_map.78 = (f32[1,2,16,512]{3,2,1,0:T(8,128)S(1)}, f32[1,2,16,512]{3,2,1,0:T(8,128)S(1)}, f32[1,2,16,512]{3,2,1,0:T(8,128)S(1)}, f32[1,2,16,512]{3,2,1,0:T(...) custom-call(f32[5,128,128]{2,1,0:T(8,128)S(1)} %get-tuple-element.16.steps, ...), custom_call_target="tpu_custom_call" | custom-call | flops 100000000 | bytes 1000000 | tf_op jit(solution)/shard_map/pallas_call | solution.py:343
  37.7 0.1 collective-permute-start.14
  37.8 2.3 %collective-permute-start.10 = (f32[1,2,16,512]{3,2,1,0:T(8,128)S(1)}, f32[1,2,16,512]{3,2,1,0:T(8,128)S(1)}, u32[]{:S(2)}, u32[]{:S(2)}) collective-permute-start(f32[1,2,16,512]{3,2,1,0:T(8,128)S(1)} %get-tuple-element.21), channel_id=1, source_target_pairs={{0,24},{4,28},{8,16},{12,20},{16,8},{20,12},{24,0},{28,4},{1,25},{... | collective-permute-start | bytes 196616 | tf_op jit(solution)/shard_map/ppermute | solution.py:251
  40.0 2.6 %collective-permute-start.11 = (f32[1,2,16,512]{3,2,1,0:T(8,128)S(1)}, f32[1,2,16,512]{3,2,1,0:T(8,128)S(1)}, u32[]{:S(2)}, u32[]{:S(2)}) collective-permute-start(f32[1,2,16,512]{3,2,1,0:T(8,128)S(1)} %get-tuple-element.22), channel_id=1, source_target_pairs={{0,28},{4,24},{8,20},{12,16},{16,12},{20,8},{24,4},{28,0},{1,29},{... | collective-permute-start | bytes 196616 | tf_op jit(solution)/shard_map/ppermute | solution.py:251
  42.6 0.2 collective-permute-start.12
  42.8 2.7 %collective-permute-start.13 = (f32[1,2,16,512]{3,2,1,0:T(8,128)S(1)}, f32[1,2,16,512]{3,2,1,0:T(8,128)S(1)}, u32[]{:S(2)}, u32[]{:S(2)}) collective-permute-start(f32[1,2,16,512]{3,2,1,0:T(8,128)S(1)} %get-tuple-element.24), channel_id=1, source_target_pairs={{0,20},{4,16},{8,28},{12,24},{16,4},{20,0},{24,12},{28,8},{1,21},{... | collective-permute-start | bytes 196616 | tf_op jit(solution)/shard_map/ppermute | solution.py:251
  45.5 0.0 collective-permute-done.14.refs_5_
  45.5 1.5 %collective-permute-start.15 = (f32[1,2,16,512]{3,2,1,0:T(8,128)S(1)}, f32[1,2,16,512]{3,2,1,0:T(8,128)S(1)}, u32[]{:S(2)}, u32[]{:S(2)}) collective-permute-start(f32[1,2,16,512]{3,2,1,0:T(8,128)S(1)} %get-tuple-element.26), channel_id=1, source_target_pairs={{0,4},{4,0},{8,12},{12,8},{16,20},{20,16},{24,28},{28,24},{1,5},{5... | collective-permute-start | bytes 196616 | tf_op jit(solution)/shard_map/ppermute | solution.py:251
  47.0 0.0 collective-permute-done.10.refs_1_
  47.0 0.6 %collective-permute-start.16 = (f32[1,2,16,512]{3,2,1,0:T(8,128)S(1)}, f32[1,2,16,512]{3,2,1,0:T(8,128)S(1)}, u32[]{:S(2)}, u32[]{:S(2)}) collective-permute-start(f32[1,2,16,512]{3,2,1,0:T(8,128)S(1)} %slice.4), channel_id=1, source_target_pairs={{0,4},{4,0},{8,12},{12,8},{16,20},{20,16},{24,28},{28,24},{1,5},{5... | collective-permute-start | bytes 196616 | tf_op jit(solution)/shard_map/ppermute | solution.py:251
  47.6 0.0 collective-permute-done.11.refs_2_
  47.6 3.9 %collective-permute-done.12.refs_3_ = f32[1,2,16,512]{3,2,1,0:T(8,128)S(1)} collective-permute-done((f32[1,2,16,512]{3,2,1,0:T(8,128)S(1)}, f32[1,2,16,512]{3,2,1,0:T(8,128)S(1)}, u32[]{:S(2)}, u32[]{:S(2)}) %collective-permute-start.12) | collective-permute-done | bytes 65568 | tf_op jit(solution)/shard_map/ppermute | solution.py:251
  51.5 1.2 %collective-permute-done.13.refs_4_ = f32[1,2,16,512]{3,2,1,0:T(8,128)S(1)} collective-permute-done((f32[1,2,16,512]{3,2,1,0:T(8,128)S(1)}, f32[1,2,16,512]{3,2,1,0:T(8,128)S(1)}, u32[]{:S(2)}, u32[]{:S(2)}) %collective-permute-start.13) | collective-permute-done | bytes 65568 | tf_op jit(solution)/shard_map/ppermute | solution.py:251
  52.6 0.0 collective-permute-done.15.refs_6_
  52.6 0.0 collective-permute-done.16.refs_7_
  52.6 0.9 %shard_map.79 = f32[16,2,4096]{2,1,0:T(2,128)} custom-call(f32[1,2,16,512]{3,2,1,0:T(8,128)S(1)} %get-tuple-element.20.refs_0_, f32[1,2,16,512]{3,2,1,0:T(8,128)S(1)} %collective-permute-done.10.refs_1_, f32[1,2,16,512]{3,2,1,0:T(8,128)S(1)} %collective-permute-done.11.refs_2_, f32[1,2,16,512]{3,2,1,0:T(8,128)S(1)} %collective-permute-done.12.refs_3_, ...), custom_call_target="tpu_custom_call" | custom-call | bytes 1000000 | tf_op jit(solution)/shard_map/pallas_call | solution.py:353
  (10 shorter events, 0.0 us)
Async XLA Ops:
  0.0 15.6 %copy-start = (f32[16,2,4096]{2,1,0:T(2,128)S(1)}, f32[16,2,4096]{2,1,0:T(2,128)}, u32[]{:S(2)}) copy-start(f32[16,2,4096]{2,1,0:T(2,128)} %refs_4_.1) | copy-start | bytes 1572868
  2.5 14.1 %copy-start.2 = (s32[4,4,64]{2,1,0:T(4,128)S(1)}, s32[4,4,64]{2,1,0:T(4,128)}, u32[]{:S(2)}) copy-start(s32[4,4,64]{2,1,0:T(4,128)} %refs_2_.1) | copy-start | bytes 12292
  2.5 14.0 %copy-start.3 = (s32[4,1,1,128]{3,2,1,0:T(1,128)S(1)}, s32[4,1,1,128]{3,2,1,0:T(1,128)}, u32[]{:S(2)}) copy-start(s32[4,1,1,128]{3,2,1,0:T(1,128)} %param.13) | copy-start | bytes 6148
  2.5 14.0 %copy-start.4 = (s32[4]{0:T(128)S(1)}, s32[4]{0:T(128)}, u32[]{:S(2)}) copy-start(s32[4]{0:T(128)} %owner.3) | copy-start | bytes 52
  2.5 14.0 %copy-start.5 = (f32[4,1,64]{2,1,0:T(1,128)S(1)}, f32[4,1,64]{2,1,0:T(1,128)}, u32[]{:S(2)}) copy-start(f32[4,1,64]{2,1,0:T(1,128)} %values.1) | copy-start | bytes 3076
  2.5 14.0 %copy-start.6 = (f32[4,1,64]{2,1,0:T(1,128)S(1)}, f32[4,1,64]{2,1,0:T(1,128)}, u32[]{:S(2)}) copy-start(f32[4,1,64]{2,1,0:T(1,128)} %errors.1) | copy-start | bytes 3076
  2.5 16.8 %copy-start.1 = (f32[136,128]{1,0:T(8,128)S(1)}, f32[136,128]{1,0:T(8,128)}, u32[]{:S(2)}) copy-start(f32[136,128]{1,0:T(8,128)} %shard_map.75.refs_0_) | copy-start | bytes 208900
  2.5 11.0 %collective-permute-start.1 = (f32[136,128]{1,0:T(8,128)}, f32[136,128]{1,0:T(8,128)S(1)}, u32[]{:S(2)}, u32[]{:S(2)}) collective-permute-start(f32[136,128]{1,0:T(8,128)} %shard_map.75.refs_0_), channel_id=1, source_target_pairs={{0,8},{4,12},{8,0},{12,4},{16,24},{20,28},{24,16},{28,20},{1,9},{5... | collective-permute-start | bytes 208904 | tf_op jit(solution)/shard_map/ppermute | solution.py:251
  5.6 9.4 %collective-permute-start.3 = (f32[136,128]{1,0:T(8,128)}, f32[136,128]{1,0:T(8,128)S(1)}, u32[]{:S(2)}, u32[]{:S(2)}) collective-permute-start(f32[136,128]{1,0:T(8,128)} %shard_map.75.refs_0_), channel_id=1, source_target_pairs={{0,16},{4,20},{8,24},{12,28},{16,0},{20,4},{24,8},{28,12},{1,17},{... | collective-permute-start | bytes 208904 | tf_op jit(solution)/shard_map/ppermute | solution.py:251
  8.2 9.3 %collective-permute-start = (f32[136,128]{1,0:T(8,128)}, f32[136,128]{1,0:T(8,128)S(1)}, u32[]{:S(2)}, u32[]{:S(2)}) collective-permute-start(f32[136,128]{1,0:T(8,128)} %shard_map.75.refs_0_), channel_id=1, source_target_pairs={{0,4},{4,0},{8,12},{12,8},{16,20},{20,16},{24,28},{28,24},{1,5},{5... | collective-permute-start | bytes 208904 | tf_op jit(solution)/shard_map/ppermute | solution.py:251
  9.7 7.8 %collective-permute-start.5 = (f32[136,128]{1,0:T(8,128)}, f32[136,128]{1,0:T(8,128)S(1)}, u32[]{:S(2)}, u32[]{:S(2)}) collective-permute-start(f32[136,128]{1,0:T(8,128)} %shard_map.75.refs_0_), channel_id=1, source_target_pairs={{0,24},{4,28},{8,16},{12,20},{16,8},{20,12},{24,0},{28,4},{1,25},{... | collective-permute-start | bytes 208904 | tf_op jit(solution)/shard_map/ppermute | solution.py:251
  10.0 7.6 %collective-permute-start.6 = (f32[136,128]{1,0:T(8,128)}, f32[136,128]{1,0:T(8,128)S(1)}, u32[]{:S(2)}, u32[]{:S(2)}) collective-permute-start(f32[136,128]{1,0:T(8,128)} %shard_map.75.refs_0_), channel_id=1, source_target_pairs={{0,28},{4,24},{8,20},{12,16},{16,12},{20,8},{24,4},{28,0},{1,29},{... | collective-permute-start | bytes 208904 | tf_op jit(solution)/shard_map/ppermute | solution.py:251
  13.5 4.5 %collective-permute-start.2 = (f32[136,128]{1,0:T(8,128)S(1)}, f32[136,128]{1,0:T(8,128)S(1)}, u32[]{:S(2)}, u32[]{:S(2)}) collective-permute-start(f32[136,128]{1,0:T(8,128)S(1)} %collective-permute-done.1.refs_2_), channel_id=1, source_target_pairs={{0,4},{4,0},{8,12},{12,8},{16,20},{20,16},{24,28},{28,24},{1,5},{5... | collective-permute-start | bytes 208904 | tf_op jit(solution)/shard_map/ppermute | solution.py:251
  15.0 4.3 %collective-permute-start.4 = (f32[136,128]{1,0:T(8,128)S(1)}, f32[136,128]{1,0:T(8,128)S(1)}, u32[]{:S(2)}, u32[]{:S(2)}) collective-permute-start(f32[136,128]{1,0:T(8,128)S(1)} %collective-permute-done.3.refs_4_), channel_id=1, source_target_pairs={{0,4},{4,0},{8,12},{12,8},{16,20},{20,16},{24,28},{28,24},{1,5},{5... | collective-permute-start | bytes 208904 | tf_op jit(solution)/shard_map/ppermute | solution.py:251
  20.2 10.2 %collective-permute-start.8 = (f32[928,128]{1,0:T(8,128)S(1)}, f32[928,128]{1,0:T(8,128)S(1)}, u32[]{:S(2)}, u32[]{:S(2)}) collective-permute-start(f32[928,128]{1,0:T(8,128)S(1)} %get-tuple-element.19), channel_id=1, source_target_pairs={{0,2},{1,3},{2,0},{3,1},{4,6},{5,7},{6,4},{7,5},{8,10},{9,11},{10,... | collective-permute-start | bytes 1425416 | tf_op jit(solution)/shard_map/ppermute | solution.py:328
  21.7 15.4 %all-to-all-start = ((f32[8,2,16,512]{3,2,1,0:T(8,128)}), f32[8,2,16,512]{3,2,1,0:T(8,128)S(1)}, u32[]{:S(2)}, u32[]{:S(2)}) async-start(f32[8,2,16,512]{3,2,1,0:T(8,128)} %shard_map.74.ahead), calls=%async_computation | async-start | bytes 1048576 | tf_op jit(solution)/shard_map/all_to_all | solution.py:311
  26.7 3.7 %collective-permute-start.7 = (f32[1056,128]{1,0:T(8,128)S(1)}, f32[1056,128]{1,0:T(8,128)S(1)}, u32[]{:S(2)}, u32[]{:S(2)}) collective-permute-start(f32[1056,128]{1,0:T(8,128)S(1)} %get-tuple-element.18.own), channel_id=1, source_target_pairs={{0,1},{1,0},{2,3},{3,2},{4,5},{5,4},{6,7},{7,6},{8,9},{9,8},{10,11... | collective-permute-start | bytes 1622024 | tf_op jit(solution)/shard_map/ppermute | solution.py:329
  30.3 1.8 %collective-permute-start.9 = (f32[928,128]{1,0:T(8,128)S(1)}, f32[928,128]{1,0:T(8,128)S(1)}, u32[]{:S(2)}, u32[]{:S(2)}) collective-permute-start(f32[928,128]{1,0:T(8,128)S(1)} %collective-permute-done.8.far), channel_id=1, source_target_pairs={{0,1},{1,0},{2,3},{3,2},{4,5},{5,4},{6,7},{7,6},{8,9},{9,8},{10,11... | collective-permute-start | bytes 1425416 | tf_op jit(solution)/shard_map/ppermute | solution.py:330
  37.7 7.8 %collective-permute-start.14 = (f32[2,2,16,512]{3,2,1,0:T(8,128)S(1)}, f32[2,2,16,512]{3,2,1,0:T(8,128)S(1)}, u32[]{:S(2)}, u32[]{:S(2)}) collective-permute-start(f32[2,2,16,512]{3,2,1,0:T(8,128)S(1)} %get-tuple-element.25), channel_id=1, source_target_pairs={{0,8},{4,12},{8,0},{12,4},{16,24},{20,28},{24,16},{28,20},{1,9},{5... | collective-permute-start | bytes 393224 | tf_op jit(solution)/shard_map/ppermute | solution.py:251
  37.8 9.2 %collective-permute-start.10 = (f32[1,2,16,512]{3,2,1,0:T(8,128)S(1)}, f32[1,2,16,512]{3,2,1,0:T(8,128)S(1)}, u32[]{:S(2)}, u32[]{:S(2)}) collective-permute-start(f32[1,2,16,512]{3,2,1,0:T(8,128)S(1)} %get-tuple-element.21), channel_id=1, source_target_pairs={{0,24},{4,28},{8,16},{12,20},{16,8},{20,12},{24,0},{28,4},{1,25},{... | collective-permute-start | bytes 196616 | tf_op jit(solution)/shard_map/ppermute | solution.py:251
  40.0 7.6 %collective-permute-start.11 = (f32[1,2,16,512]{3,2,1,0:T(8,128)S(1)}, f32[1,2,16,512]{3,2,1,0:T(8,128)S(1)}, u32[]{:S(2)}, u32[]{:S(2)}) collective-permute-start(f32[1,2,16,512]{3,2,1,0:T(8,128)S(1)} %get-tuple-element.22), channel_id=1, source_target_pairs={{0,28},{4,24},{8,20},{12,16},{16,12},{20,8},{24,4},{28,0},{1,29},{... | collective-permute-start | bytes 196616 | tf_op jit(solution)/shard_map/ppermute | solution.py:251
  42.6 8.9 %collective-permute-start.12 = (f32[1,2,16,512]{3,2,1,0:T(8,128)S(1)}, f32[1,2,16,512]{3,2,1,0:T(8,128)S(1)}, u32[]{:S(2)}, u32[]{:S(2)}) collective-permute-start(f32[1,2,16,512]{3,2,1,0:T(8,128)S(1)} %get-tuple-element.23), channel_id=1, source_target_pairs={{0,16},{4,20},{8,24},{12,28},{16,0},{20,4},{24,8},{28,12},{1,17},{... | collective-permute-start | bytes 196616 | tf_op jit(solution)/shard_map/ppermute | solution.py:251
  42.8 9.9 %collective-permute-start.13 = (f32[1,2,16,512]{3,2,1,0:T(8,128)S(1)}, f32[1,2,16,512]{3,2,1,0:T(8,128)S(1)}, u32[]{:S(2)}, u32[]{:S(2)}) collective-permute-start(f32[1,2,16,512]{3,2,1,0:T(8,128)S(1)} %get-tuple-element.24), channel_id=1, source_target_pairs={{0,20},{4,16},{8,28},{12,24},{16,4},{20,0},{24,12},{28,8},{1,21},{... | collective-permute-start | bytes 196616 | tf_op jit(solution)/shard_map/ppermute | solution.py:251
  45.5 7.2 %collective-permute-start.15 = (f32[1,2,16,512]{3,2,1,0:T(8,128)S(1)}, f32[1,2,16,512]{3,2,1,0:T(8,128)S(1)}, u32[]{:S(2)}, u32[]{:S(2)}) collective-permute-start(f32[1,2,16,512]{3,2,1,0:T(8,128)S(1)} %get-tuple-element.26), channel_id=1, source_target_pairs={{0,4},{4,0},{8,12},{12,8},{16,20},{20,16},{24,28},{28,24},{1,5},{5... | collective-permute-start | bytes 196616 | tf_op jit(solution)/shard_map/ppermute | solution.py:251
  47.0 5.6 %collective-permute-start.16 = (f32[1,2,16,512]{3,2,1,0:T(8,128)S(1)}, f32[1,2,16,512]{3,2,1,0:T(8,128)S(1)}, u32[]{:S(2)}, u32[]{:S(2)}) collective-permute-start(f32[1,2,16,512]{3,2,1,0:T(8,128)S(1)} %slice.4), channel_id=1, source_target_pairs={{0,4},{4,0},{8,12},{12,8},{16,20},{20,16},{24,28},{28,24},{1,5},{5... | collective-permute-start | bytes 196616 | tf_op jit(solution)/shard_map/ppermute | solution.py:251

commit v16 on v14

--- a/solution.py
+++ b/solution.py
@@ -16,8 +16,8 @@
 PLACE = pl.BlockSpec(memory_space=pl.ANY)
 LIMIT = 48 * 1024 * 1024
 
-PARTS = ((0,), (6, 7), (4,), (5,), (2, 3), (1,))
-ORDER = (0, 6, 4, 5, 2, 1, 3, 7)
+PARTS = ((0,), (4,), (5,), (6,), (7,), (2, 3), (1,))
+ORDER = (0, 4, 5, 6, 7, 2, 1, 3)
 PAIRS = [(e, b) for b in range(1, NB) for e in range(b)]
 PARENT, ALPHA, LATER, VALUE, OWN, SPARE = 0, 6, 12, 18, 22, 32
 
@@ -239,8 +239,8 @@
     for i in range(n):
         region = i if len(pieces) == 1 else lax.bitwise_xor(block, ORDER[i])
         cells = pl.ds(pl.multiple_of(region * block_cells, LANES), block_cells)
-        piece, at = (pieces[0], i) if len(pieces) == 1 else (pieces[i], 0)
-        out[:, :, cells] = jnp.stack([piece[at, level] for level in range(depth)], axis=1)
+        for level in range(depth):
+            out[:, level, cells] = pieces[0][i, level] if len(pieces) == 1 else pieces[i][0, level]
 
 
 def hop(value, distance, n):

time: 53.3 us -> 53.3 us (level)
  starting transfers between devices: 27.5 us -> 30.2 us
  waiting for transfers between devices: 15.8 us -> 13.4 us
    ppermute x14, starting transfers between devices: 21 us -> 23.7 us  [hop(): return lax.ppermute(value, 'grid', [(j, j ^ distance) for j in range(n)])]
    ppermute x14, waiting for transfers between devices: 8.13 us -> 5.66 us  [hop(): return lax.ppermute(value, 'grid', [(j, j ^ distance) for j in range(n)])]
where the time goes in v16:
time: 53.3 us; the launch traced here: 53 us
  starting transfers between devices  30.2 us (57%)
  waiting for transfers between devices  13.4 us (25%)
  Pallas kernels  9.29 us (17%)
    ppermute x14, starting transfers between devices, hop(): return lax.ppermute(value, 'grid', [(j, j ^ distance) for j in range(n)])  23.7 us
    ppermute x14, waiting for transfers between devices, hop(): return lax.ppermute(value, 'grid', [(j, j ^ distance) for j in range(n)])  5.66 us
    all_to_all x1, starting transfers between devices, body(): fields = lax.all_to_all(send, 'grid', 0, 0, tiled=True)  4.95 us
    ppermute x1, waiting for transfers between devices, body(): far = lax.ppermute(slim, 'lev', [(j, j ^ 2) for j in range(lev)])  3.64 us
    pallas_call x1, Pallas kernels, body(): call(functools.partial(chain_kernel, (members, groups, count)), shape((8,...  2.72 us
    pallas_call x1, Pallas kernels, body(): call(functools.partial(pick_kernel, (slab, depth, block_cells, groups, co...  2.39 us
    all_to_all x1, waiting for transfers between devices, body(): fields = lax.all_to_all(send, 'grid', 0, 0, tiled=True)  2.22 us
    ppermute x1, waiting for transfers between devices, body(): cross = lax.ppermute(far, 'lev', [(j, j ^ 1) for j in range(lev)])  1.83 us
  transfers between devices with their start and end apart: 18, of which 9 were waited for; matrix products, arithmetic and copies ran while one was open for 0% of the time, Pallas kernels for 9%

profile of v16, /device:TPU:0, one launch (start us, length us, event | category | flops | bytes accessed | tf_op | source)
XLA Modules:
  0.0 53.0 jit_solution(4936019781602646082)
XLA Ops:
  0.0 2.4 %shard_map.75.refs_0_ = f32[136,128]{1,0:T(8,128)} custom-call(s32[4]{0:T(128)} %owner.3, f32[2,4]{1,0:T(2,128)} %refs_1_.1, s32[4,4,64]{2,1,0:T(4,128)} %refs_2_.1, s32[4,1,128]{2,1,0:T(1,128)} %bitcast.1, f32[16,2,4096]{2,1,0:T(2,128)} %refs_4_.1), custom_call_target="tpu_custom_call" | custom-call | bytes 1000000 | tf_op jit(solution)/shard_map/pallas_call | solution.py:285
  2.4 0.0 copy-start.2
  2.4 0.0 copy-start.3
  2.4 0.0 copy-start.4
  2.4 0.0 copy-start.5
  2.4 0.0 copy-start.6
  2.5 3.1 %collective-permute-start.1 = (f32[136,128]{1,0:T(8,128)}, f32[136,128]{1,0:T(8,128)S(1)}, u32[]{:S(2)}, u32[]{:S(2)}) collective-permute-start(f32[136,128]{1,0:T(8,128)} %shard_map.75.refs_0_), channel_id=1, source_target_pairs={{0,8},{4,12},{8,0},{12,4},{16,24},{20,28},{24,16},{28,20},{1,9},{5... | collective-permute-start | bytes 208904 | tf_op jit(solution)/shard_map/ppermute | solution.py:247
  5.6 2.6 %collective-permute-start.3 = (f32[136,128]{1,0:T(8,128)}, f32[136,128]{1,0:T(8,128)S(1)}, u32[]{:S(2)}, u32[]{:S(2)}) collective-permute-start(f32[136,128]{1,0:T(8,128)} %shard_map.75.refs_0_), channel_id=1, source_target_pairs={{0,16},{4,20},{8,24},{12,28},{16,0},{20,4},{24,8},{28,12},{1,17},{... | collective-permute-start | bytes 208904 | tf_op jit(solution)/shard_map/ppermute | solution.py:247
  8.1 1.5 %collective-permute-start = (f32[136,128]{1,0:T(8,128)}, f32[136,128]{1,0:T(8,128)S(1)}, u32[]{:S(2)}, u32[]{:S(2)}) collective-permute-start(f32[136,128]{1,0:T(8,128)} %shard_map.75.refs_0_), channel_id=1, source_target_pairs={{0,4},{4,0},{8,12},{12,8},{16,20},{20,16},{24,28},{28,24},{1,5},{5... | collective-permute-start | bytes 208904 | tf_op jit(solution)/shard_map/ppermute | solution.py:247
  9.7 0.2 collective-permute-start.5
  9.9 3.5 %collective-permute-start.6 = (f32[136,128]{1,0:T(8,128)}, f32[136,128]{1,0:T(8,128)S(1)}, u32[]{:S(2)}, u32[]{:S(2)}) collective-permute-start(f32[136,128]{1,0:T(8,128)} %shard_map.75.refs_0_), channel_id=1, source_target_pairs={{0,28},{4,24},{8,20},{12,16},{16,12},{20,8},{24,4},{28,0},{1,29},{... | collective-permute-start | bytes 208904 | tf_op jit(solution)/shard_map/ppermute | solution.py:247
  13.4 0.0 collective-permute-done.1.refs_2_
  13.4 1.5 %collective-permute-start.2 = (f32[136,128]{1,0:T(8,128)S(1)}, f32[136,128]{1,0:T(8,128)S(1)}, u32[]{:S(2)}, u32[]{:S(2)}) collective-permute-start(f32[136,128]{1,0:T(8,128)S(1)} %collective-permute-done.1.refs_2_), channel_id=1, source_target_pairs={{0,4},{4,0},{8,12},{12,8},{16,20},{20,16},{24,28},{28,24},{1,5},{5... | collective-permute-start | bytes 208904 | tf_op jit(solution)/shard_map/ppermute | solution.py:247
  15.0 0.0 collective-permute-done.3.refs_4_
  15.0 0.6 %collective-permute-start.4 = (f32[136,128]{1,0:T(8,128)S(1)}, f32[136,128]{1,0:T(8,128)S(1)}, u32[]{:S(2)}, u32[]{:S(2)}) collective-permute-start(f32[136,128]{1,0:T(8,128)S(1)} %collective-permute-done.3.refs_4_), channel_id=1, source_target_pairs={{0,4},{4,0},{8,12},{12,8},{16,20},{20,16},{24,28},{28,24},{1,5},{5... | collective-permute-start | bytes 208904 | tf_op jit(solution)/shard_map/ppermute | solution.py:247
  15.6 0.9 %shard_map.74.ahead = f32[8,2,16,512]{3,2,1,0:T(8,128)} custom-call(f32[16,2,4096]{2,1,0:T(2,128)S(1)} %copy-done), custom_call_target="tpu_custom_call" | custom-call | bytes 1000000 | tf_op jit(solution)/shard_map/pallas_call | solution.py:301
  16.5 1.0 %shard_map.73 = (f32[32,128]{1,0:T(8,128)S(1)}, f32[5,128,128]{2,1,0:T(8,128)S(1)}) custom-call(s32[4]{0:T(128)S(1)} %copy-done.4, s32[4,4,64]{2,1,0:T(4,128)S(1)} %copy-done.2, f32[4,1,64]{2,1,0:T(1,128)S(1)} %copy-done.5, f32[4,1,64]{2,1,0:T(1,128)S(1)} %copy-done.6, s32[4,1,128]{2,1,0:T(1,128)S(1)} %bitcast.2), custom_call_target="tpu_custom_call" | custom-call | bytes 1000000 | tf_op jit(solution)/shard_map/pallas_call | solution.py:309
  17.5 0.0 collective-permute-done.refs_1_
  17.5 0.0 collective-permute-done.5.refs_6_
  17.5 0.0 collective-permute-done.6.refs_7_
  17.5 0.4 collective-permute-done.2.refs_3_
  18.0 1.3 %collective-permute-done.4.refs_5_ = f32[136,128]{1,0:T(8,128)S(1)} collective-permute-done((f32[136,128]{1,0:T(8,128)S(1)}, f32[136,128]{1,0:T(8,128)S(1)}, u32[]{:S(2)}, u32[]{:S(2)}) %collective-permute-start.4) | collective-permute-done | bytes 69664 | tf_op jit(solution)/shard_map/ppermute | solution.py:247
  19.3 0.8 %shard_map.76 = (f32[1056,128]{1,0:T(8,128)S(1)}, f32[928,128]{1,0:T(8,128)S(1)}) custom-call(s32[4]{0:T(128)S(1)} %copy-done.4, f32[32,128]{1,0:T(8,128)S(1)} %get-tuple-element.17.rows, f32[8,2,16,512]{3,2,1,0:T(8,128)} %shard_map.74.ahead, f32[136,128]{1,0:T(8,128)S(1)} %copy-done.1, f32[136,128]{1,0:T(8,128)S(1)} %collective-permute-done.refs_1_, ...), custom_call_target="tpu_custom_call" | custom-call | bytes 1000000 | tf_op jit(solution)/shard_map/pallas_call | solution.py:317
  20.1 1.6 %collective-permute-start.8 = (f32[928,128]{1,0:T(8,128)S(1)}, f32[928,128]{1,0:T(8,128)S(1)}, u32[]{:S(2)}, u32[]{:S(2)}) collective-permute-start(f32[928,128]{1,0:T(8,128)S(1)} %get-tuple-element.19), channel_id=1, source_target_pairs={{0,2},{1,3},{2,0},{3,1},{4,6},{5,7},{6,4},{7,5},{8,10},{9,11},{10,... | collective-permute-start | bytes 1425416 | tf_op jit(solution)/shard_map/ppermute | solution.py:324
  21.6 4.9 %all-to-all-start = ((f32[8,2,16,512]{3,2,1,0:T(8,128)}), f32[8,2,16,512]{3,2,1,0:T(8,128)S(1)}, u32[]{:S(2)}, u32[]{:S(2)}) async-start(f32[8,2,16,512]{3,2,1,0:T(8,128)} %shard_map.74.ahead), calls=%async_computation | async-start | bytes 1048576 | tf_op jit(solution)/shard_map/all_to_all | solution.py:307
  26.6 0.0 collective-permute-start.7
  26.6 3.6 %collective-permute-done.8.far = f32[928,128]{1,0:T(8,128)S(1)} collective-permute-done((f32[928,128]{1,0:T(8,128)S(1)}, f32[928,128]{1,0:T(8,128)S(1)}, u32[]{:S(2)}, u32[]{:S(2)}) %collective-permute-start.8) | collective-permute-done | bytes 475168 | tf_op jit(solution)/shard_map/ppermute | solution.py:324
  30.2 0.0 collective-permute-start.9
  30.2 0.0 collective-permute-done.7.near
  30.2 1.8 %collective-permute-done.9.cross = f32[928,128]{1,0:T(8,128)S(1)} collective-permute-done((f32[928,128]{1,0:T(8,128)S(1)}, f32[928,128]{1,0:T(8,128)S(1)}, u32[]{:S(2)}, u32[]{:S(2)}) %collective-permute-start.9) | collective-permute-done | bytes 475168 | tf_op jit(solution)/shard_map/ppermute | solution.py:326
  32.1 2.7 %shard_map.77.pull = f32[8,128]{1,0:T(8,128)S(1)} custom-call(f32[1056,128]{1,0:T(8,128)S(1)} %get-tuple-element.18.own, f32[1056,128]{1,0:T(8,128)S(1)} %collective-permute-done.7.near, f32[928,128]{1,0:T(8,128)S(1)} %collective-permute-done.8.far, f32[928,128]{1,0:T(8,128)S(1)} %collective-permute-done.9.cross, f32[5,128,128]{2,1,0:T(8,128)S(1)} %get-tuple-element.16.steps), custom_call_target="tpu_custom_call" | custom-call | bytes 100000 | tf_op jit(solution)/shard_map/pallas_call | solution.py:328
  34.8 2.2 %all-to-all-done.fields = f32[8,2,16,512]{3,2,1,0:T(8,128)S(1)} async-done(((f32[8,2,16,512]{3,2,1,0:T(8,128)}), f32[8,2,16,512]{3,2,1,0:T(8,128)S(1)}, u32[]{:S(2)}, u32[]{:S(2)}) %all-to-all-start) | async-done | bytes 524320 | tf_op jit(solution)/shard_map/all_to_all | solution.py:307
  37.0 0.6 %shard_map.78 = (f32[1,2,16,512]{3,2,1,0:T(8,128)S(1)}, f32[1,2,16,512]{3,2,1,0:T(8,128)S(1)}, f32[1,2,16,512]{3,2,1,0:T(8,128)S(1)}, f32[1,2,16,512]{3,2,1,0:T(...) custom-call(f32[5,128,128]{2,1,0:T(8,128)S(1)} %get-tuple-element.16.steps, ...), custom_call_target="tpu_custom_call" | custom-call | flops 100000000 | bytes 1000000 | tf_op jit(solution)/shard_map/pallas_call | solution.py:339
  37.6 0.1 collective-permute-start.14
  37.7 1.8 %collective-permute-start.10 = (f32[1,2,16,512]{3,2,1,0:T(8,128)S(1)}, f32[1,2,16,512]{3,2,1,0:T(8,128)S(1)}, u32[]{:S(2)}, u32[]{:S(2)}) collective-permute-start(f32[1,2,16,512]{3,2,1,0:T(8,128)S(1)} %get-tuple-element.21), channel_id=1, source_target_pairs={{0,16},{4,20},{8,24},{12,28},{16,0},{20,4},{24,8},{28,12},{1,17},{... | collective-permute-start | bytes 196616 | tf_op jit(solution)/shard_map/ppermute | solution.py:247
  39.4 2.2 %collective-permute-start.11 = (f32[1,2,16,512]{3,2,1,0:T(8,128)S(1)}, f32[1,2,16,512]{3,2,1,0:T(8,128)S(1)}, u32[]{:S(2)}, u32[]{:S(2)}) collective-permute-start(f32[1,2,16,512]{3,2,1,0:T(8,128)S(1)} %get-tuple-element.22), channel_id=1, source_target_pairs={{0,20},{4,16},{8,28},{12,24},{16,4},{20,0},{24,12},{28,8},{1,21},{... | collective-permute-start | bytes 196616 | tf_op jit(solution)/shard_map/ppermute | solution.py:247
  41.6 1.5 %collective-permute-start.12 = (f32[1,2,16,512]{3,2,1,0:T(8,128)S(1)}, f32[1,2,16,512]{3,2,1,0:T(8,128)S(1)}, u32[]{:S(2)}, u32[]{:S(2)}) collective-permute-start(f32[1,2,16,512]{3,2,1,0:T(8,128)S(1)} %get-tuple-element.23), channel_id=1, source_target_pairs={{0,24},{4,28},{8,16},{12,20},{16,8},{20,12},{24,0},{28,4},{1,25},{... | collective-permute-start | bytes 196616 | tf_op jit(solution)/shard_map/ppermute | solution.py:247
  43.1 2.3 %collective-permute-start.13 = (f32[1,2,16,512]{3,2,1,0:T(8,128)S(1)}, f32[1,2,16,512]{3,2,1,0:T(8,128)S(1)}, u32[]{:S(2)}, u32[]{:S(2)}) collective-permute-start(f32[1,2,16,512]{3,2,1,0:T(8,128)S(1)} %get-tuple-element.24), channel_id=1, source_target_pairs={{0,28},{4,24},{8,20},{12,16},{16,12},{20,8},{24,4},{28,0},{1,29},{... | collective-permute-start | bytes 196616 | tf_op jit(solution)/shard_map/ppermute | solution.py:247
  45.4 0.0 collective-permute-done.14.refs_5_
  45.4 1.5 %collective-permute-start.15 = (f32[1,2,16,512]{3,2,1,0:T(8,128)S(1)}, f32[1,2,16,512]{3,2,1,0:T(8,128)S(1)}, u32[]{:S(2)}, u32[]{:S(2)}) collective-permute-start(f32[1,2,16,512]{3,2,1,0:T(8,128)S(1)} %get-tuple-element.26), channel_id=1, source_target_pairs={{0,4},{4,0},{8,12},{12,8},{16,20},{20,16},{24,28},{28,24},{1,5},{5... | collective-permute-start | bytes 196616 | tf_op jit(solution)/shard_map/ppermute | solution.py:247
  46.9 0.9 %collective-permute-done.10.refs_1_ = f32[1,2,16,512]{3,2,1,0:T(8,128)S(1)} collective-permute-done((f32[1,2,16,512]{3,2,1,0:T(8,128)S(1)}, f32[1,2,16,512]{3,2,1,0:T(8,128)S(1)}, u32[]{:S(2)}, u32[]{:S(2)}) %collective-permute-start.10) | collective-permute-done | bytes 65568 | tf_op jit(solution)/shard_map/ppermute | solution.py:247
  47.9 1.3 %collective-permute-start.16 = (f32[1,2,16,512]{3,2,1,0:T(8,128)S(1)}, f32[1,2,16,512]{3,2,1,0:T(8,128)S(1)}, u32[]{:S(2)}, u32[]{:S(2)}) collective-permute-start(f32[1,2,16,512]{3,2,1,0:T(8,128)S(1)} %slice.4), channel_id=1, source_target_pairs={{0,4},{4,0},{8,12},{12,8},{16,20},{20,16},{24,28},{28,24},{1,5},{5... | collective-permute-start | bytes 196616 | tf_op jit(solution)/shard_map/ppermute | solution.py:247
  49.2 1.5 %collective-permute-done.11.refs_2_ = f32[1,2,16,512]{3,2,1,0:T(8,128)S(1)} collective-permute-done((f32[1,2,16,512]{3,2,1,0:T(8,128)S(1)}, f32[1,2,16,512]{3,2,1,0:T(8,128)S(1)}, u32[]{:S(2)}, u32[]{:S(2)}) %collective-permute-start.11) | collective-permute-done | bytes 65568 | tf_op jit(solution)/shard_map/ppermute | solution.py:247
  50.7 0.0 collective-permute-done.12.refs_3_
  50.7 0.0 collective-permute-done.13.refs_4_
  50.7 0.2 collective-permute-done.15.refs_6_
  50.9 1.2 %collective-permute-done.16.refs_7_ = f32[1,2,16,512]{3,2,1,0:T(8,128)S(1)} collective-permute-done((f32[1,2,16,512]{3,2,1,0:T(8,128)S(1)}, f32[1,2,16,512]{3,2,1,0:T(8,128)S(1)}, u32[]{:S(2)}, u32[]{:S(2)}) %collective-permute-start.16) | collective-permute-done | bytes 65568 | tf_op jit(solution)/shard_map/ppermute | solution.py:247
  52.1 0.9 %shard_map.79 = f32[16,2,4096]{2,1,0:T(2,128)} custom-call(f32[1,2,16,512]{3,2,1,0:T(8,128)S(1)} %get-tuple-element.20.refs_0_, f32[1,2,16,512]{3,2,1,0:T(8,128)S(1)} %collective-permute-done.10.refs_1_, f32[1,2,16,512]{3,2,1,0:T(8,128)S(1)} %collective-permute-done.11.refs_2_, f32[1,2,16,512]{3,2,1,0:T(8,128)S(1)} %collective-permute-done.12.refs_3_, ...), custom_call_target="tpu_custom_call" | custom-call | bytes 1000000 | tf_op jit(solution)/shard_map/pallas_call | solution.py:349
  (10 shorter events, 0.0 us)
Async XLA Ops:
  0.0 15.6 %copy-start = (f32[16,2,4096]{2,1,0:T(2,128)S(1)}, f32[16,2,4096]{2,1,0:T(2,128)}, u32[]{:S(2)}) copy-start(f32[16,2,4096]{2,1,0:T(2,128)} %refs_4_.1) | copy-start | bytes 1572868
  2.4 14.1 %copy-start.2 = (s32[4,4,64]{2,1,0:T(4,128)S(1)}, s32[4,4,64]{2,1,0:T(4,128)}, u32[]{:S(2)}) copy-start(s32[4,4,64]{2,1,0:T(4,128)} %refs_2_.1) | copy-start | bytes 12292
  2.4 14.0 %copy-start.3 = (s32[4,1,1,128]{3,2,1,0:T(1,128)S(1)}, s32[4,1,1,128]{3,2,1,0:T(1,128)}, u32[]{:S(2)}) copy-start(s32[4,1,1,128]{3,2,1,0:T(1,128)} %param.13) | copy-start | bytes 6148
  2.4 14.0 %copy-start.4 = (s32[4]{0:T(128)S(1)}, s32[4]{0:T(128)}, u32[]{:S(2)}) copy-start(s32[4]{0:T(128)} %owner.3) | copy-start | bytes 52
  2.4 14.0 %copy-start.5 = (f32[4,1,64]{2,1,0:T(1,128)S(1)}, f32[4,1,64]{2,1,0:T(1,128)}, u32[]{:S(2)}) copy-start(f32[4,1,64]{2,1,0:T(1,128)} %values.1) | copy-start | bytes 3076
  2.4 14.0 %copy-start.6 = (f32[4,1,64]{2,1,0:T(1,128)S(1)}, f32[4,1,64]{2,1,0:T(1,128)}, u32[]{:S(2)}) copy-start(f32[4,1,64]{2,1,0:T(1,128)} %errors.1) | copy-start | bytes 3076
  2.5 16.8 %copy-start.1 = (f32[136,128]{1,0:T(8,128)S(1)}, f32[136,128]{1,0:T(8,128)}, u32[]{:S(2)}) copy-start(f32[136,128]{1,0:T(8,128)} %shard_map.75.refs_0_) | copy-start | bytes 208900
  2.5 11.0 %collective-permute-start.1 = (f32[136,128]{1,0:T(8,128)}, f32[136,128]{1,0:T(8,128)S(1)}, u32[]{:S(2)}, u32[]{:S(2)}) collective-permute-start(f32[136,128]{1,0:T(8,128)} %shard_map.75.refs_0_), channel_id=1, source_target_pairs={{0,8},{4,12},{8,0},{12,4},{16,24},{20,28},{24,16},{28,20},{1,9},{5... | collective-permute-start | bytes 208904 | tf_op jit(solution)/shard_map/ppermute | solution.py:247
  5.6 9.4 %collective-permute-start.3 = (f32[136,128]{1,0:T(8,128)}, f32[136,128]{1,0:T(8,128)S(1)}, u32[]{:S(2)}, u32[]{:S(2)}) collective-permute-start(f32[136,128]{1,0:T(8,128)} %shard_map.75.refs_0_), channel_id=1, source_target_pairs={{0,16},{4,20},{8,24},{12,28},{16,0},{20,4},{24,8},{28,12},{1,17},{... | collective-permute-start | bytes 208904 | tf_op jit(solution)/shard_map/ppermute | solution.py:247
  8.1 9.3 %collective-permute-start = (f32[136,128]{1,0:T(8,128)}, f32[136,128]{1,0:T(8,128)S(1)}, u32[]{:S(2)}, u32[]{:S(2)}) collective-permute-start(f32[136,128]{1,0:T(8,128)} %shard_map.75.refs_0_), channel_id=1, source_target_pairs={{0,4},{4,0},{8,12},{12,8},{16,20},{20,16},{24,28},{28,24},{1,5},{5... | collective-permute-start | bytes 208904 | tf_op jit(solution)/shard_map/ppermute | solution.py:247
  9.7 7.8 %collective-permute-start.5 = (f32[136,128]{1,0:T(8,128)}, f32[136,128]{1,0:T(8,128)S(1)}, u32[]{:S(2)}, u32[]{:S(2)}) collective-permute-start(f32[136,128]{1,0:T(8,128)} %shard_map.75.refs_0_), channel_id=1, source_target_pairs={{0,24},{4,28},{8,16},{12,20},{16,8},{20,12},{24,0},{28,4},{1,25},{... | collective-permute-start | bytes 208904 | tf_op jit(solution)/shard_map/ppermute | solution.py:247
  9.9 7.6 %collective-permute-start.6 = (f32[136,128]{1,0:T(8,128)}, f32[136,128]{1,0:T(8,128)S(1)}, u32[]{:S(2)}, u32[]{:S(2)}) collective-permute-start(f32[136,128]{1,0:T(8,128)} %shard_map.75.refs_0_), channel_id=1, source_target_pairs={{0,28},{4,24},{8,20},{12,16},{16,12},{20,8},{24,4},{28,0},{1,29},{... | collective-permute-start | bytes 208904 | tf_op jit(solution)/shard_map/ppermute | solution.py:247
  13.4 4.5 %collective-permute-start.2 = (f32[136,128]{1,0:T(8,128)S(1)}, f32[136,128]{1,0:T(8,128)S(1)}, u32[]{:S(2)}, u32[]{:S(2)}) collective-permute-start(f32[136,128]{1,0:T(8,128)S(1)} %collective-permute-done.1.refs_2_), channel_id=1, source_target_pairs={{0,4},{4,0},{8,12},{12,8},{16,20},{20,16},{24,28},{28,24},{1,5},{5... | collective-permute-start | bytes 208904 | tf_op jit(solution)/shard_map/ppermute | solution.py:247
  15.0 4.3 %collective-permute-start.4 = (f32[136,128]{1,0:T(8,128)S(1)}, f32[136,128]{1,0:T(8,128)S(1)}, u32[]{:S(2)}, u32[]{:S(2)}) collective-permute-start(f32[136,128]{1,0:T(8,128)S(1)} %collective-permute-done.3.refs_4_), channel_id=1, source_target_pairs={{0,4},{4,0},{8,12},{12,8},{16,20},{20,16},{24,28},{28,24},{1,5},{5... | collective-permute-start | bytes 208904 | tf_op jit(solution)/shard_map/ppermute | solution.py:247
  20.1 10.2 %collective-permute-start.8 = (f32[928,128]{1,0:T(8,128)S(1)}, f32[928,128]{1,0:T(8,128)S(1)}, u32[]{:S(2)}, u32[]{:S(2)}) collective-permute-start(f32[928,128]{1,0:T(8,128)S(1)} %get-tuple-element.19), channel_id=1, source_target_pairs={{0,2},{1,3},{2,0},{3,1},{4,6},{5,7},{6,4},{7,5},{8,10},{9,11},{10,... | collective-permute-start | bytes 1425416 | tf_op jit(solution)/shard_map/ppermute | solution.py:324
  21.6 15.4 %all-to-all-start = ((f32[8,2,16,512]{3,2,1,0:T(8,128)}), f32[8,2,16,512]{3,2,1,0:T(8,128)S(1)}, u32[]{:S(2)}, u32[]{:S(2)}) async-start(f32[8,2,16,512]{3,2,1,0:T(8,128)} %shard_map.74.ahead), calls=%async_computation | async-start | bytes 1048576 | tf_op jit(solution)/shard_map/all_to_all | solution.py:307
  26.6 3.7 %collective-permute-start.7 = (f32[1056,128]{1,0:T(8,128)S(1)}, f32[1056,128]{1,0:T(8,128)S(1)}, u32[]{:S(2)}, u32[]{:S(2)}) collective-permute-start(f32[1056,128]{1,0:T(8,128)S(1)} %get-tuple-element.18.own), channel_id=1, source_target_pairs={{0,1},{1,0},{2,3},{3,2},{4,5},{5,4},{6,7},{7,6},{8,9},{9,8},{10,11... | collective-permute-start | bytes 1622024 | tf_op jit(solution)/shard_map/ppermute | solution.py:325
  30.2 1.8 %collective-permute-start.9 = (f32[928,128]{1,0:T(8,128)S(1)}, f32[928,128]{1,0:T(8,128)S(1)}, u32[]{:S(2)}, u32[]{:S(2)}) collective-permute-start(f32[928,128]{1,0:T(8,128)S(1)} %collective-permute-done.8.far), channel_id=1, source_target_pairs={{0,1},{1,0},{2,3},{3,2},{4,5},{5,4},{6,7},{7,6},{8,9},{9,8},{10,11... | collective-permute-start | bytes 1425416 | tf_op jit(solution)/shard_map/ppermute | solution.py:326
  37.6 7.8 %collective-permute-start.14 = (f32[2,2,16,512]{3,2,1,0:T(8,128)S(1)}, f32[2,2,16,512]{3,2,1,0:T(8,128)S(1)}, u32[]{:S(2)}, u32[]{:S(2)}) collective-permute-start(f32[2,2,16,512]{3,2,1,0:T(8,128)S(1)} %get-tuple-element.25), channel_id=1, source_target_pairs={{0,8},{4,12},{8,0},{12,4},{16,24},{20,28},{24,16},{28,20},{1,9},{5... | collective-permute-start | bytes 393224 | tf_op jit(solution)/shard_map/ppermute | solution.py:247
  37.7 10.2 %collective-permute-start.10 = (f32[1,2,16,512]{3,2,1,0:T(8,128)S(1)}, f32[1,2,16,512]{3,2,1,0:T(8,128)S(1)}, u32[]{:S(2)}, u32[]{:S(2)}) collective-permute-start(f32[1,2,16,512]{3,2,1,0:T(8,128)S(1)} %get-tuple-element.21), channel_id=1, source_target_pairs={{0,16},{4,20},{8,24},{12,28},{16,0},{20,4},{24,8},{28,12},{1,17},{... | collective-permute-start | bytes 196616 | tf_op jit(solution)/shard_map/ppermute | solution.py:247
  39.4 11.3 %collective-permute-start.11 = (f32[1,2,16,512]{3,2,1,0:T(8,128)S(1)}, f32[1,2,16,512]{3,2,1,0:T(8,128)S(1)}, u32[]{:S(2)}, u32[]{:S(2)}) collective-permute-start(f32[1,2,16,512]{3,2,1,0:T(8,128)S(1)} %get-tuple-element.22), channel_id=1, source_target_pairs={{0,20},{4,16},{8,28},{12,24},{16,4},{20,0},{24,12},{28,8},{1,21},{... | collective-permute-start | bytes 196616 | tf_op jit(solution)/shard_map/ppermute | solution.py:247
  41.6 9.1 %collective-permute-start.12 = (f32[1,2,16,512]{3,2,1,0:T(8,128)S(1)}, f32[1,2,16,512]{3,2,1,0:T(8,128)S(1)}, u32[]{:S(2)}, u32[]{:S(2)}) collective-permute-start(f32[1,2,16,512]{3,2,1,0:T(8,128)S(1)} %get-tuple-element.23), channel_id=1, source_target_pairs={{0,24},{4,28},{8,16},{12,20},{16,8},{20,12},{24,0},{28,4},{1,25},{... | collective-permute-start | bytes 196616 | tf_op jit(solution)/shard_map/ppermute | solution.py:247
  43.1 7.6 %collective-permute-start.13 = (f32[1,2,16,512]{3,2,1,0:T(8,128)S(1)}, f32[1,2,16,512]{3,2,1,0:T(8,128)S(1)}, u32[]{:S(2)}, u32[]{:S(2)}) collective-permute-start(f32[1,2,16,512]{3,2,1,0:T(8,128)S(1)} %get-tuple-element.24), channel_id=1, source_target_pairs={{0,28},{4,24},{8,20},{12,16},{16,12},{20,8},{24,4},{28,0},{1,29},{... | collective-permute-start | bytes 196616 | tf_op jit(solution)/shard_map/ppermute | solution.py:247
  45.4 5.5 %collective-permute-start.15 = (f32[1,2,16,512]{3,2,1,0:T(8,128)S(1)}, f32[1,2,16,512]{3,2,1,0:T(8,128)S(1)}, u32[]{:S(2)}, u32[]{:S(2)}) collective-permute-start(f32[1,2,16,512]{3,2,1,0:T(8,128)S(1)} %get-tuple-element.26), channel_id=1, source_target_pairs={{0,4},{4,0},{8,12},{12,8},{16,20},{20,16},{24,28},{28,24},{1,5},{5... | collective-permute-start | bytes 196616 | tf_op jit(solution)/shard_map/ppermute | solution.py:247
  47.9 4.3 %collective-permute-start.16 = (f32[1,2,16,512]{3,2,1,0:T(8,128)S(1)}, f32[1,2,16,512]{3,2,1,0:T(8,128)S(1)}, u32[]{:S(2)}, u32[]{:S(2)}) collective-permute-start(f32[1,2,16,512]{3,2,1,0:T(8,128)S(1)} %slice.4), channel_id=1, source_target_pairs={{0,4},{4,0},{8,12},{12,8},{16,20},{20,16},{24,28},{28,24},{1,5},{5... | collective-permute-start | bytes 196616 | tf_op jit(solution)/shard_map/ppermute | solution.py:247

commit v17 on v16

--- a/solution.py
+++ b/solution.py
@@ -134,8 +134,8 @@
     if len(pieces) == 1:
         held[...] = pieces[0][...]
     else:
-        for i, piece in enumerate(pieces):
-            held[lax.bitwise_xor(block, i)] = piece[...]
+        for distance, piece in zip(ORDER, pieces):
+            held[lax.bitwise_xor(block, distance)] = piece[...]
     common = width // NB * (NB - 1)
     for i in range(width // LANES):
         value = held[:, i * slab : (i + 1) * slab, :].reshape(members, LANES).T
@@ -255,7 +255,7 @@
         pieces[i] = hop(piece, i, n)
     for i in (4, 2):
         pieces[i + 1] = hop(pieces[i], 1, n)
-    return [pieces[i] for i in range(n)]
+    return [pieces[i] for i in ORDER]
 
 
 def exchange_parts(parts, n):

time: 53.3 us -> 55.4 us (1.039)
  waiting for transfers between devices: 13.4 us -> 17.8 us
  starting transfers between devices: 30.2 us -> 27.9 us
    ppermute x14, waiting for transfers between devices: 5.66 us -> 7.92 us  [hop(): return lax.ppermute(value, 'grid', [(j, j ^ distance) for j in range(n)])]
    ppermute x1, waiting for transfers between devices: 3.64 us -> 5.81 us  [body(): far = lax.ppermute(slim, 'lev', [(j, j ^ 2) for j in range(lev)])]
    ppermute x14, starting transfers between devices: 23.7 us -> 22.2 us  [hop(): return lax.ppermute(value, 'grid', [(j, j ^ distance) for j in range(n)])]
    all_to_all x1, starting transfers between devices: 4.95 us -> 4.12 us  [body(): fields = lax.all_to_all(send, 'grid', 0, 0, tiled=True)]
  transfers between devices with their start and end apart: 18 -> 18, of which waited for: 9 -> 10; matrix products, arithmetic and copies ran while one was open for 0% -> 0% of each run, Pallas kernels for 9% -> 8%
where the time goes in v17:
time: 55.4 us; the launch traced here: 55.2 us
  starting transfers between devices  27.9 us (50%)
  waiting for transfers between devices  17.8 us (32%)
  Pallas kernels  9.29 us (17%)
    ppermute x14, starting transfers between devices, hop(): return lax.ppermute(value, 'grid', [(j, j ^ distance) for j in range(n)])  22.2 us
    ppermute x14, waiting for transfers between devices, hop(): return lax.ppermute(value, 'grid', [(j, j ^ distance) for j in range(n)])  7.92 us
    ppermute x1, waiting for transfers between devices, body(): far = lax.ppermute(slim, 'lev', [(j, j ^ 2) for j in range(lev)])  5.81 us
    all_to_all x1, starting transfers between devices, body(): fields = lax.all_to_all(send, 'grid', 0, 0, tiled=True)  4.12 us
    pallas_call x1, Pallas kernels, body(): call(functools.partial(chain_kernel, (members, groups, count)), shape((8,...  2.72 us
    pallas_call x1, Pallas kernels, body(): call(functools.partial(pick_kernel, (slab, depth, block_cells, groups, co...  2.39 us
    all_to_all x1, waiting for transfers between devices, body(): fields = lax.all_to_all(send, 'grid', 0, 0, tiled=True)  2.27 us
    ppermute x1, waiting for transfers between devices, body(): cross = lax.ppermute(far, 'lev', [(j, j ^ 1) for j in range(lev)])  1.83 us
  transfers between devices with their start and end apart: 18, of which 10 were waited for; matrix products, arithmetic and copies ran while one was open for 0% of the time, Pallas kernels for 8%

profile of v17, /device:TPU:0, one launch (start us, length us, event | category | flops | bytes accessed | tf_op | source)
XLA Modules:
  0.0 55.2 jit_solution(7152081064877266272)
XLA Ops:
  0.0 2.4 %shard_map.75.refs_0_ = f32[136,128]{1,0:T(8,128)} custom-call(s32[4]{0:T(128)} %owner.3, f32[2,4]{1,0:T(2,128)} %refs_1_.1, s32[4,4,64]{2,1,0:T(4,128)} %refs_2_.1, s32[4,1,128]{2,1,0:T(1,128)} %bitcast.1, f32[16,2,4096]{2,1,0:T(2,128)} %refs_4_.1), custom_call_target="tpu_custom_call" | custom-call | bytes 1000000 | tf_op jit(solution)/shard_map/pallas_call | solution.py:285
  2.4 0.0 copy-start.2
  2.4 0.0 copy-start.3
  2.4 0.0 copy-start.4
  2.4 0.0 copy-start.5
  2.4 0.0 copy-start.6
  2.5 4.1 %collective-permute-start = (f32[136,128]{1,0:T(8,128)}, f32[136,128]{1,0:T(8,128)S(1)}, u32[]{:S(2)}, u32[]{:S(2)}) collective-permute-start(f32[136,128]{1,0:T(8,128)} %shard_map.75.refs_0_), channel_id=1, source_target_pairs={{0,16},{4,20},{8,24},{12,28},{16,0},{20,4},{24,8},{28,12},{1,17},{... | collective-permute-start | bytes 208904 | tf_op jit(solution)/shard_map/ppermute | solution.py:247
  6.6 1.6 %collective-permute-start.4 = (f32[136,128]{1,0:T(8,128)}, f32[136,128]{1,0:T(8,128)S(1)}, u32[]{:S(2)}, u32[]{:S(2)}) collective-permute-start(f32[136,128]{1,0:T(8,128)} %shard_map.75.refs_0_), channel_id=1, source_target_pairs={{0,8},{4,12},{8,0},{12,4},{16,24},{20,28},{24,16},{28,20},{1,9},{5... | collective-permute-start | bytes 208904 | tf_op jit(solution)/shard_map/ppermute | solution.py:247
  8.1 0.0 collective-permute-start.2
  8.2 4.8 %collective-permute-start.3 = (f32[136,128]{1,0:T(8,128)}, f32[136,128]{1,0:T(8,128)S(1)}, u32[]{:S(2)}, u32[]{:S(2)}) collective-permute-start(f32[136,128]{1,0:T(8,128)} %shard_map.75.refs_0_), channel_id=1, source_target_pairs={{0,28},{4,24},{8,20},{12,16},{16,12},{20,8},{24,4},{28,0},{1,29},{... | collective-permute-start | bytes 208904 | tf_op jit(solution)/shard_map/ppermute | solution.py:247
  12.9 0.5 collective-permute-start.5
  13.4 0.0 collective-permute-done.refs_1_
  13.4 1.5 %collective-permute-start.1 = (f32[136,128]{1,0:T(8,128)S(1)}, f32[136,128]{1,0:T(8,128)S(1)}, u32[]{:S(2)}, u32[]{:S(2)}) collective-permute-start(f32[136,128]{1,0:T(8,128)S(1)} %collective-permute-done.refs_1_), channel_id=1, source_target_pairs={{0,4},{4,0},{8,12},{12,8},{16,20},{20,16},{24,28},{28,24},{1,5},{5... | collective-permute-start | bytes 208904 | tf_op jit(solution)/shard_map/ppermute | solution.py:247
  15.0 0.0 collective-permute-done.4.refs_5_
  15.0 0.5 collective-permute-start.6
  15.5 0.9 %shard_map.74.ahead = f32[8,2,16,512]{3,2,1,0:T(8,128)} custom-call(f32[16,2,4096]{2,1,0:T(2,128)S(1)} %copy-done), custom_call_target="tpu_custom_call" | custom-call | bytes 1000000 | tf_op jit(solution)/shard_map/pallas_call | solution.py:301
  16.4 1.0 %shard_map.73 = (f32[32,128]{1,0:T(8,128)S(1)}, f32[5,128,128]{2,1,0:T(8,128)S(1)}) custom-call(s32[4]{0:T(128)S(1)} %copy-done.4, s32[4,4,64]{2,1,0:T(4,128)S(1)} %copy-done.2, f32[4,1,64]{2,1,0:T(1,128)S(1)} %copy-done.5, f32[4,1,64]{2,1,0:T(1,128)S(1)} %copy-done.6, s32[4,1,128]{2,1,0:T(1,128)S(1)} %bitcast.2), custom_call_target="tpu_custom_call" | custom-call | bytes 1000000 | tf_op jit(solution)/shard_map/pallas_call | solution.py:309
  17.4 0.0 collective-permute-done.2.refs_3_
  17.4 0.0 collective-permute-done.3.refs_4_
  17.4 0.9 %collective-permute-done.5.refs_6_ = f32[136,128]{1,0:T(8,128)S(1)} collective-permute-done((f32[136,128]{1,0:T(8,128)}, f32[136,128]{1,0:T(8,128)S(1)}, u32[]{:S(2)}, u32[]{:S(2)}) %collective-permute-start.5) | collective-permute-done | bytes 69664 | tf_op jit(solution)/shard_map/ppermute | solution.py:247
  18.3 0.8 %collective-permute-done.1.refs_2_ = f32[136,128]{1,0:T(8,128)S(1)} collective-permute-done((f32[136,128]{1,0:T(8,128)S(1)}, f32[136,128]{1,0:T(8,128)S(1)}, u32[]{:S(2)}, u32[]{:S(2)}) %collective-permute-start.1) | collective-permute-done | bytes 69664 | tf_op jit(solution)/shard_map/ppermute | solution.py:247
  19.1 0.7 %collective-permute-done.6.refs_7_ = f32[136,128]{1,0:T(8,128)S(1)} collective-permute-done((f32[136,128]{1,0:T(8,128)S(1)}, f32[136,128]{1,0:T(8,128)S(1)}, u32[]{:S(2)}, u32[]{:S(2)}) %collective-permute-start.6) | collective-permute-done | bytes 69664 | tf_op jit(solution)/shard_map/ppermute | solution.py:247
  19.8 0.8 %shard_map.76 = (f32[1056,128]{1,0:T(8,128)S(1)}, f32[928,128]{1,0:T(8,128)S(1)}) custom-call(s32[4]{0:T(128)S(1)} %copy-done.4, f32[32,128]{1,0:T(8,128)S(1)} %get-tuple-element.17.rows, f32[8,2,16,512]{3,2,1,0:T(8,128)} %shard_map.74.ahead, f32[136,128]{1,0:T(8,128)S(1)} %copy-done.1, f32[136,128]{1,0:T(8,128)S(1)} %collective-permute-done.refs_1_, ...), custom_call_target="tpu_custom_call" | custom-call | bytes 1000000 | tf_op jit(solution)/shard_map/pallas_call | solution.py:317
  20.6 1.6 %collective-permute-start.8 = (f32[928,128]{1,0:T(8,128)S(1)}, f32[928,128]{1,0:T(8,128)S(1)}, u32[]{:S(2)}, u32[]{:S(2)}) collective-permute-start(f32[928,128]{1,0:T(8,128)S(1)} %get-tuple-element.19), channel_id=1, source_target_pairs={{0,2},{1,3},{2,0},{3,1},{4,6},{5,7},{6,4},{7,5},{8,10},{9,11},{10,... | collective-permute-start | bytes 1425416 | tf_op jit(solution)/shard_map/ppermute | solution.py:324
  22.2 4.1 %all-to-all-start = ((f32[8,2,16,512]{3,2,1,0:T(8,128)}), f32[8,2,16,512]{3,2,1,0:T(8,128)S(1)}, u32[]{:S(2)}, u32[]{:S(2)}) async-start(f32[8,2,16,512]{3,2,1,0:T(8,128)} %shard_map.74.ahead), calls=%async_computation | async-start | bytes 1048576 | tf_op jit(solution)/shard_map/all_to_all | solution.py:307
  26.3 0.0 collective-permute-start.7
  26.3 5.8 %collective-permute-done.8.far = f32[928,128]{1,0:T(8,128)S(1)} collective-permute-done((f32[928,128]{1,0:T(8,128)S(1)}, f32[928,128]{1,0:T(8,128)S(1)}, u32[]{:S(2)}, u32[]{:S(2)}) %collective-permute-start.8) | collective-permute-done | bytes 475168 | tf_op jit(solution)/shard_map/ppermute | solution.py:324
  32.1 0.0 collective-permute-start.9
  32.1 0.0 collective-permute-done.7.near
  32.1 1.8 %collective-permute-done.9.cross = f32[928,128]{1,0:T(8,128)S(1)} collective-permute-done((f32[928,128]{1,0:T(8,128)S(1)}, f32[928,128]{1,0:T(8,128)S(1)}, u32[]{:S(2)}, u32[]{:S(2)}) %collective-permute-start.9) | collective-permute-done | bytes 475168 | tf_op jit(solution)/shard_map/ppermute | solution.py:326
  33.9 2.7 %shard_map.77.pull = f32[8,128]{1,0:T(8,128)S(1)} custom-call(f32[1056,128]{1,0:T(8,128)S(1)} %get-tuple-element.18.own, f32[1056,128]{1,0:T(8,128)S(1)} %collective-permute-done.7.near, f32[928,128]{1,0:T(8,128)S(1)} %collective-permute-done.8.far, f32[928,128]{1,0:T(8,128)S(1)} %collective-permute-done.9.cross, f32[5,128,128]{2,1,0:T(8,128)S(1)} %get-tuple-element.16.steps), custom_call_target="tpu_custom_call" | custom-call | bytes 100000 | tf_op jit(solution)/shard_map/pallas_call | solution.py:328
  36.7 2.3 %all-to-all-done.fields = f32[8,2,16,512]{3,2,1,0:T(8,128)S(1)} async-done(((f32[8,2,16,512]{3,2,1,0:T(8,128)}), f32[8,2,16,512]{3,2,1,0:T(8,128)S(1)}, u32[]{:S(2)}, u32[]{:S(2)}) %all-to-all-start) | async-done | bytes 524320 | tf_op jit(solution)/shard_map/all_to_all | solution.py:307
  38.9 0.6 %shard_map.78 = (f32[1,2,16,512]{3,2,1,0:T(8,128)S(1)}, f32[1,2,16,512]{3,2,1,0:T(8,128)S(1)}, f32[1,2,16,512]{3,2,1,0:T(8,128)S(1)}, f32[1,2,16,512]{3,2,1,0:T(...) custom-call(f32[5,128,128]{2,1,0:T(8,128)S(1)} %get-tuple-element.16.steps, ...), custom_call_target="tpu_custom_call" | custom-call | flops 100000000 | bytes 1000000 | tf_op jit(solution)/shard_map/pallas_call | solution.py:339
  39.5 0.8 %collective-permute-start.14 = (f32[2,2,16,512]{3,2,1,0:T(8,128)S(1)}, f32[2,2,16,512]{3,2,1,0:T(8,128)S(1)}, u32[]{:S(2)}, u32[]{:S(2)}) collective-permute-start(f32[2,2,16,512]{3,2,1,0:T(8,128)S(1)} %get-tuple-element.25), channel_id=1, source_target_pairs={{0,8},{4,12},{8,0},{12,4},{16,24},{20,28},{24,16},{28,20},{1,9},{5... | collective-permute-start | bytes 393224 | tf_op jit(solution)/shard_map/ppermute | solution.py:247
  40.3 1.0 %collective-permute-start.10 = (f32[1,2,16,512]{3,2,1,0:T(8,128)S(1)}, f32[1,2,16,512]{3,2,1,0:T(8,128)S(1)}, u32[]{:S(2)}, u32[]{:S(2)}) collective-permute-start(f32[1,2,16,512]{3,2,1,0:T(8,128)S(1)} %get-tuple-element.21), channel_id=1, source_target_pairs={{0,16},{4,20},{8,24},{12,28},{16,0},{20,4},{24,8},{28,12},{1,17},{... | collective-permute-start | bytes 196616 | tf_op jit(solution)/shard_map/ppermute | solution.py:247
  41.3 2.1 %collective-permute-start.11 = (f32[1,2,16,512]{3,2,1,0:T(8,128)S(1)}, f32[1,2,16,512]{3,2,1,0:T(8,128)S(1)}, u32[]{:S(2)}, u32[]{:S(2)}) collective-permute-start(f32[1,2,16,512]{3,2,1,0:T(8,128)S(1)} %get-tuple-element.22), channel_id=1, source_target_pairs={{0,20},{4,16},{8,28},{12,24},{16,4},{20,0},{24,12},{28,8},{1,21},{... | collective-permute-start | bytes 196616 | tf_op jit(solution)/shard_map/ppermute | solution.py:247
  43.5 1.5 %collective-permute-start.12 = (f32[1,2,16,512]{3,2,1,0:T(8,128)S(1)}, f32[1,2,16,512]{3,2,1,0:T(8,128)S(1)}, u32[]{:S(2)}, u32[]{:S(2)}) collective-permute-start(f32[1,2,16,512]{3,2,1,0:T(8,128)S(1)} %get-tuple-element.23), channel_id=1, source_target_pairs={{0,24},{4,28},{8,16},{12,20},{16,8},{20,12},{24,0},{28,4},{1,25},{... | collective-permute-start | bytes 196616 | tf_op jit(solution)/shard_map/ppermute | solution.py:247
  44.9 3.0 %collective-permute-start.13 = (f32[1,2,16,512]{3,2,1,0:T(8,128)S(1)}, f32[1,2,16,512]{3,2,1,0:T(8,128)S(1)}, u32[]{:S(2)}, u32[]{:S(2)}) collective-permute-start(f32[1,2,16,512]{3,2,1,0:T(8,128)S(1)} %get-tuple-element.24), channel_id=1, source_target_pairs={{0,28},{4,24},{8,20},{12,16},{16,12},{20,8},{24,4},{28,0},{1,29},{... | collective-permute-start | bytes 196616 | tf_op jit(solution)/shard_map/ppermute | solution.py:247
  48.0 0.0 collective-permute-done.14.refs_5_
  48.0 0.8 %collective-permute-start.15 = (f32[1,2,16,512]{3,2,1,0:T(8,128)S(1)}, f32[1,2,16,512]{3,2,1,0:T(8,128)S(1)}, u32[]{:S(2)}, u32[]{:S(2)}) collective-permute-start(f32[1,2,16,512]{3,2,1,0:T(8,128)S(1)} %get-tuple-element.26), channel_id=1, source_target_pairs={{0,4},{4,0},{8,12},{12,8},{16,20},{20,16},{24,28},{28,24},{1,5},{5... | collective-permute-start | bytes 196616 | tf_op jit(solution)/shard_map/ppermute | solution.py:247
  48.8 1.3 %collective-permute-done.10.refs_1_ = f32[1,2,16,512]{3,2,1,0:T(8,128)S(1)} collective-permute-done((f32[1,2,16,512]{3,2,1,0:T(8,128)S(1)}, f32[1,2,16,512]{3,2,1,0:T(8,128)S(1)}, u32[]{:S(2)}, u32[]{:S(2)}) %collective-permute-start.10) | collective-permute-done | bytes 65568 | tf_op jit(solution)/shard_map/ppermute | solution.py:247
  50.0 0.0 collective-permute-start.16
  50.1 2.2 %collective-permute-done.11.refs_2_ = f32[1,2,16,512]{3,2,1,0:T(8,128)S(1)} collective-permute-done((f32[1,2,16,512]{3,2,1,0:T(8,128)S(1)}, f32[1,2,16,512]{3,2,1,0:T(8,128)S(1)}, u32[]{:S(2)}, u32[]{:S(2)}) %collective-permute-start.11) | collective-permute-done | bytes 65568 | tf_op jit(solution)/shard_map/ppermute | solution.py:247
  52.3 0.0 collective-permute-done.12.refs_3_
  52.3 0.0 collective-permute-done.13.refs_4_
  52.3 0.6 %collective-permute-done.15.refs_6_ = f32[1,2,16,512]{3,2,1,0:T(8,128)S(1)} collective-permute-done((f32[1,2,16,512]{3,2,1,0:T(8,128)S(1)}, f32[1,2,16,512]{3,2,1,0:T(8,128)S(1)}, u32[]{:S(2)}, u32[]{:S(2)}) %collective-permute-start.15) | collective-permute-done | bytes 65568 | tf_op jit(solution)/shard_map/ppermute | solution.py:247
  52.8 1.5 %collective-permute-done.16.refs_7_ = f32[1,2,16,512]{3,2,1,0:T(8,128)S(1)} collective-permute-done((f32[1,2,16,512]{3,2,1,0:T(8,128)S(1)}, f32[1,2,16,512]{3,2,1,0:T(8,128)S(1)}, u32[]{:S(2)}, u32[]{:S(2)}) %collective-permute-start.16) | collective-permute-done | bytes 65568 | tf_op jit(solution)/shard_map/ppermute | solution.py:247
  54.3 0.9 %shard_map.79 = f32[16,2,4096]{2,1,0:T(2,128)} custom-call(f32[1,2,16,512]{3,2,1,0:T(8,128)S(1)} %get-tuple-element.20.refs_0_, f32[1,2,16,512]{3,2,1,0:T(8,128)S(1)} %collective-permute-done.10.refs_1_, f32[1,2,16,512]{3,2,1,0:T(8,128)S(1)} %collective-permute-done.11.refs_2_, f32[1,2,16,512]{3,2,1,0:T(8,128)S(1)} %collective-permute-done.12.refs_3_, ...), custom_call_target="tpu_custom_call" | custom-call | bytes 1000000 | tf_op jit(solution)/shard_map/pallas_call | solution.py:349
  (10 shorter events, 0.0 us)
Async XLA Ops:
  0.0 15.5 %copy-start = (f32[16,2,4096]{2,1,0:T(2,128)S(1)}, f32[16,2,4096]{2,1,0:T(2,128)}, u32[]{:S(2)}) copy-start(f32[16,2,4096]{2,1,0:T(2,128)} %refs_4_.1) | copy-start | bytes 1572868
  2.4 14.0 %copy-start.2 = (s32[4,4,64]{2,1,0:T(4,128)S(1)}, s32[4,4,64]{2,1,0:T(4,128)}, u32[]{:S(2)}) copy-start(s32[4,4,64]{2,1,0:T(4,128)} %refs_2_.1) | copy-start | bytes 12292
  2.4 14.0 %copy-start.3 = (s32[4,1,1,128]{3,2,1,0:T(1,128)S(1)}, s32[4,1,1,128]{3,2,1,0:T(1,128)}, u32[]{:S(2)}) copy-start(s32[4,1,1,128]{3,2,1,0:T(1,128)} %param.13) | copy-start | bytes 6148
  2.4 13.9 %copy-start.4 = (s32[4]{0:T(128)S(1)}, s32[4]{0:T(128)}, u32[]{:S(2)}) copy-start(s32[4]{0:T(128)} %owner.3) | copy-start | bytes 52
  2.4 13.9 %copy-start.5 = (f32[4,1,64]{2,1,0:T(1,128)S(1)}, f32[4,1,64]{2,1,0:T(1,128)}, u32[]{:S(2)}) copy-start(f32[4,1,64]{2,1,0:T(1,128)} %values.1) | copy-start | bytes 3076
  2.4 13.9 %copy-start.6 = (f32[4,1,64]{2,1,0:T(1,128)S(1)}, f32[4,1,64]{2,1,0:T(1,128)}, u32[]{:S(2)}) copy-start(f32[4,1,64]{2,1,0:T(1,128)} %errors.1) | copy-start | bytes 3076
  2.5 17.3 %copy-start.1 = (f32[136,128]{1,0:T(8,128)S(1)}, f32[136,128]{1,0:T(8,128)}, u32[]{:S(2)}) copy-start(f32[136,128]{1,0:T(8,128)} %shard_map.75.refs_0_) | copy-start | bytes 208900
  2.5 11.0 %collective-permute-start = (f32[136,128]{1,0:T(8,128)}, f32[136,128]{1,0:T(8,128)S(1)}, u32[]{:S(2)}, u32[]{:S(2)}) collective-permute-start(f32[136,128]{1,0:T(8,128)} %shard_map.75.refs_0_), channel_id=1, source_target_pairs={{0,16},{4,20},{8,24},{12,28},{16,0},{20,4},{24,8},{28,12},{1,17},{... | collective-permute-start | bytes 208904 | tf_op jit(solution)/shard_map/ppermute | solution.py:247
  6.6 8.4 %collective-permute-start.4 = (f32[136,128]{1,0:T(8,128)}, f32[136,128]{1,0:T(8,128)S(1)}, u32[]{:S(2)}, u32[]{:S(2)}) collective-permute-start(f32[136,128]{1,0:T(8,128)} %shard_map.75.refs_0_), channel_id=1, source_target_pairs={{0,8},{4,12},{8,0},{12,4},{16,24},{20,28},{24,16},{28,20},{1,9},{5... | collective-permute-start | bytes 208904 | tf_op jit(solution)/shard_map/ppermute | solution.py:247
  8.1 9.2 %collective-permute-start.2 = (f32[136,128]{1,0:T(8,128)}, f32[136,128]{1,0:T(8,128)S(1)}, u32[]{:S(2)}, u32[]{:S(2)}) collective-permute-start(f32[136,128]{1,0:T(8,128)} %shard_map.75.refs_0_), channel_id=1, source_target_pairs={{0,24},{4,28},{8,16},{12,20},{16,8},{20,12},{24,0},{28,4},{1,25},{... | collective-permute-start | bytes 208904 | tf_op jit(solution)/shard_map/ppermute | solution.py:247
  8.2 9.3 %collective-permute-start.3 = (f32[136,128]{1,0:T(8,128)}, f32[136,128]{1,0:T(8,128)S(1)}, u32[]{:S(2)}, u32[]{:S(2)}) collective-permute-start(f32[136,128]{1,0:T(8,128)} %shard_map.75.refs_0_), channel_id=1, source_target_pairs={{0,28},{4,24},{8,20},{12,16},{16,12},{20,8},{24,4},{28,0},{1,29},{... | collective-permute-start | bytes 208904 | tf_op jit(solution)/shard_map/ppermute | solution.py:247
  12.9 5.3 %collective-permute-start.5 = (f32[136,128]{1,0:T(8,128)}, f32[136,128]{1,0:T(8,128)S(1)}, u32[]{:S(2)}, u32[]{:S(2)}) collective-permute-start(f32[136,128]{1,0:T(8,128)} %shard_map.75.refs_0_), channel_id=1, source_target_pairs={{0,4},{4,0},{8,12},{12,8},{16,20},{20,16},{24,28},{28,24},{1,5},{5... | collective-permute-start | bytes 208904 | tf_op jit(solution)/shard_map/ppermute | solution.py:247
  13.4 5.6 %collective-permute-start.1 = (f32[136,128]{1,0:T(8,128)S(1)}, f32[136,128]{1,0:T(8,128)S(1)}, u32[]{:S(2)}, u32[]{:S(2)}) collective-permute-start(f32[136,128]{1,0:T(8,128)S(1)} %collective-permute-done.refs_1_), channel_id=1, source_target_pairs={{0,4},{4,0},{8,12},{12,8},{16,20},{20,16},{24,28},{28,24},{1,5},{5... | collective-permute-start | bytes 208904 | tf_op jit(solution)/shard_map/ppermute | solution.py:247
  15.0 4.8 %collective-permute-start.6 = (f32[136,128]{1,0:T(8,128)S(1)}, f32[136,128]{1,0:T(8,128)S(1)}, u32[]{:S(2)}, u32[]{:S(2)}) collective-permute-start(f32[136,128]{1,0:T(8,128)S(1)} %collective-permute-done.4.refs_5_), channel_id=1, source_target_pairs={{0,4},{4,0},{8,12},{12,8},{16,20},{20,16},{24,28},{28,24},{1,5},{5... | collective-permute-start | bytes 208904 | tf_op jit(solution)/shard_map/ppermute | solution.py:247
  20.6 11.5 %collective-permute-start.8 = (f32[928,128]{1,0:T(8,128)S(1)}, f32[928,128]{1,0:T(8,128)S(1)}, u32[]{:S(2)}, u32[]{:S(2)}) collective-permute-start(f32[928,128]{1,0:T(8,128)S(1)} %get-tuple-element.19), channel_id=1, source_target_pairs={{0,2},{1,3},{2,0},{3,1},{4,6},{5,7},{6,4},{7,5},{8,10},{9,11},{10,... | collective-permute-start | bytes 1425416 | tf_op jit(solution)/shard_map/ppermute | solution.py:324
  22.2 16.8 %all-to-all-start = ((f32[8,2,16,512]{3,2,1,0:T(8,128)}), f32[8,2,16,512]{3,2,1,0:T(8,128)S(1)}, u32[]{:S(2)}, u32[]{:S(2)}) async-start(f32[8,2,16,512]{3,2,1,0:T(8,128)} %shard_map.74.ahead), calls=%async_computation | async-start | bytes 1048576 | tf_op jit(solution)/shard_map/all_to_all | solution.py:307
  26.3 5.8 %collective-permute-start.7 = (f32[1056,128]{1,0:T(8,128)S(1)}, f32[1056,128]{1,0:T(8,128)S(1)}, u32[]{:S(2)}, u32[]{:S(2)}) collective-permute-start(f32[1056,128]{1,0:T(8,128)S(1)} %get-tuple-element.18.own), channel_id=1, source_target_pairs={{0,1},{1,0},{2,3},{3,2},{4,5},{5,4},{6,7},{7,6},{8,9},{9,8},{10,11... | collective-permute-start | bytes 1622024 | tf_op jit(solution)/shard_map/ppermute | solution.py:325
  32.1 1.8 %collective-permute-start.9 = (f32[928,128]{1,0:T(8,128)S(1)}, f32[928,128]{1,0:T(8,128)S(1)}, u32[]{:S(2)}, u32[]{:S(2)}) collective-permute-start(f32[928,128]{1,0:T(8,128)S(1)} %collective-permute-done.8.far), channel_id=1, source_target_pairs={{0,1},{1,0},{2,3},{3,2},{4,5},{5,4},{6,7},{7,6},{8,9},{9,8},{10,11... | collective-permute-start | bytes 1425416 | tf_op jit(solution)/shard_map/ppermute | solution.py:326
  39.5 8.4 %collective-permute-start.14 = (f32[2,2,16,512]{3,2,1,0:T(8,128)S(1)}, f32[2,2,16,512]{3,2,1,0:T(8,128)S(1)}, u32[]{:S(2)}, u32[]{:S(2)}) collective-permute-start(f32[2,2,16,512]{3,2,1,0:T(8,128)S(1)} %get-tuple-element.25), channel_id=1, source_target_pairs={{0,8},{4,12},{8,0},{12,4},{16,24},{20,28},{24,16},{28,20},{1,9},{5... | collective-permute-start | bytes 393224 | tf_op jit(solution)/shard_map/ppermute | solution.py:247
  40.3 9.7 %collective-permute-start.10 = (f32[1,2,16,512]{3,2,1,0:T(8,128)S(1)}, f32[1,2,16,512]{3,2,1,0:T(8,128)S(1)}, u32[]{:S(2)}, u32[]{:S(2)}) collective-permute-start(f32[1,2,16,512]{3,2,1,0:T(8,128)S(1)} %get-tuple-element.21), channel_id=1, source_target_pairs={{0,16},{4,20},{8,24},{12,28},{16,0},{20,4},{24,8},{28,12},{1,17},{... | collective-permute-start | bytes 196616 | tf_op jit(solution)/shard_map/ppermute | solution.py:247
  41.3 10.9 %collective-permute-start.11 = (f32[1,2,16,512]{3,2,1,0:T(8,128)S(1)}, f32[1,2,16,512]{3,2,1,0:T(8,128)S(1)}, u32[]{:S(2)}, u32[]{:S(2)}) collective-permute-start(f32[1,2,16,512]{3,2,1,0:T(8,128)S(1)} %get-tuple-element.22), channel_id=1, source_target_pairs={{0,20},{4,16},{8,28},{12,24},{16,4},{20,0},{24,12},{28,8},{1,21},{... | collective-permute-start | bytes 196616 | tf_op jit(solution)/shard_map/ppermute | solution.py:247
  43.5 8.8 %collective-permute-start.12 = (f32[1,2,16,512]{3,2,1,0:T(8,128)S(1)}, f32[1,2,16,512]{3,2,1,0:T(8,128)S(1)}, u32[]{:S(2)}, u32[]{:S(2)}) collective-permute-start(f32[1,2,16,512]{3,2,1,0:T(8,128)S(1)} %get-tuple-element.23), channel_id=1, source_target_pairs={{0,24},{4,28},{8,16},{12,20},{16,8},{20,12},{24,0},{28,4},{1,25},{... | collective-permute-start | bytes 196616 | tf_op jit(solution)/shard_map/ppermute | solution.py:247
  44.9 7.3 %collective-permute-start.13 = (f32[1,2,16,512]{3,2,1,0:T(8,128)S(1)}, f32[1,2,16,512]{3,2,1,0:T(8,128)S(1)}, u32[]{:S(2)}, u32[]{:S(2)}) collective-permute-start(f32[1,2,16,512]{3,2,1,0:T(8,128)S(1)} %get-tuple-element.24), channel_id=1, source_target_pairs={{0,28},{4,24},{8,20},{12,16},{16,12},{20,8},{24,4},{28,0},{1,29},{... | collective-permute-start | bytes 196616 | tf_op jit(solution)/shard_map/ppermute | solution.py:247
  48.0 4.9 %collective-permute-start.15 = (f32[1,2,16,512]{3,2,1,0:T(8,128)S(1)}, f32[1,2,16,512]{3,2,1,0:T(8,128)S(1)}, u32[]{:S(2)}, u32[]{:S(2)}) collective-permute-start(f32[1,2,16,512]{3,2,1,0:T(8,128)S(1)} %get-tuple-element.26), channel_id=1, source_target_pairs={{0,4},{4,0},{8,12},{12,8},{16,20},{20,16},{24,28},{28,24},{1,5},{5... | collective-permute-start | bytes 196616 | tf_op jit(solution)/shard_map/ppermute | solution.py:247
  50.0 4.3 %collective-permute-start.16 = (f32[1,2,16,512]{3,2,1,0:T(8,128)S(1)}, f32[1,2,16,512]{3,2,1,0:T(8,128)S(1)}, u32[]{:S(2)}, u32[]{:S(2)}) collective-permute-start(f32[1,2,16,512]{3,2,1,0:T(8,128)S(1)} %slice.4), channel_id=1, source_target_pairs={{0,4},{4,0},{8,12},{12,8},{16,20},{20,16},{24,28},{28,24},{1,5},{5... | collective-permute-start | bytes 196616 | tf_op jit(solution)/shard_map/ppermute | solution.py:247

commit v18 on v16

--- a/solution.py
+++ b/solution.py
@@ -17,18 +17,18 @@
 LIMIT = 48 * 1024 * 1024
 
 PARTS = ((0,), (4,), (5,), (6,), (7,), (2, 3), (1,))
-ORDER = (0, 4, 5, 6, 7, 2, 1, 3)
 PAIRS = [(e, b) for b in range(1, NB) for e in range(b)]
 PARENT, ALPHA, LATER, VALUE, OWN, SPARE = 0, 6, 12, 18, 22, 32
 
 
-def call(kernel, out_shapes, in_specs, scratch=(), flops=0, moved=0, limit=LIMIT):
+def call(kernel, out_shapes, in_specs, scratch=(), flops=0, moved=0, limit=LIMIT, out_specs=None, aliases={}):
     many = isinstance(out_shapes, (list, tuple))
     return pl.pallas_call(
         kernel,
         out_shape=out_shapes,
         in_specs=in_specs,
-        out_specs=[VMEM] * len(out_shapes) if many else VMEM,
+        out_specs=out_specs or ([VMEM] * len(out_shapes) if many else VMEM),
+        input_output_aliases=aliases,
         scratch_shapes=list(scratch),
         compiler_params=pltpu.CompilerParams(vmem_limit_bytes=limit),
         cost_estimate=pl.CostEstimate(flops=flops, bytes_accessed=moved, transcendentals=0),
@@ -232,15 +232,43 @@
     out[...] = pull
 
 
-def final_kernel(shape, *refs):
+def final_kernel(shape, arrived, out):
     n, slab, depth, block_cells = shape
-    pieces, out = refs[:-1], refs[-1]
+    for i in range(n):
+        for level in range(depth):
+            out[:, level, i * block_cells : (i + 1) * block_cells] = arrived[i, level]
+
+
+def place_kernel(shape, places, skip, *refs):
+    slab, depth, block_cells = shape
+    pieces, out, held, done = refs[skip:-3], refs[-3], refs[-2], refs[-1]
     block = lax.axis_index("grid")
-    for i in range(n):
-        region = i if len(pieces) == 1 else lax.bitwise_xor(block, ORDER[i])
-        cells = pl.ds(pl.multiple_of(region * block_cells, LANES), block_cells)
+    copies = []
+    for k, (i, j, distance) in enumerate(places):
         for level in range(depth):
-            out[:, level, cells] = pieces[0][i, level] if len(pieces) == 1 else pieces[i][0, level]
+            held[k, :, level, :] = pieces[i][j, level]
+        start = pl.multiple_of(lax.bitwise_xor(block, distance) * block_cells, LANES)
+        copies.append(pltpu.make_async_copy(held.at[k], out.at[:, :, pl.ds(start, block_cells)], done.at[k]))
+        copies[-1].start()
+    for copy in copies:
+        copy.wait()
+
+
+def place(shape, whole, places, pieces, before=None, moved=0):
+    slab, depth, block_cells = shape
+    given = [] if before is None else [before]
+    return call(
+        functools.partial(place_kernel, shape, places, len(given)),
+        whole,
+        [PLACE] * len(given) + [VMEM] * len(pieces),
+        scratch=[
+            pltpu.VMEM((len(places), slab, depth, block_cells), F32),
+            pltpu.SemaphoreType.DMA((len(places),)),
+        ],
+        moved=moved,
+        out_specs=PLACE,
+        aliases={0: 0} if given else {},
+    )(*given, *pieces)
 
 
 def hop(value, distance, n):
@@ -258,15 +286,12 @@
     return [pieces[i] for i in range(n)]
 
 
-def exchange_parts(parts, n):
-    if len(parts) == 1:
-        return [lax.all_to_all(parts[0], "grid", 0, 0, tiled=True)]
-    pieces = {0: parts[0]}
-    for part, distances in zip(parts[1:], PARTS[1:]):
-        pieces[distances[0]] = hop(part, distances[0], n)
-        if len(distances) == 2:
-            pieces[distances[1]] = hop(pieces[distances[0]][1:], 1, n)
-    return [pieces[i] for i in ORDER]
+def exchange_parts(parts, shape, whole, n):
+    far = [parts[0]] + [hop(part, distances[0], n) for part, distances in zip(parts[1:5], PARTS[1:5])]
+    near = hop(parts[5], PARTS[5][0], n)
+    beside, onward = hop(parts[6], 1, n), hop(near[1:], 1, n)
+    out = place(shape, whole, [(i, 0, PARTS[i][0]) for i in range(5)], far, moved=10**6)
+    return place(shape, whole, [(0, 0, 2), (1, 0, 1), (2, 0, 3)], [near, beside, onward], out, moved=10**6)
 
 
 def body(prior, channel_weights, obs_owner, obs_offset, obs_value, obs_error, ancestors):
@@ -344,14 +369,11 @@
         flops=10**8,
         moved=10**6,
     )(steps, pull, fields)
-    moved = exchange_parts(send, n)
-
-    return call(
-        functools.partial(final_kernel, (n, slab, depth, block_cells)),
-        shape((slab, depth, cells), F32),
-        [VMEM] * len(moved),
-        moved=10**6,
-    )(*moved)
+    whole = shape((slab, depth, cells), F32)
+    if n == 8:
+        return exchange_parts(send, (slab, depth, block_cells), whole, n)
+    moved = lax.all_to_all(send[0], "grid", 0, 0, tiled=True)
+    return call(functools.partial(final_kernel, (n, slab, depth, block_cells)), whole, [VMEM], moved=10**6)(moved)
 
 
 def solution(mesh):

time: 53.3 us -> 53 us (level)
  waiting for transfers between devices: 13.4 us -> 12.6 us
  Pallas kernels: 9.29 us -> 9.86 us
    ppermute x14, waiting for transfers between devices: 5.66 us -> 4.87 us  [hop(): return lax.ppermute(value, 'grid', [(j, j ^ distance) for j in range(n)])]
    pallas_call x1 -> x2, Pallas kernels: 0.92 us -> 1.49 us  [place(): call(functools.partial(place_kernel, shape, places, len(given)), whole, [...]
  transfers between devices with their start and end apart: 18 -> 18, of which waited for: 9 -> 8; matrix products, arithmetic and copies ran while one was open for 0% -> 0% of each run, Pallas kernels for 9% -> 10%
where the time goes in v18:
time: 53 us; the launch traced here: 52.8 us
  starting transfers between devices  30.2 us (57%)
  waiting for transfers between devices  12.6 us (24%)
  Pallas kernels  9.86 us (19%)
    ppermute x14, starting transfers between devices, hop(): return lax.ppermute(value, 'grid', [(j, j ^ distance) for j in range(n)])  23.7 us
    all_to_all x1, starting transfers between devices, body(): fields = lax.all_to_all(send, 'grid', 0, 0, tiled=True)  4.95 us
    ppermute x14, waiting for transfers between devices, hop(): return lax.ppermute(value, 'grid', [(j, j ^ distance) for j in range(n)])  4.87 us
    ppermute x1, waiting for transfers between devices, body(): far = lax.ppermute(slim, 'lev', [(j, j ^ 2) for j in range(lev)])  3.64 us
    pallas_call x1, Pallas kernels, body(): call(functools.partial(chain_kernel, (members, groups, count)), shape((8,...  2.72 us
    pallas_call x1, Pallas kernels, body(): call(functools.partial(pick_kernel, (slab, depth, block_cells, groups, co...  2.39 us
    all_to_all x1, waiting for transfers between devices, body(): fields = lax.all_to_all(send, 'grid', 0, 0, tiled=True)  2.22 us
    ppermute x1, waiting for transfers between devices, body(): cross = lax.ppermute(far, 'lev', [(j, j ^ 1) for j in range(lev)])  1.83 us
  transfers between devices with their start and end apart: 18, of which 8 were waited for; matrix products, arithmetic and copies ran while one was open for 0% of the time, Pallas kernels for 10%

profile of v18, /device:TPU:0, one launch (start us, length us, event | category | flops | bytes accessed | tf_op | source)
XLA Modules:
  0.0 52.8 jit_solution(10377346699592634926)
XLA Ops:
  0.0 2.4 %shard_map.75.refs_0_ = f32[136,128]{1,0:T(8,128)} custom-call(s32[4]{0:T(128)} %owner.3, f32[2,4]{1,0:T(2,128)} %refs_1_.1, s32[4,4,64]{2,1,0:T(4,128)} %refs_2_.1, s32[4,1,128]{2,1,0:T(1,128)} %bitcast.1, f32[16,2,4096]{2,1,0:T(2,128)} %refs_4_.1), custom_call_target="tpu_custom_call" | custom-call | bytes 1000000 | tf_op jit(solution)/shard_map/pallas_call | solution.py:310
  2.4 0.0 copy-start.2
  2.4 0.0 copy-start.3
  2.4 0.0 copy-start.4
  2.4 0.0 copy-start.5
  2.4 0.0 copy-start.6
  2.5 3.1 %collective-permute-start.1 = (f32[136,128]{1,0:T(8,128)}, f32[136,128]{1,0:T(8,128)S(1)}, u32[]{:S(2)}, u32[]{:S(2)}) collective-permute-start(f32[136,128]{1,0:T(8,128)} %shard_map.75.refs_0_), channel_id=1, source_target_pairs={{0,8},{4,12},{8,0},{12,4},{16,24},{20,28},{24,16},{28,20},{1,9},{5... | collective-permute-start | bytes 208904 | tf_op jit(solution)/shard_map/ppermute | solution.py:275
  5.6 2.6 %collective-permute-start.3 = (f32[136,128]{1,0:T(8,128)}, f32[136,128]{1,0:T(8,128)S(1)}, u32[]{:S(2)}, u32[]{:S(2)}) collective-permute-start(f32[136,128]{1,0:T(8,128)} %shard_map.75.refs_0_), channel_id=1, source_target_pairs={{0,16},{4,20},{8,24},{12,28},{16,0},{20,4},{24,8},{28,12},{1,17},{... | collective-permute-start | bytes 208904 | tf_op jit(solution)/shard_map/ppermute | solution.py:275
  8.2 1.5 %collective-permute-start = (f32[136,128]{1,0:T(8,128)}, f32[136,128]{1,0:T(8,128)S(1)}, u32[]{:S(2)}, u32[]{:S(2)}) collective-permute-start(f32[136,128]{1,0:T(8,128)} %shard_map.75.refs_0_), channel_id=1, source_target_pairs={{0,4},{4,0},{8,12},{12,8},{16,20},{20,16},{24,28},{28,24},{1,5},{5... | collective-permute-start | bytes 208904 | tf_op jit(solution)/shard_map/ppermute | solution.py:275
  9.7 0.2 collective-permute-start.5
  9.9 3.5 %collective-permute-start.6 = (f32[136,128]{1,0:T(8,128)}, f32[136,128]{1,0:T(8,128)S(1)}, u32[]{:S(2)}, u32[]{:S(2)}) collective-permute-start(f32[136,128]{1,0:T(8,128)} %shard_map.75.refs_0_), channel_id=1, source_target_pairs={{0,28},{4,24},{8,20},{12,16},{16,12},{20,8},{24,4},{28,0},{1,29},{... | collective-permute-start | bytes 208904 | tf_op jit(solution)/shard_map/ppermute | solution.py:275
  13.4 0.0 collective-permute-done.1.refs_2_
  13.4 1.5 %collective-permute-start.2 = (f32[136,128]{1,0:T(8,128)S(1)}, f32[136,128]{1,0:T(8,128)S(1)}, u32[]{:S(2)}, u32[]{:S(2)}) collective-permute-start(f32[136,128]{1,0:T(8,128)S(1)} %collective-permute-done.1.refs_2_), channel_id=1, source_target_pairs={{0,4},{4,0},{8,12},{12,8},{16,20},{20,16},{24,28},{28,24},{1,5},{5... | collective-permute-start | bytes 208904 | tf_op jit(solution)/shard_map/ppermute | solution.py:275
  15.0 0.0 collective-permute-done.3.refs_4_
  15.0 0.6 %collective-permute-start.4 = (f32[136,128]{1,0:T(8,128)S(1)}, f32[136,128]{1,0:T(8,128)S(1)}, u32[]{:S(2)}, u32[]{:S(2)}) collective-permute-start(f32[136,128]{1,0:T(8,128)S(1)} %collective-permute-done.3.refs_4_), channel_id=1, source_target_pairs={{0,4},{4,0},{8,12},{12,8},{16,20},{20,16},{24,28},{28,24},{1,5},{5... | collective-permute-start | bytes 208904 | tf_op jit(solution)/shard_map/ppermute | solution.py:275
  15.6 0.9 %shard_map.74.ahead = f32[8,2,16,512]{3,2,1,0:T(8,128)} custom-call(f32[16,2,4096]{2,1,0:T(2,128)S(1)} %copy-done), custom_call_target="tpu_custom_call" | custom-call | bytes 1000000 | tf_op jit(solution)/shard_map/pallas_call | solution.py:326
  16.5 1.0 %shard_map.73 = (f32[32,128]{1,0:T(8,128)S(1)}, f32[5,128,128]{2,1,0:T(8,128)S(1)}) custom-call(s32[4]{0:T(128)S(1)} %copy-done.4, s32[4,4,64]{2,1,0:T(4,128)S(1)} %copy-done.2, f32[4,1,64]{2,1,0:T(1,128)S(1)} %copy-done.5, f32[4,1,64]{2,1,0:T(1,128)S(1)} %copy-done.6, s32[4,1,128]{2,1,0:T(1,128)S(1)} %bitcast.2), custom_call_target="tpu_custom_call" | custom-call | bytes 1000000 | tf_op jit(solution)/shard_map/pallas_call | solution.py:334
  17.5 0.0 collective-permute-done.refs_1_
  17.5 0.0 collective-permute-done.5.refs_6_
  17.5 0.0 collective-permute-done.6.refs_7_
  17.5 0.4 collective-permute-done.2.refs_3_
  18.0 1.3 %collective-permute-done.4.refs_5_ = f32[136,128]{1,0:T(8,128)S(1)} collective-permute-done((f32[136,128]{1,0:T(8,128)S(1)}, f32[136,128]{1,0:T(8,128)S(1)}, u32[]{:S(2)}, u32[]{:S(2)}) %collective-permute-start.4) | collective-permute-done | bytes 69664 | tf_op jit(solution)/shard_map/ppermute | solution.py:275
  19.3 0.8 %shard_map.76 = (f32[1056,128]{1,0:T(8,128)S(1)}, f32[928,128]{1,0:T(8,128)S(1)}) custom-call(s32[4]{0:T(128)S(1)} %copy-done.4, f32[32,128]{1,0:T(8,128)S(1)} %get-tuple-element.17.rows, f32[8,2,16,512]{3,2,1,0:T(8,128)} %shard_map.74.ahead, f32[136,128]{1,0:T(8,128)S(1)} %copy-done.1, f32[136,128]{1,0:T(8,128)S(1)} %collective-permute-done.refs_1_, ...), custom_call_target="tpu_custom_call" | custom-call | bytes 1000000 | tf_op jit(solution)/shard_map/pallas_call | solution.py:342
  20.1 1.6 %collective-permute-start.8 = (f32[928,128]{1,0:T(8,128)S(1)}, f32[928,128]{1,0:T(8,128)S(1)}, u32[]{:S(2)}, u32[]{:S(2)}) collective-permute-start(f32[928,128]{1,0:T(8,128)S(1)} %get-tuple-element.19), channel_id=1, source_target_pairs={{0,2},{1,3},{2,0},{3,1},{4,6},{5,7},{6,4},{7,5},{8,10},{9,11},{10,... | collective-permute-start | bytes 1425416 | tf_op jit(solution)/shard_map/ppermute | solution.py:349
  21.6 4.9 %all-to-all-start = ((f32[8,2,16,512]{3,2,1,0:T(8,128)}), f32[8,2,16,512]{3,2,1,0:T(8,128)S(1)}, u32[]{:S(2)}, u32[]{:S(2)}) async-start(f32[8,2,16,512]{3,2,1,0:T(8,128)} %shard_map.74.ahead), calls=%async_computation | async-start | bytes 1048576 | tf_op jit(solution)/shard_map/all_to_all | solution.py:332
  26.6 0.0 collective-permute-start.7
  26.6 3.6 %collective-permute-done.8.far = f32[928,128]{1,0:T(8,128)S(1)} collective-permute-done((f32[928,128]{1,0:T(8,128)S(1)}, f32[928,128]{1,0:T(8,128)S(1)}, u32[]{:S(2)}, u32[]{:S(2)}) %collective-permute-start.8) | collective-permute-done | bytes 475168 | tf_op jit(solution)/shard_map/ppermute | solution.py:349
  30.2 0.0 collective-permute-start.9
  30.2 0.0 collective-permute-done.7.near
  30.2 1.8 %collective-permute-done.9.cross = f32[928,128]{1,0:T(8,128)S(1)} collective-permute-done((f32[928,128]{1,0:T(8,128)S(1)}, f32[928,128]{1,0:T(8,128)S(1)}, u32[]{:S(2)}, u32[]{:S(2)}) %collective-permute-start.9) | collective-permute-done | bytes 475168 | tf_op jit(solution)/shard_map/ppermute | solution.py:351
  32.1 2.7 %shard_map.77.pull = f32[8,128]{1,0:T(8,128)S(1)} custom-call(f32[1056,128]{1,0:T(8,128)S(1)} %get-tuple-element.18.own, f32[1056,128]{1,0:T(8,128)S(1)} %collective-permute-done.7.near, f32[928,128]{1,0:T(8,128)S(1)} %collective-permute-done.8.far, f32[928,128]{1,0:T(8,128)S(1)} %collective-permute-done.9.cross, f32[5,128,128]{2,1,0:T(8,128)S(1)} %get-tuple-element.16.steps), custom_call_target="tpu_custom_call" | custom-call | bytes 100000 | tf_op jit(solution)/shard_map/pallas_call | solution.py:353
  34.8 2.2 %all-to-all-done.fields = f32[8,2,16,512]{3,2,1,0:T(8,128)S(1)} async-done(((f32[8,2,16,512]{3,2,1,0:T(8,128)}), f32[8,2,16,512]{3,2,1,0:T(8,128)S(1)}, u32[]{:S(2)}, u32[]{:S(2)}) %all-to-all-start) | async-done | bytes 524320 | tf_op jit(solution)/shard_map/all_to_all | solution.py:332
  37.0 0.6 %shard_map.78 = (f32[1,2,16,512]{3,2,1,0:T(8,128)S(1)}, f32[1,2,16,512]{3,2,1,0:T(8,128)S(1)}, f32[1,2,16,512]{3,2,1,0:T(8,128)S(1)}, f32[1,2,16,512]{3,2,1,0:T(...) custom-call(f32[5,128,128]{2,1,0:T(8,128)S(1)} %get-tuple-element.16.steps, ...), custom_call_target="tpu_custom_call" | custom-call | flops 100000000 | bytes 1000000 | tf_op jit(solution)/shard_map/pallas_call | solution.py:364
  37.6 0.1 collective-permute-start.14
  37.7 1.8 %collective-permute-start.10 = (f32[1,2,16,512]{3,2,1,0:T(8,128)S(1)}, f32[1,2,16,512]{3,2,1,0:T(8,128)S(1)}, u32[]{:S(2)}, u32[]{:S(2)}) collective-permute-start(f32[1,2,16,512]{3,2,1,0:T(8,128)S(1)} %get-tuple-element.21), channel_id=1, source_target_pairs={{0,16},{4,20},{8,24},{12,28},{16,0},{20,4},{24,8},{28,12},{1,17},{... | collective-permute-start | bytes 196616 | tf_op jit(solution)/shard_map/ppermute | solution.py:275
  39.4 2.2 %collective-permute-start.11 = (f32[1,2,16,512]{3,2,1,0:T(8,128)S(1)}, f32[1,2,16,512]{3,2,1,0:T(8,128)S(1)}, u32[]{:S(2)}, u32[]{:S(2)}) collective-permute-start(f32[1,2,16,512]{3,2,1,0:T(8,128)S(1)} %get-tuple-element.22), channel_id=1, source_target_pairs={{0,20},{4,16},{8,28},{12,24},{16,4},{20,0},{24,12},{28,8},{1,21},{... | collective-permute-start | bytes 196616 | tf_op jit(solution)/shard_map/ppermute | solution.py:275
  41.6 1.5 %collective-permute-start.12 = (f32[1,2,16,512]{3,2,1,0:T(8,128)S(1)}, f32[1,2,16,512]{3,2,1,0:T(8,128)S(1)}, u32[]{:S(2)}, u32[]{:S(2)}) collective-permute-start(f32[1,2,16,512]{3,2,1,0:T(8,128)S(1)} %get-tuple-element.23), channel_id=1, source_target_pairs={{0,24},{4,28},{8,16},{12,20},{16,8},{20,12},{24,0},{28,4},{1,25},{... | collective-permute-start | bytes 196616 | tf_op jit(solution)/shard_map/ppermute | solution.py:275
  43.1 2.3 %collective-permute-start.13 = (f32[1,2,16,512]{3,2,1,0:T(8,128)S(1)}, f32[1,2,16,512]{3,2,1,0:T(8,128)S(1)}, u32[]{:S(2)}, u32[]{:S(2)}) collective-permute-start(f32[1,2,16,512]{3,2,1,0:T(8,128)S(1)} %get-tuple-element.24), channel_id=1, source_target_pairs={{0,28},{4,24},{8,20},{12,16},{16,12},{20,8},{24,4},{28,0},{1,29},{... | collective-permute-start | bytes 196616 | tf_op jit(solution)/shard_map/ppermute | solution.py:275
  45.4 0.0 collective-permute-done.14.refs_1_
  45.4 1.5 %collective-permute-start.15 = (f32[1,2,16,512]{3,2,1,0:T(8,128)S(1)}, f32[1,2,16,512]{3,2,1,0:T(8,128)S(1)}, u32[]{:S(2)}, u32[]{:S(2)}) collective-permute-start(f32[1,2,16,512]{3,2,1,0:T(8,128)S(1)} %get-tuple-element.26), channel_id=1, source_target_pairs={{0,4},{4,0},{8,12},{12,8},{16,20},{20,16},{24,28},{28,24},{1,5},{5... | collective-permute-start | bytes 196616 | tf_op jit(solution)/shard_map/ppermute | solution.py:275
  46.9 0.9 %collective-permute-done.10.refs_1_ = f32[1,2,16,512]{3,2,1,0:T(8,128)S(1)} collective-permute-done((f32[1,2,16,512]{3,2,1,0:T(8,128)S(1)}, f32[1,2,16,512]{3,2,1,0:T(8,128)S(1)}, u32[]{:S(2)}, u32[]{:S(2)}) %collective-permute-start.10) | collective-permute-done | bytes 65568 | tf_op jit(solution)/shard_map/ppermute | solution.py:275
  47.9 1.3 %collective-permute-start.16 = (f32[1,2,16,512]{3,2,1,0:T(8,128)S(1)}, f32[1,2,16,512]{3,2,1,0:T(8,128)S(1)}, u32[]{:S(2)}, u32[]{:S(2)}) collective-permute-start(f32[1,2,16,512]{3,2,1,0:T(8,128)S(1)} %slice.4), channel_id=1, source_target_pairs={{0,4},{4,0},{8,12},{12,8},{16,20},{20,16},{24,28},{28,24},{1,5},{5... | collective-permute-start | bytes 196616 | tf_op jit(solution)/shard_map/ppermute | solution.py:275
  49.2 1.5 %collective-permute-done.11.refs_2_ = f32[1,2,16,512]{3,2,1,0:T(8,128)S(1)} collective-permute-done((f32[1,2,16,512]{3,2,1,0:T(8,128)S(1)}, f32[1,2,16,512]{3,2,1,0:T(8,128)S(1)}, u32[]{:S(2)}, u32[]{:S(2)}) %collective-permute-start.11) | collective-permute-done | bytes 65568 | tf_op jit(solution)/shard_map/ppermute | solution.py:275
  50.7 0.0 collective-permute-done.12.refs_3_
  50.7 0.8 %shard_map.79.refs_0_ = f32[16,2,4096]{2,1,0:T(2,128)} custom-call(f32[1,2,16,512]{3,2,1,0:T(8,128)S(1)} %get-tuple-element.20.refs_0_, f32[1,2,16,512]{3,2,1,0:T(8,128)S(1)} %collective-permute-done.10.refs_1_, f32[1,2,16,512]{3,2,1,0:T(8,128)S(1)} %collective-permute-done.11.refs_2_, f32[1,2,16,512]{3,2,1,0:T(8,128)S(1)} %collective-permute-done.12.refs_3_, ...), custom_call_target="tpu_custom_call" | custom-call | bytes 1000000 | tf_op jit(solution)/shard_map/pallas_call | solution.py:260
  51.5 0.0 collective-permute-done.15.refs_2_
  51.5 0.6 %collective-permute-done.16.refs_3_ = f32[1,2,16,512]{3,2,1,0:T(8,128)S(1)} collective-permute-done((f32[1,2,16,512]{3,2,1,0:T(8,128)S(1)}, f32[1,2,16,512]{3,2,1,0:T(8,128)S(1)}, u32[]{:S(2)}, u32[]{:S(2)}) %collective-permute-start.16) | collective-permute-done | bytes 65568 | tf_op jit(solution)/shard_map/ppermute | solution.py:275
  52.1 0.7 %shard_map.80 = f32[16,2,4096]{2,1,0:T(2,128)} custom-call(f32[16,2,4096]{2,1,0:T(2,128)} %shard_map.79.refs_0_, f32[2,2,16,512]{3,2,1,0:T(8,128)S(1)} %collective-permute-done.14.refs_1_, f32[1,2,16,512]{3,2,1,0:T(8,128)S(1)} %collective-permute-done.15.refs_2_, f32[1,2,16,512]{3,2,1,0:T(8,128)S(1)} %collective-permute-done.16.refs_3_), custom_call_target="tpu_custom_call", output_to_operand_aliasing={{}: (0, {})} | custom-call | bytes 1000000 | tf_op jit(solution)/shard_map/pallas_call | solution.py:260
  (11 shorter events, 0.0 us)
Async XLA Ops:
  0.0 15.6 %copy-start = (f32[16,2,4096]{2,1,0:T(2,128)S(1)}, f32[16,2,4096]{2,1,0:T(2,128)}, u32[]{:S(2)}) copy-start(f32[16,2,4096]{2,1,0:T(2,128)} %refs_4_.1) | copy-start | bytes 1572868
  2.4 14.1 %copy-start.2 = (s32[4,4,64]{2,1,0:T(4,128)S(1)}, s32[4,4,64]{2,1,0:T(4,128)}, u32[]{:S(2)}) copy-start(s32[4,4,64]{2,1,0:T(4,128)} %refs_2_.1) | copy-start | bytes 12292
  2.4 14.0 %copy-start.3 = (s32[4,1,1,128]{3,2,1,0:T(1,128)S(1)}, s32[4,1,1,128]{3,2,1,0:T(1,128)}, u32[]{:S(2)}) copy-start(s32[4,1,1,128]{3,2,1,0:T(1,128)} %param.13) | copy-start | bytes 6148
  2.4 14.0 %copy-start.4 = (s32[4]{0:T(128)S(1)}, s32[4]{0:T(128)}, u32[]{:S(2)}) copy-start(s32[4]{0:T(128)} %owner.3) | copy-start | bytes 52
  2.4 14.0 %copy-start.5 = (f32[4,1,64]{2,1,0:T(1,128)S(1)}, f32[4,1,64]{2,1,0:T(1,128)}, u32[]{:S(2)}) copy-start(f32[4,1,64]{2,1,0:T(1,128)} %values.1) | copy-start | bytes 3076
  2.4 14.0 %copy-start.6 = (f32[4,1,64]{2,1,0:T(1,128)S(1)}, f32[4,1,64]{2,1,0:T(1,128)}, u32[]{:S(2)}) copy-start(f32[4,1,64]{2,1,0:T(1,128)} %errors.1) | copy-start | bytes 3076
  2.5 16.8 %copy-start.1 = (f32[136,128]{1,0:T(8,128)S(1)}, f32[136,128]{1,0:T(8,128)}, u32[]{:S(2)}) copy-start(f32[136,128]{1,0:T(8,128)} %shard_map.75.refs_0_) | copy-start | bytes 208900
  2.5 11.0 %collective-permute-start.1 = (f32[136,128]{1,0:T(8,128)}, f32[136,128]{1,0:T(8,128)S(1)}, u32[]{:S(2)}, u32[]{:S(2)}) collective-permute-start(f32[136,128]{1,0:T(8,128)} %shard_map.75.refs_0_), channel_id=1, source_target_pairs={{0,8},{4,12},{8,0},{12,4},{16,24},{20,28},{24,16},{28,20},{1,9},{5... | collective-permute-start | bytes 208904 | tf_op jit(solution)/shard_map/ppermute | solution.py:275
  5.6 9.4 %collective-permute-start.3 = (f32[136,128]{1,0:T(8,128)}, f32[136,128]{1,0:T(8,128)S(1)}, u32[]{:S(2)}, u32[]{:S(2)}) collective-permute-start(f32[136,128]{1,0:T(8,128)} %shard_map.75.refs_0_), channel_id=1, source_target_pairs={{0,16},{4,20},{8,24},{12,28},{16,0},{20,4},{24,8},{28,12},{1,17},{... | collective-permute-start | bytes 208904 | tf_op jit(solution)/shard_map/ppermute | solution.py:275
  8.2 9.3 %collective-permute-start = (f32[136,128]{1,0:T(8,128)}, f32[136,128]{1,0:T(8,128)S(1)}, u32[]{:S(2)}, u32[]{:S(2)}) collective-permute-start(f32[136,128]{1,0:T(8,128)} %shard_map.75.refs_0_), channel_id=1, source_target_pairs={{0,4},{4,0},{8,12},{12,8},{16,20},{20,16},{24,28},{28,24},{1,5},{5... | collective-permute-start | bytes 208904 | tf_op jit(solution)/shard_map/ppermute | solution.py:275
  9.7 7.8 %collective-permute-start.5 = (f32[136,128]{1,0:T(8,128)}, f32[136,128]{1,0:T(8,128)S(1)}, u32[]{:S(2)}, u32[]{:S(2)}) collective-permute-start(f32[136,128]{1,0:T(8,128)} %shard_map.75.refs_0_), channel_id=1, source_target_pairs={{0,24},{4,28},{8,16},{12,20},{16,8},{20,12},{24,0},{28,4},{1,25},{... | collective-permute-start | bytes 208904 | tf_op jit(solution)/shard_map/ppermute | solution.py:275
  9.9 7.6 %collective-permute-start.6 = (f32[136,128]{1,0:T(8,128)}, f32[136,128]{1,0:T(8,128)S(1)}, u32[]{:S(2)}, u32[]{:S(2)}) collective-permute-start(f32[136,128]{1,0:T(8,128)} %shard_map.75.refs_0_), channel_id=1, source_target_pairs={{0,28},{4,24},{8,20},{12,16},{16,12},{20,8},{24,4},{28,0},{1,29},{... | collective-permute-start | bytes 208904 | tf_op jit(solution)/shard_map/ppermute | solution.py:275
  13.4 4.5 %collective-permute-start.2 = (f32[136,128]{1,0:T(8,128)S(1)}, f32[136,128]{1,0:T(8,128)S(1)}, u32[]{:S(2)}, u32[]{:S(2)}) collective-permute-start(f32[136,128]{1,0:T(8,128)S(1)} %collective-permute-done.1.refs_2_), channel_id=1, source_target_pairs={{0,4},{4,0},{8,12},{12,8},{16,20},{20,16},{24,28},{28,24},{1,5},{5... | collective-permute-start | bytes 208904 | tf_op jit(solution)/shard_map/ppermute | solution.py:275
  15.0 4.3 %collective-permute-start.4 = (f32[136,128]{1,0:T(8,128)S(1)}, f32[136,128]{1,0:T(8,128)S(1)}, u32[]{:S(2)}, u32[]{:S(2)}) collective-permute-start(f32[136,128]{1,0:T(8,128)S(1)} %collective-permute-done.3.refs_4_), channel_id=1, source_target_pairs={{0,4},{4,0},{8,12},{12,8},{16,20},{20,16},{24,28},{28,24},{1,5},{5... | collective-permute-start | bytes 208904 | tf_op jit(solution)/shard_map/ppermute | solution.py:275
  20.1 10.2 %collective-permute-start.8 = (f32[928,128]{1,0:T(8,128)S(1)}, f32[928,128]{1,0:T(8,128)S(1)}, u32[]{:S(2)}, u32[]{:S(2)}) collective-permute-start(f32[928,128]{1,0:T(8,128)S(1)} %get-tuple-element.19), channel_id=1, source_target_pairs={{0,2},{1,3},{2,0},{3,1},{4,6},{5,7},{6,4},{7,5},{8,10},{9,11},{10,... | collective-permute-start | bytes 1425416 | tf_op jit(solution)/shard_map/ppermute | solution.py:349
  21.6 15.4 %all-to-all-start = ((f32[8,2,16,512]{3,2,1,0:T(8,128)}), f32[8,2,16,512]{3,2,1,0:T(8,128)S(1)}, u32[]{:S(2)}, u32[]{:S(2)}) async-start(f32[8,2,16,512]{3,2,1,0:T(8,128)} %shard_map.74.ahead), calls=%async_computation | async-start | bytes 1048576 | tf_op jit(solution)/shard_map/all_to_all | solution.py:332
  26.6 3.7 %collective-permute-start.7 = (f32[1056,128]{1,0:T(8,128)S(1)}, f32[1056,128]{1,0:T(8,128)S(1)}, u32[]{:S(2)}, u32[]{:S(2)}) collective-permute-start(f32[1056,128]{1,0:T(8,128)S(1)} %get-tuple-element.18.own), channel_id=1, source_target_pairs={{0,1},{1,0},{2,3},{3,2},{4,5},{5,4},{6,7},{7,6},{8,9},{9,8},{10,11... | collective-permute-start | bytes 1622024 | tf_op jit(solution)/shard_map/ppermute | solution.py:350
  30.2 1.8 %collective-permute-start.9 = (f32[928,128]{1,0:T(8,128)S(1)}, f32[928,128]{1,0:T(8,128)S(1)}, u32[]{:S(2)}, u32[]{:S(2)}) collective-permute-start(f32[928,128]{1,0:T(8,128)S(1)} %collective-permute-done.8.far), channel_id=1, source_target_pairs={{0,1},{1,0},{2,3},{3,2},{4,5},{5,4},{6,7},{7,6},{8,9},{9,8},{10,11... | collective-permute-start | bytes 1425416 | tf_op jit(solution)/shard_map/ppermute | solution.py:351
  37.6 7.8 %collective-permute-start.14 = (f32[2,2,16,512]{3,2,1,0:T(8,128)S(1)}, f32[2,2,16,512]{3,2,1,0:T(8,128)S(1)}, u32[]{:S(2)}, u32[]{:S(2)}) collective-permute-start(f32[2,2,16,512]{3,2,1,0:T(8,128)S(1)} %get-tuple-element.25), channel_id=1, source_target_pairs={{0,8},{4,12},{8,0},{12,4},{16,24},{20,28},{24,16},{28,20},{1,9},{5... | collective-permute-start | bytes 393224 | tf_op jit(solution)/shard_map/ppermute | solution.py:275
  37.7 10.2 %collective-permute-start.10 = (f32[1,2,16,512]{3,2,1,0:T(8,128)S(1)}, f32[1,2,16,512]{3,2,1,0:T(8,128)S(1)}, u32[]{:S(2)}, u32[]{:S(2)}) collective-permute-start(f32[1,2,16,512]{3,2,1,0:T(8,128)S(1)} %get-tuple-element.21), channel_id=1, source_target_pairs={{0,16},{4,20},{8,24},{12,28},{16,0},{20,4},{24,8},{28,12},{1,17},{... | collective-permute-start | bytes 196616 | tf_op jit(solution)/shard_map/ppermute | solution.py:275
  39.4 11.3 %collective-permute-start.11 = (f32[1,2,16,512]{3,2,1,0:T(8,128)S(1)}, f32[1,2,16,512]{3,2,1,0:T(8,128)S(1)}, u32[]{:S(2)}, u32[]{:S(2)}) collective-permute-start(f32[1,2,16,512]{3,2,1,0:T(8,128)S(1)} %get-tuple-element.22), channel_id=1, source_target_pairs={{0,20},{4,16},{8,28},{12,24},{16,4},{20,0},{24,12},{28,8},{1,21},{... | collective-permute-start | bytes 196616 | tf_op jit(solution)/shard_map/ppermute | solution.py:275
  41.6 9.1 %collective-permute-start.12 = (f32[1,2,16,512]{3,2,1,0:T(8,128)S(1)}, f32[1,2,16,512]{3,2,1,0:T(8,128)S(1)}, u32[]{:S(2)}, u32[]{:S(2)}) collective-permute-start(f32[1,2,16,512]{3,2,1,0:T(8,128)S(1)} %get-tuple-element.23), channel_id=1, source_target_pairs={{0,24},{4,28},{8,16},{12,20},{16,8},{20,12},{24,0},{28,4},{1,25},{... | collective-permute-start | bytes 196616 | tf_op jit(solution)/shard_map/ppermute | solution.py:275
  43.1 7.6 %collective-permute-start.13 = (f32[1,2,16,512]{3,2,1,0:T(8,128)S(1)}, f32[1,2,16,512]{3,2,1,0:T(8,128)S(1)}, u32[]{:S(2)}, u32[]{:S(2)}) collective-permute-start(f32[1,2,16,512]{3,2,1,0:T(8,128)S(1)} %get-tuple-element.24), channel_id=1, source_target_pairs={{0,28},{4,24},{8,20},{12,16},{16,12},{20,8},{24,4},{28,0},{1,29},{... | collective-permute-start | bytes 196616 | tf_op jit(solution)/shard_map/ppermute | solution.py:275
  45.4 6.1 %collective-permute-start.15 = (f32[1,2,16,512]{3,2,1,0:T(8,128)S(1)}, f32[1,2,16,512]{3,2,1,0:T(8,128)S(1)}, u32[]{:S(2)}, u32[]{:S(2)}) collective-permute-start(f32[1,2,16,512]{3,2,1,0:T(8,128)S(1)} %get-tuple-element.26), channel_id=1, source_target_pairs={{0,4},{4,0},{8,12},{12,8},{16,20},{20,16},{24,28},{28,24},{1,5},{5... | collective-permute-start | bytes 196616 | tf_op jit(solution)/shard_map/ppermute | solution.py:275
  47.9 4.3 %collective-permute-start.16 = (f32[1,2,16,512]{3,2,1,0:T(8,128)S(1)}, f32[1,2,16,512]{3,2,1,0:T(8,128)S(1)}, u32[]{:S(2)}, u32[]{:S(2)}) collective-permute-start(f32[1,2,16,512]{3,2,1,0:T(8,128)S(1)} %slice.4), channel_id=1, source_target_pairs={{0,4},{4,0},{8,12},{12,8},{16,20},{20,16},{24,28},{28,24},{1,5},{5... | collective-permute-start | bytes 196616 | tf_op jit(solution)/shard_map/ppermute | solution.py:275

commit v19 on v18

--- a/solution.py
+++ b/solution.py
@@ -16,6 +16,7 @@
 PLACE = pl.BlockSpec(memory_space=pl.ANY)
 LIMIT = 48 * 1024 * 1024
 
+GATHERED = (0, 4, 5, 2, 3, 1, 6, 7)
 PARTS = ((0,), (4,), (5,), (6,), (7,), (2, 3), (1,))
 PAIRS = [(e, b) for b in range(1, NB) for e in range(b)]
 PARENT, ALPHA, LATER, VALUE, OWN, SPARE = 0, 6, 12, 18, 22, 32
@@ -134,8 +135,8 @@
     if len(pieces) == 1:
         held[...] = pieces[0][...]
     else:
-        for i, piece in enumerate(pieces):
-            held[lax.bitwise_xor(block, i)] = piece[...]
+        for distance, piece in zip(GATHERED, pieces):
+            held[lax.bitwise_xor(block, distance)] = piece[...]
     common = width // NB * (NB - 1)
     for i in range(width // LANES):
         value = held[:, i * slab : (i + 1) * slab, :].reshape(members, LANES).T
@@ -283,7 +284,7 @@
         pieces[i] = hop(piece, i, n)
     for i in (4, 2):
         pieces[i + 1] = hop(pieces[i], 1, n)
-    return [pieces[i] for i in range(n)]
+    return [pieces[i] for i in GATHERED]
 
 
 def exchange_parts(parts, shape, whole, n):

time: 53 us -> 53.8 us (1.015)
  waiting for transfers between devices: 12.6 us -> 14.3 us
  starting transfers between devices: 30.2 us -> 29.2 us
    all_to_all x1, starting transfers between devices: 4.95 us -> 4.25 us  [body(): fields = lax.all_to_all(send, 'grid', 0, 0, tiled=True)]
    ppermute x1, waiting for transfers between devices: 3.64 us -> 4.33 us  [body(): far = lax.ppermute(slim, 'lev', [(j, j ^ 2) for j in range(lev)])]
    all_to_all x1, waiting for transfers between devices: 2.22 us -> 2.82 us  [body(): fields = lax.all_to_all(send, 'grid', 0, 0, tiled=True)]
where the time goes in v19:
time: 53.8 us; the launch traced here: 53.6 us
  starting transfers between devices  29.2 us (54%)
  waiting for transfers between devices  14.3 us (27%)
  Pallas kernels  9.86 us (18%)
    ppermute x14, starting transfers between devices, hop(): return lax.ppermute(value, 'grid', [(j, j ^ distance) for j in range(n)])  23.4 us
    ppermute x14, waiting for transfers between devices, hop(): return lax.ppermute(value, 'grid', [(j, j ^ distance) for j in range(n)])  5.29 us
    ppermute x1, waiting for transfers between devices, body(): far = lax.ppermute(slim, 'lev', [(j, j ^ 2) for j in range(lev)])  4.33 us
    all_to_all x1, starting transfers between devices, body(): fields = lax.all_to_all(send, 'grid', 0, 0, tiled=True)  4.25 us
    all_to_all x1, waiting for transfers between devices, body(): fields = lax.all_to_all(send, 'grid', 0, 0, tiled=True)  2.82 us
    pallas_call x1, Pallas kernels, body(): call(functools.partial(chain_kernel, (members, groups, count)), shape((8,...  2.72 us
    pallas_call x1, Pallas kernels, body(): call(functools.partial(pick_kernel, (slab, depth, block_cells, groups, co...  2.39 us
    ppermute x1, waiting for transfers between devices, body(): cross = lax.ppermute(far, 'lev', [(j, j ^ 1) for j in range(lev)])  1.83 us
  transfers between devices with their start and end apart: 18, of which 8 were waited for; matrix products, arithmetic and copies ran while one was open for 0% of the time, Pallas kernels for 10%

profile of v19, /device:TPU:0, one launch (start us, length us, event | category | flops | bytes accessed | tf_op | source)
XLA Modules:
  0.0 53.6 jit_solution(3889068897270149143)
XLA Ops:
  0.0 2.4 %shard_map.75.refs_0_ = f32[136,128]{1,0:T(8,128)} custom-call(s32[4]{0:T(128)} %owner.3, f32[2,4]{1,0:T(2,128)} %refs_1_.1, s32[4,4,64]{2,1,0:T(4,128)} %refs_2_.1, s32[4,1,128]{2,1,0:T(1,128)} %bitcast.1, f32[16,2,4096]{2,1,0:T(2,128)} %refs_4_.1), custom_call_target="tpu_custom_call" | custom-call | bytes 1000000 | tf_op jit(solution)/shard_map/pallas_call | solution.py:311
  2.4 0.0 copy-start.2
  2.4 0.0 copy-start.3
  2.4 0.0 copy-start.4
  2.4 0.0 copy-start.5
  2.4 0.0 copy-start.6
  2.5 4.1 %collective-permute-start = (f32[136,128]{1,0:T(8,128)}, f32[136,128]{1,0:T(8,128)S(1)}, u32[]{:S(2)}, u32[]{:S(2)}) collective-permute-start(f32[136,128]{1,0:T(8,128)} %shard_map.75.refs_0_), channel_id=1, source_target_pairs={{0,16},{4,20},{8,24},{12,28},{16,0},{20,4},{24,8},{28,12},{1,17},{... | collective-permute-start | bytes 208904 | tf_op jit(solution)/shard_map/ppermute | solution.py:276
  6.6 1.6 %collective-permute-start.2 = (f32[136,128]{1,0:T(8,128)}, f32[136,128]{1,0:T(8,128)S(1)}, u32[]{:S(2)}, u32[]{:S(2)}) collective-permute-start(f32[136,128]{1,0:T(8,128)} %shard_map.75.refs_0_), channel_id=1, source_target_pairs={{0,8},{4,12},{8,0},{12,4},{16,24},{20,28},{24,16},{28,20},{1,9},{5... | collective-permute-start | bytes 208904 | tf_op jit(solution)/shard_map/ppermute | solution.py:276
  8.1 1.5 %collective-permute-start.4 = (f32[136,128]{1,0:T(8,128)}, f32[136,128]{1,0:T(8,128)S(1)}, u32[]{:S(2)}, u32[]{:S(2)}) collective-permute-start(f32[136,128]{1,0:T(8,128)} %shard_map.75.refs_0_), channel_id=1, source_target_pairs={{0,4},{4,0},{8,12},{12,8},{16,20},{20,16},{24,28},{28,24},{1,5},{5... | collective-permute-start | bytes 208904 | tf_op jit(solution)/shard_map/ppermute | solution.py:276
  9.7 0.2 collective-permute-start.5
  9.9 3.5 %collective-permute-start.6 = (f32[136,128]{1,0:T(8,128)}, f32[136,128]{1,0:T(8,128)S(1)}, u32[]{:S(2)}, u32[]{:S(2)}) collective-permute-start(f32[136,128]{1,0:T(8,128)} %shard_map.75.refs_0_), channel_id=1, source_target_pairs={{0,28},{4,24},{8,20},{12,16},{16,12},{20,8},{24,4},{28,0},{1,29},{... | collective-permute-start | bytes 208904 | tf_op jit(solution)/shard_map/ppermute | solution.py:276
  13.4 0.0 collective-permute-done.refs_1_
  13.4 1.5 %collective-permute-start.1 = (f32[136,128]{1,0:T(8,128)S(1)}, f32[136,128]{1,0:T(8,128)S(1)}, u32[]{:S(2)}, u32[]{:S(2)}) collective-permute-start(f32[136,128]{1,0:T(8,128)S(1)} %collective-permute-done.refs_1_), channel_id=1, source_target_pairs={{0,4},{4,0},{8,12},{12,8},{16,20},{20,16},{24,28},{28,24},{1,5},{5... | collective-permute-start | bytes 208904 | tf_op jit(solution)/shard_map/ppermute | solution.py:276
  15.0 0.0 collective-permute-done.2.refs_3_
  15.0 0.5 collective-permute-start.3
  15.5 0.9 %shard_map.74.ahead = f32[8,2,16,512]{3,2,1,0:T(8,128)} custom-call(f32[16,2,4096]{2,1,0:T(2,128)S(1)} %copy-done), custom_call_target="tpu_custom_call" | custom-call | bytes 1000000 | tf_op jit(solution)/shard_map/pallas_call | solution.py:327
  16.4 1.0 %shard_map.73 = (f32[32,128]{1,0:T(8,128)S(1)}, f32[5,128,128]{2,1,0:T(8,128)S(1)}) custom-call(s32[4]{0:T(128)S(1)} %copy-done.4, s32[4,4,64]{2,1,0:T(4,128)S(1)} %copy-done.2, f32[4,1,64]{2,1,0:T(1,128)S(1)} %copy-done.5, f32[4,1,64]{2,1,0:T(1,128)S(1)} %copy-done.6, s32[4,1,128]{2,1,0:T(1,128)S(1)} %bitcast.2), custom_call_target="tpu_custom_call" | custom-call | bytes 1000000 | tf_op jit(solution)/shard_map/pallas_call | solution.py:335
  17.4 0.0 collective-permute-done.4.refs_5_
  17.4 0.0 collective-permute-done.5.refs_6_
  17.4 0.0 collective-permute-done.6.refs_7_
  17.4 0.5 collective-permute-done.1.refs_2_
  18.0 1.3 %collective-permute-done.3.refs_4_ = f32[136,128]{1,0:T(8,128)S(1)} collective-permute-done((f32[136,128]{1,0:T(8,128)S(1)}, f32[136,128]{1,0:T(8,128)S(1)}, u32[]{:S(2)}, u32[]{:S(2)}) %collective-permute-start.3) | collective-permute-done | bytes 69664 | tf_op jit(solution)/shard_map/ppermute | solution.py:276
  19.3 0.8 %shard_map.76 = (f32[1056,128]{1,0:T(8,128)S(1)}, f32[928,128]{1,0:T(8,128)S(1)}) custom-call(s32[4]{0:T(128)S(1)} %copy-done.4, f32[32,128]{1,0:T(8,128)S(1)} %get-tuple-element.17.rows, f32[8,2,16,512]{3,2,1,0:T(8,128)} %shard_map.74.ahead, f32[136,128]{1,0:T(8,128)S(1)} %copy-done.1, f32[136,128]{1,0:T(8,128)S(1)} %collective-permute-done.refs_1_, ...), custom_call_target="tpu_custom_call" | custom-call | bytes 1000000 | tf_op jit(solution)/shard_map/pallas_call | solution.py:343
  20.1 1.6 %collective-permute-start.8 = (f32[928,128]{1,0:T(8,128)S(1)}, f32[928,128]{1,0:T(8,128)S(1)}, u32[]{:S(2)}, u32[]{:S(2)}) collective-permute-start(f32[928,128]{1,0:T(8,128)S(1)} %get-tuple-element.19), channel_id=1, source_target_pairs={{0,2},{1,3},{2,0},{3,1},{4,6},{5,7},{6,4},{7,5},{8,10},{9,11},{10,... | collective-permute-start | bytes 1425416 | tf_op jit(solution)/shard_map/ppermute | solution.py:350
  21.6 4.3 %all-to-all-start = ((f32[8,2,16,512]{3,2,1,0:T(8,128)}), f32[8,2,16,512]{3,2,1,0:T(8,128)S(1)}, u32[]{:S(2)}, u32[]{:S(2)}) async-start(f32[8,2,16,512]{3,2,1,0:T(8,128)} %shard_map.74.ahead), calls=%async_computation | async-start | bytes 1048576 | tf_op jit(solution)/shard_map/all_to_all | solution.py:333
  25.9 0.0 collective-permute-start.7
  25.9 4.3 %collective-permute-done.8.far = f32[928,128]{1,0:T(8,128)S(1)} collective-permute-done((f32[928,128]{1,0:T(8,128)S(1)}, f32[928,128]{1,0:T(8,128)S(1)}, u32[]{:S(2)}, u32[]{:S(2)}) %collective-permute-start.8) | collective-permute-done | bytes 475168 | tf_op jit(solution)/shard_map/ppermute | solution.py:350
  30.2 0.0 collective-permute-start.9
  30.2 0.0 collective-permute-done.7.near
  30.2 1.8 %collective-permute-done.9.cross = f32[928,128]{1,0:T(8,128)S(1)} collective-permute-done((f32[928,128]{1,0:T(8,128)S(1)}, f32[928,128]{1,0:T(8,128)S(1)}, u32[]{:S(2)}, u32[]{:S(2)}) %collective-permute-start.9) | collective-permute-done | bytes 475168 | tf_op jit(solution)/shard_map/ppermute | solution.py:352
  32.1 2.7 %shard_map.77.pull = f32[8,128]{1,0:T(8,128)S(1)} custom-call(f32[1056,128]{1,0:T(8,128)S(1)} %get-tuple-element.18.own, f32[1056,128]{1,0:T(8,128)S(1)} %collective-permute-done.7.near, f32[928,128]{1,0:T(8,128)S(1)} %collective-permute-done.8.far, f32[928,128]{1,0:T(8,128)S(1)} %collective-permute-done.9.cross, f32[5,128,128]{2,1,0:T(8,128)S(1)} %get-tuple-element.16.steps), custom_call_target="tpu_custom_call" | custom-call | bytes 100000 | tf_op jit(solution)/shard_map/pallas_call | solution.py:354
  34.8 2.8 %all-to-all-done.fields = f32[8,2,16,512]{3,2,1,0:T(8,128)S(1)} async-done(((f32[8,2,16,512]{3,2,1,0:T(8,128)}), f32[8,2,16,512]{3,2,1,0:T(8,128)S(1)}, u32[]{:S(2)}, u32[]{:S(2)}) %all-to-all-start) | async-done | bytes 524320 | tf_op jit(solution)/shard_map/all_to_all | solution.py:333
  37.6 0.6 %shard_map.78 = (f32[1,2,16,512]{3,2,1,0:T(8,128)S(1)}, f32[1,2,16,512]{3,2,1,0:T(8,128)S(1)}, f32[1,2,16,512]{3,2,1,0:T(8,128)S(1)}, f32[1,2,16,512]{3,2,1,0:T(...) custom-call(f32[5,128,128]{2,1,0:T(8,128)S(1)} %get-tuple-element.16.steps, ...), custom_call_target="tpu_custom_call" | custom-call | flops 100000000 | bytes 1000000 | tf_op jit(solution)/shard_map/pallas_call | solution.py:365
  38.2 0.9 %collective-permute-start.14 = (f32[2,2,16,512]{3,2,1,0:T(8,128)S(1)}, f32[2,2,16,512]{3,2,1,0:T(8,128)S(1)}, u32[]{:S(2)}, u32[]{:S(2)}) collective-permute-start(f32[2,2,16,512]{3,2,1,0:T(8,128)S(1)} %get-tuple-element.25), channel_id=1, source_target_pairs={{0,8},{4,12},{8,0},{12,4},{16,24},{20,28},{24,16},{28,20},{1,9},{5... | collective-permute-start | bytes 393224 | tf_op jit(solution)/shard_map/ppermute | solution.py:276
  39.1 0.9 %collective-permute-start.10 = (f32[1,2,16,512]{3,2,1,0:T(8,128)S(1)}, f32[1,2,16,512]{3,2,1,0:T(8,128)S(1)}, u32[]{:S(2)}, u32[]{:S(2)}) collective-permute-start(f32[1,2,16,512]{3,2,1,0:T(8,128)S(1)} %get-tuple-element.21), channel_id=1, source_target_pairs={{0,16},{4,20},{8,24},{12,28},{16,0},{20,4},{24,8},{28,12},{1,17},{... | collective-permute-start | bytes 196616 | tf_op jit(solution)/shard_map/ppermute | solution.py:276
  40.0 2.2 %collective-permute-start.11 = (f32[1,2,16,512]{3,2,1,0:T(8,128)S(1)}, f32[1,2,16,512]{3,2,1,0:T(8,128)S(1)}, u32[]{:S(2)}, u32[]{:S(2)}) collective-permute-start(f32[1,2,16,512]{3,2,1,0:T(8,128)S(1)} %get-tuple-element.22), channel_id=1, source_target_pairs={{0,20},{4,16},{8,28},{12,24},{16,4},{20,0},{24,12},{28,8},{1,21},{... | collective-permute-start | bytes 196616 | tf_op jit(solution)/shard_map/ppermute | solution.py:276
  42.2 1.5 %collective-permute-start.12 = (f32[1,2,16,512]{3,2,1,0:T(8,128)S(1)}, f32[1,2,16,512]{3,2,1,0:T(8,128)S(1)}, u32[]{:S(2)}, u32[]{:S(2)}) collective-permute-start(f32[1,2,16,512]{3,2,1,0:T(8,128)S(1)} %get-tuple-element.23), channel_id=1, source_target_pairs={{0,24},{4,28},{8,16},{12,20},{16,8},{20,12},{24,0},{28,4},{1,25},{... | collective-permute-start | bytes 196616 | tf_op jit(solution)/shard_map/ppermute | solution.py:276
  43.7 3.0 %collective-permute-start.13 = (f32[1,2,16,512]{3,2,1,0:T(8,128)S(1)}, f32[1,2,16,512]{3,2,1,0:T(8,128)S(1)}, u32[]{:S(2)}, u32[]{:S(2)}) collective-permute-start(f32[1,2,16,512]{3,2,1,0:T(8,128)S(1)} %get-tuple-element.24), channel_id=1, source_target_pairs={{0,28},{4,24},{8,20},{12,16},{16,12},{20,8},{24,4},{28,0},{1,29},{... | collective-permute-start | bytes 196616 | tf_op jit(solution)/shard_map/ppermute | solution.py:276
  46.7 0.8 %collective-permute-start.15 = (f32[1,2,16,512]{3,2,1,0:T(8,128)S(1)}, f32[1,2,16,512]{3,2,1,0:T(8,128)S(1)}, u32[]{:S(2)}, u32[]{:S(2)}) collective-permute-start(f32[1,2,16,512]{3,2,1,0:T(8,128)S(1)} %get-tuple-element.26), channel_id=1, source_target_pairs={{0,4},{4,0},{8,12},{12,8},{16,20},{20,16},{24,28},{28,24},{1,5},{5... | collective-permute-start | bytes 196616 | tf_op jit(solution)/shard_map/ppermute | solution.py:276
  47.5 1.1 %collective-permute-done.10.refs_1_ = f32[1,2,16,512]{3,2,1,0:T(8,128)S(1)} collective-permute-done((f32[1,2,16,512]{3,2,1,0:T(8,128)S(1)}, f32[1,2,16,512]{3,2,1,0:T(8,128)S(1)}, u32[]{:S(2)}, u32[]{:S(2)}) %collective-permute-start.10) | collective-permute-done | bytes 65568 | tf_op jit(solution)/shard_map/ppermute | solution.py:276
  48.6 1.1 %collective-permute-start.16 = (f32[1,2,16,512]{3,2,1,0:T(8,128)S(1)}, f32[1,2,16,512]{3,2,1,0:T(8,128)S(1)}, u32[]{:S(2)}, u32[]{:S(2)}) collective-permute-start(f32[1,2,16,512]{3,2,1,0:T(8,128)S(1)} %slice.4), channel_id=1, source_target_pairs={{0,4},{4,0},{8,12},{12,8},{16,20},{20,16},{24,28},{28,24},{1,5},{5... | collective-permute-start | bytes 196616 | tf_op jit(solution)/shard_map/ppermute | solution.py:276
  49.7 1.4 %collective-permute-done.11.refs_2_ = f32[1,2,16,512]{3,2,1,0:T(8,128)S(1)} collective-permute-done((f32[1,2,16,512]{3,2,1,0:T(8,128)S(1)}, f32[1,2,16,512]{3,2,1,0:T(8,128)S(1)}, u32[]{:S(2)}, u32[]{:S(2)}) %collective-permute-start.11) | collective-permute-done | bytes 65568 | tf_op jit(solution)/shard_map/ppermute | solution.py:276
  51.1 0.0 collective-permute-done.12.refs_3_
  51.1 0.0 collective-permute-done.13.refs_4_
  51.1 0.8 %shard_map.79.refs_0_ = f32[16,2,4096]{2,1,0:T(2,128)} custom-call(f32[1,2,16,512]{3,2,1,0:T(8,128)S(1)} %get-tuple-element.20.refs_0_, f32[1,2,16,512]{3,2,1,0:T(8,128)S(1)} %collective-permute-done.10.refs_1_, f32[1,2,16,512]{3,2,1,0:T(8,128)S(1)} %collective-permute-done.11.refs_2_, f32[1,2,16,512]{3,2,1,0:T(8,128)S(1)} %collective-permute-done.12.refs_3_, ...), custom_call_target="tpu_custom_call" | custom-call | bytes 1000000 | tf_op jit(solution)/shard_map/pallas_call | solution.py:261
  51.9 0.0 collective-permute-done.15.refs_2_
  51.9 1.0 %collective-permute-done.16.refs_3_ = f32[1,2,16,512]{3,2,1,0:T(8,128)S(1)} collective-permute-done((f32[1,2,16,512]{3,2,1,0:T(8,128)S(1)}, f32[1,2,16,512]{3,2,1,0:T(8,128)S(1)}, u32[]{:S(2)}, u32[]{:S(2)}) %collective-permute-start.16) | collective-permute-done | bytes 65568 | tf_op jit(solution)/shard_map/ppermute | solution.py:276
  52.9 0.7 %shard_map.80 = f32[16,2,4096]{2,1,0:T(2,128)} custom-call(f32[16,2,4096]{2,1,0:T(2,128)} %shard_map.79.refs_0_, f32[2,2,16,512]{3,2,1,0:T(8,128)S(1)} %collective-permute-done.14.refs_1_, f32[1,2,16,512]{3,2,1,0:T(8,128)S(1)} %collective-permute-done.15.refs_2_, f32[1,2,16,512]{3,2,1,0:T(8,128)S(1)} %collective-permute-done.16.refs_3_), custom_call_target="tpu_custom_call", output_to_operand_aliasing={{}: (0, {})} | custom-call | bytes 1000000 | tf_op jit(solution)/shard_map/pallas_call | solution.py:261
  (11 shorter events, 0.0 us)
Async XLA Ops:
  0.0 15.5 %copy-start = (f32[16,2,4096]{2,1,0:T(2,128)S(1)}, f32[16,2,4096]{2,1,0:T(2,128)}, u32[]{:S(2)}) copy-start(f32[16,2,4096]{2,1,0:T(2,128)} %refs_4_.1) | copy-start | bytes 1572868
  2.4 14.0 %copy-start.2 = (s32[4,4,64]{2,1,0:T(4,128)S(1)}, s32[4,4,64]{2,1,0:T(4,128)}, u32[]{:S(2)}) copy-start(s32[4,4,64]{2,1,0:T(4,128)} %refs_2_.1) | copy-start | bytes 12292
  2.4 14.0 %copy-start.3 = (s32[4,1,1,128]{3,2,1,0:T(1,128)S(1)}, s32[4,1,1,128]{3,2,1,0:T(1,128)}, u32[]{:S(2)}) copy-start(s32[4,1,1,128]{3,2,1,0:T(1,128)} %param.13) | copy-start | bytes 6148
  2.4 13.9 %copy-start.4 = (s32[4]{0:T(128)S(1)}, s32[4]{0:T(128)}, u32[]{:S(2)}) copy-start(s32[4]{0:T(128)} %owner.3) | copy-start | bytes 52
  2.4 13.9 %copy-start.5 = (f32[4,1,64]{2,1,0:T(1,128)S(1)}, f32[4,1,64]{2,1,0:T(1,128)}, u32[]{:S(2)}) copy-start(f32[4,1,64]{2,1,0:T(1,128)} %values.1) | copy-start | bytes 3076
  2.4 13.9 %copy-start.6 = (f32[4,1,64]{2,1,0:T(1,128)S(1)}, f32[4,1,64]{2,1,0:T(1,128)}, u32[]{:S(2)}) copy-start(f32[4,1,64]{2,1,0:T(1,128)} %errors.1) | copy-start | bytes 3076
  2.5 16.8 %copy-start.1 = (f32[136,128]{1,0:T(8,128)S(1)}, f32[136,128]{1,0:T(8,128)}, u32[]{:S(2)}) copy-start(f32[136,128]{1,0:T(8,128)} %shard_map.75.refs_0_) | copy-start | bytes 208900
  2.5 11.0 %collective-permute-start = (f32[136,128]{1,0:T(8,128)}, f32[136,128]{1,0:T(8,128)S(1)}, u32[]{:S(2)}, u32[]{:S(2)}) collective-permute-start(f32[136,128]{1,0:T(8,128)} %shard_map.75.refs_0_), channel_id=1, source_target_pairs={{0,16},{4,20},{8,24},{12,28},{16,0},{20,4},{24,8},{28,12},{1,17},{... | collective-permute-start | bytes 208904 | tf_op jit(solution)/shard_map/ppermute | solution.py:276
  6.6 8.4 %collective-permute-start.2 = (f32[136,128]{1,0:T(8,128)}, f32[136,128]{1,0:T(8,128)S(1)}, u32[]{:S(2)}, u32[]{:S(2)}) collective-permute-start(f32[136,128]{1,0:T(8,128)} %shard_map.75.refs_0_), channel_id=1, source_target_pairs={{0,8},{4,12},{8,0},{12,4},{16,24},{20,28},{24,16},{28,20},{1,9},{5... | collective-permute-start | bytes 208904 | tf_op jit(solution)/shard_map/ppermute | solution.py:276
  8.1 9.2 %collective-permute-start.4 = (f32[136,128]{1,0:T(8,128)}, f32[136,128]{1,0:T(8,128)S(1)}, u32[]{:S(2)}, u32[]{:S(2)}) collective-permute-start(f32[136,128]{1,0:T(8,128)} %shard_map.75.refs_0_), channel_id=1, source_target_pairs={{0,4},{4,0},{8,12},{12,8},{16,20},{20,16},{24,28},{28,24},{1,5},{5... | collective-permute-start | bytes 208904 | tf_op jit(solution)/shard_map/ppermute | solution.py:276
  9.7 7.7 %collective-permute-start.5 = (f32[136,128]{1,0:T(8,128)}, f32[136,128]{1,0:T(8,128)S(1)}, u32[]{:S(2)}, u32[]{:S(2)}) collective-permute-start(f32[136,128]{1,0:T(8,128)} %shard_map.75.refs_0_), channel_id=1, source_target_pairs={{0,24},{4,28},{8,16},{12,20},{16,8},{20,12},{24,0},{28,4},{1,25},{... | collective-permute-start | bytes 208904 | tf_op jit(solution)/shard_map/ppermute | solution.py:276
  9.9 7.5 %collective-permute-start.6 = (f32[136,128]{1,0:T(8,128)}, f32[136,128]{1,0:T(8,128)S(1)}, u32[]{:S(2)}, u32[]{:S(2)}) collective-permute-start(f32[136,128]{1,0:T(8,128)} %shard_map.75.refs_0_), channel_id=1, source_target_pairs={{0,28},{4,24},{8,20},{12,16},{16,12},{20,8},{24,4},{28,0},{1,29},{... | collective-permute-start | bytes 208904 | tf_op jit(solution)/shard_map/ppermute | solution.py:276
  13.4 4.5 %collective-permute-start.1 = (f32[136,128]{1,0:T(8,128)S(1)}, f32[136,128]{1,0:T(8,128)S(1)}, u32[]{:S(2)}, u32[]{:S(2)}) collective-permute-start(f32[136,128]{1,0:T(8,128)S(1)} %collective-permute-done.refs_1_), channel_id=1, source_target_pairs={{0,4},{4,0},{8,12},{12,8},{16,20},{20,16},{24,28},{28,24},{1,5},{5... | collective-permute-start | bytes 208904 | tf_op jit(solution)/shard_map/ppermute | solution.py:276
  15.0 4.3 %collective-permute-start.3 = (f32[136,128]{1,0:T(8,128)S(1)}, f32[136,128]{1,0:T(8,128)S(1)}, u32[]{:S(2)}, u32[]{:S(2)}) collective-permute-start(f32[136,128]{1,0:T(8,128)S(1)} %collective-permute-done.2.refs_3_), channel_id=1, source_target_pairs={{0,4},{4,0},{8,12},{12,8},{16,20},{20,16},{24,28},{28,24},{1,5},{5... | collective-permute-start | bytes 208904 | tf_op jit(solution)/shard_map/ppermute | solution.py:276
  20.1 10.2 %collective-permute-start.8 = (f32[928,128]{1,0:T(8,128)S(1)}, f32[928,128]{1,0:T(8,128)S(1)}, u32[]{:S(2)}, u32[]{:S(2)}) collective-permute-start(f32[928,128]{1,0:T(8,128)S(1)} %get-tuple-element.19), channel_id=1, source_target_pairs={{0,2},{1,3},{2,0},{3,1},{4,6},{5,7},{6,4},{7,5},{8,10},{9,11},{10,... | collective-permute-start | bytes 1425416 | tf_op jit(solution)/shard_map/ppermute | solution.py:350
  21.6 16.0 %all-to-all-start = ((f32[8,2,16,512]{3,2,1,0:T(8,128)}), f32[8,2,16,512]{3,2,1,0:T(8,128)S(1)}, u32[]{:S(2)}, u32[]{:S(2)}) async-start(f32[8,2,16,512]{3,2,1,0:T(8,128)} %shard_map.74.ahead), calls=%async_computation | async-start | bytes 1048576 | tf_op jit(solution)/shard_map/all_to_all | solution.py:333
  25.9 4.3 %collective-permute-start.7 = (f32[1056,128]{1,0:T(8,128)S(1)}, f32[1056,128]{1,0:T(8,128)S(1)}, u32[]{:S(2)}, u32[]{:S(2)}) collective-permute-start(f32[1056,128]{1,0:T(8,128)S(1)} %get-tuple-element.18.own), channel_id=1, source_target_pairs={{0,1},{1,0},{2,3},{3,2},{4,5},{5,4},{6,7},{7,6},{8,9},{9,8},{10,11... | collective-permute-start | bytes 1622024 | tf_op jit(solution)/shard_map/ppermute | solution.py:351
  30.2 1.8 %collective-permute-start.9 = (f32[928,128]{1,0:T(8,128)S(1)}, f32[928,128]{1,0:T(8,128)S(1)}, u32[]{:S(2)}, u32[]{:S(2)}) collective-permute-start(f32[928,128]{1,0:T(8,128)S(1)} %collective-permute-done.8.far), channel_id=1, source_target_pairs={{0,1},{1,0},{2,3},{3,2},{4,5},{5,4},{6,7},{7,6},{8,9},{9,8},{10,11... | collective-permute-start | bytes 1425416 | tf_op jit(solution)/shard_map/ppermute | solution.py:352
  38.2 8.5 %collective-permute-start.14 = (f32[2,2,16,512]{3,2,1,0:T(8,128)S(1)}, f32[2,2,16,512]{3,2,1,0:T(8,128)S(1)}, u32[]{:S(2)}, u32[]{:S(2)}) collective-permute-start(f32[2,2,16,512]{3,2,1,0:T(8,128)S(1)} %get-tuple-element.25), channel_id=1, source_target_pairs={{0,8},{4,12},{8,0},{12,4},{16,24},{20,28},{24,16},{28,20},{1,9},{5... | collective-permute-start | bytes 393224 | tf_op jit(solution)/shard_map/ppermute | solution.py:276
  39.1 9.5 %collective-permute-start.10 = (f32[1,2,16,512]{3,2,1,0:T(8,128)S(1)}, f32[1,2,16,512]{3,2,1,0:T(8,128)S(1)}, u32[]{:S(2)}, u32[]{:S(2)}) collective-permute-start(f32[1,2,16,512]{3,2,1,0:T(8,128)S(1)} %get-tuple-element.21), channel_id=1, source_target_pairs={{0,16},{4,20},{8,24},{12,28},{16,0},{20,4},{24,8},{28,12},{1,17},{... | collective-permute-start | bytes 196616 | tf_op jit(solution)/shard_map/ppermute | solution.py:276
  40.0 11.1 %collective-permute-start.11 = (f32[1,2,16,512]{3,2,1,0:T(8,128)S(1)}, f32[1,2,16,512]{3,2,1,0:T(8,128)S(1)}, u32[]{:S(2)}, u32[]{:S(2)}) collective-permute-start(f32[1,2,16,512]{3,2,1,0:T(8,128)S(1)} %get-tuple-element.22), channel_id=1, source_target_pairs={{0,20},{4,16},{8,28},{12,24},{16,4},{20,0},{24,12},{28,8},{1,21},{... | collective-permute-start | bytes 196616 | tf_op jit(solution)/shard_map/ppermute | solution.py:276
  42.2 8.9 %collective-permute-start.12 = (f32[1,2,16,512]{3,2,1,0:T(8,128)S(1)}, f32[1,2,16,512]{3,2,1,0:T(8,128)S(1)}, u32[]{:S(2)}, u32[]{:S(2)}) collective-permute-start(f32[1,2,16,512]{3,2,1,0:T(8,128)S(1)} %get-tuple-element.23), channel_id=1, source_target_pairs={{0,24},{4,28},{8,16},{12,20},{16,8},{20,12},{24,0},{28,4},{1,25},{... | collective-permute-start | bytes 196616 | tf_op jit(solution)/shard_map/ppermute | solution.py:276
  43.7 7.4 %collective-permute-start.13 = (f32[1,2,16,512]{3,2,1,0:T(8,128)S(1)}, f32[1,2,16,512]{3,2,1,0:T(8,128)S(1)}, u32[]{:S(2)}, u32[]{:S(2)}) collective-permute-start(f32[1,2,16,512]{3,2,1,0:T(8,128)S(1)} %get-tuple-element.24), channel_id=1, source_target_pairs={{0,28},{4,24},{8,20},{12,16},{16,12},{20,8},{24,4},{28,0},{1,29},{... | collective-permute-start | bytes 196616 | tf_op jit(solution)/shard_map/ppermute | solution.py:276
  46.7 5.2 %collective-permute-start.15 = (f32[1,2,16,512]{3,2,1,0:T(8,128)S(1)}, f32[1,2,16,512]{3,2,1,0:T(8,128)S(1)}, u32[]{:S(2)}, u32[]{:S(2)}) collective-permute-start(f32[1,2,16,512]{3,2,1,0:T(8,128)S(1)} %get-tuple-element.26), channel_id=1, source_target_pairs={{0,4},{4,0},{8,12},{12,8},{16,20},{20,16},{24,28},{28,24},{1,5},{5... | collective-permute-start | bytes 196616 | tf_op jit(solution)/shard_map/ppermute | solution.py:276
  48.6 4.3 %collective-permute-start.16 = (f32[1,2,16,512]{3,2,1,0:T(8,128)S(1)}, f32[1,2,16,512]{3,2,1,0:T(8,128)S(1)}, u32[]{:S(2)}, u32[]{:S(2)}) collective-permute-start(f32[1,2,16,512]{3,2,1,0:T(8,128)S(1)} %slice.4), channel_id=1, source_target_pairs={{0,4},{4,0},{8,12},{12,8},{16,20},{20,16},{24,28},{28,24},{1,5},{5... | collective-permute-start | bytes 196616 | tf_op jit(solution)/shard_map/ppermute | solution.py:276

commit v20 on v18

--- a/solution.py
+++ b/solution.py
@@ -88,8 +88,11 @@
         out[line + b : line + b + 1, :] = ancestors[b].astype(F32)
 
 
-def retile_kernel(shape, prior, out):
+def retile_kernel(shape, source, out, prior, arrived):
     n, slab, depth, block_cells = shape
+    copy = pltpu.make_async_copy(source, prior, arrived)
+    copy.start()
+    copy.wait()
     for i in range(n):
         for level in range(depth):
             out[i, level] = prior[:, level, i * block_cells : (i + 1) * block_cells]
@@ -326,8 +329,10 @@
     send = call(
         functools.partial(retile_kernel, (n, slab, depth, block_cells)),
         shape((n, depth, slab, block_cells), F32),
-        [VMEM],
-        moved=10**6,
+        [PLACE],
+        scratch=[pltpu.VMEM(prior.shape, F32), pltpu.SemaphoreType.DMA],
+        moved=10**6,
+        limit=None,
     )(prior)
     fields = lax.all_to_all(send, "grid", 0, 0, tiled=True)
 

time: 53 us -> 53 us (level)
  waiting for transfers between devices: 12.6 us -> 11.5 us
  Pallas kernels: 9.86 us -> 10.8 us
    ppermute x14, waiting for transfers between devices: 4.87 us -> 3.78 us  [hop(): return lax.ppermute(value, 'grid', [(j, j ^ distance) for j in range(n)])]
    pallas_call x1, Pallas kernels: 0.89 us -> 1.94 us  [body(): call(functools.partial(retile_kernel, (n, slab, depth, block_cells)), sha...]
  transfers between devices with their start and end apart: 18 -> 18, of which waited for: 8 -> 7; matrix products, arithmetic and copies ran while one was open for 0% -> 0% of each run, Pallas kernels for 10% -> 12%
where the time goes in v20:
time: 53 us; the launch traced here: 52.8 us
  starting transfers between devices  30.2 us (57%)
  waiting for transfers between devices  11.5 us (22%)
  Pallas kernels  10.8 us (20%)
    ppermute x14, starting transfers between devices, hop(): return lax.ppermute(value, 'grid', [(j, j ^ distance) for j in range(n)])  23.7 us
    all_to_all x1, starting transfers between devices, body(): fields = lax.all_to_all(send, 'grid', 0, 0, tiled=True)  4.95 us
    ppermute x14, waiting for transfers between devices, hop(): return lax.ppermute(value, 'grid', [(j, j ^ distance) for j in range(n)])  3.78 us
    ppermute x1, waiting for transfers between devices, body(): far = lax.ppermute(slim, 'lev', [(j, j ^ 2) for j in range(lev)])  3.64 us
    pallas_call x1, Pallas kernels, body(): call(functools.partial(chain_kernel, (members, groups, count)), shape((8,...  2.72 us
    pallas_call x1, Pallas kernels, body(): call(functools.partial(pick_kernel, (slab, depth, block_cells, groups, co...  2.33 us
    all_to_all x1, waiting for transfers between devices, body(): fields = lax.all_to_all(send, 'grid', 0, 0, tiled=True)  2.22 us
    pallas_call x1, Pallas kernels, body(): call(functools.partial(retile_kernel, (n, slab, depth, block_cells)), sha...  1.94 us
  transfers between devices with their start and end apart: 18, of which 7 were waited for; matrix products, arithmetic and copies ran while one was open for 0% of the time, Pallas kernels for 12%

profile of v20, /device:TPU:0, one launch (start us, length us, event | category | flops | bytes accessed | tf_op | source)
XLA Modules:
  0.0 52.8 jit_solution(3612925889333909429)
XLA Ops:
  0.0 2.3 %shard_map.75.refs_0_ = f32[136,128]{1,0:T(8,128)} custom-call(s32[4]{0:T(128)} %owner.3, f32[2,4]{1,0:T(2,128)} %refs_1_.1, s32[4,4,64]{2,1,0:T(4,128)} %refs_2_.1, s32[4,1,128]{2,1,0:T(1,128)} %bitcast.1, f32[16,2,4096]{2,1,0:T(2,128)} %refs_4_.1), custom_call_target="tpu_custom_call" | custom-call | bytes 1000000 | tf_op jit(solution)/shard_map/pallas_call | solution.py:313
  2.3 0.0 copy-start.1
  2.3 0.0 copy-start.2
  2.4 0.0 copy-start.3
  2.4 0.0 copy-start.4
  2.4 0.0 copy-start.5
  2.4 3.1 %collective-permute-start.1 = (f32[136,128]{1,0:T(8,128)}, f32[136,128]{1,0:T(8,128)S(1)}, u32[]{:S(2)}, u32[]{:S(2)}) collective-permute-start(f32[136,128]{1,0:T(8,128)} %shard_map.75.refs_0_), channel_id=1, source_target_pairs={{0,8},{4,12},{8,0},{12,4},{16,24},{20,28},{24,16},{28,20},{1,9},{5... | collective-permute-start | bytes 208904 | tf_op jit(solution)/shard_map/ppermute | solution.py:278
  5.5 2.6 %collective-permute-start.3 = (f32[136,128]{1,0:T(8,128)}, f32[136,128]{1,0:T(8,128)S(1)}, u32[]{:S(2)}, u32[]{:S(2)}) collective-permute-start(f32[136,128]{1,0:T(8,128)} %shard_map.75.refs_0_), channel_id=1, source_target_pairs={{0,16},{4,20},{8,24},{12,28},{16,0},{20,4},{24,8},{28,12},{1,17},{... | collective-permute-start | bytes 208904 | tf_op jit(solution)/shard_map/ppermute | solution.py:278
  8.1 1.5 %collective-permute-start = (f32[136,128]{1,0:T(8,128)}, f32[136,128]{1,0:T(8,128)S(1)}, u32[]{:S(2)}, u32[]{:S(2)}) collective-permute-start(f32[136,128]{1,0:T(8,128)} %shard_map.75.refs_0_), channel_id=1, source_target_pairs={{0,4},{4,0},{8,12},{12,8},{16,20},{20,16},{24,28},{28,24},{1,5},{5... | collective-permute-start | bytes 208904 | tf_op jit(solution)/shard_map/ppermute | solution.py:278
  9.6 0.2 collective-permute-start.5
  9.8 3.5 %collective-permute-start.6 = (f32[136,128]{1,0:T(8,128)}, f32[136,128]{1,0:T(8,128)S(1)}, u32[]{:S(2)}, u32[]{:S(2)}) collective-permute-start(f32[136,128]{1,0:T(8,128)} %shard_map.75.refs_0_), channel_id=1, source_target_pairs={{0,28},{4,24},{8,20},{12,16},{16,12},{20,8},{24,4},{28,0},{1,29},{... | collective-permute-start | bytes 208904 | tf_op jit(solution)/shard_map/ppermute | solution.py:278
  13.4 0.0 collective-permute-done.1.refs_2_
  13.4 1.5 %collective-permute-start.2 = (f32[136,128]{1,0:T(8,128)S(1)}, f32[136,128]{1,0:T(8,128)S(1)}, u32[]{:S(2)}, u32[]{:S(2)}) collective-permute-start(f32[136,128]{1,0:T(8,128)S(1)} %collective-permute-done.1.refs_2_), channel_id=1, source_target_pairs={{0,4},{4,0},{8,12},{12,8},{16,20},{20,16},{24,28},{28,24},{1,5},{5... | collective-permute-start | bytes 208904 | tf_op jit(solution)/shard_map/ppermute | solution.py:278
  14.9 0.0 collective-permute-done.3.refs_4_
  14.9 0.6 %collective-permute-start.4 = (f32[136,128]{1,0:T(8,128)S(1)}, f32[136,128]{1,0:T(8,128)S(1)}, u32[]{:S(2)}, u32[]{:S(2)}) collective-permute-start(f32[136,128]{1,0:T(8,128)S(1)} %collective-permute-done.3.refs_4_), channel_id=1, source_target_pairs={{0,4},{4,0},{8,12},{12,8},{16,20},{20,16},{24,28},{28,24},{1,5},{5... | collective-permute-start | bytes 208904 | tf_op jit(solution)/shard_map/ppermute | solution.py:278
  15.5 1.9 %shard_map.74.ahead = f32[8,2,16,512]{3,2,1,0:T(8,128)} custom-call(f32[16,2,4096]{2,1,0:T(2,128)} %refs_4_.1), custom_call_target="tpu_custom_call" | custom-call | bytes 1000000 | tf_op jit(solution)/shard_map/pallas_call | solution.py:329
  17.5 1.0 %shard_map.73 = (f32[32,128]{1,0:T(8,128)S(1)}, f32[5,128,128]{2,1,0:T(8,128)S(1)}) custom-call(s32[4]{0:T(128)S(1)} %copy-done.3, s32[4,4,64]{2,1,0:T(4,128)S(1)} %copy-done.1, f32[4,1,64]{2,1,0:T(1,128)S(1)} %copy-done.4, f32[4,1,64]{2,1,0:T(1,128)S(1)} %copy-done.5, s32[4,1,128]{2,1,0:T(1,128)S(1)} %bitcast.2), custom_call_target="tpu_custom_call" | custom-call | bytes 1000000 | tf_op jit(solution)/shard_map/pallas_call | solution.py:339
  18.5 0.0 collective-permute-done.refs_1_
  18.5 0.0 collective-permute-done.5.refs_6_
  18.5 0.0 collective-permute-done.6.refs_7_
  18.5 0.0 collective-permute-done.2.refs_3_
  18.5 0.7 %collective-permute-done.4.refs_5_ = f32[136,128]{1,0:T(8,128)S(1)} collective-permute-done((f32[136,128]{1,0:T(8,128)S(1)}, f32[136,128]{1,0:T(8,128)S(1)}, u32[]{:S(2)}, u32[]{:S(2)}) %collective-permute-start.4) | collective-permute-done | bytes 69664 | tf_op jit(solution)/shard_map/ppermute | solution.py:278
  19.2 0.8 %shard_map.76 = (f32[1056,128]{1,0:T(8,128)S(1)}, f32[928,128]{1,0:T(8,128)S(1)}) custom-call(s32[4]{0:T(128)S(1)} %copy-done.3, f32[32,128]{1,0:T(8,128)S(1)} %get-tuple-element.17.rows, f32[8,2,16,512]{3,2,1,0:T(8,128)} %shard_map.74.ahead, f32[136,128]{1,0:T(8,128)S(1)} %copy-done, f32[136,128]{1,0:T(8,128)S(1)} %collective-permute-done.refs_1_, ...), custom_call_target="tpu_custom_call" | custom-call | bytes 1000000 | tf_op jit(solution)/shard_map/pallas_call | solution.py:347
  20.0 1.6 %collective-permute-start.8 = (f32[928,128]{1,0:T(8,128)S(1)}, f32[928,128]{1,0:T(8,128)S(1)}, u32[]{:S(2)}, u32[]{:S(2)}) collective-permute-start(f32[928,128]{1,0:T(8,128)S(1)} %get-tuple-element.19), channel_id=1, source_target_pairs={{0,2},{1,3},{2,0},{3,1},{4,6},{5,7},{6,4},{7,5},{8,10},{9,11},{10,... | collective-permute-start | bytes 1425416 | tf_op jit(solution)/shard_map/ppermute | solution.py:354
  21.6 4.9 %all-to-all-start = ((f32[8,2,16,512]{3,2,1,0:T(8,128)}), f32[8,2,16,512]{3,2,1,0:T(8,128)S(1)}, u32[]{:S(2)}, u32[]{:S(2)}) async-start(f32[8,2,16,512]{3,2,1,0:T(8,128)} %shard_map.74.ahead), calls=%async_computation | async-start | bytes 1048576 | tf_op jit(solution)/shard_map/all_to_all | solution.py:337
  26.5 0.0 collective-permute-start.7
  26.5 3.6 %collective-permute-done.8.far = f32[928,128]{1,0:T(8,128)S(1)} collective-permute-done((f32[928,128]{1,0:T(8,128)S(1)}, f32[928,128]{1,0:T(8,128)S(1)}, u32[]{:S(2)}, u32[]{:S(2)}) %collective-permute-start.8) | collective-permute-done | bytes 475168 | tf_op jit(solution)/shard_map/ppermute | solution.py:354
  30.2 0.0 collective-permute-start.9
  30.2 0.0 collective-permute-done.7.near
  30.2 1.8 %collective-permute-done.9.cross = f32[928,128]{1,0:T(8,128)S(1)} collective-permute-done((f32[928,128]{1,0:T(8,128)S(1)}, f32[928,128]{1,0:T(8,128)S(1)}, u32[]{:S(2)}, u32[]{:S(2)}) %collective-permute-start.9) | collective-permute-done | bytes 475168 | tf_op jit(solution)/shard_map/ppermute | solution.py:356
  32.0 2.7 %shard_map.77.pull = f32[8,128]{1,0:T(8,128)S(1)} custom-call(f32[1056,128]{1,0:T(8,128)S(1)} %get-tuple-element.18.own, f32[1056,128]{1,0:T(8,128)S(1)} %collective-permute-done.7.near, f32[928,128]{1,0:T(8,128)S(1)} %collective-permute-done.8.far, f32[928,128]{1,0:T(8,128)S(1)} %collective-permute-done.9.cross, f32[5,128,128]{2,1,0:T(8,128)S(1)} %get-tuple-element.16.steps), custom_call_target="tpu_custom_call" | custom-call | bytes 100000 | tf_op jit(solution)/shard_map/pallas_call | solution.py:358
  34.7 2.2 %all-to-all-done.fields = f32[8,2,16,512]{3,2,1,0:T(8,128)S(1)} async-done(((f32[8,2,16,512]{3,2,1,0:T(8,128)}), f32[8,2,16,512]{3,2,1,0:T(8,128)S(1)}, u32[]{:S(2)}, u32[]{:S(2)}) %all-to-all-start) | async-done | bytes 524320 | tf_op jit(solution)/shard_map/all_to_all | solution.py:337
  37.0 0.6 %shard_map.78 = (f32[1,2,16,512]{3,2,1,0:T(8,128)S(1)}, f32[1,2,16,512]{3,2,1,0:T(8,128)S(1)}, f32[1,2,16,512]{3,2,1,0:T(8,128)S(1)}, f32[1,2,16,512]{3,2,1,0:T(...) custom-call(f32[5,128,128]{2,1,0:T(8,128)S(1)} %get-tuple-element.16.steps, ...), custom_call_target="tpu_custom_call" | custom-call | flops 100000000 | bytes 1000000 | tf_op jit(solution)/shard_map/pallas_call | solution.py:369
  37.5 0.1 collective-permute-start.14
  37.6 1.8 %collective-permute-start.10 = (f32[1,2,16,512]{3,2,1,0:T(8,128)S(1)}, f32[1,2,16,512]{3,2,1,0:T(8,128)S(1)}, u32[]{:S(2)}, u32[]{:S(2)}) collective-permute-start(f32[1,2,16,512]{3,2,1,0:T(8,128)S(1)} %get-tuple-element.21), channel_id=1, source_target_pairs={{0,16},{4,20},{8,24},{12,28},{16,0},{20,4},{24,8},{28,12},{1,17},{... | collective-permute-start | bytes 196616 | tf_op jit(solution)/shard_map/ppermute | solution.py:278
  39.4 2.2 %collective-permute-start.11 = (f32[1,2,16,512]{3,2,1,0:T(8,128)S(1)}, f32[1,2,16,512]{3,2,1,0:T(8,128)S(1)}, u32[]{:S(2)}, u32[]{:S(2)}) collective-permute-start(f32[1,2,16,512]{3,2,1,0:T(8,128)S(1)} %get-tuple-element.22), channel_id=1, source_target_pairs={{0,20},{4,16},{8,28},{12,24},{16,4},{20,0},{24,12},{28,8},{1,21},{... | collective-permute-start | bytes 196616 | tf_op jit(solution)/shard_map/ppermute | solution.py:278
  41.6 1.5 %collective-permute-start.12 = (f32[1,2,16,512]{3,2,1,0:T(8,128)S(1)}, f32[1,2,16,512]{3,2,1,0:T(8,128)S(1)}, u32[]{:S(2)}, u32[]{:S(2)}) collective-permute-start(f32[1,2,16,512]{3,2,1,0:T(8,128)S(1)} %get-tuple-element.23), channel_id=1, source_target_pairs={{0,24},{4,28},{8,16},{12,20},{16,8},{20,12},{24,0},{28,4},{1,25},{... | collective-permute-start | bytes 196616 | tf_op jit(solution)/shard_map/ppermute | solution.py:278
  43.0 2.3 %collective-permute-start.13 = (f32[1,2,16,512]{3,2,1,0:T(8,128)S(1)}, f32[1,2,16,512]{3,2,1,0:T(8,128)S(1)}, u32[]{:S(2)}, u32[]{:S(2)}) collective-permute-start(f32[1,2,16,512]{3,2,1,0:T(8,128)S(1)} %get-tuple-element.24), channel_id=1, source_target_pairs={{0,28},{4,24},{8,20},{12,16},{16,12},{20,8},{24,4},{28,0},{1,29},{... | collective-permute-start | bytes 196616 | tf_op jit(solution)/shard_map/ppermute | solution.py:278
  45.3 0.0 collective-permute-done.14.refs_1_
  45.3 1.5 %collective-permute-start.15 = (f32[1,2,16,512]{3,2,1,0:T(8,128)S(1)}, f32[1,2,16,512]{3,2,1,0:T(8,128)S(1)}, u32[]{:S(2)}, u32[]{:S(2)}) collective-permute-start(f32[1,2,16,512]{3,2,1,0:T(8,128)S(1)} %get-tuple-element.26), channel_id=1, source_target_pairs={{0,4},{4,0},{8,12},{12,8},{16,20},{20,16},{24,28},{28,24},{1,5},{5... | collective-permute-start | bytes 196616 | tf_op jit(solution)/shard_map/ppermute | solution.py:278
  46.9 0.9 %collective-permute-done.10.refs_1_ = f32[1,2,16,512]{3,2,1,0:T(8,128)S(1)} collective-permute-done((f32[1,2,16,512]{3,2,1,0:T(8,128)S(1)}, f32[1,2,16,512]{3,2,1,0:T(8,128)S(1)}, u32[]{:S(2)}, u32[]{:S(2)}) %collective-permute-start.10) | collective-permute-done | bytes 65568 | tf_op jit(solution)/shard_map/ppermute | solution.py:278
  47.8 1.3 %collective-permute-start.16 = (f32[1,2,16,512]{3,2,1,0:T(8,128)S(1)}, f32[1,2,16,512]{3,2,1,0:T(8,128)S(1)}, u32[]{:S(2)}, u32[]{:S(2)}) collective-permute-start(f32[1,2,16,512]{3,2,1,0:T(8,128)S(1)} %slice.4), channel_id=1, source_target_pairs={{0,4},{4,0},{8,12},{12,8},{16,20},{20,16},{24,28},{28,24},{1,5},{5... | collective-permute-start | bytes 196616 | tf_op jit(solution)/shard_map/ppermute | solution.py:278
  49.1 1.5 %collective-permute-done.11.refs_2_ = f32[1,2,16,512]{3,2,1,0:T(8,128)S(1)} collective-permute-done((f32[1,2,16,512]{3,2,1,0:T(8,128)S(1)}, f32[1,2,16,512]{3,2,1,0:T(8,128)S(1)}, u32[]{:S(2)}, u32[]{:S(2)}) %collective-permute-start.11) | collective-permute-done | bytes 65568 | tf_op jit(solution)/shard_map/ppermute | solution.py:278
  50.7 0.0 collective-permute-done.12.refs_3_
  50.7 0.0 collective-permute-done.13.refs_4_
  50.7 0.8 %shard_map.79.refs_0_ = f32[16,2,4096]{2,1,0:T(2,128)} custom-call(f32[1,2,16,512]{3,2,1,0:T(8,128)S(1)} %get-tuple-element.20.refs_0_, f32[1,2,16,512]{3,2,1,0:T(8,128)S(1)} %collective-permute-done.10.refs_1_, f32[1,2,16,512]{3,2,1,0:T(8,128)S(1)} %collective-permute-done.11.refs_2_, f32[1,2,16,512]{3,2,1,0:T(8,128)S(1)} %collective-permute-done.12.refs_3_, ...), custom_call_target="tpu_custom_call" | custom-call | bytes 1000000 | tf_op jit(solution)/shard_map/pallas_call | solution.py:263
  51.5 0.6 %collective-permute-done.16.refs_3_ = f32[1,2,16,512]{3,2,1,0:T(8,128)S(1)} collective-permute-done((f32[1,2,16,512]{3,2,1,0:T(8,128)S(1)}, f32[1,2,16,512]{3,2,1,0:T(8,128)S(1)}, u32[]{:S(2)}, u32[]{:S(2)}) %collective-permute-start.16) | collective-permute-done | bytes 65568 | tf_op jit(solution)/shard_map/ppermute | solution.py:278
  52.1 0.7 %shard_map.80 = f32[16,2,4096]{2,1,0:T(2,128)} custom-call(f32[16,2,4096]{2,1,0:T(2,128)} %shard_map.79.refs_0_, f32[2,2,16,512]{3,2,1,0:T(8,128)S(1)} %collective-permute-done.14.refs_1_, f32[1,2,16,512]{3,2,1,0:T(8,128)S(1)} %collective-permute-done.15.refs_2_, f32[1,2,16,512]{3,2,1,0:T(8,128)S(1)} %collective-permute-done.16.refs_3_), custom_call_target="tpu_custom_call", output_to_operand_aliasing={{}: (0, {})} | custom-call | bytes 1000000 | tf_op jit(solution)/shard_map/pallas_call | solution.py:263
  (9 shorter events, 0.0 us)
Async XLA Ops:
  2.3 15.1 %copy-start.1 = (s32[4,4,64]{2,1,0:T(4,128)S(1)}, s32[4,4,64]{2,1,0:T(4,128)}, u32[]{:S(2)}) copy-start(s32[4,4,64]{2,1,0:T(4,128)} %refs_2_.1) | copy-start | bytes 12292
  2.3 15.1 %copy-start.2 = (s32[4,1,1,128]{3,2,1,0:T(1,128)S(1)}, s32[4,1,1,128]{3,2,1,0:T(1,128)}, u32[]{:S(2)}) copy-start(s32[4,1,1,128]{3,2,1,0:T(1,128)} %param.13) | copy-start | bytes 6148
  2.4 15.1 %copy-start.3 = (s32[4]{0:T(128)S(1)}, s32[4]{0:T(128)}, u32[]{:S(2)}) copy-start(s32[4]{0:T(128)} %owner.3) | copy-start | bytes 52
  2.4 15.1 %copy-start.4 = (f32[4,1,64]{2,1,0:T(1,128)S(1)}, f32[4,1,64]{2,1,0:T(1,128)}, u32[]{:S(2)}) copy-start(f32[4,1,64]{2,1,0:T(1,128)} %values.1) | copy-start | bytes 3076
  2.4 15.1 %copy-start.5 = (f32[4,1,64]{2,1,0:T(1,128)S(1)}, f32[4,1,64]{2,1,0:T(1,128)}, u32[]{:S(2)}) copy-start(f32[4,1,64]{2,1,0:T(1,128)} %errors.1) | copy-start | bytes 3076
  2.4 16.8 %copy-start = (f32[136,128]{1,0:T(8,128)S(1)}, f32[136,128]{1,0:T(8,128)}, u32[]{:S(2)}) copy-start(f32[136,128]{1,0:T(8,128)} %shard_map.75.refs_0_) | copy-start | bytes 208900
  2.4 11.0 %collective-permute-start.1 = (f32[136,128]{1,0:T(8,128)}, f32[136,128]{1,0:T(8,128)S(1)}, u32[]{:S(2)}, u32[]{:S(2)}) collective-permute-start(f32[136,128]{1,0:T(8,128)} %shard_map.75.refs_0_), channel_id=1, source_target_pairs={{0,8},{4,12},{8,0},{12,4},{16,24},{20,28},{24,16},{28,20},{1,9},{5... | collective-permute-start | bytes 208904 | tf_op jit(solution)/shard_map/ppermute | solution.py:278
  5.5 9.4 %collective-permute-start.3 = (f32[136,128]{1,0:T(8,128)}, f32[136,128]{1,0:T(8,128)S(1)}, u32[]{:S(2)}, u32[]{:S(2)}) collective-permute-start(f32[136,128]{1,0:T(8,128)} %shard_map.75.refs_0_), channel_id=1, source_target_pairs={{0,16},{4,20},{8,24},{12,28},{16,0},{20,4},{24,8},{28,12},{1,17},{... | collective-permute-start | bytes 208904 | tf_op jit(solution)/shard_map/ppermute | solution.py:278
  8.1 10.4 %collective-permute-start = (f32[136,128]{1,0:T(8,128)}, f32[136,128]{1,0:T(8,128)S(1)}, u32[]{:S(2)}, u32[]{:S(2)}) collective-permute-start(f32[136,128]{1,0:T(8,128)} %shard_map.75.refs_0_), channel_id=1, source_target_pairs={{0,4},{4,0},{8,12},{12,8},{16,20},{20,16},{24,28},{28,24},{1,5},{5... | collective-permute-start | bytes 208904 | tf_op jit(solution)/shard_map/ppermute | solution.py:278
  9.6 8.9 %collective-permute-start.5 = (f32[136,128]{1,0:T(8,128)}, f32[136,128]{1,0:T(8,128)S(1)}, u32[]{:S(2)}, u32[]{:S(2)}) collective-permute-start(f32[136,128]{1,0:T(8,128)} %shard_map.75.refs_0_), channel_id=1, source_target_pairs={{0,24},{4,28},{8,16},{12,20},{16,8},{20,12},{24,0},{28,4},{1,25},{... | collective-permute-start | bytes 208904 | tf_op jit(solution)/shard_map/ppermute | solution.py:278
  9.8 8.7 %collective-permute-start.6 = (f32[136,128]{1,0:T(8,128)}, f32[136,128]{1,0:T(8,128)S(1)}, u32[]{:S(2)}, u32[]{:S(2)}) collective-permute-start(f32[136,128]{1,0:T(8,128)} %shard_map.75.refs_0_), channel_id=1, source_target_pairs={{0,28},{4,24},{8,20},{12,16},{16,12},{20,8},{24,4},{28,0},{1,29},{... | collective-permute-start | bytes 208904 | tf_op jit(solution)/shard_map/ppermute | solution.py:278
  13.4 5.1 %collective-permute-start.2 = (f32[136,128]{1,0:T(8,128)S(1)}, f32[136,128]{1,0:T(8,128)S(1)}, u32[]{:S(2)}, u32[]{:S(2)}) collective-permute-start(f32[136,128]{1,0:T(8,128)S(1)} %collective-permute-done.1.refs_2_), channel_id=1, source_target_pairs={{0,4},{4,0},{8,12},{12,8},{16,20},{20,16},{24,28},{28,24},{1,5},{5... | collective-permute-start | bytes 208904 | tf_op jit(solution)/shard_map/ppermute | solution.py:278
  14.9 4.3 %collective-permute-start.4 = (f32[136,128]{1,0:T(8,128)S(1)}, f32[136,128]{1,0:T(8,128)S(1)}, u32[]{:S(2)}, u32[]{:S(2)}) collective-permute-start(f32[136,128]{1,0:T(8,128)S(1)} %collective-permute-done.3.refs_4_), channel_id=1, source_target_pairs={{0,4},{4,0},{8,12},{12,8},{16,20},{20,16},{24,28},{28,24},{1,5},{5... | collective-permute-start | bytes 208904 | tf_op jit(solution)/shard_map/ppermute | solution.py:278
  20.0 10.2 %collective-permute-start.8 = (f32[928,128]{1,0:T(8,128)S(1)}, f32[928,128]{1,0:T(8,128)S(1)}, u32[]{:S(2)}, u32[]{:S(2)}) collective-permute-start(f32[928,128]{1,0:T(8,128)S(1)} %get-tuple-element.19), channel_id=1, source_target_pairs={{0,2},{1,3},{2,0},{3,1},{4,6},{5,7},{6,4},{7,5},{8,10},{9,11},{10,... | collective-permute-start | bytes 1425416 | tf_op jit(solution)/shard_map/ppermute | solution.py:354
  21.6 15.4 %all-to-all-start = ((f32[8,2,16,512]{3,2,1,0:T(8,128)}), f32[8,2,16,512]{3,2,1,0:T(8,128)S(1)}, u32[]{:S(2)}, u32[]{:S(2)}) async-start(f32[8,2,16,512]{3,2,1,0:T(8,128)} %shard_map.74.ahead), calls=%async_computation | async-start | bytes 1048576 | tf_op jit(solution)/shard_map/all_to_all | solution.py:337
  26.5 3.7 %collective-permute-start.7 = (f32[1056,128]{1,0:T(8,128)S(1)}, f32[1056,128]{1,0:T(8,128)S(1)}, u32[]{:S(2)}, u32[]{:S(2)}) collective-permute-start(f32[1056,128]{1,0:T(8,128)S(1)} %get-tuple-element.18.own), channel_id=1, source_target_pairs={{0,1},{1,0},{2,3},{3,2},{4,5},{5,4},{6,7},{7,6},{8,9},{9,8},{10,11... | collective-permute-start | bytes 1622024 | tf_op jit(solution)/shard_map/ppermute | solution.py:355
  30.2 1.8 %collective-permute-start.9 = (f32[928,128]{1,0:T(8,128)S(1)}, f32[928,128]{1,0:T(8,128)S(1)}, u32[]{:S(2)}, u32[]{:S(2)}) collective-permute-start(f32[928,128]{1,0:T(8,128)S(1)} %collective-permute-done.8.far), channel_id=1, source_target_pairs={{0,1},{1,0},{2,3},{3,2},{4,5},{5,4},{6,7},{7,6},{8,9},{9,8},{10,11... | collective-permute-start | bytes 1425416 | tf_op jit(solution)/shard_map/ppermute | solution.py:356
  37.5 7.8 %collective-permute-start.14 = (f32[2,2,16,512]{3,2,1,0:T(8,128)S(1)}, f32[2,2,16,512]{3,2,1,0:T(8,128)S(1)}, u32[]{:S(2)}, u32[]{:S(2)}) collective-permute-start(f32[2,2,16,512]{3,2,1,0:T(8,128)S(1)} %get-tuple-element.25), channel_id=1, source_target_pairs={{0,8},{4,12},{8,0},{12,4},{16,24},{20,28},{24,16},{28,20},{1,9},{5... | collective-permute-start | bytes 393224 | tf_op jit(solution)/shard_map/ppermute | solution.py:278
  37.6 10.2 %collective-permute-start.10 = (f32[1,2,16,512]{3,2,1,0:T(8,128)S(1)}, f32[1,2,16,512]{3,2,1,0:T(8,128)S(1)}, u32[]{:S(2)}, u32[]{:S(2)}) collective-permute-start(f32[1,2,16,512]{3,2,1,0:T(8,128)S(1)} %get-tuple-element.21), channel_id=1, source_target_pairs={{0,16},{4,20},{8,24},{12,28},{16,0},{20,4},{24,8},{28,12},{1,17},{... | collective-permute-start | bytes 196616 | tf_op jit(solution)/shard_map/ppermute | solution.py:278
  39.4 11.3 %collective-permute-start.11 = (f32[1,2,16,512]{3,2,1,0:T(8,128)S(1)}, f32[1,2,16,512]{3,2,1,0:T(8,128)S(1)}, u32[]{:S(2)}, u32[]{:S(2)}) collective-permute-start(f32[1,2,16,512]{3,2,1,0:T(8,128)S(1)} %get-tuple-element.22), channel_id=1, source_target_pairs={{0,20},{4,16},{8,28},{12,24},{16,4},{20,0},{24,12},{28,8},{1,21},{... | collective-permute-start | bytes 196616 | tf_op jit(solution)/shard_map/ppermute | solution.py:278
  41.6 9.1 %collective-permute-start.12 = (f32[1,2,16,512]{3,2,1,0:T(8,128)S(1)}, f32[1,2,16,512]{3,2,1,0:T(8,128)S(1)}, u32[]{:S(2)}, u32[]{:S(2)}) collective-permute-start(f32[1,2,16,512]{3,2,1,0:T(8,128)S(1)} %get-tuple-element.23), channel_id=1, source_target_pairs={{0,24},{4,28},{8,16},{12,20},{16,8},{20,12},{24,0},{28,4},{1,25},{... | collective-permute-start | bytes 196616 | tf_op jit(solution)/shard_map/ppermute | solution.py:278
  43.0 7.6 %collective-permute-start.13 = (f32[1,2,16,512]{3,2,1,0:T(8,128)S(1)}, f32[1,2,16,512]{3,2,1,0:T(8,128)S(1)}, u32[]{:S(2)}, u32[]{:S(2)}) collective-permute-start(f32[1,2,16,512]{3,2,1,0:T(8,128)S(1)} %get-tuple-element.24), channel_id=1, source_target_pairs={{0,28},{4,24},{8,20},{12,16},{16,12},{20,8},{24,4},{28,0},{1,29},{... | collective-permute-start | bytes 196616 | tf_op jit(solution)/shard_map/ppermute | solution.py:278
  45.3 6.1 %collective-permute-start.15 = (f32[1,2,16,512]{3,2,1,0:T(8,128)S(1)}, f32[1,2,16,512]{3,2,1,0:T(8,128)S(1)}, u32[]{:S(2)}, u32[]{:S(2)}) collective-permute-start(f32[1,2,16,512]{3,2,1,0:T(8,128)S(1)} %get-tuple-element.26), channel_id=1, source_target_pairs={{0,4},{4,0},{8,12},{12,8},{16,20},{20,16},{24,28},{28,24},{1,5},{5... | collective-permute-start | bytes 196616 | tf_op jit(solution)/shard_map/ppermute | solution.py:278
  47.8 4.3 %collective-permute-start.16 = (f32[1,2,16,512]{3,2,1,0:T(8,128)S(1)}, f32[1,2,16,512]{3,2,1,0:T(8,128)S(1)}, u32[]{:S(2)}, u32[]{:S(2)}) collective-permute-start(f32[1,2,16,512]{3,2,1,0:T(8,128)S(1)} %slice.4), channel_id=1, source_target_pairs={{0,4},{4,0},{8,12},{12,8},{16,20},{20,16},{24,28},{28,24},{1,5},{5... | collective-permute-start | bytes 196616 | tf_op jit(solution)/shard_map/ppermute | solution.py:278

commit v21 on v18

--- a/solution.py
+++ b/solution.py
@@ -290,8 +290,8 @@
     far = [parts[0]] + [hop(part, distances[0], n) for part, distances in zip(parts[1:5], PARTS[1:5])]
     near = hop(parts[5], PARTS[5][0], n)
     beside, onward = hop(parts[6], 1, n), hop(near[1:], 1, n)
-    out = place(shape, whole, [(i, 0, PARTS[i][0]) for i in range(5)], far, moved=10**6)
-    return place(shape, whole, [(0, 0, 2), (1, 0, 1), (2, 0, 3)], [near, beside, onward], out, moved=10**6)
+    out = place(shape, whole, [(i, 0, PARTS[i][0]) for i in range(6)], far + [near], moved=10**6)
+    return place(shape, whole, [(0, 0, 1), (1, 0, 3)], [beside, onward], out, moved=10**6)
 
 
 def body(prior, channel_weights, obs_owner, obs_offset, obs_value, obs_error, ancestors):

time: 53 us -> 53 us (level)
  no operation moved by 1% of the time
where the time goes in v21:
time: 53 us; the launch traced here: 52.8 us
  starting transfers between devices  30.2 us (57%)
  waiting for transfers between devices  12.5 us (24%)
  Pallas kernels  9.86 us (19%)
    ppermute x14, starting transfers between devices, hop(): return lax.ppermute(value, 'grid', [(j, j ^ distance) for j in range(n)])  23.7 us
    all_to_all x1, starting transfers between devices, body(): fields = lax.all_to_all(send, 'grid', 0, 0, tiled=True)  4.95 us
    ppermute x14, waiting for transfers between devices, hop(): return lax.ppermute(value, 'grid', [(j, j ^ distance) for j in range(n)])  4.84 us
    ppermute x1, waiting for transfers between devices, body(): far = lax.ppermute(slim, 'lev', [(j, j ^ 2) for j in range(lev)])  3.64 us
    pallas_call x1, Pallas kernels, body(): call(functools.partial(chain_kernel, (members, groups, count)), shape((8,...  2.72 us
    pallas_call x1, Pallas kernels, body(): call(functools.partial(pick_kernel, (slab, depth, block_cells, groups, co...  2.39 us
    all_to_all x1, waiting for transfers between devices, body(): fields = lax.all_to_all(send, 'grid', 0, 0, tiled=True)  2.22 us
    ppermute x1, waiting for transfers between devices, body(): cross = lax.ppermute(far, 'lev', [(j, j ^ 1) for j in range(lev)])  1.83 us
  transfers between devices with their start and end apart: 18, of which 8 were waited for; matrix products, arithmetic and copies ran while one was open for 0% of the time, Pallas kernels for 10%

profile of v21, /device:TPU:0, one launch (start us, length us, event | category | flops | bytes accessed | tf_op | source)
XLA Modules:
  0.0 52.8 jit_solution(11987147614270958344)
XLA Ops:
  0.0 2.4 %shard_map.75.refs_0_ = f32[136,128]{1,0:T(8,128)} custom-call(s32[4]{0:T(128)} %owner.3, f32[2,4]{1,0:T(2,128)} %refs_1_.1, s32[4,4,64]{2,1,0:T(4,128)} %refs_2_.1, s32[4,1,128]{2,1,0:T(1,128)} %bitcast.1, f32[16,2,4096]{2,1,0:T(2,128)} %refs_4_.1), custom_call_target="tpu_custom_call" | custom-call | bytes 1000000 | tf_op jit(solution)/shard_map/pallas_call | solution.py:310
  2.4 0.0 copy-start.2
  2.4 0.0 copy-start.3
  2.4 0.0 copy-start.4
  2.4 0.0 copy-start.5
  2.4 0.0 copy-start.6
  2.5 3.1 %collective-permute-start.1 = (f32[136,128]{1,0:T(8,128)}, f32[136,128]{1,0:T(8,128)S(1)}, u32[]{:S(2)}, u32[]{:S(2)}) collective-permute-start(f32[136,128]{1,0:T(8,128)} %shard_map.75.refs_0_), channel_id=1, source_target_pairs={{0,8},{4,12},{8,0},{12,4},{16,24},{20,28},{24,16},{28,20},{1,9},{5... | collective-permute-start | bytes 208904 | tf_op jit(solution)/shard_map/ppermute | solution.py:275
  5.6 2.6 %collective-permute-start.3 = (f32[136,128]{1,0:T(8,128)}, f32[136,128]{1,0:T(8,128)S(1)}, u32[]{:S(2)}, u32[]{:S(2)}) collective-permute-start(f32[136,128]{1,0:T(8,128)} %shard_map.75.refs_0_), channel_id=1, source_target_pairs={{0,16},{4,20},{8,24},{12,28},{16,0},{20,4},{24,8},{28,12},{1,17},{... | collective-permute-start | bytes 208904 | tf_op jit(solution)/shard_map/ppermute | solution.py:275
  8.1 1.5 %collective-permute-start = (f32[136,128]{1,0:T(8,128)}, f32[136,128]{1,0:T(8,128)S(1)}, u32[]{:S(2)}, u32[]{:S(2)}) collective-permute-start(f32[136,128]{1,0:T(8,128)} %shard_map.75.refs_0_), channel_id=1, source_target_pairs={{0,4},{4,0},{8,12},{12,8},{16,20},{20,16},{24,28},{28,24},{1,5},{5... | collective-permute-start | bytes 208904 | tf_op jit(solution)/shard_map/ppermute | solution.py:275
  9.7 0.2 collective-permute-start.5
  9.9 3.5 %collective-permute-start.6 = (f32[136,128]{1,0:T(8,128)}, f32[136,128]{1,0:T(8,128)S(1)}, u32[]{:S(2)}, u32[]{:S(2)}) collective-permute-start(f32[136,128]{1,0:T(8,128)} %shard_map.75.refs_0_), channel_id=1, source_target_pairs={{0,28},{4,24},{8,20},{12,16},{16,12},{20,8},{24,4},{28,0},{1,29},{... | collective-permute-start | bytes 208904 | tf_op jit(solution)/shard_map/ppermute | solution.py:275
  13.4 0.0 collective-permute-done.1.refs_2_
  13.4 1.5 %collective-permute-start.2 = (f32[136,128]{1,0:T(8,128)S(1)}, f32[136,128]{1,0:T(8,128)S(1)}, u32[]{:S(2)}, u32[]{:S(2)}) collective-permute-start(f32[136,128]{1,0:T(8,128)S(1)} %collective-permute-done.1.refs_2_), channel_id=1, source_target_pairs={{0,4},{4,0},{8,12},{12,8},{16,20},{20,16},{24,28},{28,24},{1,5},{5... | collective-permute-start | bytes 208904 | tf_op jit(solution)/shard_map/ppermute | solution.py:275
  15.0 0.0 collective-permute-done.3.refs_4_
  15.0 0.6 %collective-permute-start.4 = (f32[136,128]{1,0:T(8,128)S(1)}, f32[136,128]{1,0:T(8,128)S(1)}, u32[]{:S(2)}, u32[]{:S(2)}) collective-permute-start(f32[136,128]{1,0:T(8,128)S(1)} %collective-permute-done.3.refs_4_), channel_id=1, source_target_pairs={{0,4},{4,0},{8,12},{12,8},{16,20},{20,16},{24,28},{28,24},{1,5},{5... | collective-permute-start | bytes 208904 | tf_op jit(solution)/shard_map/ppermute | solution.py:275
  15.6 0.9 %shard_map.74.ahead = f32[8,2,16,512]{3,2,1,0:T(8,128)} custom-call(f32[16,2,4096]{2,1,0:T(2,128)S(1)} %copy-done), custom_call_target="tpu_custom_call" | custom-call | bytes 1000000 | tf_op jit(solution)/shard_map/pallas_call | solution.py:326
  16.5 1.0 %shard_map.73 = (f32[32,128]{1,0:T(8,128)S(1)}, f32[5,128,128]{2,1,0:T(8,128)S(1)}) custom-call(s32[4]{0:T(128)S(1)} %copy-done.4, s32[4,4,64]{2,1,0:T(4,128)S(1)} %copy-done.2, f32[4,1,64]{2,1,0:T(1,128)S(1)} %copy-done.5, f32[4,1,64]{2,1,0:T(1,128)S(1)} %copy-done.6, s32[4,1,128]{2,1,0:T(1,128)S(1)} %bitcast.2), custom_call_target="tpu_custom_call" | custom-call | bytes 1000000 | tf_op jit(solution)/shard_map/pallas_call | solution.py:334
  17.5 0.0 collective-permute-done.refs_1_
  17.5 0.0 collective-permute-done.5.refs_6_
  17.5 0.0 collective-permute-done.6.refs_7_
  17.5 0.4 collective-permute-done.2.refs_3_
  18.0 1.3 %collective-permute-done.4.refs_5_ = f32[136,128]{1,0:T(8,128)S(1)} collective-permute-done((f32[136,128]{1,0:T(8,128)S(1)}, f32[136,128]{1,0:T(8,128)S(1)}, u32[]{:S(2)}, u32[]{:S(2)}) %collective-permute-start.4) | collective-permute-done | bytes 69664 | tf_op jit(solution)/shard_map/ppermute | solution.py:275
  19.3 0.8 %shard_map.76 = (f32[1056,128]{1,0:T(8,128)S(1)}, f32[928,128]{1,0:T(8,128)S(1)}) custom-call(s32[4]{0:T(128)S(1)} %copy-done.4, f32[32,128]{1,0:T(8,128)S(1)} %get-tuple-element.17.rows, f32[8,2,16,512]{3,2,1,0:T(8,128)} %shard_map.74.ahead, f32[136,128]{1,0:T(8,128)S(1)} %copy-done.1, f32[136,128]{1,0:T(8,128)S(1)} %collective-permute-done.refs_1_, ...), custom_call_target="tpu_custom_call" | custom-call | bytes 1000000 | tf_op jit(solution)/shard_map/pallas_call | solution.py:342
  20.1 1.6 %collective-permute-start.8 = (f32[928,128]{1,0:T(8,128)S(1)}, f32[928,128]{1,0:T(8,128)S(1)}, u32[]{:S(2)}, u32[]{:S(2)}) collective-permute-start(f32[928,128]{1,0:T(8,128)S(1)} %get-tuple-element.19), channel_id=1, source_target_pairs={{0,2},{1,3},{2,0},{3,1},{4,6},{5,7},{6,4},{7,5},{8,10},{9,11},{10,... | collective-permute-start | bytes 1425416 | tf_op jit(solution)/shard_map/ppermute | solution.py:349
  21.6 4.9 %all-to-all-start = ((f32[8,2,16,512]{3,2,1,0:T(8,128)}), f32[8,2,16,512]{3,2,1,0:T(8,128)S(1)}, u32[]{:S(2)}, u32[]{:S(2)}) async-start(f32[8,2,16,512]{3,2,1,0:T(8,128)} %shard_map.74.ahead), calls=%async_computation | async-start | bytes 1048576 | tf_op jit(solution)/shard_map/all_to_all | solution.py:332
  26.6 0.0 collective-permute-start.7
  26.6 3.6 %collective-permute-done.8.far = f32[928,128]{1,0:T(8,128)S(1)} collective-permute-done((f32[928,128]{1,0:T(8,128)S(1)}, f32[928,128]{1,0:T(8,128)S(1)}, u32[]{:S(2)}, u32[]{:S(2)}) %collective-permute-start.8) | collective-permute-done | bytes 475168 | tf_op jit(solution)/shard_map/ppermute | solution.py:349
  30.2 0.0 collective-permute-start.9
  30.2 0.0 collective-permute-done.7.near
  30.2 1.8 %collective-permute-done.9.cross = f32[928,128]{1,0:T(8,128)S(1)} collective-permute-done((f32[928,128]{1,0:T(8,128)S(1)}, f32[928,128]{1,0:T(8,128)S(1)}, u32[]{:S(2)}, u32[]{:S(2)}) %collective-permute-start.9) | collective-permute-done | bytes 475168 | tf_op jit(solution)/shard_map/ppermute | solution.py:351
  32.1 2.7 %shard_map.77.pull = f32[8,128]{1,0:T(8,128)S(1)} custom-call(f32[1056,128]{1,0:T(8,128)S(1)} %get-tuple-element.18.own, f32[1056,128]{1,0:T(8,128)S(1)} %collective-permute-done.7.near, f32[928,128]{1,0:T(8,128)S(1)} %collective-permute-done.8.far, f32[928,128]{1,0:T(8,128)S(1)} %collective-permute-done.9.cross, f32[5,128,128]{2,1,0:T(8,128)S(1)} %get-tuple-element.16.steps), custom_call_target="tpu_custom_call" | custom-call | bytes 100000 | tf_op jit(solution)/shard_map/pallas_call | solution.py:353
  34.8 2.2 %all-to-all-done.fields = f32[8,2,16,512]{3,2,1,0:T(8,128)S(1)} async-done(((f32[8,2,16,512]{3,2,1,0:T(8,128)}), f32[8,2,16,512]{3,2,1,0:T(8,128)S(1)}, u32[]{:S(2)}, u32[]{:S(2)}) %all-to-all-start) | async-done | bytes 524320 | tf_op jit(solution)/shard_map/all_to_all | solution.py:332
  37.0 0.6 %shard_map.78 = (f32[1,2,16,512]{3,2,1,0:T(8,128)S(1)}, f32[1,2,16,512]{3,2,1,0:T(8,128)S(1)}, f32[1,2,16,512]{3,2,1,0:T(8,128)S(1)}, f32[1,2,16,512]{3,2,1,0:T(...) custom-call(f32[5,128,128]{2,1,0:T(8,128)S(1)} %get-tuple-element.16.steps, ...), custom_call_target="tpu_custom_call" | custom-call | flops 100000000 | bytes 1000000 | tf_op jit(solution)/shard_map/pallas_call | solution.py:364
  37.6 0.1 collective-permute-start.14
  37.7 1.8 %collective-permute-start.10 = (f32[1,2,16,512]{3,2,1,0:T(8,128)S(1)}, f32[1,2,16,512]{3,2,1,0:T(8,128)S(1)}, u32[]{:S(2)}, u32[]{:S(2)}) collective-permute-start(f32[1,2,16,512]{3,2,1,0:T(8,128)S(1)} %get-tuple-element.21), channel_id=1, source_target_pairs={{0,16},{4,20},{8,24},{12,28},{16,0},{20,4},{24,8},{28,12},{1,17},{... | collective-permute-start | bytes 196616 | tf_op jit(solution)/shard_map/ppermute | solution.py:275
  39.4 2.2 %collective-permute-start.11 = (f32[1,2,16,512]{3,2,1,0:T(8,128)S(1)}, f32[1,2,16,512]{3,2,1,0:T(8,128)S(1)}, u32[]{:S(2)}, u32[]{:S(2)}) collective-permute-start(f32[1,2,16,512]{3,2,1,0:T(8,128)S(1)} %get-tuple-element.22), channel_id=1, source_target_pairs={{0,20},{4,16},{8,28},{12,24},{16,4},{20,0},{24,12},{28,8},{1,21},{... | collective-permute-start | bytes 196616 | tf_op jit(solution)/shard_map/ppermute | solution.py:275
  41.6 1.5 %collective-permute-start.12 = (f32[1,2,16,512]{3,2,1,0:T(8,128)S(1)}, f32[1,2,16,512]{3,2,1,0:T(8,128)S(1)}, u32[]{:S(2)}, u32[]{:S(2)}) collective-permute-start(f32[1,2,16,512]{3,2,1,0:T(8,128)S(1)} %get-tuple-element.23), channel_id=1, source_target_pairs={{0,24},{4,28},{8,16},{12,20},{16,8},{20,12},{24,0},{28,4},{1,25},{... | collective-permute-start | bytes 196616 | tf_op jit(solution)/shard_map/ppermute | solution.py:275
  43.1 2.3 %collective-permute-start.13 = (f32[1,2,16,512]{3,2,1,0:T(8,128)S(1)}, f32[1,2,16,512]{3,2,1,0:T(8,128)S(1)}, u32[]{:S(2)}, u32[]{:S(2)}) collective-permute-start(f32[1,2,16,512]{3,2,1,0:T(8,128)S(1)} %get-tuple-element.24), channel_id=1, source_target_pairs={{0,28},{4,24},{8,20},{12,16},{16,12},{20,8},{24,4},{28,0},{1,29},{... | collective-permute-start | bytes 196616 | tf_op jit(solution)/shard_map/ppermute | solution.py:275
  45.4 0.0 collective-permute-done.14.refs_5_
  45.4 1.5 %collective-permute-start.15 = (f32[1,2,16,512]{3,2,1,0:T(8,128)S(1)}, f32[1,2,16,512]{3,2,1,0:T(8,128)S(1)}, u32[]{:S(2)}, u32[]{:S(2)}) collective-permute-start(f32[1,2,16,512]{3,2,1,0:T(8,128)S(1)} %get-tuple-element.26), channel_id=1, source_target_pairs={{0,4},{4,0},{8,12},{12,8},{16,20},{20,16},{24,28},{28,24},{1,5},{5... | collective-permute-start | bytes 196616 | tf_op jit(solution)/shard_map/ppermute | solution.py:275
  46.9 0.9 %collective-permute-done.10.refs_1_ = f32[1,2,16,512]{3,2,1,0:T(8,128)S(1)} collective-permute-done((f32[1,2,16,512]{3,2,1,0:T(8,128)S(1)}, f32[1,2,16,512]{3,2,1,0:T(8,128)S(1)}, u32[]{:S(2)}, u32[]{:S(2)}) %collective-permute-start.10) | collective-permute-done | bytes 65568 | tf_op jit(solution)/shard_map/ppermute | solution.py:275
  47.9 1.3 %collective-permute-start.16 = (f32[1,2,16,512]{3,2,1,0:T(8,128)S(1)}, f32[1,2,16,512]{3,2,1,0:T(8,128)S(1)}, u32[]{:S(2)}, u32[]{:S(2)}) collective-permute-start(f32[1,2,16,512]{3,2,1,0:T(8,128)S(1)} %slice.4), channel_id=1, source_target_pairs={{0,4},{4,0},{8,12},{12,8},{16,20},{20,16},{24,28},{28,24},{1,5},{5... | collective-permute-start | bytes 196616 | tf_op jit(solution)/shard_map/ppermute | solution.py:275
  49.2 1.5 %collective-permute-done.11.refs_2_ = f32[1,2,16,512]{3,2,1,0:T(8,128)S(1)} collective-permute-done((f32[1,2,16,512]{3,2,1,0:T(8,128)S(1)}, f32[1,2,16,512]{3,2,1,0:T(8,128)S(1)}, u32[]{:S(2)}, u32[]{:S(2)}) %collective-permute-start.11) | collective-permute-done | bytes 65568 | tf_op jit(solution)/shard_map/ppermute | solution.py:275
  50.7 0.0 collective-permute-done.12.refs_3_
  50.7 0.0 collective-permute-done.13.refs_4_
  50.7 0.8 %shard_map.79.refs_0_ = f32[16,2,4096]{2,1,0:T(2,128)} custom-call(f32[1,2,16,512]{3,2,1,0:T(8,128)S(1)} %get-tuple-element.20.refs_0_, f32[1,2,16,512]{3,2,1,0:T(8,128)S(1)} %collective-permute-done.10.refs_1_, f32[1,2,16,512]{3,2,1,0:T(8,128)S(1)} %collective-permute-done.11.refs_2_, f32[1,2,16,512]{3,2,1,0:T(8,128)S(1)} %collective-permute-done.12.refs_3_, ...), custom_call_target="tpu_custom_call" | custom-call | bytes 1000000 | tf_op jit(solution)/shard_map/pallas_call | solution.py:260
  51.5 0.6 %collective-permute-done.16.refs_2_ = f32[1,2,16,512]{3,2,1,0:T(8,128)S(1)} collective-permute-done((f32[1,2,16,512]{3,2,1,0:T(8,128)S(1)}, f32[1,2,16,512]{3,2,1,0:T(8,128)S(1)}, u32[]{:S(2)}, u32[]{:S(2)}) %collective-permute-start.16) | collective-permute-done | bytes 65568 | tf_op jit(solution)/shard_map/ppermute | solution.py:275
  52.1 0.7 %shard_map.80 = f32[16,2,4096]{2,1,0:T(2,128)} custom-call(f32[16,2,4096]{2,1,0:T(2,128)} %shard_map.79.refs_0_, f32[1,2,16,512]{3,2,1,0:T(8,128)S(1)} %collective-permute-done.15.refs_1_, f32[1,2,16,512]{3,2,1,0:T(8,128)S(1)} %collective-permute-done.16.refs_2_), custom_call_target="tpu_custom_call", output_to_operand_aliasing={{}: (0, {})} | custom-call | bytes 1000000 | tf_op jit(solution)/shard_map/pallas_call | solution.py:260
  (11 shorter events, 0.0 us)
Async XLA Ops:
  0.0 15.6 %copy-start = (f32[16,2,4096]{2,1,0:T(2,128)S(1)}, f32[16,2,4096]{2,1,0:T(2,128)}, u32[]{:S(2)}) copy-start(f32[16,2,4096]{2,1,0:T(2,128)} %refs_4_.1) | copy-start | bytes 1572868
  2.4 14.1 %copy-start.2 = (s32[4,4,64]{2,1,0:T(4,128)S(1)}, s32[4,4,64]{2,1,0:T(4,128)}, u32[]{:S(2)}) copy-start(s32[4,4,64]{2,1,0:T(4,128)} %refs_2_.1) | copy-start | bytes 12292
  2.4 14.0 %copy-start.3 = (s32[4,1,1,128]{3,2,1,0:T(1,128)S(1)}, s32[4,1,1,128]{3,2,1,0:T(1,128)}, u32[]{:S(2)}) copy-start(s32[4,1,1,128]{3,2,1,0:T(1,128)} %param.13) | copy-start | bytes 6148
  2.4 14.0 %copy-start.4 = (s32[4]{0:T(128)S(1)}, s32[4]{0:T(128)}, u32[]{:S(2)}) copy-start(s32[4]{0:T(128)} %owner.3) | copy-start | bytes 52
  2.4 14.0 %copy-start.5 = (f32[4,1,64]{2,1,0:T(1,128)S(1)}, f32[4,1,64]{2,1,0:T(1,128)}, u32[]{:S(2)}) copy-start(f32[4,1,64]{2,1,0:T(1,128)} %values.1) | copy-start | bytes 3076
  2.4 14.0 %copy-start.6 = (f32[4,1,64]{2,1,0:T(1,128)S(1)}, f32[4,1,64]{2,1,0:T(1,128)}, u32[]{:S(2)}) copy-start(f32[4,1,64]{2,1,0:T(1,128)} %errors.1) | copy-start | bytes 3076
  2.5 16.8 %copy-start.1 = (f32[136,128]{1,0:T(8,128)S(1)}, f32[136,128]{1,0:T(8,128)}, u32[]{:S(2)}) copy-start(f32[136,128]{1,0:T(8,128)} %shard_map.75.refs_0_) | copy-start | bytes 208900
  2.5 11.0 %collective-permute-start.1 = (f32[136,128]{1,0:T(8,128)}, f32[136,128]{1,0:T(8,128)S(1)}, u32[]{:S(2)}, u32[]{:S(2)}) collective-permute-start(f32[136,128]{1,0:T(8,128)} %shard_map.75.refs_0_), channel_id=1, source_target_pairs={{0,8},{4,12},{8,0},{12,4},{16,24},{20,28},{24,16},{28,20},{1,9},{5... | collective-permute-start | bytes 208904 | tf_op jit(solution)/shard_map/ppermute | solution.py:275
  5.6 9.4 %collective-permute-start.3 = (f32[136,128]{1,0:T(8,128)}, f32[136,128]{1,0:T(8,128)S(1)}, u32[]{:S(2)}, u32[]{:S(2)}) collective-permute-start(f32[136,128]{1,0:T(8,128)} %shard_map.75.refs_0_), channel_id=1, source_target_pairs={{0,16},{4,20},{8,24},{12,28},{16,0},{20,4},{24,8},{28,12},{1,17},{... | collective-permute-start | bytes 208904 | tf_op jit(solution)/shard_map/ppermute | solution.py:275
  8.1 9.3 %collective-permute-start = (f32[136,128]{1,0:T(8,128)}, f32[136,128]{1,0:T(8,128)S(1)}, u32[]{:S(2)}, u32[]{:S(2)}) collective-permute-start(f32[136,128]{1,0:T(8,128)} %shard_map.75.refs_0_), channel_id=1, source_target_pairs={{0,4},{4,0},{8,12},{12,8},{16,20},{20,16},{24,28},{28,24},{1,5},{5... | collective-permute-start | bytes 208904 | tf_op jit(solution)/shard_map/ppermute | solution.py:275
  9.7 7.8 %collective-permute-start.5 = (f32[136,128]{1,0:T(8,128)}, f32[136,128]{1,0:T(8,128)S(1)}, u32[]{:S(2)}, u32[]{:S(2)}) collective-permute-start(f32[136,128]{1,0:T(8,128)} %shard_map.75.refs_0_), channel_id=1, source_target_pairs={{0,24},{4,28},{8,16},{12,20},{16,8},{20,12},{24,0},{28,4},{1,25},{... | collective-permute-start | bytes 208904 | tf_op jit(solution)/shard_map/ppermute | solution.py:275
  9.9 7.6 %collective-permute-start.6 = (f32[136,128]{1,0:T(8,128)}, f32[136,128]{1,0:T(8,128)S(1)}, u32[]{:S(2)}, u32[]{:S(2)}) collective-permute-start(f32[136,128]{1,0:T(8,128)} %shard_map.75.refs_0_), channel_id=1, source_target_pairs={{0,28},{4,24},{8,20},{12,16},{16,12},{20,8},{24,4},{28,0},{1,29},{... | collective-permute-start | bytes 208904 | tf_op jit(solution)/shard_map/ppermute | solution.py:275
  13.4 4.5 %collective-permute-start.2 = (f32[136,128]{1,0:T(8,128)S(1)}, f32[136,128]{1,0:T(8,128)S(1)}, u32[]{:S(2)}, u32[]{:S(2)}) collective-permute-start(f32[136,128]{1,0:T(8,128)S(1)} %collective-permute-done.1.refs_2_), channel_id=1, source_target_pairs={{0,4},{4,0},{8,12},{12,8},{16,20},{20,16},{24,28},{28,24},{1,5},{5... | collective-permute-start | bytes 208904 | tf_op jit(solution)/shard_map/ppermute | solution.py:275
  15.0 4.3 %collective-permute-start.4 = (f32[136,128]{1,0:T(8,128)S(1)}, f32[136,128]{1,0:T(8,128)S(1)}, u32[]{:S(2)}, u32[]{:S(2)}) collective-permute-start(f32[136,128]{1,0:T(8,128)S(1)} %collective-permute-done.3.refs_4_), channel_id=1, source_target_pairs={{0,4},{4,0},{8,12},{12,8},{16,20},{20,16},{24,28},{28,24},{1,5},{5... | collective-permute-start | bytes 208904 | tf_op jit(solution)/shard_map/ppermute | solution.py:275
  20.1 10.2 %collective-permute-start.8 = (f32[928,128]{1,0:T(8,128)S(1)}, f32[928,128]{1,0:T(8,128)S(1)}, u32[]{:S(2)}, u32[]{:S(2)}) collective-permute-start(f32[928,128]{1,0:T(8,128)S(1)} %get-tuple-element.19), channel_id=1, source_target_pairs={{0,2},{1,3},{2,0},{3,1},{4,6},{5,7},{6,4},{7,5},{8,10},{9,11},{10,... | collective-permute-start | bytes 1425416 | tf_op jit(solution)/shard_map/ppermute | solution.py:349
  21.6 15.4 %all-to-all-start = ((f32[8,2,16,512]{3,2,1,0:T(8,128)}), f32[8,2,16,512]{3,2,1,0:T(8,128)S(1)}, u32[]{:S(2)}, u32[]{:S(2)}) async-start(f32[8,2,16,512]{3,2,1,0:T(8,128)} %shard_map.74.ahead), calls=%async_computation | async-start | bytes 1048576 | tf_op jit(solution)/shard_map/all_to_all | solution.py:332
  26.6 3.7 %collective-permute-start.7 = (f32[1056,128]{1,0:T(8,128)S(1)}, f32[1056,128]{1,0:T(8,128)S(1)}, u32[]{:S(2)}, u32[]{:S(2)}) collective-permute-start(f32[1056,128]{1,0:T(8,128)S(1)} %get-tuple-element.18.own), channel_id=1, source_target_pairs={{0,1},{1,0},{2,3},{3,2},{4,5},{5,4},{6,7},{7,6},{8,9},{9,8},{10,11... | collective-permute-start | bytes 1622024 | tf_op jit(solution)/shard_map/ppermute | solution.py:350
  30.2 1.8 %collective-permute-start.9 = (f32[928,128]{1,0:T(8,128)S(1)}, f32[928,128]{1,0:T(8,128)S(1)}, u32[]{:S(2)}, u32[]{:S(2)}) collective-permute-start(f32[928,128]{1,0:T(8,128)S(1)} %collective-permute-done.8.far), channel_id=1, source_target_pairs={{0,1},{1,0},{2,3},{3,2},{4,5},{5,4},{6,7},{7,6},{8,9},{9,8},{10,11... | collective-permute-start | bytes 1425416 | tf_op jit(solution)/shard_map/ppermute | solution.py:351
  37.6 7.8 %collective-permute-start.14 = (f32[2,2,16,512]{3,2,1,0:T(8,128)S(1)}, f32[2,2,16,512]{3,2,1,0:T(8,128)S(1)}, u32[]{:S(2)}, u32[]{:S(2)}) collective-permute-start(f32[2,2,16,512]{3,2,1,0:T(8,128)S(1)} %get-tuple-element.25), channel_id=1, source_target_pairs={{0,8},{4,12},{8,0},{12,4},{16,24},{20,28},{24,16},{28,20},{1,9},{5... | collective-permute-start | bytes 393224 | tf_op jit(solution)/shard_map/ppermute | solution.py:275
  37.7 10.2 %collective-permute-start.10 = (f32[1,2,16,512]{3,2,1,0:T(8,128)S(1)}, f32[1,2,16,512]{3,2,1,0:T(8,128)S(1)}, u32[]{:S(2)}, u32[]{:S(2)}) collective-permute-start(f32[1,2,16,512]{3,2,1,0:T(8,128)S(1)} %get-tuple-element.21), channel_id=1, source_target_pairs={{0,16},{4,20},{8,24},{12,28},{16,0},{20,4},{24,8},{28,12},{1,17},{... | collective-permute-start | bytes 196616 | tf_op jit(solution)/shard_map/ppermute | solution.py:275
  39.4 11.3 %collective-permute-start.11 = (f32[1,2,16,512]{3,2,1,0:T(8,128)S(1)}, f32[1,2,16,512]{3,2,1,0:T(8,128)S(1)}, u32[]{:S(2)}, u32[]{:S(2)}) collective-permute-start(f32[1,2,16,512]{3,2,1,0:T(8,128)S(1)} %get-tuple-element.22), channel_id=1, source_target_pairs={{0,20},{4,16},{8,28},{12,24},{16,4},{20,0},{24,12},{28,8},{1,21},{... | collective-permute-start | bytes 196616 | tf_op jit(solution)/shard_map/ppermute | solution.py:275
  41.6 9.1 %collective-permute-start.12 = (f32[1,2,16,512]{3,2,1,0:T(8,128)S(1)}, f32[1,2,16,512]{3,2,1,0:T(8,128)S(1)}, u32[]{:S(2)}, u32[]{:S(2)}) collective-permute-start(f32[1,2,16,512]{3,2,1,0:T(8,128)S(1)} %get-tuple-element.23), channel_id=1, source_target_pairs={{0,24},{4,28},{8,16},{12,20},{16,8},{20,12},{24,0},{28,4},{1,25},{... | collective-permute-start | bytes 196616 | tf_op jit(solution)/shard_map/ppermute | solution.py:275
  43.1 7.6 %collective-permute-start.13 = (f32[1,2,16,512]{3,2,1,0:T(8,128)S(1)}, f32[1,2,16,512]{3,2,1,0:T(8,128)S(1)}, u32[]{:S(2)}, u32[]{:S(2)}) collective-permute-start(f32[1,2,16,512]{3,2,1,0:T(8,128)S(1)} %get-tuple-element.24), channel_id=1, source_target_pairs={{0,28},{4,24},{8,20},{12,16},{16,12},{20,8},{24,4},{28,0},{1,29},{... | collective-permute-start | bytes 196616 | tf_op jit(solution)/shard_map/ppermute | solution.py:275
  45.4 6.1 %collective-permute-start.15 = (f32[1,2,16,512]{3,2,1,0:T(8,128)S(1)}, f32[1,2,16,512]{3,2,1,0:T(8,128)S(1)}, u32[]{:S(2)}, u32[]{:S(2)}) collective-permute-start(f32[1,2,16,512]{3,2,1,0:T(8,128)S(1)} %get-tuple-element.26), channel_id=1, source_target_pairs={{0,4},{4,0},{8,12},{12,8},{16,20},{20,16},{24,28},{28,24},{1,5},{5... | collective-permute-start | bytes 196616 | tf_op jit(solution)/shard_map/ppermute | solution.py:275
  47.9 4.3 %collective-permute-start.16 = (f32[1,2,16,512]{3,2,1,0:T(8,128)S(1)}, f32[1,2,16,512]{3,2,1,0:T(8,128)S(1)}, u32[]{:S(2)}, u32[]{:S(2)}) collective-permute-start(f32[1,2,16,512]{3,2,1,0:T(8,128)S(1)} %slice.4), channel_id=1, source_target_pairs={{0,4},{4,0},{8,12},{12,8},{16,20},{20,16},{24,28},{28,24},{1,5},{5... | collective-permute-start | bytes 196616 | tf_op jit(solution)/shard_map/ppermute | solution.py:275

commit v22 on v18

--- a/solution.py
+++ b/solution.py
@@ -291,7 +291,7 @@
     near = hop(parts[5], PARTS[5][0], n)
     beside, onward = hop(parts[6], 1, n), hop(near[1:], 1, n)
     out = place(shape, whole, [(i, 0, PARTS[i][0]) for i in range(5)], far, moved=10**6)
-    return place(shape, whole, [(0, 0, 2), (1, 0, 1), (2, 0, 3)], [near, beside, onward], out, moved=10**6)
+    return place(shape, whole, [(0, 0, 2), (1, 0, 3), (2, 0, 1)], [near, onward, beside], out, moved=10**6)
 
 
 def body(prior, channel_weights, obs_owner, obs_offset, obs_value, obs_error, ancestors):

time: 53 us -> 53 us (level)
  no operation moved by 1% of the time
where the time goes in v22:
time: 53 us; the launch traced here: 52.8 us
  starting transfers between devices  30.2 us (57%)
  waiting for transfers between devices  12.6 us (24%)
  Pallas kernels  9.86 us (19%)
    ppermute x14, starting transfers between devices, hop(): return lax.ppermute(value, 'grid', [(j, j ^ distance) for j in range(n)])  23.7 us
    all_to_all x1, starting transfers between devices, body(): fields = lax.all_to_all(send, 'grid', 0, 0, tiled=True)  4.95 us
    ppermute x14, waiting for transfers between devices, hop(): return lax.ppermute(value, 'grid', [(j, j ^ distance) for j in range(n)])  4.86 us
    ppermute x1, waiting for transfers between devices, body(): far = lax.ppermute(slim, 'lev', [(j, j ^ 2) for j in range(lev)])  3.64 us
    pallas_call x1, Pallas kernels, body(): call(functools.partial(chain_kernel, (members, groups, count)), shape((8,...  2.72 us
    pallas_call x1, Pallas kernels, body(): call(functools.partial(pick_kernel, (slab, depth, block_cells, groups, co...  2.39 us
    all_to_all x1, waiting for transfers between devices, body(): fields = lax.all_to_all(send, 'grid', 0, 0, tiled=True)  2.22 us
    ppermute x1, waiting for transfers between devices, body(): cross = lax.ppermute(far, 'lev', [(j, j ^ 1) for j in range(lev)])  1.83 us
  transfers between devices with their start and end apart: 18, of which 8 were waited for; matrix products, arithmetic and copies ran while one was open for 0% of the time, Pallas kernels for 10%

profile of v22, /device:TPU:0, one launch (start us, length us, event | category | flops | bytes accessed | tf_op | source)
XLA Modules:
  0.0 52.8 jit_solution(18162492336906541651)
XLA Ops:
  0.0 2.4 %shard_map.75.refs_0_ = f32[136,128]{1,0:T(8,128)} custom-call(s32[4]{0:T(128)} %owner.3, f32[2,4]{1,0:T(2,128)} %refs_1_.1, s32[4,4,64]{2,1,0:T(4,128)} %refs_2_.1, s32[4,1,128]{2,1,0:T(1,128)} %bitcast.1, f32[16,2,4096]{2,1,0:T(2,128)} %refs_4_.1), custom_call_target="tpu_custom_call" | custom-call | bytes 1000000 | tf_op jit(solution)/shard_map/pallas_call | solution.py:310
  2.4 0.0 copy-start.2
  2.4 0.0 copy-start.3
  2.4 0.0 copy-start.4
  2.4 0.0 copy-start.5
  2.4 0.0 copy-start.6
  2.5 3.1 %collective-permute-start.1 = (f32[136,128]{1,0:T(8,128)}, f32[136,128]{1,0:T(8,128)S(1)}, u32[]{:S(2)}, u32[]{:S(2)}) collective-permute-start(f32[136,128]{1,0:T(8,128)} %shard_map.75.refs_0_), channel_id=1, source_target_pairs={{0,8},{4,12},{8,0},{12,4},{16,24},{20,28},{24,16},{28,20},{1,9},{5... | collective-permute-start | bytes 208904 | tf_op jit(solution)/shard_map/ppermute | solution.py:275
  5.6 2.6 %collective-permute-start.3 = (f32[136,128]{1,0:T(8,128)}, f32[136,128]{1,0:T(8,128)S(1)}, u32[]{:S(2)}, u32[]{:S(2)}) collective-permute-start(f32[136,128]{1,0:T(8,128)} %shard_map.75.refs_0_), channel_id=1, source_target_pairs={{0,16},{4,20},{8,24},{12,28},{16,0},{20,4},{24,8},{28,12},{1,17},{... | collective-permute-start | bytes 208904 | tf_op jit(solution)/shard_map/ppermute | solution.py:275
  8.1 1.5 %collective-permute-start = (f32[136,128]{1,0:T(8,128)}, f32[136,128]{1,0:T(8,128)S(1)}, u32[]{:S(2)}, u32[]{:S(2)}) collective-permute-start(f32[136,128]{1,0:T(8,128)} %shard_map.75.refs_0_), channel_id=1, source_target_pairs={{0,4},{4,0},{8,12},{12,8},{16,20},{20,16},{24,28},{28,24},{1,5},{5... | collective-permute-start | bytes 208904 | tf_op jit(solution)/shard_map/ppermute | solution.py:275
  9.7 0.2 collective-permute-start.5
  9.9 3.5 %collective-permute-start.6 = (f32[136,128]{1,0:T(8,128)}, f32[136,128]{1,0:T(8,128)S(1)}, u32[]{:S(2)}, u32[]{:S(2)}) collective-permute-start(f32[136,128]{1,0:T(8,128)} %shard_map.75.refs_0_), channel_id=1, source_target_pairs={{0,28},{4,24},{8,20},{12,16},{16,12},{20,8},{24,4},{28,0},{1,29},{... | collective-permute-start | bytes 208904 | tf_op jit(solution)/shard_map/ppermute | solution.py:275
  13.4 0.0 collective-permute-done.1.refs_2_
  13.4 1.5 %collective-permute-start.2 = (f32[136,128]{1,0:T(8,128)S(1)}, f32[136,128]{1,0:T(8,128)S(1)}, u32[]{:S(2)}, u32[]{:S(2)}) collective-permute-start(f32[136,128]{1,0:T(8,128)S(1)} %collective-permute-done.1.refs_2_), channel_id=1, source_target_pairs={{0,4},{4,0},{8,12},{12,8},{16,20},{20,16},{24,28},{28,24},{1,5},{5... | collective-permute-start | bytes 208904 | tf_op jit(solution)/shard_map/ppermute | solution.py:275
  15.0 0.0 collective-permute-done.3.refs_4_
  15.0 0.6 %collective-permute-start.4 = (f32[136,128]{1,0:T(8,128)S(1)}, f32[136,128]{1,0:T(8,128)S(1)}, u32[]{:S(2)}, u32[]{:S(2)}) collective-permute-start(f32[136,128]{1,0:T(8,128)S(1)} %collective-permute-done.3.refs_4_), channel_id=1, source_target_pairs={{0,4},{4,0},{8,12},{12,8},{16,20},{20,16},{24,28},{28,24},{1,5},{5... | collective-permute-start | bytes 208904 | tf_op jit(solution)/shard_map/ppermute | solution.py:275
  15.6 0.9 %shard_map.74.ahead = f32[8,2,16,512]{3,2,1,0:T(8,128)} custom-call(f32[16,2,4096]{2,1,0:T(2,128)S(1)} %copy-done), custom_call_target="tpu_custom_call" | custom-call | bytes 1000000 | tf_op jit(solution)/shard_map/pallas_call | solution.py:326
  16.5 1.0 %shard_map.73 = (f32[32,128]{1,0:T(8,128)S(1)}, f32[5,128,128]{2,1,0:T(8,128)S(1)}) custom-call(s32[4]{0:T(128)S(1)} %copy-done.4, s32[4,4,64]{2,1,0:T(4,128)S(1)} %copy-done.2, f32[4,1,64]{2,1,0:T(1,128)S(1)} %copy-done.5, f32[4,1,64]{2,1,0:T(1,128)S(1)} %copy-done.6, s32[4,1,128]{2,1,0:T(1,128)S(1)} %bitcast.2), custom_call_target="tpu_custom_call" | custom-call | bytes 1000000 | tf_op jit(solution)/shard_map/pallas_call | solution.py:334
  17.5 0.0 collective-permute-done.refs_1_
  17.5 0.0 collective-permute-done.5.refs_6_
  17.5 0.0 collective-permute-done.6.refs_7_
  17.5 0.4 collective-permute-done.2.refs_3_
  18.0 1.3 %collective-permute-done.4.refs_5_ = f32[136,128]{1,0:T(8,128)S(1)} collective-permute-done((f32[136,128]{1,0:T(8,128)S(1)}, f32[136,128]{1,0:T(8,128)S(1)}, u32[]{:S(2)}, u32[]{:S(2)}) %collective-permute-start.4) | collective-permute-done | bytes 69664 | tf_op jit(solution)/shard_map/ppermute | solution.py:275
  19.3 0.8 %shard_map.76 = (f32[1056,128]{1,0:T(8,128)S(1)}, f32[928,128]{1,0:T(8,128)S(1)}) custom-call(s32[4]{0:T(128)S(1)} %copy-done.4, f32[32,128]{1,0:T(8,128)S(1)} %get-tuple-element.17.rows, f32[8,2,16,512]{3,2,1,0:T(8,128)} %shard_map.74.ahead, f32[136,128]{1,0:T(8,128)S(1)} %copy-done.1, f32[136,128]{1,0:T(8,128)S(1)} %collective-permute-done.refs_1_, ...), custom_call_target="tpu_custom_call" | custom-call | bytes 1000000 | tf_op jit(solution)/shard_map/pallas_call | solution.py:342
  20.1 1.6 %collective-permute-start.8 = (f32[928,128]{1,0:T(8,128)S(1)}, f32[928,128]{1,0:T(8,128)S(1)}, u32[]{:S(2)}, u32[]{:S(2)}) collective-permute-start(f32[928,128]{1,0:T(8,128)S(1)} %get-tuple-element.19), channel_id=1, source_target_pairs={{0,2},{1,3},{2,0},{3,1},{4,6},{5,7},{6,4},{7,5},{8,10},{9,11},{10,... | collective-permute-start | bytes 1425416 | tf_op jit(solution)/shard_map/ppermute | solution.py:349
  21.6 4.9 %all-to-all-start = ((f32[8,2,16,512]{3,2,1,0:T(8,128)}), f32[8,2,16,512]{3,2,1,0:T(8,128)S(1)}, u32[]{:S(2)}, u32[]{:S(2)}) async-start(f32[8,2,16,512]{3,2,1,0:T(8,128)} %shard_map.74.ahead), calls=%async_computation | async-start | bytes 1048576 | tf_op jit(solution)/shard_map/all_to_all | solution.py:332
  26.6 3.6 %collective-permute-done.8.far = f32[928,128]{1,0:T(8,128)S(1)} collective-permute-done((f32[928,128]{1,0:T(8,128)S(1)}, f32[928,128]{1,0:T(8,128)S(1)}, u32[]{:S(2)}, u32[]{:S(2)}) %collective-permute-start.8) | collective-permute-done | bytes 475168 | tf_op jit(solution)/shard_map/ppermute | solution.py:349
  30.2 0.0 collective-permute-start.9
  30.2 0.0 collective-permute-done.7.near
  30.2 1.8 %collective-permute-done.9.cross = f32[928,128]{1,0:T(8,128)S(1)} collective-permute-done((f32[928,128]{1,0:T(8,128)S(1)}, f32[928,128]{1,0:T(8,128)S(1)}, u32[]{:S(2)}, u32[]{:S(2)}) %collective-permute-start.9) | collective-permute-done | bytes 475168 | tf_op jit(solution)/shard_map/ppermute | solution.py:351
  32.1 2.7 %shard_map.77.pull = f32[8,128]{1,0:T(8,128)S(1)} custom-call(f32[1056,128]{1,0:T(8,128)S(1)} %get-tuple-element.18.own, f32[1056,128]{1,0:T(8,128)S(1)} %collective-permute-done.7.near, f32[928,128]{1,0:T(8,128)S(1)} %collective-permute-done.8.far, f32[928,128]{1,0:T(8,128)S(1)} %collective-permute-done.9.cross, f32[5,128,128]{2,1,0:T(8,128)S(1)} %get-tuple-element.16.steps), custom_call_target="tpu_custom_call" | custom-call | bytes 100000 | tf_op jit(solution)/shard_map/pallas_call | solution.py:353
  34.8 2.2 %all-to-all-done.fields = f32[8,2,16,512]{3,2,1,0:T(8,128)S(1)} async-done(((f32[8,2,16,512]{3,2,1,0:T(8,128)}), f32[8,2,16,512]{3,2,1,0:T(8,128)S(1)}, u32[]{:S(2)}, u32[]{:S(2)}) %all-to-all-start) | async-done | bytes 524320 | tf_op jit(solution)/shard_map/all_to_all | solution.py:332
  37.0 0.6 %shard_map.78 = (f32[1,2,16,512]{3,2,1,0:T(8,128)S(1)}, f32[1,2,16,512]{3,2,1,0:T(8,128)S(1)}, f32[1,2,16,512]{3,2,1,0:T(8,128)S(1)}, f32[1,2,16,512]{3,2,1,0:T(...) custom-call(f32[5,128,128]{2,1,0:T(8,128)S(1)} %get-tuple-element.16.steps, ...), custom_call_target="tpu_custom_call" | custom-call | flops 100000000 | bytes 1000000 | tf_op jit(solution)/shard_map/pallas_call | solution.py:364
  37.6 0.1 collective-permute-start.14
  37.7 1.8 %collective-permute-start.10 = (f32[1,2,16,512]{3,2,1,0:T(8,128)S(1)}, f32[1,2,16,512]{3,2,1,0:T(8,128)S(1)}, u32[]{:S(2)}, u32[]{:S(2)}) collective-permute-start(f32[1,2,16,512]{3,2,1,0:T(8,128)S(1)} %get-tuple-element.21), channel_id=1, source_target_pairs={{0,16},{4,20},{8,24},{12,28},{16,0},{20,4},{24,8},{28,12},{1,17},{... | collective-permute-start | bytes 196616 | tf_op jit(solution)/shard_map/ppermute | solution.py:275
  39.4 2.2 %collective-permute-start.11 = (f32[1,2,16,512]{3,2,1,0:T(8,128)S(1)}, f32[1,2,16,512]{3,2,1,0:T(8,128)S(1)}, u32[]{:S(2)}, u32[]{:S(2)}) collective-permute-start(f32[1,2,16,512]{3,2,1,0:T(8,128)S(1)} %get-tuple-element.22), channel_id=1, source_target_pairs={{0,20},{4,16},{8,28},{12,24},{16,4},{20,0},{24,12},{28,8},{1,21},{... | collective-permute-start | bytes 196616 | tf_op jit(solution)/shard_map/ppermute | solution.py:275
  41.6 1.5 %collective-permute-start.12 = (f32[1,2,16,512]{3,2,1,0:T(8,128)S(1)}, f32[1,2,16,512]{3,2,1,0:T(8,128)S(1)}, u32[]{:S(2)}, u32[]{:S(2)}) collective-permute-start(f32[1,2,16,512]{3,2,1,0:T(8,128)S(1)} %get-tuple-element.23), channel_id=1, source_target_pairs={{0,24},{4,28},{8,16},{12,20},{16,8},{20,12},{24,0},{28,4},{1,25},{... | collective-permute-start | bytes 196616 | tf_op jit(solution)/shard_map/ppermute | solution.py:275
  43.1 2.3 %collective-permute-start.13 = (f32[1,2,16,512]{3,2,1,0:T(8,128)S(1)}, f32[1,2,16,512]{3,2,1,0:T(8,128)S(1)}, u32[]{:S(2)}, u32[]{:S(2)}) collective-permute-start(f32[1,2,16,512]{3,2,1,0:T(8,128)S(1)} %get-tuple-element.24), channel_id=1, source_target_pairs={{0,28},{4,24},{8,20},{12,16},{16,12},{20,8},{24,4},{28,0},{1,29},{... | collective-permute-start | bytes 196616 | tf_op jit(solution)/shard_map/ppermute | solution.py:275
  45.4 0.0 collective-permute-done.14.refs_1_
  45.4 1.5 %collective-permute-start.16 = (f32[1,2,16,512]{3,2,1,0:T(8,128)S(1)}, f32[1,2,16,512]{3,2,1,0:T(8,128)S(1)}, u32[]{:S(2)}, u32[]{:S(2)}) collective-permute-start(f32[1,2,16,512]{3,2,1,0:T(8,128)S(1)} %get-tuple-element.26), channel_id=1, source_target_pairs={{0,4},{4,0},{8,12},{12,8},{16,20},{20,16},{24,28},{28,24},{1,5},{5... | collective-permute-start | bytes 196616 | tf_op jit(solution)/shard_map/ppermute | solution.py:275
  46.9 0.9 %collective-permute-done.10.refs_1_ = f32[1,2,16,512]{3,2,1,0:T(8,128)S(1)} collective-permute-done((f32[1,2,16,512]{3,2,1,0:T(8,128)S(1)}, f32[1,2,16,512]{3,2,1,0:T(8,128)S(1)}, u32[]{:S(2)}, u32[]{:S(2)}) %collective-permute-start.10) | collective-permute-done | bytes 65568 | tf_op jit(solution)/shard_map/ppermute | solution.py:275
  47.8 1.3 %collective-permute-start.15 = (f32[1,2,16,512]{3,2,1,0:T(8,128)S(1)}, f32[1,2,16,512]{3,2,1,0:T(8,128)S(1)}, u32[]{:S(2)}, u32[]{:S(2)}) collective-permute-start(f32[1,2,16,512]{3,2,1,0:T(8,128)S(1)} %slice.4), channel_id=1, source_target_pairs={{0,4},{4,0},{8,12},{12,8},{16,20},{20,16},{24,28},{28,24},{1,5},{5... | collective-permute-start | bytes 196616 | tf_op jit(solution)/shard_map/ppermute | solution.py:275
  49.2 1.5 %collective-permute-done.11.refs_2_ = f32[1,2,16,512]{3,2,1,0:T(8,128)S(1)} collective-permute-done((f32[1,2,16,512]{3,2,1,0:T(8,128)S(1)}, f32[1,2,16,512]{3,2,1,0:T(8,128)S(1)}, u32[]{:S(2)}, u32[]{:S(2)}) %collective-permute-start.11) | collective-permute-done | bytes 65568 | tf_op jit(solution)/shard_map/ppermute | solution.py:275
  50.7 0.0 collective-permute-done.12.refs_3_
  50.7 0.0 collective-permute-done.13.refs_4_
  50.7 0.8 %shard_map.79.refs_0_ = f32[16,2,4096]{2,1,0:T(2,128)} custom-call(f32[1,2,16,512]{3,2,1,0:T(8,128)S(1)} %get-tuple-element.20.refs_0_, f32[1,2,16,512]{3,2,1,0:T(8,128)S(1)} %collective-permute-done.10.refs_1_, f32[1,2,16,512]{3,2,1,0:T(8,128)S(1)} %collective-permute-done.11.refs_2_, f32[1,2,16,512]{3,2,1,0:T(8,128)S(1)} %collective-permute-done.12.refs_3_, ...), custom_call_target="tpu_custom_call" | custom-call | bytes 1000000 | tf_op jit(solution)/shard_map/pallas_call | solution.py:260
  51.5 0.0 collective-permute-done.16.refs_3_
  51.5 0.6 %collective-permute-done.15.refs_2_ = f32[1,2,16,512]{3,2,1,0:T(8,128)S(1)} collective-permute-done((f32[1,2,16,512]{3,2,1,0:T(8,128)S(1)}, f32[1,2,16,512]{3,2,1,0:T(8,128)S(1)}, u32[]{:S(2)}, u32[]{:S(2)}) %collective-permute-start.15) | collective-permute-done | bytes 65568 | tf_op jit(solution)/shard_map/ppermute | solution.py:275
  52.1 0.7 %shard_map.80 = f32[16,2,4096]{2,1,0:T(2,128)} custom-call(f32[16,2,4096]{2,1,0:T(2,128)} %shard_map.79.refs_0_, f32[2,2,16,512]{3,2,1,0:T(8,128)S(1)} %collective-permute-done.14.refs_1_, f32[1,2,16,512]{3,2,1,0:T(8,128)S(1)} %collective-permute-done.15.refs_2_, f32[1,2,16,512]{3,2,1,0:T(8,128)S(1)} %collective-permute-done.16.refs_3_), custom_call_target="tpu_custom_call", output_to_operand_aliasing={{}: (0, {})} | custom-call | bytes 1000000 | tf_op jit(solution)/shard_map/pallas_call | solution.py:260
  (11 shorter events, 0.0 us)
Async XLA Ops:
  0.0 15.6 %copy-start = (f32[16,2,4096]{2,1,0:T(2,128)S(1)}, f32[16,2,4096]{2,1,0:T(2,128)}, u32[]{:S(2)}) copy-start(f32[16,2,4096]{2,1,0:T(2,128)} %refs_4_.1) | copy-start | bytes 1572868
  2.4 14.1 %copy-start.2 = (s32[4,4,64]{2,1,0:T(4,128)S(1)}, s32[4,4,64]{2,1,0:T(4,128)}, u32[]{:S(2)}) copy-start(s32[4,4,64]{2,1,0:T(4,128)} %refs_2_.1) | copy-start | bytes 12292
  2.4 14.0 %copy-start.3 = (s32[4,1,1,128]{3,2,1,0:T(1,128)S(1)}, s32[4,1,1,128]{3,2,1,0:T(1,128)}, u32[]{:S(2)}) copy-start(s32[4,1,1,128]{3,2,1,0:T(1,128)} %param.13) | copy-start | bytes 6148
  2.4 14.0 %copy-start.4 = (s32[4]{0:T(128)S(1)}, s32[4]{0:T(128)}, u32[]{:S(2)}) copy-start(s32[4]{0:T(128)} %owner.3) | copy-start | bytes 52
  2.4 14.0 %copy-start.5 = (f32[4,1,64]{2,1,0:T(1,128)S(1)}, f32[4,1,64]{2,1,0:T(1,128)}, u32[]{:S(2)}) copy-start(f32[4,1,64]{2,1,0:T(1,128)} %values.1) | copy-start | bytes 3076
  2.4 14.0 %copy-start.6 = (f32[4,1,64]{2,1,0:T(1,128)S(1)}, f32[4,1,64]{2,1,0:T(1,128)}, u32[]{:S(2)}) copy-start(f32[4,1,64]{2,1,0:T(1,128)} %errors.1) | copy-start | bytes 3076
  2.5 16.8 %copy-start.1 = (f32[136,128]{1,0:T(8,128)S(1)}, f32[136,128]{1,0:T(8,128)}, u32[]{:S(2)}) copy-start(f32[136,128]{1,0:T(8,128)} %shard_map.75.refs_0_) | copy-start | bytes 208900
  2.5 11.0 %collective-permute-start.1 = (f32[136,128]{1,0:T(8,128)}, f32[136,128]{1,0:T(8,128)S(1)}, u32[]{:S(2)}, u32[]{:S(2)}) collective-permute-start(f32[136,128]{1,0:T(8,128)} %shard_map.75.refs_0_), channel_id=1, source_target_pairs={{0,8},{4,12},{8,0},{12,4},{16,24},{20,28},{24,16},{28,20},{1,9},{5... | collective-permute-start | bytes 208904 | tf_op jit(solution)/shard_map/ppermute | solution.py:275
  5.6 9.4 %collective-permute-start.3 = (f32[136,128]{1,0:T(8,128)}, f32[136,128]{1,0:T(8,128)S(1)}, u32[]{:S(2)}, u32[]{:S(2)}) collective-permute-start(f32[136,128]{1,0:T(8,128)} %shard_map.75.refs_0_), channel_id=1, source_target_pairs={{0,16},{4,20},{8,24},{12,28},{16,0},{20,4},{24,8},{28,12},{1,17},{... | collective-permute-start | bytes 208904 | tf_op jit(solution)/shard_map/ppermute | solution.py:275
  8.1 9.3 %collective-permute-start = (f32[136,128]{1,0:T(8,128)}, f32[136,128]{1,0:T(8,128)S(1)}, u32[]{:S(2)}, u32[]{:S(2)}) collective-permute-start(f32[136,128]{1,0:T(8,128)} %shard_map.75.refs_0_), channel_id=1, source_target_pairs={{0,4},{4,0},{8,12},{12,8},{16,20},{20,16},{24,28},{28,24},{1,5},{5... | collective-permute-start | bytes 208904 | tf_op jit(solution)/shard_map/ppermute | solution.py:275
  9.7 7.8 %collective-permute-start.5 = (f32[136,128]{1,0:T(8,128)}, f32[136,128]{1,0:T(8,128)S(1)}, u32[]{:S(2)}, u32[]{:S(2)}) collective-permute-start(f32[136,128]{1,0:T(8,128)} %shard_map.75.refs_0_), channel_id=1, source_target_pairs={{0,24},{4,28},{8,16},{12,20},{16,8},{20,12},{24,0},{28,4},{1,25},{... | collective-permute-start | bytes 208904 | tf_op jit(solution)/shard_map/ppermute | solution.py:275
  9.9 7.6 %collective-permute-start.6 = (f32[136,128]{1,0:T(8,128)}, f32[136,128]{1,0:T(8,128)S(1)}, u32[]{:S(2)}, u32[]{:S(2)}) collective-permute-start(f32[136,128]{1,0:T(8,128)} %shard_map.75.refs_0_), channel_id=1, source_target_pairs={{0,28},{4,24},{8,20},{12,16},{16,12},{20,8},{24,4},{28,0},{1,29},{... | collective-permute-start | bytes 208904 | tf_op jit(solution)/shard_map/ppermute | solution.py:275
  13.4 4.5 %collective-permute-start.2 = (f32[136,128]{1,0:T(8,128)S(1)}, f32[136,128]{1,0:T(8,128)S(1)}, u32[]{:S(2)}, u32[]{:S(2)}) collective-permute-start(f32[136,128]{1,0:T(8,128)S(1)} %collective-permute-done.1.refs_2_), channel_id=1, source_target_pairs={{0,4},{4,0},{8,12},{12,8},{16,20},{20,16},{24,28},{28,24},{1,5},{5... | collective-permute-start | bytes 208904 | tf_op jit(solution)/shard_map/ppermute | solution.py:275
  15.0 4.3 %collective-permute-start.4 = (f32[136,128]{1,0:T(8,128)S(1)}, f32[136,128]{1,0:T(8,128)S(1)}, u32[]{:S(2)}, u32[]{:S(2)}) collective-permute-start(f32[136,128]{1,0:T(8,128)S(1)} %collective-permute-done.3.refs_4_), channel_id=1, source_target_pairs={{0,4},{4,0},{8,12},{12,8},{16,20},{20,16},{24,28},{28,24},{1,5},{5... | collective-permute-start | bytes 208904 | tf_op jit(solution)/shard_map/ppermute | solution.py:275
  20.1 10.2 %collective-permute-start.8 = (f32[928,128]{1,0:T(8,128)S(1)}, f32[928,128]{1,0:T(8,128)S(1)}, u32[]{:S(2)}, u32[]{:S(2)}) collective-permute-start(f32[928,128]{1,0:T(8,128)S(1)} %get-tuple-element.19), channel_id=1, source_target_pairs={{0,2},{1,3},{2,0},{3,1},{4,6},{5,7},{6,4},{7,5},{8,10},{9,11},{10,... | collective-permute-start | bytes 1425416 | tf_op jit(solution)/shard_map/ppermute | solution.py:349
  21.6 15.4 %all-to-all-start = ((f32[8,2,16,512]{3,2,1,0:T(8,128)}), f32[8,2,16,512]{3,2,1,0:T(8,128)S(1)}, u32[]{:S(2)}, u32[]{:S(2)}) async-start(f32[8,2,16,512]{3,2,1,0:T(8,128)} %shard_map.74.ahead), calls=%async_computation | async-start | bytes 1048576 | tf_op jit(solution)/shard_map/all_to_all | solution.py:332
  26.6 3.7 %collective-permute-start.7 = (f32[1056,128]{1,0:T(8,128)S(1)}, f32[1056,128]{1,0:T(8,128)S(1)}, u32[]{:S(2)}, u32[]{:S(2)}) collective-permute-start(f32[1056,128]{1,0:T(8,128)S(1)} %get-tuple-element.18.own), channel_id=1, source_target_pairs={{0,1},{1,0},{2,3},{3,2},{4,5},{5,4},{6,7},{7,6},{8,9},{9,8},{10,11... | collective-permute-start | bytes 1622024 | tf_op jit(solution)/shard_map/ppermute | solution.py:350
  30.2 1.8 %collective-permute-start.9 = (f32[928,128]{1,0:T(8,128)S(1)}, f32[928,128]{1,0:T(8,128)S(1)}, u32[]{:S(2)}, u32[]{:S(2)}) collective-permute-start(f32[928,128]{1,0:T(8,128)S(1)} %collective-permute-done.8.far), channel_id=1, source_target_pairs={{0,1},{1,0},{2,3},{3,2},{4,5},{5,4},{6,7},{7,6},{8,9},{9,8},{10,11... | collective-permute-start | bytes 1425416 | tf_op jit(solution)/shard_map/ppermute | solution.py:351
  37.6 7.8 %collective-permute-start.14 = (f32[2,2,16,512]{3,2,1,0:T(8,128)S(1)}, f32[2,2,16,512]{3,2,1,0:T(8,128)S(1)}, u32[]{:S(2)}, u32[]{:S(2)}) collective-permute-start(f32[2,2,16,512]{3,2,1,0:T(8,128)S(1)} %get-tuple-element.25), channel_id=1, source_target_pairs={{0,8},{4,12},{8,0},{12,4},{16,24},{20,28},{24,16},{28,20},{1,9},{5... | collective-permute-start | bytes 393224 | tf_op jit(solution)/shard_map/ppermute | solution.py:275
  37.7 10.2 %collective-permute-start.10 = (f32[1,2,16,512]{3,2,1,0:T(8,128)S(1)}, f32[1,2,16,512]{3,2,1,0:T(8,128)S(1)}, u32[]{:S(2)}, u32[]{:S(2)}) collective-permute-start(f32[1,2,16,512]{3,2,1,0:T(8,128)S(1)} %get-tuple-element.21), channel_id=1, source_target_pairs={{0,16},{4,20},{8,24},{12,28},{16,0},{20,4},{24,8},{28,12},{1,17},{... | collective-permute-start | bytes 196616 | tf_op jit(solution)/shard_map/ppermute | solution.py:275
  39.4 11.3 %collective-permute-start.11 = (f32[1,2,16,512]{3,2,1,0:T(8,128)S(1)}, f32[1,2,16,512]{3,2,1,0:T(8,128)S(1)}, u32[]{:S(2)}, u32[]{:S(2)}) collective-permute-start(f32[1,2,16,512]{3,2,1,0:T(8,128)S(1)} %get-tuple-element.22), channel_id=1, source_target_pairs={{0,20},{4,16},{8,28},{12,24},{16,4},{20,0},{24,12},{28,8},{1,21},{... | collective-permute-start | bytes 196616 | tf_op jit(solution)/shard_map/ppermute | solution.py:275
  41.6 9.1 %collective-permute-start.12 = (f32[1,2,16,512]{3,2,1,0:T(8,128)S(1)}, f32[1,2,16,512]{3,2,1,0:T(8,128)S(1)}, u32[]{:S(2)}, u32[]{:S(2)}) collective-permute-start(f32[1,2,16,512]{3,2,1,0:T(8,128)S(1)} %get-tuple-element.23), channel_id=1, source_target_pairs={{0,24},{4,28},{8,16},{12,20},{16,8},{20,12},{24,0},{28,4},{1,25},{... | collective-permute-start | bytes 196616 | tf_op jit(solution)/shard_map/ppermute | solution.py:275
  43.1 7.6 %collective-permute-start.13 = (f32[1,2,16,512]{3,2,1,0:T(8,128)S(1)}, f32[1,2,16,512]{3,2,1,0:T(8,128)S(1)}, u32[]{:S(2)}, u32[]{:S(2)}) collective-permute-start(f32[1,2,16,512]{3,2,1,0:T(8,128)S(1)} %get-tuple-element.24), channel_id=1, source_target_pairs={{0,28},{4,24},{8,20},{12,16},{16,12},{20,8},{24,4},{28,0},{1,29},{... | collective-permute-start | bytes 196616 | tf_op jit(solution)/shard_map/ppermute | solution.py:275
  45.4 6.1 %collective-permute-start.16 = (f32[1,2,16,512]{3,2,1,0:T(8,128)S(1)}, f32[1,2,16,512]{3,2,1,0:T(8,128)S(1)}, u32[]{:S(2)}, u32[]{:S(2)}) collective-permute-start(f32[1,2,16,512]{3,2,1,0:T(8,128)S(1)} %get-tuple-element.26), channel_id=1, source_target_pairs={{0,4},{4,0},{8,12},{12,8},{16,20},{20,16},{24,28},{28,24},{1,5},{5... | collective-permute-start | bytes 196616 | tf_op jit(solution)/shard_map/ppermute | solution.py:275
  47.8 4.3 %collective-permute-start.15 = (f32[1,2,16,512]{3,2,1,0:T(8,128)S(1)}, f32[1,2,16,512]{3,2,1,0:T(8,128)S(1)}, u32[]{:S(2)}, u32[]{:S(2)}) collective-permute-start(f32[1,2,16,512]{3,2,1,0:T(8,128)S(1)} %slice.4), channel_id=1, source_target_pairs={{0,4},{4,0},{8,12},{12,8},{16,20},{20,16},{24,28},{28,24},{1,5},{5... | collective-permute-start | bytes 196616 | tf_op jit(solution)/shard_map/ppermute | solution.py:275
